TPU v7x, 32 devices: a whole 2x2x4 slice. The times are simulated.
32 devices in a mesh: subset: 2 (over x), tile: 16 (over z, y, core).
Axes of the slice: x: 2, y: 2, z: 4, core: 2. Of those that a mesh axis runs over, the one named last changes fastest.
Arguments:
- images: float32 [64, 32768], P('subset', 'tile'), may hold values from 0.5 to 2
- system_tiles: bfloat16 [2, 512, 128, 128], P('subset', 'tile'), may hold values from 5.197525e-05 to 0.0025939941
- tile_vox: int32 [2, 512], P('subset', 'tile'), may hold values from 0 to 15, as said below
- tile_ray: int32 [2, 512], P('subset', 'tile'), may hold values from 0 to 15, as said below
- live_blocks: int32 [2, 16], P('subset', 'tile'), may hold values from 1 to 1, as said below
- counts: int32 [2, 64, 2048], P('subset', None, 'tile'), may hold values from 1 to 7
Outputs:
- updated: float32 [64, 32768], P('subset', 'tile')
Inputs may be any that keep to these rules, and one draw needn't show every extreme that they name: `tile_vox`: within each image tile and subset, the first 16 tile slots name every voxel block of that image tile once. `tile_ray`: in each subset every ray block is named by one of the first 1 tile slots of some image tile. `live_blocks`: slots in use are the first ones of an image tile; in every draw some image tile uses all of its blocks.
All inputs are finite; a program needn't handle non-finite values.
Results may differ from a plain program's by a relative error of at most 0.00063.
Values may be sent and summed in bfloat16 or wider, within the bound.
No kernel may reach another device: no remote copies, remote signals or barrier semaphores. Data moves between devices by JAX's collectives and lax.ppermute only.
A program may use at most 64 MiB of HBM per device.

v0:
```python
import jax
import jax.numpy as jnp
from jax import lax
from jax.sharding import PartitionSpec as P

TILE_GROUP = 32
ROUNDS = 4


HIGHEST = lax.Precision.HIGHEST


def shifted(array, axis, by):
    peers = lax.axis_size(axis)
    return lax.ppermute(array, axis, [(i, (i + by) % peers) for i in range(peers)])


def project(panel, system_tiles, voxel_index, ray_index, live_count, ray_total):
    frame_count = panel.shape[0]
    block_size = system_tiles.shape[-1]
    lowered = panel.astype(jnp.bfloat16).reshape(frame_count, -1, block_size)
    ray_ids = jnp.arange(ray_total, dtype=jnp.int32)

    def project_accumulate(counter, running):
        chosen = jnp.take(lowered, voxel_index, axis=1)
        contrib = jnp.einsum(
            "ftv,trv->tfr", chosen, system_tiles, preferred_element_type=jnp.float32
        )
        onehot = (ray_index[None, :] == ray_ids[:, None]).astype(jnp.float32)
        return running + jnp.einsum("bt,tfr->fbr", onehot, contrib, precision=HIGHEST)

    start_value = jnp.zeros((frame_count, ray_total, block_size), jnp.float32)
    summed = lax.fori_loop(0, live_count, project_accumulate, start_value)
    return summed.reshape(frame_count, ray_total * block_size)


def backproject(all_ratios, system_tiles, voxel_index, ray_index, live_count, vox_blocks):
    frame_count = all_ratios.shape[0]
    block_size = system_tiles.shape[-1]
    ratio_grid = all_ratios.reshape(frame_count, -1, block_size)
    vox_ids = jnp.arange(vox_blocks, dtype=jnp.int32)

    def backproject_accumulate(counter, running):
        chosen = jnp.take(ratio_grid, ray_index, axis=1)
        contrib = jnp.einsum(
            "ftr,trv->tfv", chosen, system_tiles, preferred_element_type=jnp.float32
        )
        onehot = (voxel_index[None, :] == vox_ids[:, None]).astype(jnp.float32)
        return running + jnp.einsum("ct,tfv->fcv", onehot, contrib, precision=HIGHEST)

    start_value = jnp.zeros((frame_count, vox_blocks, block_size), jnp.float32)
    return lax.fori_loop(0, live_count, backproject_accumulate, start_value)


def shards(images, system_tiles, tile_vox, tile_ray, live_blocks, counts):
    frame_count = images.shape[0]
    block_size = system_tiles.shape[-1]
    vox_blocks = images.shape[1] // block_size
    tile_set = system_tiles[0]
    voxel_index = tile_vox[0]
    ray_index = tile_ray[0]
    live_count = live_blocks[0, 0]
    measured = counts[0]
    ray_total = measured.shape[1] // block_size * lax.axis_size("tile")
    slot_count = tile_set.shape[0]
    tile_mask = (jnp.arange(slot_count, dtype=jnp.int32) // TILE_GROUP < live_count).astype(
        jnp.float32
    )
    column = jnp.einsum(
        "r,trv->tv",
        jnp.ones((block_size,), jnp.bfloat16),
        tile_set,
        preferred_element_type=jnp.float32,
    )
    vox_onehot = (voxel_index[None, :] == jnp.arange(vox_blocks, dtype=jnp.int32)[:, None]).astype(
        jnp.float32
    )
    sensitivity = jnp.einsum(
        "ct,tv->cv", vox_onehot, column * tile_mask[:, None], precision=HIGHEST
    )
    position = lax.axis_index("subset")
    subset_count = lax.axis_size("subset")
    panel = images
    for round_index in range(ROUNDS):
        panel_index = (position - round_index) % subset_count
        counts_now = lax.dynamic_slice_in_dim(measured, panel_index * frame_count, frame_count, 0)
        counts_now = counts_now.astype(jnp.float32)
        partial_value = project(panel, tile_set, voxel_index, ray_index, live_count, ray_total)
        own_sums = lax.psum_scatter(partial_value, "tile", scatter_dimension=1, tiled=True)
        ratios = (counts_now / own_sums).astype(jnp.bfloat16)
        all_ratios = lax.all_gather(ratios, "tile", axis=1, tiled=True)
        back_sum = backproject(all_ratios, tile_set, voxel_index, ray_index, live_count, vox_blocks)
        shaped = panel.reshape(frame_count, vox_blocks, block_size)
        panel = (shaped * back_sum / sensitivity[None]).reshape(
            frame_count, vox_blocks * block_size
        )
        if round_index + 1 < ROUNDS:
            panel = shifted(panel, "subset", 1)
    return panel


def solution(mesh):
    in_specs = (
        P("subset", "tile"),
        P("subset", "tile", None, None),
        P("subset", "tile"),
        P("subset", "tile"),
        P("subset", "tile"),
        P("subset", None, "tile"),
    )
    out_specs = P("subset", "tile")
    return jax.shard_map(shards, mesh=mesh, in_specs=in_specs, out_specs=out_specs, check_vma=False)
```

profile of v0, /device:TPU:0, one launch (start us, length us, event | category | flops | bytes accessed | tf_op | source)
XLA Modules:
  0.0 369.9 jit_solution(11571844102434476083)
XLA Ops:
  6.5 0.7 copy-done.4
  7.3 0.6 copy-done.3
  8.0 1.0 copy_bitcast_fusion.15
  8.9 0.6 gather_fusion
  9.6 0.7 fusion.16
  10.2 0.6 fusion.32
  10.9 1.4 while.96
  12.3 0.8 copy.83
  14.4 56.8 %reduce-scatter.5.cloned.1.call-done = f32[32,128]{1,0:T(8,128)} async-done(((f32[32,2048]{1,0:T(8,128)}), f32[32,128]{1,0:T(8,128)}) %reduce-scatter.5.cloned.1.call-update) | async-done | bytes 16400 | tf_op jit(solution)/shard_map/reduce_scatter | solution.py:89
  71.3 0.7 fusion.73
  72.0 19.8 %all_gather.12 = bf16[32,2048]{1,0:T(8,128)(2,1)S(1)} all-gather(bf16[32,128]{1,0:T(8,128)(2,1)S(1)} %fusion.73), channel_id=1, replica_groups=mesh['subset'=2,'tile'=16] {'tile'}, dimensions={1}, use_global_device_ids=true | all-gather | bytes 139264 | tf_op jit(solution)/shard_map/all_gather | solution.py:91
  92.8 0.6 fusion.30
  93.5 1.4 while.97
  95.0 1.5 collective-permute-start
  96.6 7.1 %collective-permute-done = f32[32,2048]{1,0:T(8,128)S(1)} collective-permute-done((f32[32,2048]{1,0:T(8,128)S(1)}, f32[32,2048]{1,0:T(8,128)S(1)}, u32[]{:S(2)}, u32[]{:S(2)}) %collective-permute-start) | collective-permute-done | bytes 262176 | tf_op jit(solution)/shard_map/ppermute | solution.py:15
  103.7 0.6 gather_fusion.2
  104.3 0.7 fusion.10
  105.0 0.6 fusion.28
  105.6 1.4 while.98
  107.0 0.8 copy.81
  107.9 52.6 %reduce-scatter.7.cloned.1.call-done = f32[32,128]{1,0:T(8,128)} async-done(((f32[32,2048]{1,0:T(8,128)}), f32[32,128]{1,0:T(8,128)}) %reduce-scatter.7.cloned.1.call-update) | async-done | bytes 16400 | tf_op jit(solution)/shard_map/reduce_scatter | solution.py:89
  160.5 0.7 fusion.72
  161.2 19.8 %all_gather.13 = bf16[32,2048]{1,0:T(8,128)(2,1)S(1)} all-gather(bf16[32,128]{1,0:T(8,128)(2,1)S(1)} %fusion.72), channel_id=1, replica_groups=mesh['subset'=2,'tile'=16] {'tile'}, dimensions={1}, use_global_device_ids=true | all-gather | bytes 139264 | tf_op jit(solution)/shard_map/all_gather | solution.py:91
  182.1 0.6 fusion.26
  182.7 1.4 while.99
  184.2 1.6 collective-permute-start.1
  185.8 7.1 %collective-permute-done.1 = f32[32,2048]{1,0:T(8,128)S(1)} collective-permute-done((f32[32,2048]{1,0:T(8,128)S(1)}, f32[32,2048]{1,0:T(8,128)S(1)}, u32[]{:S(2)}, u32[]{:S(2)}) %collective-permute-start.1) | collective-permute-done | bytes 262176 | tf_op jit(solution)/shard_map/ppermute | solution.py:15
  193.5 0.7 fusion.6
  194.2 0.6 fusion.24
  194.9 1.4 while.100
  196.2 0.8 copy.79
  197.2 52.6 %reduce-scatter.9.cloned.1.call-done = f32[32,128]{1,0:T(8,128)} async-done(((f32[32,2048]{1,0:T(8,128)}), f32[32,128]{1,0:T(8,128)}) %reduce-scatter.9.cloned.1.call-update) | async-done | bytes 16400 | tf_op jit(solution)/shard_map/reduce_scatter | solution.py:89
  249.8 0.7 fusion.71
  250.5 19.7 %all_gather.14 = bf16[32,2048]{1,0:T(8,128)(2,1)S(1)} all-gather(bf16[32,128]{1,0:T(8,128)(2,1)S(1)} %fusion.71), channel_id=1, replica_groups=mesh['subset'=2,'tile'=16] {'tile'}, dimensions={1}, use_global_device_ids=true | all-gather | bytes 139264 | tf_op jit(solution)/shard_map/all_gather | solution.py:91
  271.3 0.6 fusion.22
  271.9 1.4 while.101
  273.5 1.6 collective-permute-start.2
  275.0 7.1 %collective-permute-done.2 = f32[32,2048]{1,0:T(8,128)S(1)} collective-permute-done((f32[32,2048]{1,0:T(8,128)S(1)}, f32[32,2048]{1,0:T(8,128)S(1)}, u32[]{:S(2)}, u32[]{:S(2)}) %collective-permute-start.2) | collective-permute-done | bytes 262176 | tf_op jit(solution)/shard_map/ppermute | solution.py:15
  282.7 0.7 fusion.2
  283.4 0.6 fusion.20
  284.1 1.4 while.102
  285.5 0.8 copy.77
  286.3 52.7 %reduce-scatter.11.cloned.1.call-done = f32[32,128]{1,0:T(8,128)} async-done(((f32[32,2048]{1,0:T(8,128)}), f32[32,128]{1,0:T(8,128)}) %reduce-scatter.11.cloned.1.call-update) | async-done | bytes 16400 | tf_op jit(solution)/shard_map/reduce_scatter | solution.py:89
  339.0 0.7 fusion.70
  339.7 19.7 %all_gather.15 = bf16[32,2048]{1,0:T(8,128)(2,1)S(1)} all-gather(bf16[32,128]{1,0:T(8,128)(2,1)S(1)} %fusion.70), channel_id=1, replica_groups=mesh['subset'=2,'tile'=16] {'tile'}, dimensions={1}, use_global_device_ids=true | all-gather | bytes 139264 | tf_op jit(solution)/shard_map/all_gather | solution.py:91
  360.5 0.6 fusion.18
  361.2 1.4 while.103
  362.6 0.8 copy.76
  (68 shorter events, 7.5 us)
Async XLA Ops:
  6.5 3.0 copy-start
  6.5 64.7 %reduce-scatter.5.cloned.1.call-start = ((), (), s32[]{:S(2)}) async-start(), calls=%async_computation.4 | async-start | bytes 278528 | tf_op jit(solution)/shard_map/reduce_scatter | solution.py:89
  6.5 0.7 copy-start.4
  7.3 0.7 copy-start.3
  13.1 147.4 %reduce-scatter.7.cloned.1.call-start = ((), (), s32[]{:S(2)}) async-start(), calls=%async_computation.5 | async-start | bytes 278528 | tf_op jit(solution)/shard_map/reduce_scatter | solution.py:89
  13.2 1.0 copy-start.1
  14.2 57.1 %copy-start.2 = (s32[1,64,128]{2,1,0:T(8,128)S(1)}, s32[1,64,128]{2,1,0:T(8,128)}, u32[]{:S(2)}) copy-start(s32[1,64,128]{2,1,0:T(8,128)} %param.29) | copy-start | bytes 98308
  95.0 8.6 %collective-permute-start = (f32[32,2048]{1,0:T(8,128)S(1)}, f32[32,2048]{1,0:T(8,128)S(1)}, u32[]{:S(2)}, u32[]{:S(2)}) collective-permute-start(f32[32,2048]{1,0:T(8,128)S(1)} %bitcast.224), channel_id=1, source_target_pairs={{0,16},{16,0},{1,17},{17,1},{2,18},{18,2},{3,19},{19,3},{4,20},{20... | collective-permute-start | bytes 786440 | tf_op jit(solution)/shard_map/ppermute | solution.py:15
  107.8 141.9 %reduce-scatter.9.cloned.1.call-start = ((), (), s32[]{:S(2)}) async-start(), calls=%async_computation.6 | async-start | bytes 278528 | tf_op jit(solution)/shard_map/reduce_scatter | solution.py:89
  184.2 8.6 %collective-permute-start.1 = (f32[32,2048]{1,0:T(8,128)S(1)}, f32[32,2048]{1,0:T(8,128)S(1)}, u32[]{:S(2)}, u32[]{:S(2)}) collective-permute-start(f32[32,2048]{1,0:T(8,128)S(1)} %bitcast.225), channel_id=1, source_target_pairs={{0,16},{16,0},{1,17},{17,1},{2,18},{18,2},{3,19},{19,3},{4,20},{20... | collective-permute-start | bytes 786440 | tf_op jit(solution)/shard_map/ppermute | solution.py:15
  197.1 141.9 %reduce-scatter.11.cloned.1.call-start = ((), (), s32[]{:S(2)}) async-start(), calls=%async_computation.7 | async-start | bytes 278528 | tf_op jit(solution)/shard_map/reduce_scatter | solution.py:89
  273.5 8.6 %collective-permute-start.2 = (f32[32,2048]{1,0:T(8,128)S(1)}, f32[32,2048]{1,0:T(8,128)S(1)}, u32[]{:S(2)}, u32[]{:S(2)}) collective-permute-start(f32[32,2048]{1,0:T(8,128)S(1)} %bitcast.226), channel_id=1, source_target_pairs={{0,16},{16,0},{1,17},{17,1},{2,18},{18,2},{3,19},{19,3},{4,20},{20... | collective-permute-start | bytes 786440 | tf_op jit(solution)/shard_map/ppermute | solution.py:15
Sparse Core Ops, SparseCore 0:
  13.2 57.9 reduce-scatter.4
  107.9 52.5 reduce-scatter.6
  197.2 52.5 reduce-scatter.8
  286.4 52.5 reduce-scatter.10
where the time goes:
time: 371 us; the launch traced here: 370 us
  waiting for transfers between devices  236 us (64%)
  blocking collectives  79 us (21%)
  between operations  14.3 us (4%)
  local copies, waits for them, and re-layouts  10.9 us (3%)
  loops' own time  10.6 us (3%)
  matrix products  9.91 us (3%)
  starting transfers between devices  4.78 us (1%)
  other arithmetic  4.59 us (1%)
    reduce_scatter x4, waiting for transfers between devices, shards(): lax.psum_scatter(partial_value, 'tile', scatter_dimension=1, tiled=True)  215 us
    all_gather x4, blocking collectives, shards(): all_ratios = lax.all_gather(ratios, 'tile', axis=1, tiled=True)  79 us
    ppermute x3, waiting for transfers between devices, shifted(): lax.ppermute(array, axis, [(i, (i + by) % peers) for i in range(peers)])  21.2 us
  transfers between devices with their start and end apart: 7, of which 7 were waited for; matrix products, arithmetic and copies ran while one was open for 0% of the time, Pallas kernels for 0%

commit v1 on v0

v1 whole, which is shorter than its diff:
```python
import jax
import jax.numpy as jnp
from jax import lax
from jax.experimental import pallas as pl
from jax.experimental.pallas import tpu as pltpu
from jax.sharding import PartitionSpec as P

TILE_GROUP = 32
ROUNDS = 4
VMEM_LIMIT = 40 * 1024 * 1024


def whole_vmem():
    return pl.BlockSpec(memory_space=pltpu.VMEM)


def whole_smem():
    return pl.BlockSpec(memory_space=pltpu.SMEM)


def project_kernel(vox_ref, ray_ref, live_ref, panel_ref, tiles_ref, out_ref, low, acc):
    blocks, _, size = low.shape
    slots = tiles_ref.shape[0]
    for b in range(blocks):
        low[b] = panel_ref[:, b * size:(b + 1) * size].astype(jnp.bfloat16)
    acc[...] = jnp.zeros_like(acc)
    live = live_ref[0, 0]
    for group in range(max(1, slots // TILE_GROUP)):

        @pl.when(group < live)
        def _():
            for t in range(group * TILE_GROUP, min(slots, (group + 1) * TILE_GROUP)):
                part = lax.dot_general(
                    low[vox_ref[0, t]], tiles_ref[t], (((1,), (1,)), ((), ())),
                    preferred_element_type=jnp.float32)
                ray = ray_ref[0, t]
                acc[ray] = acc[ray] + part

    out_ref[...] = acc[...].astype(out_ref.dtype)


def update_kernel(vox_ref, ray_ref, live_ref, ratios_ref, panel_ref, tiles_ref, out_ref, acc, sens):
    blocks, _, size = acc.shape
    slots = tiles_ref.shape[0]
    acc[...] = jnp.zeros_like(acc)
    sens[...] = jnp.zeros_like(sens)
    live = live_ref[0, 0]
    ones = jnp.ones((16, size), jnp.bfloat16)
    for group in range(max(1, slots // TILE_GROUP)):

        @pl.when(group < live)
        def _():
            for t in range(group * TILE_GROUP, min(slots, (group + 1) * TILE_GROUP)):
                tile = tiles_ref[t]
                rows = jnp.concatenate([ratios_ref[ray_ref[0, t]], ones], axis=0)
                part = jnp.dot(rows, tile, preferred_element_type=jnp.float32)
                frames = acc.shape[1]
                vox = vox_ref[0, t]
                acc[vox] = acc[vox] + part[:frames]
                sens[vox] = sens[vox] + part[frames:frames + 8]

    for b in range(blocks):
        cols = slice(b * size, (b + 1) * size)
        out_ref[:, cols] = panel_ref[:, cols] * acc[b] / sens[b][:1]


def shards(images, system_tiles, tile_vox, tile_ray, live_blocks, counts):
    frames = images.shape[0]
    size = system_tiles.shape[-1]
    vox_blocks = images.shape[1] // size
    tiles = system_tiles[0]
    measured = counts[0]
    tile_devs = lax.axis_size("tile")
    rb_dev = measured.shape[1] // size
    ray_blocks = rb_dev * tile_devs
    subset_count = lax.axis_size("subset")
    position = lax.axis_index("subset")
    params = pltpu.CompilerParams(vmem_limit_bytes=VMEM_LIMIT)
    project = pl.pallas_call(
        project_kernel,
        out_shape=jax.ShapeDtypeStruct((ray_blocks, frames, size), jnp.bfloat16),
        in_specs=[whole_smem()] * 3 + [whole_vmem()] * 2,
        out_specs=whole_vmem(),
        scratch_shapes=[pltpu.VMEM((vox_blocks, frames, size), jnp.bfloat16),
                        pltpu.VMEM((ray_blocks, frames, size), jnp.float32)],
        compiler_params=params)
    update = pl.pallas_call(
        update_kernel,
        out_shape=jax.ShapeDtypeStruct(images.shape, jnp.float32),
        in_specs=[whole_smem()] * 3 + [whole_vmem()] * 3,
        out_specs=whole_vmem(),
        scratch_shapes=[pltpu.VMEM((vox_blocks, frames, size), jnp.float32),
                        pltpu.VMEM((vox_blocks, 8, size), jnp.float32)],
        compiler_params=params)
    panel = images
    for r in range(ROUNDS):
        panel_index = (position - r) % subset_count
        now = lax.dynamic_slice_in_dim(measured, panel_index * frames, frames, 0)
        now = now.astype(jnp.float32).reshape(frames, rb_dev, size).transpose(1, 0, 2)
        partial = project(tile_vox, tile_ray, live_blocks, panel, tiles)
        got = lax.all_to_all(partial, "tile", 0, 0, tiled=True)
        sums = got.reshape(tile_devs, rb_dev, frames, size).astype(jnp.float32).sum(0)
        ratios = (now / sums).astype(jnp.bfloat16)
        spread = jnp.broadcast_to(ratios[None], (tile_devs,) + ratios.shape)
        all_ratios = lax.all_to_all(spread.reshape(ray_blocks, frames, size), "tile", 0, 0, tiled=True)
        panel = update(tile_vox, tile_ray, live_blocks, all_ratios, panel, tiles)
        if r + 1 < ROUNDS:
            panel = lax.ppermute(panel, "subset", [(i, (i + 1) % subset_count) for i in range(subset_count)])
    return panel


def solution(mesh):
    in_specs = (
        P("subset", "tile"),
        P("subset", "tile", None, None),
        P("subset", "tile"),
        P("subset", "tile"),
        P("subset", "tile"),
        P("subset", None, "tile"),
    )
    return jax.shard_map(shards, mesh=mesh, in_specs=in_specs, out_specs=P("subset", "tile"),
                         check_vma=False)
```

time: 371 us -> 131 us (0.35)
  waiting for transfers between devices: 236 us -> 49.7 us
  blocking collectives: 79 us -> 42.1 us
  starting transfers between devices: 4.78 us -> 22.6 us
  between operations: 14.3 us -> 0.91 us
  Pallas kernels: 0 us -> 12.3 us
  loops' own time: 10.6 us -> 0 us
  matrix products: 9.91 us -> 0 us
  local copies, waits for them, and re-layouts: 10.9 us -> 2.92 us
  other arithmetic: 4.59 us -> 0.15 us
    reduce_scatter x4 -> x0, waiting for transfers between devices: 215 us -> none  [shards(): lax.psum_scatter(partial_value, 'tile', scatter_dimension=1, tiled=True)]
    all_gather x4 -> x0, blocking collectives: 79 us -> none  [shards(): all_ratios = lax.all_gather(ratios, 'tile', axis=1, tiled=True)]
    all_to_all x0 -> x4, blocking collectives: none -> 42.1 us  [shards(): lax.all_to_all(spread.reshape(ray_blocks, frames, size), 'tile', 0, 0, ti...]
    all_to_all x0 -> x4, waiting for transfers between devices: none -> 31.5 us  [shards(): got = lax.all_to_all(partial, 'tile', 0, 0, tiled=True)]
    all_to_all x0 -> x4, starting transfers between devices: none -> 17.9 us  [shards(): got = lax.all_to_all(partial, 'tile', 0, 0, tiled=True)]
    pallas_call x0 -> x8, Pallas kernels: none -> 12.3 us  [the longest x4 7.6 us: shards(): partial = project(tile_vox, tile_ray, live_blocks, panel, tiles)]
    another operation x8 -> x0, loops' own time: 10.6 us -> none  [the longest x4 5.28 us: project(): summed = lax.fori_loop(0, live_count, project_accumulate, start_value)]
    dot_general x18 -> x0, matrix products: 9.91 us -> none  [the longest x4 2.8 us: project_accumulate(): jnp.einsum('ftv,trv->tfr', chosen, system_tiles, preferred_element_type=j...]
where the time goes in v1:
time: 131 us
  waiting for transfers between devices  49.7 us (38%)
  blocking collectives  42.1 us (32%)
  starting transfers between devices  22.6 us (17%)
  Pallas kernels  12.3 us (9%)
  local copies, waits for them, and re-layouts  2.92 us (2%)
    all_to_all x4, blocking collectives, shards(): lax.all_to_all(spread.reshape(ray_blocks, frames, size), 'tile', 0, 0, ti...  42.1 us
    all_to_all x4, waiting for transfers between devices, shards(): got = lax.all_to_all(partial, 'tile', 0, 0, tiled=True)  31.5 us
    ppermute x3, waiting for transfers between devices, shards(): lax.ppermute(panel, 'subset', [(i, (i + 1) % subset_count) for i in range...  18.2 us
    all_to_all x4, starting transfers between devices, shards(): got = lax.all_to_all(partial, 'tile', 0, 0, tiled=True)  17.9 us
    pallas_call x4, Pallas kernels, shards(): partial = project(tile_vox, tile_ray, live_blocks, panel, tiles)  7.6 us
    pallas_call x4, Pallas kernels, shards(): panel = update(tile_vox, tile_ray, live_blocks, all_ratios, panel, tiles)  4.7 us
    ppermute x3, starting transfers between devices, shards(): lax.ppermute(panel, 'subset', [(i, (i + 1) % subset_count) for i in range...  4.66 us
    unnamed x14, local copies, waits for them, and re-layouts  2.85 us
  transfers between devices with their start and end apart: 7, of which 7 were waited for; matrix products, arithmetic and copies ran while one was open for 0% of the time, Pallas kernels for 0%

profile of v1, /device:TPU:0, one launch (start us, length us, event | category | flops | bytes accessed | tf_op | source)
XLA Modules:
  0.0 130.7 jit_solution(12326872345991432494)
XLA Ops:
  0.7 0.0 copy-start.4
  0.7 0.0 copy-start.5
  0.7 0.6 copy-done.4
  1.3 0.0 copy-done.5
  1.3 0.0 copy-start
  1.3 1.2 copy-done
  2.5 0.0 copy-start.2
  2.6 0.9 copy-done.2
  3.5 0.0 copy-start.1
  3.5 1.9 %shard_map.64 = bf16[16,32,128]{2,1,0:T(8,128)(2,1)} custom-call(s32[1,32]{1,0:T(1,128)S(1)} %copy-done.4, s32[1,32]{1,0:T(1,128)S(1)} %copy-done.5, s32[1,1]{1,0:T(1,128)S(6)} %copy.7.live_ref, f32[32,2048]{1,0:T(8,128)S(1)} %copy-done.2, bf16[32,128,128]{2,1,0:T(8,128)(2,1)S(1)} %bitcast.33), custom_call_target="tpu_custom_call" | custom-call | tf_op jit(solution)/shard_map/pallas_call | solution.py:100
  5.4 7.4 %all-to-all-start = ((bf16[16,32,128]{2,1,0:T(8,128)(2,1)}), bf16[16,32,128]{2,1,0:T(8,128)(2,1)S(1)}, u32[]{:S(2)}, u32[]{:S(2)}) async-start(bf16[16,32,128]{2,1,0:T(8,128)(2,1)} %shard_map.64), calls=%async_computation | async-start | bytes 262144 | tf_op jit(solution)/shard_map/all_to_all | solution.py:101
  12.8 0.0 copy-start.6
  12.8 0.0 copy-start.3
  12.8 7.9 %all-to-all-done = bf16[16,32,128]{2,1,0:T(8,128)(2,1)S(1)} async-done(((bf16[16,32,128]{2,1,0:T(8,128)(2,1)}), bf16[16,32,128]{2,1,0:T(8,128)(2,1)S(1)}, u32[]{:S(2)}, u32[]{:S(2)}) %all-to-all-start) | async-done | bytes 131104 | tf_op jit(solution)/shard_map/all_to_all | solution.py:101
  20.8 0.0 copy-done.6
  20.8 10.5 %all_to_all.40.ratios_ref = bf16[16,32,128]{2,1,0:T(8,128)(2,1)S(1)} all-to-all(bf16[16,32,128]{2,1,0:T(8,128)(2,1)S(1)} %reshape.52), channel_id=1, replica_groups=mesh['subset'=2,'tile'=16] {'tile'}, dimensions={0} | all-to-all | bytes 262144 | tf_op jit(solution)/shard_map/all_to_all | solution.py:105
  31.3 0.0 copy-done.1
  31.3 0.0 copy-done.3
  31.3 1.0 shard_map.65
  32.3 1.6 %collective-permute-start = (f32[32,2048]{1,0:T(8,128)S(1)}, f32[32,2048]{1,0:T(8,128)S(1)}, u32[]{:S(2)}, u32[]{:S(2)}) collective-permute-start(f32[32,2048]{1,0:T(8,128)S(1)} %shard_map.65), channel_id=1, source_target_pairs={{0,16},{16,0},{1,17},{17,1},{2,18},{18,2},{3,19},{19,3},{4,20},{20... | collective-permute-start | bytes 786440 | tf_op jit(solution)/shard_map/ppermute | solution.py:108
  33.9 6.1 %collective-permute-done.panel_ref = f32[32,2048]{1,0:T(8,128)S(1)} collective-permute-done((f32[32,2048]{1,0:T(8,128)S(1)}, f32[32,2048]{1,0:T(8,128)S(1)}, u32[]{:S(2)}, u32[]{:S(2)}) %collective-permute-start) | collective-permute-done | bytes 262176 | tf_op jit(solution)/shard_map/ppermute | solution.py:108
  40.0 1.9 %shard_map.66 = bf16[16,32,128]{2,1,0:T(8,128)(2,1)} custom-call(s32[1,32]{1,0:T(1,128)S(1)} %copy-done.4, s32[1,32]{1,0:T(1,128)S(1)} %copy-done.5, s32[1,1]{1,0:T(1,128)S(6)} %copy.7.live_ref, f32[32,2048]{1,0:T(8,128)S(1)} %collective-permute-done.panel_ref, bf16[32,128,128]{2,1,0:T(8,128)(2,1)S(1)} %bitcast.35), custom_call_target="tpu_custom_call" | custom-call | tf_op jit(solution)/shard_map/pallas_call | solution.py:100
  41.9 3.5 %all-to-all-start.2 = ((bf16[16,32,128]{2,1,0:T(8,128)(2,1)}), bf16[16,32,128]{2,1,0:T(8,128)(2,1)S(1)}, u32[]{:S(2)}, u32[]{:S(2)}) async-start(bf16[16,32,128]{2,1,0:T(8,128)(2,1)} %shard_map.66), calls=%async_computation.2 | async-start | bytes 262144 | tf_op jit(solution)/shard_map/all_to_all | solution.py:101
  45.4 7.9 %all-to-all-done.2 = bf16[16,32,128]{2,1,0:T(8,128)(2,1)S(1)} async-done(((bf16[16,32,128]{2,1,0:T(8,128)(2,1)}), bf16[16,32,128]{2,1,0:T(8,128)(2,1)S(1)}, u32[]{:S(2)}, u32[]{:S(2)}) %all-to-all-start.2) | async-done | bytes 131104 | tf_op jit(solution)/shard_map/all_to_all | solution.py:101
  53.4 10.5 %all_to_all.41.ratios_ref = bf16[16,32,128]{2,1,0:T(8,128)(2,1)S(1)} all-to-all(bf16[16,32,128]{2,1,0:T(8,128)(2,1)S(1)} %reshape.53), channel_id=1, replica_groups=mesh['subset'=2,'tile'=16] {'tile'}, dimensions={0} | all-to-all | bytes 262144 | tf_op jit(solution)/shard_map/all_to_all | solution.py:105
  63.9 1.0 shard_map.67
  64.9 1.6 %collective-permute-start.1 = (f32[32,2048]{1,0:T(8,128)S(1)}, f32[32,2048]{1,0:T(8,128)S(1)}, u32[]{:S(2)}, u32[]{:S(2)}) collective-permute-start(f32[32,2048]{1,0:T(8,128)S(1)} %shard_map.67), channel_id=1, source_target_pairs={{0,16},{16,0},{1,17},{17,1},{2,18},{18,2},{3,19},{19,3},{4,20},{20... | collective-permute-start | bytes 786440 | tf_op jit(solution)/shard_map/ppermute | solution.py:108
  66.4 6.1 %collective-permute-done.1.panel_ref = f32[32,2048]{1,0:T(8,128)S(1)} collective-permute-done((f32[32,2048]{1,0:T(8,128)S(1)}, f32[32,2048]{1,0:T(8,128)S(1)}, u32[]{:S(2)}, u32[]{:S(2)}) %collective-permute-start.1) | collective-permute-done | bytes 262176 | tf_op jit(solution)/shard_map/ppermute | solution.py:108
  72.5 1.9 %shard_map.68 = bf16[16,32,128]{2,1,0:T(8,128)(2,1)} custom-call(s32[1,32]{1,0:T(1,128)S(1)} %copy-done.4, s32[1,32]{1,0:T(1,128)S(1)} %copy-done.5, s32[1,1]{1,0:T(1,128)S(6)} %copy.7.live_ref, f32[32,2048]{1,0:T(8,128)S(1)} %collective-permute-done.1.panel_ref, bf16[32,128,128]{2,1,0:T(8,128)(2,1)S(1)} %bitcast.37), custom_call_target="tpu_custom_call" | custom-call | tf_op jit(solution)/shard_map/pallas_call | solution.py:100
  74.4 3.5 %all-to-all-start.4 = ((bf16[16,32,128]{2,1,0:T(8,128)(2,1)}), bf16[16,32,128]{2,1,0:T(8,128)(2,1)S(1)}, u32[]{:S(2)}, u32[]{:S(2)}) async-start(bf16[16,32,128]{2,1,0:T(8,128)(2,1)} %shard_map.68), calls=%async_computation.4 | async-start | bytes 262144 | tf_op jit(solution)/shard_map/all_to_all | solution.py:101
  77.9 7.9 %all-to-all-done.4 = bf16[16,32,128]{2,1,0:T(8,128)(2,1)S(1)} async-done(((bf16[16,32,128]{2,1,0:T(8,128)(2,1)}), bf16[16,32,128]{2,1,0:T(8,128)(2,1)S(1)}, u32[]{:S(2)}, u32[]{:S(2)}) %all-to-all-start.4) | async-done | bytes 131104 | tf_op jit(solution)/shard_map/all_to_all | solution.py:101
  85.9 10.5 %all_to_all.42.ratios_ref = bf16[16,32,128]{2,1,0:T(8,128)(2,1)S(1)} all-to-all(bf16[16,32,128]{2,1,0:T(8,128)(2,1)S(1)} %reshape.54), channel_id=1, replica_groups=mesh['subset'=2,'tile'=16] {'tile'}, dimensions={0} | all-to-all | bytes 262144 | tf_op jit(solution)/shard_map/all_to_all | solution.py:105
  96.4 1.0 shard_map.69
  97.4 1.5 %collective-permute-start.2 = (f32[32,2048]{1,0:T(8,128)S(1)}, f32[32,2048]{1,0:T(8,128)S(1)}, u32[]{:S(2)}, u32[]{:S(2)}) collective-permute-start(f32[32,2048]{1,0:T(8,128)S(1)} %shard_map.69), channel_id=1, source_target_pairs={{0,16},{16,0},{1,17},{17,1},{2,18},{18,2},{3,19},{19,3},{4,20},{20... | collective-permute-start | bytes 786440 | tf_op jit(solution)/shard_map/ppermute | solution.py:108
  99.0 6.1 %collective-permute-done.2.panel_ref = f32[32,2048]{1,0:T(8,128)S(1)} collective-permute-done((f32[32,2048]{1,0:T(8,128)S(1)}, f32[32,2048]{1,0:T(8,128)S(1)}, u32[]{:S(2)}, u32[]{:S(2)}) %collective-permute-start.2) | collective-permute-done | bytes 262176 | tf_op jit(solution)/shard_map/ppermute | solution.py:108
  105.1 1.9 %shard_map.70 = bf16[16,32,128]{2,1,0:T(8,128)(2,1)} custom-call(s32[1,32]{1,0:T(1,128)S(1)} %copy-done.4, s32[1,32]{1,0:T(1,128)S(1)} %copy-done.5, s32[1,1]{1,0:T(1,128)S(6)} %copy.7.live_ref, f32[32,2048]{1,0:T(8,128)S(1)} %collective-permute-done.2.panel_ref, bf16[32,128,128]{2,1,0:T(8,128)(2,1)S(1)} %bitcast.39), custom_call_target="tpu_custom_call" | custom-call | tf_op jit(solution)/shard_map/pallas_call | solution.py:100
  107.0 3.5 %all-to-all-start.6 = ((bf16[16,32,128]{2,1,0:T(8,128)(2,1)}), bf16[16,32,128]{2,1,0:T(8,128)(2,1)S(1)}, u32[]{:S(2)}, u32[]{:S(2)}) async-start(bf16[16,32,128]{2,1,0:T(8,128)(2,1)} %shard_map.70), calls=%async_computation.6 | async-start | bytes 262144 | tf_op jit(solution)/shard_map/all_to_all | solution.py:101
  110.5 7.9 %all-to-all-done.6 = bf16[16,32,128]{2,1,0:T(8,128)(2,1)S(1)} async-done(((bf16[16,32,128]{2,1,0:T(8,128)(2,1)}), bf16[16,32,128]{2,1,0:T(8,128)(2,1)S(1)}, u32[]{:S(2)}, u32[]{:S(2)}) %all-to-all-start.6) | async-done | bytes 131104 | tf_op jit(solution)/shard_map/all_to_all | solution.py:101
  118.4 10.5 %all_to_all.43.ratios_ref = bf16[16,32,128]{2,1,0:T(8,128)(2,1)S(1)} all-to-all(bf16[16,32,128]{2,1,0:T(8,128)(2,1)S(1)} %reshape.55), channel_id=1, replica_groups=mesh['subset'=2,'tile'=16] {'tile'}, dimensions={0} | all-to-all | bytes 262144 | tf_op jit(solution)/shard_map/all_to_all | solution.py:105
  129.0 1.7 %shard_map.71 = f32[32,2048]{1,0:T(8,128)} custom-call(s32[1,32]{1,0:T(1,128)S(1)} %copy-done.4, s32[1,32]{1,0:T(1,128)S(1)} %copy-done.5, s32[1,1]{1,0:T(1,128)S(6)} %copy.7.live_ref, bf16[16,32,128]{2,1,0:T(8,128)(2,1)S(1)} %all_to_all.43.ratios_ref, f32[32,2048]{1,0:T(8,128)S(1)} %collective-permute-done.2.panel_ref, bf16[32,128,128]{2,1,0:T(8,128)(2,1)S(1)} %bitcast.40), custom_call_target="tpu_custom_call" | custom-call | tf_op jit(solution)/shard_map/pallas_call | solution.py:106
  (12 shorter events, 0.2 us)
Async XLA Ops:
  0.7 0.7 copy-start.4
  0.7 0.7 copy-start.5
  1.3 1.2 copy-start
  2.5 0.9 copy-start.2
  3.5 27.8 %copy-start.1 = (bf16[1,32,128,128]{3,2,1,0:T(8,128)(2,1)S(1)}, bf16[1,32,128,128]{3,2,1,0:T(8,128)(2,1)}, u32[]{:S(2)}) copy-start(bf16[1,32,128,128]{3,2,1,0:T(8,128)(2,1)} %param.7) | copy-start | bytes 3145732
  5.4 15.3 %all-to-all-start = ((bf16[16,32,128]{2,1,0:T(8,128)(2,1)}), bf16[16,32,128]{2,1,0:T(8,128)(2,1)S(1)}, u32[]{:S(2)}, u32[]{:S(2)}) async-start(bf16[16,32,128]{2,1,0:T(8,128)(2,1)} %shard_map.64), calls=%async_computation | async-start | bytes 262144 | tf_op jit(solution)/shard_map/all_to_all | solution.py:101
  12.8 8.0 %copy-start.6 = (s32[1,64,128]{2,1,0:T(8,128)S(1)}, s32[1,64,128]{2,1,0:T(8,128)}, u32[]{:S(2)}) copy-start(s32[1,64,128]{2,1,0:T(8,128)} %param.11) | copy-start | bytes 98308
  12.8 18.5 %copy-start.3 = (f32[32,2048]{1,0:T(8,128)S(1)}, f32[32,2048]{1,0:T(8,128)}, u32[]{:S(2)}) copy-start(f32[32,2048]{1,0:T(8,128)} %panel_ref.3) | copy-start | bytes 786436
  32.3 7.6 %collective-permute-start = (f32[32,2048]{1,0:T(8,128)S(1)}, f32[32,2048]{1,0:T(8,128)S(1)}, u32[]{:S(2)}, u32[]{:S(2)}) collective-permute-start(f32[32,2048]{1,0:T(8,128)S(1)} %shard_map.65), channel_id=1, source_target_pairs={{0,16},{16,0},{1,17},{17,1},{2,18},{18,2},{3,19},{19,3},{4,20},{20... | collective-permute-start | bytes 786440 | tf_op jit(solution)/shard_map/ppermute | solution.py:108
  41.9 11.4 %all-to-all-start.2 = ((bf16[16,32,128]{2,1,0:T(8,128)(2,1)}), bf16[16,32,128]{2,1,0:T(8,128)(2,1)S(1)}, u32[]{:S(2)}, u32[]{:S(2)}) async-start(bf16[16,32,128]{2,1,0:T(8,128)(2,1)} %shard_map.66), calls=%async_computation.2 | async-start | bytes 262144 | tf_op jit(solution)/shard_map/all_to_all | solution.py:101
  64.9 7.6 %collective-permute-start.1 = (f32[32,2048]{1,0:T(8,128)S(1)}, f32[32,2048]{1,0:T(8,128)S(1)}, u32[]{:S(2)}, u32[]{:S(2)}) collective-permute-start(f32[32,2048]{1,0:T(8,128)S(1)} %shard_map.67), channel_id=1, source_target_pairs={{0,16},{16,0},{1,17},{17,1},{2,18},{18,2},{3,19},{19,3},{4,20},{20... | collective-permute-start | bytes 786440 | tf_op jit(solution)/shard_map/ppermute | solution.py:108
  74.4 11.4 %all-to-all-start.4 = ((bf16[16,32,128]{2,1,0:T(8,128)(2,1)}), bf16[16,32,128]{2,1,0:T(8,128)(2,1)S(1)}, u32[]{:S(2)}, u32[]{:S(2)}) async-start(bf16[16,32,128]{2,1,0:T(8,128)(2,1)} %shard_map.68), calls=%async_computation.4 | async-start | bytes 262144 | tf_op jit(solution)/shard_map/all_to_all | solution.py:101
  97.4 7.6 %collective-permute-start.2 = (f32[32,2048]{1,0:T(8,128)S(1)}, f32[32,2048]{1,0:T(8,128)S(1)}, u32[]{:S(2)}, u32[]{:S(2)}) collective-permute-start(f32[32,2048]{1,0:T(8,128)S(1)} %shard_map.69), channel_id=1, source_target_pairs={{0,16},{16,0},{1,17},{17,1},{2,18},{18,2},{3,19},{19,3},{4,20},{20... | collective-permute-start | bytes 786440 | tf_op jit(solution)/shard_map/ppermute | solution.py:108
  107.0 11.4 %all-to-all-start.6 = ((bf16[16,32,128]{2,1,0:T(8,128)(2,1)}), bf16[16,32,128]{2,1,0:T(8,128)(2,1)S(1)}, u32[]{:S(2)}, u32[]{:S(2)}) async-start(bf16[16,32,128]{2,1,0:T(8,128)(2,1)} %shard_map.70), calls=%async_computation.6 | async-start | bytes 262144 | tf_op jit(solution)/shard_map/all_to_all | solution.py:101

commit v2 on v1

v2 whole, which is shorter than its diff:
```python
import functools

import jax
import jax.numpy as jnp
from jax import lax
from jax.experimental import pallas as pl
from jax.experimental.pallas import tpu as pltpu
from jax.sharding import PartitionSpec as P

TILE_GROUP = 32
ROUNDS = 4
CORES = 2
LANES = 128
VMEM_LIMIT = 40 * 1024 * 1024


def vmem():
    return pl.BlockSpec(memory_space=pltpu.VMEM)


def smem():
    return pl.BlockSpec(memory_space=pltpu.SMEM)


def each_live(index_ref, slots, body):
    live = index_ref[2, 0]
    for group in range(-(-slots // TILE_GROUP)):

        @pl.when(group < live)
        def _():
            for t in range(group * TILE_GROUP, min(slots, (group + 1) * TILE_GROUP)):
                body(t)


def project_kernel(*refs):
    index_refs, low_ref, tile_refs, (out_ref, low, acc) = refs[:2], refs[2], refs[3:5], refs[5:]
    size = low.shape[-1]
    blocks = low.shape[0] // CORES
    for k in range(CORES):
        for b in range(blocks):
            low[k * blocks + b] = low_ref[k, :, b * size:(b + 1) * size].astype(jnp.bfloat16)
    acc[...] = jnp.zeros_like(acc)
    for k in range(CORES):
        index_ref, tiles_ref = index_refs[k], tile_refs[k]

        def body(t):
            part = lax.dot_general(low[k * blocks + index_ref[0, t]], tiles_ref[t],
                                   (((1,), (1,)), ((), ())), preferred_element_type=jnp.float32)
            ray = index_ref[1, t]
            acc[ray] = acc[ray] + part

        each_live(index_ref, tiles_ref.shape[0], body)
    out_ref[...] = acc[...].astype(out_ref.dtype)


def sensitivity_kernel(*refs):
    index_refs, tile_refs, (out_ref, acc) = refs[:2], refs[2:4], refs[4:]
    blocks = acc.shape[0] // CORES
    acc[...] = jnp.zeros_like(acc)
    ones = jnp.ones((16, tile_refs[0].shape[1]), jnp.bfloat16)
    for k in range(CORES):
        index_ref, tiles_ref = index_refs[k], tile_refs[k]

        def body(t):
            part = jnp.dot(ones, tiles_ref[t], preferred_element_type=jnp.float32)
            at = k * blocks + index_ref[0, t]
            acc[at] = acc[at] + part[:8]

        each_live(index_ref, tiles_ref.shape[0], body)
    out_ref[...] = 1.0 / acc[...]


def update_kernel(held_parts, *refs):
    index_refs, ratios_ref = refs[:2], refs[2]
    held_refs, rest = refs[3:3 + held_parts], refs[3 + held_parts:]
    inverse_ref, tile_refs, out_refs, acc = rest[0], rest[1:3], rest[3:-1], rest[-1]

    def held_of(k, cols):
        return sum(ref[k, :, cols].astype(jnp.float32) for ref in held_refs)

    size = acc.shape[-1]
    blocks = acc.shape[0] // CORES
    acc[...] = jnp.zeros_like(acc)
    for k in range(CORES):
        index_ref, tiles_ref = index_refs[k], tile_refs[k]

        def body(t):
            part = jnp.dot(ratios_ref[index_ref[1, t]], tiles_ref[t],
                           preferred_element_type=jnp.float32)
            at = k * blocks + index_ref[0, t]
            acc[at] = acc[at] + part

        each_live(index_ref, tiles_ref.shape[0], body)
    for k in range(CORES):
        for b in range(blocks):
            cols = slice(b * size, (b + 1) * size)
            at = k * blocks + b
            value = held_of(k, cols) * acc[at] * inverse_ref[at, :1]
            high = value.astype(out_refs[0].dtype)
            out_refs[0][k, :, cols] = high
            if len(out_refs) == 2:
                out_refs[1][k, :, cols] = (value - high.astype(jnp.float32)).astype(jnp.bfloat16)


def call(kernel, ins, out_shape, scratch):
    return pl.pallas_call(
        kernel,
        out_shape=out_shape,
        in_specs=[smem()] * CORES + [vmem()] * (len(ins) - CORES),
        out_specs=jax.tree.map(lambda _: vmem(), out_shape),
        scratch_shapes=scratch,
        compiler_params=pltpu.CompilerParams(vmem_limit_bytes=VMEM_LIMIT))(*ins)


def shards(images, system_tiles, tile_vox, tile_ray, live_blocks, counts):
    frames = images.shape[0]
    half = frames // CORES
    size = system_tiles.shape[-1]
    voxels = images.shape[1]
    vox_blocks = voxels // size
    own_tiles = system_tiles[0]
    slots = own_tiles.shape[0]
    measured = counts[0]
    tile_devs = lax.axis_size("tile")
    peers = tile_devs // CORES
    rb_dev = measured.shape[1] // size
    rb_chip = rb_dev * CORES
    ray_blocks = rb_dev * tile_devs
    subset_count = lax.axis_size("subset")
    position = lax.axis_index("subset")
    core = lax.axis_index("tile") % CORES
    swap = [(i, i ^ 1) for i in range(tile_devs)]
    groups = [[c + CORES * j for j in range(peers)] for c in range(CORES)]
    shift = [(i, (i + 1) % subset_count) for i in range(subset_count)]

    width = -(-slots // LANES) * LANES
    rows = jnp.concatenate([tile_vox, tile_ray, jnp.broadcast_to(live_blocks, tile_vox.shape)], axis=0)
    index_own = jnp.pad(rows, ((0, 5), (0, width - slots)))
    halves = images.reshape(CORES, half, voxels)
    counts_halves = measured.reshape(subset_count, CORES, half, rb_dev * size)
    mine = lax.dynamic_index_in_dim(halves, core, 0, keepdims=False)
    theirs = lax.dynamic_index_in_dim(halves, 1 - core, 0, keepdims=False)
    counts_mine = lax.dynamic_index_in_dim(counts_halves, core, 1, keepdims=False)
    counts_theirs = lax.dynamic_index_in_dim(counts_halves, 1 - core, 1, keepdims=False)
    other_half = lax.ppermute(theirs, "tile", swap)
    other_tiles = lax.ppermute(own_tiles, "tile", swap)
    index_other = lax.ppermute(index_own, "tile", swap)
    counts_other = lax.ppermute(counts_theirs, "tile", swap)
    counts_both = jnp.where(core == 0, jnp.stack([counts_mine, counts_other]),
                            jnp.stack([counts_other, counts_mine]))
    counts_both = counts_both.reshape(CORES, subset_count, half, rb_dev, size)
    counts_both = counts_both.transpose(1, 0, 3, 2, 4).reshape(subset_count, rb_chip, half, size)
    counts_both = counts_both.astype(jnp.float32)

    held = jnp.stack([mine, other_half])
    index = (index_own, index_other)
    tiles = (own_tiles, other_tiles)
    both = CORES * vox_blocks
    inverse = call(sensitivity_kernel, (*index, *tiles),
                   jax.ShapeDtypeStruct((both, 8, size), jnp.float32),
                   [pltpu.VMEM((both, 8, size), jnp.float32)])
    state = (held,)
    for r in range(ROUNDS):
        now = lax.dynamic_index_in_dim(counts_both, (position - r) % subset_count, 0, keepdims=False)
        partial = call(project_kernel, (*index, state[0], *tiles),
                       jax.ShapeDtypeStruct((ray_blocks, half, size), jnp.bfloat16),
                       [pltpu.VMEM((both, half, size), jnp.bfloat16),
                        pltpu.VMEM((ray_blocks, half, size), jnp.float32)])
        got = lax.all_to_all(partial, "tile", 0, 0, axis_index_groups=groups, tiled=True)
        sums = got.reshape(peers, rb_chip, half, size).astype(jnp.float32).sum(0)
        ratios = (now / sums).astype(jnp.bfloat16)
        spread = jnp.broadcast_to(ratios[None], (peers,) + ratios.shape)
        all_ratios = lax.all_to_all(spread.reshape(ray_blocks, half, size), "tile", 0, 0,
                                    axis_index_groups=groups, tiled=True)
        last = r + 1 == ROUNDS
        shape = (CORES, half, voxels)
        out_shape = (jax.ShapeDtypeStruct(shape, jnp.float32) if last else
                     (jax.ShapeDtypeStruct(shape, jnp.bfloat16),) * 2)
        state = call(functools.partial(update_kernel, len(state)), (*index, all_ratios, *state, inverse, *tiles), out_shape,
                     [pltpu.VMEM((both, half, size), jnp.float32)])
        if not last:
            high = lax.ppermute(state[0], "subset", shift)
            low, _ = lax.optimization_barrier((state[1], high))
            state = (high, lax.ppermute(low, "subset", shift))
    back_half = lax.ppermute(state[1], "tile", swap)
    return jnp.where(core == 0, jnp.concatenate([state[0], back_half]),
                     jnp.concatenate([back_half, state[0]]))


def solution(mesh):
    in_specs = (
        P("subset", "tile"),
        P("subset", "tile", None, None),
        P("subset", "tile"),
        P("subset", "tile"),
        P("subset", "tile"),
        P("subset", None, "tile"),
    )
    return jax.shard_map(shards, mesh=mesh, in_specs=in_specs, out_specs=P("subset", "tile"),
                         check_vma=False)
```

time: 131 us -> 129 us (0.985)
  blocking collectives: 42.1 us -> 0 us
  starting transfers between devices: 22.6 us -> 41.3 us
  waiting for transfers between devices: 49.7 us -> 61.7 us
  Pallas kernels: 12.3 us -> 18.1 us
  other arithmetic: 0.15 us -> 1.61 us
  local copies, waits for them, and re-layouts: 2.92 us -> 4.38 us
    all_to_all x4 -> x0, blocking collectives: 42.1 us -> none  [shards(): lax.all_to_all(spread.reshape(ray_blocks, frames, size), 'tile', 0, 0, ti...]
    all_to_all x4 -> x8, waiting for transfers between devices: 31.5 us -> 48.5 us  [the longest x4 25.9 us: shards(): lax.all_to_all(spread.reshape(ray_blocks, half, size), 'tile', 0, 0, axis...]
    all_to_all x4 -> x8, starting transfers between devices: 17.9 us -> 30.7 us  [the longest x4 17.3 us: shards(): lax.all_to_all(partial, 'tile', 0, 0, axis_index_groups=groups, tiled=True)]
    ppermute x3 -> x11, starting transfers between devices: 4.66 us -> 10.6 us  [the longest x3 4.68 us: shards(): high = lax.ppermute(state[0], 'subset', shift)]
    pallas_call x8 -> x9, Pallas kernels: 12.3 us -> 18.1 us  [call(): pl.pallas_call(kernel, out_shape=out_shape, in_specs=[smem()] * CORES + [...]
    ppermute x3 -> x11, waiting for transfers between devices: 18.2 us -> 13.1 us  [the longest x3 11.8 us: shards(): high = lax.ppermute(state[0], 'subset', shift)]
    unnamed x14 -> x2, local copies, waits for them, and re-layouts: 2.85 us -> 0.01 us
    broadcast_in_dim x0 -> x4, local copies, waits for them, and re-layouts: none -> 2.56 us  [shards(): spread = jnp.broadcast_to(ratios[None], (peers,) + ratios.shape)]
  transfers between devices with their start and end apart: 7 -> 19, of which waited for: 7 -> 12; matrix products, arithmetic and copies ran while one was open for 0% -> 4% of each run, Pallas kernels for 0% -> 3%
where the time goes in v2:
time: 129 us; the launch traced here: 128 us
  waiting for transfers between devices  61.7 us (48%)
  starting transfers between devices  41.3 us (32%)
  Pallas kernels  18.1 us (14%)
  local copies, waits for them, and re-layouts  4.38 us (3%)
  other arithmetic  1.61 us (1%)
    all_to_all x4, waiting for transfers between devices, shards(): lax.all_to_all(spread.reshape(ray_blocks, half, size), 'tile', 0, 0, axis...  25.9 us
    all_to_all x4, waiting for transfers between devices, shards(): lax.all_to_all(partial, 'tile', 0, 0, axis_index_groups=groups, tiled=True)  22.7 us
    pallas_call x9, Pallas kernels, call(): pl.pallas_call(kernel, out_shape=out_shape, in_specs=[smem()] * CORES + [...  18.1 us
    all_to_all x4, starting transfers between devices, shards(): lax.all_to_all(partial, 'tile', 0, 0, axis_index_groups=groups, tiled=True)  17.3 us
    all_to_all x4, starting transfers between devices, shards(): lax.all_to_all(spread.reshape(ray_blocks, half, size), 'tile', 0, 0, axis...  13.4 us
    ppermute x3, waiting for transfers between devices, shards(): high = lax.ppermute(state[0], 'subset', shift)  11.8 us
    ppermute x3, starting transfers between devices, shards(): high = lax.ppermute(state[0], 'subset', shift)  4.68 us
    ppermute x3, starting transfers between devices, shards(): state = (high, lax.ppermute(low, 'subset', shift))  4.68 us
  transfers between devices with their start and end apart: 19, of which 12 were waited for; matrix products, arithmetic and copies ran while one was open for 4% of the time, Pallas kernels for 3%

profile of v2, /device:TPU:0, one launch (start us, length us, event | category | flops | bytes accessed | tf_op | source)
XLA Modules:
  0.0 128.0 jit_solution(3020521196455269512)
XLA Ops:
  0.0 0.5 collective-permute-start.3
  0.5 1.0 constant_dynamic-slice_fusion
  1.4 0.2 collective-permute-start.2
  2.3 0.1 pad.17.clone
  2.4 0.7 add_add_fusion
  3.1 0.4 collective-permute-start
  3.5 0.7 dynamic-slice_bitcast_fusion.2
  4.2 0.1 collective-permute-start.1
  4.4 2.6 %shard_map.64 = bf16[16,16,128]{2,1,0:T(8,128)(2,1)} custom-call(s32[8,128]{1,0:T(8,128)S(1)} %pad.4.refs_0_, s32[8,128]{1,0:T(8,128)S(1)} %collective-permute-done.refs_1_, f32[2,16,2048]{2,1,0:T(8,128)S(1)} %pad_maximum_fusion.refs_2_.refs_3_, bf16[32,128,128]{2,1,0:T(8,128)(2,1)S(1)} %bitcast.80, ...), custom_call_target="tpu_custom_call" | custom-call | tf_op jit(solution)/shard_map/pallas_call | solution.py:106
  7.1 7.2 %all-to-all-start = ((bf16[16,16,128]{2,1,0:T(8,128)(2,1)}), bf16[16,16,128]{2,1,0:T(8,128)(2,1)S(1)}, u32[]{:S(2)}, u32[]{:S(2)}) async-start(bf16[16,16,128]{2,1,0:T(8,128)(2,1)} %shard_map.64), calls=%async_computation | async-start | bytes 131072 | tf_op jit(solution)/shard_map/all_to_all | solution.py:169
  14.3 6.9 %all-to-all-done = bf16[16,16,128]{2,1,0:T(8,128)(2,1)S(1)} async-done(((bf16[16,16,128]{2,1,0:T(8,128)(2,1)}), bf16[16,16,128]{2,1,0:T(8,128)(2,1)S(1)}, u32[]{:S(2)}, u32[]{:S(2)}) %all-to-all-start) | async-done | bytes 65568 | tf_op jit(solution)/shard_map/all_to_all | solution.py:169
  21.2 0.6 broadcast_in_dim.42
  21.9 3.4 %all-to-all-start.1 = ((bf16[16,16,128]{2,1,0:T(8,128)(2,1)}), bf16[16,16,128]{2,1,0:T(8,128)(2,1)S(1)}, u32[]{:S(2)}, u32[]{:S(2)}) async-start(bf16[16,16,128]{2,1,0:T(8,128)(2,1)} %bitcast.16), calls=%async_computation.1 | async-start | bytes 131072 | tf_op jit(solution)/shard_map/all_to_all | solution.py:173
  25.2 1.5 %shard_map.65.refs_4_.refs_5_ = f32[32,8,128]{2,1,0:T(8,128)S(1)} custom-call(s32[8,128]{1,0:T(8,128)S(1)} %pad.4.refs_0_, s32[8,128]{1,0:T(8,128)S(1)} %collective-permute-done.refs_1_, bf16[32,128,128]{2,1,0:T(8,128)(2,1)S(1)} %bitcast.81, bf16[32,128,128]{2,1,0:T(8,128)(2,1)S(1)} %collective-permute-done.3.refs_4_.refs_3_.refs_6_.refs_7_), custom_call_target="tpu_custom_call" | custom-call | tf_op jit(solution)/shard_map/pallas_call | solution.py:106
  26.7 5.4 %all-to-all-done.1.refs_2_ = bf16[16,16,128]{2,1,0:T(8,128)(2,1)S(1)} async-done(((bf16[16,16,128]{2,1,0:T(8,128)(2,1)}), bf16[16,16,128]{2,1,0:T(8,128)(2,1)S(1)}, u32[]{:S(2)}, u32[]{:S(2)}) %all-to-all-start.1) | async-done | bytes 65568 | tf_op jit(solution)/shard_map/all_to_all | solution.py:173
  32.1 1.5 %shard_map.66 = (bf16[2,16,2048]{2,1,0:T(8,128)(2,1)S(1)}, bf16[2,16,2048]{2,1,0:T(8,128)(2,1)S(1)}) custom-call(s32[8,128]{1,0:T(8,128)S(1)} %pad.4.refs_0_, s32[8,128]{1,0:T(8,128)S(1)} %collective-permute-done.refs_1_, bf16[16,16,128]{2,1,0:T(8,128)(2,1)S(1)} %all-to-all-done.1.refs_2_, f32[2,16,2048]{2,1,0:T(8,128)S(1)} %pad_maximum_fusion.refs_2_.refs_3_, ...), custom_call_target="tpu_custom_call" | custom-call | tf_op jit(solution)/shard_map/pallas_call | solution.py:106
  33.6 1.6 %collective-permute-start.4 = (bf16[2,16,2048]{2,1,0:T(8,128)(2,1)S(1)}, bf16[2,16,2048]{2,1,0:T(8,128)(2,1)S(1)}, u32[]{:S(2)}, u32[]{:S(2)}) collective-permute-start(bf16[2,16,2048]{2,1,0:T(8,128)(2,1)S(1)} %get-tuple-element.14), channel_id=1, source_target_pairs={{0,16},{16,0},{1,17},{17,1},{2,18},{18,2},{3,19},{19,3},{4,20},{20... | collective-permute-start | bytes 393224 | tf_op jit(solution)/shard_map/ppermute | solution.py:182
  35.1 3.5 %collective-permute-done.4.refs_2_.refs_3_ = bf16[2,16,2048]{2,1,0:T(8,128)(2,1)S(1)} collective-permute-done((bf16[2,16,2048]{2,1,0:T(8,128)(2,1)S(1)}, bf16[2,16,2048]{2,1,0:T(8,128)(2,1)S(1)}, u32[]{:S(2)}, u32[]{:S(2)}) %collective-permute-start.4) | collective-permute-done | bytes 131104 | tf_op jit(solution)/shard_map/ppermute | solution.py:182
  38.6 2.7 %shard_map.67 = bf16[16,16,128]{2,1,0:T(8,128)(2,1)} custom-call(s32[8,128]{1,0:T(8,128)S(1)} %pad.4.refs_0_, s32[8,128]{1,0:T(8,128)S(1)} %collective-permute-done.refs_1_, bf16[2,16,2048]{2,1,0:T(8,128)(2,1)S(1)} %collective-permute-done.4.refs_2_.refs_3_, bf16[32,128,128]{2,1,0:T(8,128)(2,1)S(1)} %bitcast.83, ...), custom_call_target="tpu_custom_call" | custom-call | tf_op jit(solution)/shard_map/pallas_call | solution.py:106
  41.3 3.4 %all-to-all-start.2 = ((bf16[16,16,128]{2,1,0:T(8,128)(2,1)}), bf16[16,16,128]{2,1,0:T(8,128)(2,1)S(1)}, u32[]{:S(2)}, u32[]{:S(2)}) async-start(bf16[16,16,128]{2,1,0:T(8,128)(2,1)} %shard_map.67), calls=%async_computation.2 | async-start | bytes 131072 | tf_op jit(solution)/shard_map/all_to_all | solution.py:169
  44.7 1.6 %collective-permute-start.5 = (bf16[2,16,2048]{2,1,0:T(8,128)(2,1)S(1)}, bf16[2,16,2048]{2,1,0:T(8,128)(2,1)S(1)}, u32[]{:S(2)}, u32[]{:S(2)}) collective-permute-start(bf16[2,16,2048]{2,1,0:T(8,128)(2,1)S(1)} %get-tuple-element.16), channel_id=1, source_target_pairs={{0,16},{16,0},{1,17},{17,1},{2,18},{18,2},{3,19},{19,3},{4,20},{20... | collective-permute-start | bytes 393224 | tf_op jit(solution)/shard_map/ppermute | solution.py:184
  46.2 5.3 %all-to-all-done.2 = bf16[16,16,128]{2,1,0:T(8,128)(2,1)S(1)} async-done(((bf16[16,16,128]{2,1,0:T(8,128)(2,1)}), bf16[16,16,128]{2,1,0:T(8,128)(2,1)S(1)}, u32[]{:S(2)}, u32[]{:S(2)}) %all-to-all-start.2) | async-done | bytes 65568 | tf_op jit(solution)/shard_map/all_to_all | solution.py:169
  51.5 0.6 broadcast_in_dim.44
  52.2 3.4 %all-to-all-start.3 = ((bf16[16,16,128]{2,1,0:T(8,128)(2,1)}), bf16[16,16,128]{2,1,0:T(8,128)(2,1)S(1)}, u32[]{:S(2)}, u32[]{:S(2)}) async-start(bf16[16,16,128]{2,1,0:T(8,128)(2,1)} %bitcast.20), calls=%async_computation.3 | async-start | bytes 131072 | tf_op jit(solution)/shard_map/all_to_all | solution.py:173
  55.5 6.8 %all-to-all-done.3.refs_2_ = bf16[16,16,128]{2,1,0:T(8,128)(2,1)S(1)} async-done(((bf16[16,16,128]{2,1,0:T(8,128)(2,1)}), bf16[16,16,128]{2,1,0:T(8,128)(2,1)S(1)}, u32[]{:S(2)}, u32[]{:S(2)}) %all-to-all-start.3) | async-done | bytes 65568 | tf_op jit(solution)/shard_map/all_to_all | solution.py:173
  62.4 1.5 %shard_map.68 = (bf16[2,16,2048]{2,1,0:T(8,128)(2,1)S(1)}, bf16[2,16,2048]{2,1,0:T(8,128)(2,1)S(1)}) custom-call(s32[8,128]{1,0:T(8,128)S(1)} %pad.4.refs_0_, s32[8,128]{1,0:T(8,128)S(1)} %collective-permute-done.refs_1_, bf16[16,16,128]{2,1,0:T(8,128)(2,1)S(1)} %all-to-all-done.3.refs_2_, bf16[2,16,2048]{2,1,0:T(8,128)(2,1)S(1)} %collective-permute-done.4.refs_2_.refs_3_, ...), custom_call_target="tpu_custom_call" | custom-call | tf_op jit(solution)/shard_map/pallas_call | solution.py:106
  63.9 1.6 %collective-permute-start.6 = (bf16[2,16,2048]{2,1,0:T(8,128)(2,1)S(1)}, bf16[2,16,2048]{2,1,0:T(8,128)(2,1)S(1)}, u32[]{:S(2)}, u32[]{:S(2)}) collective-permute-start(bf16[2,16,2048]{2,1,0:T(8,128)(2,1)S(1)} %get-tuple-element.17), channel_id=1, source_target_pairs={{0,16},{16,0},{1,17},{17,1},{2,18},{18,2},{3,19},{19,3},{4,20},{20... | collective-permute-start | bytes 393224 | tf_op jit(solution)/shard_map/ppermute | solution.py:182
  65.5 3.5 %collective-permute-done.6.refs_2_.refs_3_ = bf16[2,16,2048]{2,1,0:T(8,128)(2,1)S(1)} collective-permute-done((bf16[2,16,2048]{2,1,0:T(8,128)(2,1)S(1)}, bf16[2,16,2048]{2,1,0:T(8,128)(2,1)S(1)}, u32[]{:S(2)}, u32[]{:S(2)}) %collective-permute-start.6) | collective-permute-done | bytes 131104 | tf_op jit(solution)/shard_map/ppermute | solution.py:182
  68.9 2.7 %shard_map.69 = bf16[16,16,128]{2,1,0:T(8,128)(2,1)} custom-call(s32[8,128]{1,0:T(8,128)S(1)} %pad.4.refs_0_, s32[8,128]{1,0:T(8,128)S(1)} %collective-permute-done.refs_1_, bf16[2,16,2048]{2,1,0:T(8,128)(2,1)S(1)} %collective-permute-done.6.refs_2_.refs_3_, bf16[32,128,128]{2,1,0:T(8,128)(2,1)S(1)} %bitcast.85, ...), custom_call_target="tpu_custom_call" | custom-call | tf_op jit(solution)/shard_map/pallas_call | solution.py:106
  71.6 3.4 %all-to-all-start.4 = ((bf16[16,16,128]{2,1,0:T(8,128)(2,1)}), bf16[16,16,128]{2,1,0:T(8,128)(2,1)S(1)}, u32[]{:S(2)}, u32[]{:S(2)}) async-start(bf16[16,16,128]{2,1,0:T(8,128)(2,1)} %shard_map.69), calls=%async_computation.4 | async-start | bytes 131072 | tf_op jit(solution)/shard_map/all_to_all | solution.py:169
  75.0 1.6 %collective-permute-start.7 = (bf16[2,16,2048]{2,1,0:T(8,128)(2,1)S(1)}, bf16[2,16,2048]{2,1,0:T(8,128)(2,1)S(1)}, u32[]{:S(2)}, u32[]{:S(2)}) collective-permute-start(bf16[2,16,2048]{2,1,0:T(8,128)(2,1)S(1)} %get-tuple-element.19), channel_id=1, source_target_pairs={{0,16},{16,0},{1,17},{17,1},{2,18},{18,2},{3,19},{19,3},{4,20},{20... | collective-permute-start | bytes 393224 | tf_op jit(solution)/shard_map/ppermute | solution.py:184
  76.5 5.3 %all-to-all-done.4 = bf16[16,16,128]{2,1,0:T(8,128)(2,1)S(1)} async-done(((bf16[16,16,128]{2,1,0:T(8,128)(2,1)}), bf16[16,16,128]{2,1,0:T(8,128)(2,1)S(1)}, u32[]{:S(2)}, u32[]{:S(2)}) %all-to-all-start.4) | async-done | bytes 65568 | tf_op jit(solution)/shard_map/all_to_all | solution.py:169
  81.8 0.6 broadcast_in_dim.46
  82.5 3.4 %all-to-all-start.5 = ((bf16[16,16,128]{2,1,0:T(8,128)(2,1)}), bf16[16,16,128]{2,1,0:T(8,128)(2,1)S(1)}, u32[]{:S(2)}, u32[]{:S(2)}) async-start(bf16[16,16,128]{2,1,0:T(8,128)(2,1)} %bitcast.24), calls=%async_computation.5 | async-start | bytes 131072 | tf_op jit(solution)/shard_map/all_to_all | solution.py:173
  85.8 6.8 %all-to-all-done.5.refs_2_ = bf16[16,16,128]{2,1,0:T(8,128)(2,1)S(1)} async-done(((bf16[16,16,128]{2,1,0:T(8,128)(2,1)}), bf16[16,16,128]{2,1,0:T(8,128)(2,1)S(1)}, u32[]{:S(2)}, u32[]{:S(2)}) %all-to-all-start.5) | async-done | bytes 65568 | tf_op jit(solution)/shard_map/all_to_all | solution.py:173
  92.7 1.5 %shard_map.70 = (bf16[2,16,2048]{2,1,0:T(8,128)(2,1)S(1)}, bf16[2,16,2048]{2,1,0:T(8,128)(2,1)S(1)}) custom-call(s32[8,128]{1,0:T(8,128)S(1)} %pad.4.refs_0_, s32[8,128]{1,0:T(8,128)S(1)} %collective-permute-done.refs_1_, bf16[16,16,128]{2,1,0:T(8,128)(2,1)S(1)} %all-to-all-done.5.refs_2_, bf16[2,16,2048]{2,1,0:T(8,128)(2,1)S(1)} %collective-permute-done.6.refs_2_.refs_3_, ...), custom_call_target="tpu_custom_call" | custom-call | tf_op jit(solution)/shard_map/pallas_call | solution.py:106
  94.2 1.6 %collective-permute-start.8 = (bf16[2,16,2048]{2,1,0:T(8,128)(2,1)S(1)}, bf16[2,16,2048]{2,1,0:T(8,128)(2,1)S(1)}, u32[]{:S(2)}, u32[]{:S(2)}) collective-permute-start(bf16[2,16,2048]{2,1,0:T(8,128)(2,1)S(1)} %get-tuple-element.20), channel_id=1, source_target_pairs={{0,16},{16,0},{1,17},{17,1},{2,18},{18,2},{3,19},{19,3},{4,20},{20... | collective-permute-start | bytes 393224 | tf_op jit(solution)/shard_map/ppermute | solution.py:182
  95.8 4.8 %collective-permute-done.8.refs_2_.refs_3_ = bf16[2,16,2048]{2,1,0:T(8,128)(2,1)S(1)} collective-permute-done((bf16[2,16,2048]{2,1,0:T(8,128)(2,1)S(1)}, bf16[2,16,2048]{2,1,0:T(8,128)(2,1)S(1)}, u32[]{:S(2)}, u32[]{:S(2)}) %collective-permute-start.8) | collective-permute-done | bytes 131104 | tf_op jit(solution)/shard_map/ppermute | solution.py:182
  100.6 2.7 %shard_map.71 = bf16[16,16,128]{2,1,0:T(8,128)(2,1)} custom-call(s32[8,128]{1,0:T(8,128)S(1)} %pad.4.refs_0_, s32[8,128]{1,0:T(8,128)S(1)} %collective-permute-done.refs_1_, bf16[2,16,2048]{2,1,0:T(8,128)(2,1)S(1)} %collective-permute-done.8.refs_2_.refs_3_, bf16[32,128,128]{2,1,0:T(8,128)(2,1)S(1)} %bitcast.87, ...), custom_call_target="tpu_custom_call" | custom-call | tf_op jit(solution)/shard_map/pallas_call | solution.py:106
  103.3 3.4 %all-to-all-start.6 = ((bf16[16,16,128]{2,1,0:T(8,128)(2,1)}), bf16[16,16,128]{2,1,0:T(8,128)(2,1)S(1)}, u32[]{:S(2)}, u32[]{:S(2)}) async-start(bf16[16,16,128]{2,1,0:T(8,128)(2,1)} %shard_map.71), calls=%async_computation.6 | async-start | bytes 131072 | tf_op jit(solution)/shard_map/all_to_all | solution.py:169
  106.6 1.6 %collective-permute-start.9 = (bf16[2,16,2048]{2,1,0:T(8,128)(2,1)S(1)}, bf16[2,16,2048]{2,1,0:T(8,128)(2,1)S(1)}, u32[]{:S(2)}, u32[]{:S(2)}) collective-permute-start(bf16[2,16,2048]{2,1,0:T(8,128)(2,1)S(1)} %get-tuple-element.22), channel_id=1, source_target_pairs={{0,16},{16,0},{1,17},{17,1},{2,18},{18,2},{3,19},{19,3},{4,20},{20... | collective-permute-start | bytes 393224 | tf_op jit(solution)/shard_map/ppermute | solution.py:184
  108.2 5.3 %all-to-all-done.6 = bf16[16,16,128]{2,1,0:T(8,128)(2,1)S(1)} async-done(((bf16[16,16,128]{2,1,0:T(8,128)(2,1)}), bf16[16,16,128]{2,1,0:T(8,128)(2,1)S(1)}, u32[]{:S(2)}, u32[]{:S(2)}) %all-to-all-start.6) | async-done | bytes 65568 | tf_op jit(solution)/shard_map/all_to_all | solution.py:169
  113.5 0.6 broadcast_in_dim.48
  114.1 3.4 %all-to-all-start.7 = ((bf16[16,16,128]{2,1,0:T(8,128)(2,1)}), bf16[16,16,128]{2,1,0:T(8,128)(2,1)S(1)}, u32[]{:S(2)}, u32[]{:S(2)}) async-start(bf16[16,16,128]{2,1,0:T(8,128)(2,1)} %bitcast.28), calls=%async_computation.7 | async-start | bytes 131072 | tf_op jit(solution)/shard_map/all_to_all | solution.py:173
  117.5 6.8 %all-to-all-done.7.refs_2_ = bf16[16,16,128]{2,1,0:T(8,128)(2,1)S(1)} async-done(((bf16[16,16,128]{2,1,0:T(8,128)(2,1)}), bf16[16,16,128]{2,1,0:T(8,128)(2,1)S(1)}, u32[]{:S(2)}, u32[]{:S(2)}) %all-to-all-start.7) | async-done | bytes 65568 | tf_op jit(solution)/shard_map/all_to_all | solution.py:173
  124.3 1.5 %shard_map.72 = f32[2,16,2048]{2,1,0:T(8,128)S(1)} custom-call(s32[8,128]{1,0:T(8,128)S(1)} %pad.4.refs_0_, s32[8,128]{1,0:T(8,128)S(1)} %collective-permute-done.refs_1_, bf16[16,16,128]{2,1,0:T(8,128)(2,1)S(1)} %all-to-all-done.7.refs_2_, bf16[2,16,2048]{2,1,0:T(8,128)(2,1)S(1)} %collective-permute-done.8.refs_2_.refs_3_, ...), custom_call_target="tpu_custom_call" | custom-call | tf_op jit(solution)/shard_map/pallas_call | solution.py:106
  125.9 1.3 %collective-permute-done.10 = f32[16,2048]{1,0:T(8,128)S(1)} collective-permute-done((f32[16,2048]{1,0:T(8,128)S(1)}, f32[16,2048]{1,0:T(8,128)S(1)}, u32[]{:S(2)}, u32[]{:S(2)}) %collective-permute-start.10) | collective-permute-done | bytes 131104 | tf_op jit(solution)/shard_map/ppermute | solution.py:185
  127.3 0.7 maximum_select_fusion
  (22 shorter events, 0.3 us)
Async XLA Ops:
  0.0 4.4 %copy-start = (bf16[1,32,128,128]{3,2,1,0:T(8,128)(2,1)S(1)}, bf16[1,32,128,128]{3,2,1,0:T(8,128)(2,1)}, u32[]{:S(2)}) copy-start(bf16[1,32,128,128]{3,2,1,0:T(8,128)(2,1)} %param.7) | copy-start | bytes 3145732
  0.0 4.4 %collective-permute-start.3 = (bf16[32,128,128]{2,1,0:T(8,128)(2,1)}, bf16[32,128,128]{2,1,0:T(8,128)(2,1)S(1)}, u32[]{:S(2)}, u32[]{:S(2)}) collective-permute-start(bf16[32,128,128]{2,1,0:T(8,128)(2,1)} %bitcast.79), channel_id=1, source_target_pairs={{0,1},{1,0},{2,3},{3,2},{4,5},{5,4},{6,7},{7,6},{8,9},{9,8},{10,11... | collective-permute-start | bytes 3145736 | tf_op jit(solution)/shard_map/ppermute | solution.py:146
  1.4 2.9 %collective-permute-start.2 = (f32[16,2048]{1,0:T(8,128)S(1)}, f32[16,2048]{1,0:T(8,128)S(1)}, u32[]{:S(2)}, u32[]{:S(2)}) collective-permute-start(f32[16,2048]{1,0:T(8,128)S(1)} %get-tuple-element.26), channel_id=1, source_target_pairs={{0,1},{1,0},{2,3},{3,2},{4,5},{5,4},{6,7},{7,6},{8,9},{9,8},{10,11... | collective-permute-start | bytes 393224 | tf_op jit(solution)/shard_map/ppermute | solution.py:145
  3.1 1.3 %collective-permute-start = (s32[8,128]{1,0:T(8,128)S(1)}, s32[8,128]{1,0:T(8,128)S(1)}, u32[]{:S(2)}, u32[]{:S(2)}) collective-permute-start(s32[8,128]{1,0:T(8,128)S(1)} %pad.4.refs_0_), channel_id=1, source_target_pairs={{0,1},{1,0},{2,3},{3,2},{4,5},{5,4},{6,7},{7,6},{8,9},{9,8},{10,11... | collective-permute-start | bytes 12296 | tf_op jit(solution)/shard_map/ppermute | solution.py:147
  4.2 10.0 %collective-permute-start.1 = (s32[2,16,128]{2,1,0:T(8,128)S(1)}, s32[2,16,128]{2,1,0:T(8,128)S(1)}, u32[]{:S(2)}, u32[]{:S(2)}) collective-permute-start(s32[2,16,128]{2,1,0:T(8,128)S(1)} %get-tuple-element.28), channel_id=1, source_target_pairs={{0,1},{1,0},{2,3},{3,2},{4,5},{5,4},{6,7},{7,6},{8,9},{9,8},{10,11... | collective-permute-start | bytes 49160 | tf_op jit(solution)/shard_map/ppermute | solution.py:148
  7.1 14.1 %all-to-all-start = ((bf16[16,16,128]{2,1,0:T(8,128)(2,1)}), bf16[16,16,128]{2,1,0:T(8,128)(2,1)S(1)}, u32[]{:S(2)}, u32[]{:S(2)}) async-start(bf16[16,16,128]{2,1,0:T(8,128)(2,1)} %shard_map.64), calls=%async_computation | async-start | bytes 131072 | tf_op jit(solution)/shard_map/all_to_all | solution.py:169
  21.9 10.2 %all-to-all-start.1 = ((bf16[16,16,128]{2,1,0:T(8,128)(2,1)}), bf16[16,16,128]{2,1,0:T(8,128)(2,1)S(1)}, u32[]{:S(2)}, u32[]{:S(2)}) async-start(bf16[16,16,128]{2,1,0:T(8,128)(2,1)} %bitcast.16), calls=%async_computation.1 | async-start | bytes 131072 | tf_op jit(solution)/shard_map/all_to_all | solution.py:173
  33.6 5.0 %collective-permute-start.4 = (bf16[2,16,2048]{2,1,0:T(8,128)(2,1)S(1)}, bf16[2,16,2048]{2,1,0:T(8,128)(2,1)S(1)}, u32[]{:S(2)}, u32[]{:S(2)}) collective-permute-start(bf16[2,16,2048]{2,1,0:T(8,128)(2,1)S(1)} %get-tuple-element.14), channel_id=1, source_target_pairs={{0,16},{16,0},{1,17},{17,1},{2,18},{18,2},{3,19},{19,3},{4,20},{20... | collective-permute-start | bytes 393224 | tf_op jit(solution)/shard_map/ppermute | solution.py:182
  41.3 10.2 %all-to-all-start.2 = ((bf16[16,16,128]{2,1,0:T(8,128)(2,1)}), bf16[16,16,128]{2,1,0:T(8,128)(2,1)S(1)}, u32[]{:S(2)}, u32[]{:S(2)}) async-start(bf16[16,16,128]{2,1,0:T(8,128)(2,1)} %shard_map.67), calls=%async_computation.2 | async-start | bytes 131072 | tf_op jit(solution)/shard_map/all_to_all | solution.py:169
  44.7 10.9 %collective-permute-start.5 = (bf16[2,16,2048]{2,1,0:T(8,128)(2,1)S(1)}, bf16[2,16,2048]{2,1,0:T(8,128)(2,1)S(1)}, u32[]{:S(2)}, u32[]{:S(2)}) collective-permute-start(bf16[2,16,2048]{2,1,0:T(8,128)(2,1)S(1)} %get-tuple-element.16), channel_id=1, source_target_pairs={{0,16},{16,0},{1,17},{17,1},{2,18},{18,2},{3,19},{19,3},{4,20},{20... | collective-permute-start | bytes 393224 | tf_op jit(solution)/shard_map/ppermute | solution.py:184
  52.2 10.2 %all-to-all-start.3 = ((bf16[16,16,128]{2,1,0:T(8,128)(2,1)}), bf16[16,16,128]{2,1,0:T(8,128)(2,1)S(1)}, u32[]{:S(2)}, u32[]{:S(2)}) async-start(bf16[16,16,128]{2,1,0:T(8,128)(2,1)} %bitcast.20), calls=%async_computation.3 | async-start | bytes 131072 | tf_op jit(solution)/shard_map/all_to_all | solution.py:173
  63.9 5.0 %collective-permute-start.6 = (bf16[2,16,2048]{2,1,0:T(8,128)(2,1)S(1)}, bf16[2,16,2048]{2,1,0:T(8,128)(2,1)S(1)}, u32[]{:S(2)}, u32[]{:S(2)}) collective-permute-start(bf16[2,16,2048]{2,1,0:T(8,128)(2,1)S(1)} %get-tuple-element.17), channel_id=1, source_target_pairs={{0,16},{16,0},{1,17},{17,1},{2,18},{18,2},{3,19},{19,3},{4,20},{20... | collective-permute-start | bytes 393224 | tf_op jit(solution)/shard_map/ppermute | solution.py:182
  71.6 10.2 %all-to-all-start.4 = ((bf16[16,16,128]{2,1,0:T(8,128)(2,1)}), bf16[16,16,128]{2,1,0:T(8,128)(2,1)S(1)}, u32[]{:S(2)}, u32[]{:S(2)}) async-start(bf16[16,16,128]{2,1,0:T(8,128)(2,1)} %shard_map.69), calls=%async_computation.4 | async-start | bytes 131072 | tf_op jit(solution)/shard_map/all_to_all | solution.py:169
  75.0 10.9 %collective-permute-start.7 = (bf16[2,16,2048]{2,1,0:T(8,128)(2,1)S(1)}, bf16[2,16,2048]{2,1,0:T(8,128)(2,1)S(1)}, u32[]{:S(2)}, u32[]{:S(2)}) collective-permute-start(bf16[2,16,2048]{2,1,0:T(8,128)(2,1)S(1)} %get-tuple-element.19), channel_id=1, source_target_pairs={{0,16},{16,0},{1,17},{17,1},{2,18},{18,2},{3,19},{19,3},{4,20},{20... | collective-permute-start | bytes 393224 | tf_op jit(solution)/shard_map/ppermute | solution.py:184
  82.5 10.2 %all-to-all-start.5 = ((bf16[16,16,128]{2,1,0:T(8,128)(2,1)}), bf16[16,16,128]{2,1,0:T(8,128)(2,1)S(1)}, u32[]{:S(2)}, u32[]{:S(2)}) async-start(bf16[16,16,128]{2,1,0:T(8,128)(2,1)} %bitcast.24), calls=%async_computation.5 | async-start | bytes 131072 | tf_op jit(solution)/shard_map/all_to_all | solution.py:173
  94.2 6.4 %collective-permute-start.8 = (bf16[2,16,2048]{2,1,0:T(8,128)(2,1)S(1)}, bf16[2,16,2048]{2,1,0:T(8,128)(2,1)S(1)}, u32[]{:S(2)}, u32[]{:S(2)}) collective-permute-start(bf16[2,16,2048]{2,1,0:T(8,128)(2,1)S(1)} %get-tuple-element.20), channel_id=1, source_target_pairs={{0,16},{16,0},{1,17},{17,1},{2,18},{18,2},{3,19},{19,3},{4,20},{20... | collective-permute-start | bytes 393224 | tf_op jit(solution)/shard_map/ppermute | solution.py:182
  103.3 10.2 %all-to-all-start.6 = ((bf16[16,16,128]{2,1,0:T(8,128)(2,1)}), bf16[16,16,128]{2,1,0:T(8,128)(2,1)S(1)}, u32[]{:S(2)}, u32[]{:S(2)}) async-start(bf16[16,16,128]{2,1,0:T(8,128)(2,1)} %shard_map.71), calls=%async_computation.6 | async-start | bytes 131072 | tf_op jit(solution)/shard_map/all_to_all | solution.py:169
  106.6 10.9 %collective-permute-start.9 = (bf16[2,16,2048]{2,1,0:T(8,128)(2,1)S(1)}, bf16[2,16,2048]{2,1,0:T(8,128)(2,1)S(1)}, u32[]{:S(2)}, u32[]{:S(2)}) collective-permute-start(bf16[2,16,2048]{2,1,0:T(8,128)(2,1)S(1)} %get-tuple-element.22), channel_id=1, source_target_pairs={{0,16},{16,0},{1,17},{17,1},{2,18},{18,2},{3,19},{19,3},{4,20},{20... | collective-permute-start | bytes 393224 | tf_op jit(solution)/shard_map/ppermute | solution.py:184
  114.1 10.2 %all-to-all-start.7 = ((bf16[16,16,128]{2,1,0:T(8,128)(2,1)}), bf16[16,16,128]{2,1,0:T(8,128)(2,1)S(1)}, u32[]{:S(2)}, u32[]{:S(2)}) async-start(bf16[16,16,128]{2,1,0:T(8,128)(2,1)} %bitcast.28), calls=%async_computation.7 | async-start | bytes 131072 | tf_op jit(solution)/shard_map/all_to_all | solution.py:173
  125.9 1.4 %collective-permute-start.10 = (f32[16,2048]{1,0:T(8,128)S(1)}, f32[16,2048]{1,0:T(8,128)S(1)}, u32[]{:S(2)}, u32[]{:S(2)}) collective-permute-start(f32[16,2048]{1,0:T(8,128)S(1)} %get-tuple-element.24), channel_id=1, source_target_pairs={{0,1},{1,0},{2,3},{3,2},{4,5},{5,4},{6,7},{7,6},{8,9},{9,8},{10,11... | collective-permute-start | bytes 393224 | tf_op jit(solution)/shard_map/ppermute | solution.py:185

commit v3 on v1

v3 whole, which is shorter than its diff:
```python
import jax
import jax.numpy as jnp
from jax import lax
from jax.experimental import pallas as pl
from jax.experimental.pallas import tpu as pltpu
from jax.sharding import PartitionSpec as P

TILE_GROUP = 32
ROUNDS = 4
CORES = 2
LANES = 128
VMEM_LIMIT = 40 * 1024 * 1024


def each_live(index_ref, slots, body):
    live = index_ref[2, 0]
    for group in range(-(-slots // TILE_GROUP)):
        first, last = group * TILE_GROUP, min(slots, (group + 1) * TILE_GROUP)

        @pl.when(group < live)
        def _():
            for t in range(first, last, 2):
                body(tuple(range(t, min(t + 2, last))))


def add_products(acc, left_of, targets, wide, transposed):
    left = jnp.concatenate(left_of, axis=0)
    dims = (((1,), (1,)), ((), ())) if transposed else (((1,), (0,)), ((), ()))
    part = lax.dot_general(left, wide, dims, preferred_element_type=jnp.float32)
    rows, size = acc.shape[1:]
    for i, at in enumerate(targets):
        used = part[i * left_of[i].shape[0]:, i * size:(i + 1) * size][:rows]
        acc[at] = acc[at] + used


def project_into(acc, low, index_refs, tile_refs):
    blocks = low.shape[0] // CORES
    acc[...] = jnp.zeros_like(acc)
    for k in range(CORES):
        index_ref, tiles_ref = index_refs[k], tile_refs[k]

        def body(ts):
            wide = jnp.concatenate([tiles_ref[t] for t in ts], axis=0)
            add_products(acc, [low[k * blocks + index_ref[0, t]] for t in ts],
                         [index_ref[1, t] for t in ts], wide, True)

        each_live(index_ref, tiles_ref.shape[0], body)


def back_into(acc, ratios, index_refs, tile_refs):
    blocks = acc.shape[0] // CORES
    acc[...] = jnp.zeros_like(acc)
    for k in range(CORES):
        index_ref, tiles_ref = index_refs[k], tile_refs[k]

        def body(ts):
            wide = jnp.concatenate([tiles_ref[t] for t in ts], axis=1)
            add_products(acc, [ratios(index_ref[1, t]) for t in ts],
                         [k * blocks + index_ref[0, t] for t in ts], wide, False)

        each_live(index_ref, tiles_ref.shape[0], body)


def columns(blocks, size):
    for k in range(CORES):
        for b in range(blocks):
            yield k, slice(b * size, (b + 1) * size), k * blocks + b


def project_kernel(ins, outs, low, acc):
    blocks, size = low.shape[0] // CORES, low.shape[-1]
    for k, cols, at in columns(blocks, size):
        low[at] = ins["held"][k][:, cols].astype(jnp.bfloat16)
    project_into(acc, low, ins["index"], ins["tiles"])
    outs["wide"][...] = acc[...]
    outs["sent"][...] = acc[...].astype(jnp.bfloat16)


def sensitivity_kernel(ins, outs, acc):
    ones = jnp.ones((16, ins["tiles"][0].shape[1]), jnp.bfloat16)
    back_into(acc, lambda ray: ones, ins["index"], ins["tiles"])
    outs["inverse"][...] = 1.0 / acc[...]


def update_kernel(ins, outs, ratios, back, *scratch):
    blocks, size = back.shape[0] // CORES, back.shape[-1]
    total = ins["wide"][...] + ins["got"][...].astype(jnp.float32)
    ratios[...] = (ins["counts"][...].astype(jnp.float32) / total).astype(jnp.bfloat16)
    back_into(back, lambda ray: ratios[ray], ins["index"], ins["tiles"])
    for k, cols, at in columns(blocks, size):
        held = sum(part[k][:, cols].astype(jnp.float32) for part in ins["held"])
        value = held * back[at] * ins["inverse"][at, :1]
        high = value.astype(jnp.bfloat16)
        if "high" in outs:
            outs["high"][k, :, cols] = high
            outs["low"][k, :, cols] = (value - high.astype(jnp.float32)).astype(jnp.bfloat16)
        else:
            outs["held"][k, :, cols] = value
        if "sent" in outs:
            scratch[0][at] = high
    if "sent" in outs:
        project_into(scratch[1], scratch[0], ins["next_index"], ins["next_tiles"])
        outs["wide"][...] = scratch[1][...]
        outs["sent"][...] = scratch[1][...].astype(jnp.bfloat16)


def call(kernel, ins, outs, scratch):
    def spec(path, _):
        name = path[0].key
        return pl.BlockSpec(memory_space=pltpu.SMEM if name.endswith("index") else pltpu.VMEM)

    return pl.pallas_call(
        kernel,
        out_shape=outs,
        in_specs=[jax.tree_util.tree_map_with_path(spec, ins)],
        out_specs=jax.tree_util.tree_map_with_path(spec, outs),
        scratch_shapes=scratch,
        compiler_params=pltpu.CompilerParams(vmem_limit_bytes=VMEM_LIMIT))(ins)


def shards(images, system_tiles, tile_vox, tile_ray, live_blocks, counts):
    frames, voxels = images.shape
    half = frames // CORES
    size = system_tiles.shape[-1]
    vox_blocks = voxels // size
    own_tiles = system_tiles[0]
    slots = own_tiles.shape[0]
    tile_devs = lax.axis_size("tile")
    chips = tile_devs // CORES
    rb_dev = counts.shape[2] // size
    ray_blocks = rb_dev * tile_devs
    subset_count = lax.axis_size("subset")
    position = lax.axis_index("subset")
    core = lax.axis_index("tile") % CORES
    both = CORES * vox_blocks
    f32, bf16 = jnp.float32, jnp.bfloat16
    shaped = jax.ShapeDtypeStruct

    def swap_cores(array):
        return lax.ppermute(array, "tile", [(i, i ^ 1) for i in range(tile_devs)])

    def swap_chips(array, step):
        pairs = [(CORES * j + c, CORES * (j ^ step) + c) for j in range(chips) for c in range(CORES)]
        return lax.ppermute(array, "tile", pairs)

    def joined(side, own, other):
        return jnp.where(side == 0, jnp.concatenate([own, other]), jnp.concatenate([other, own]))

    def shift(array):
        return lax.ppermute(array, "subset", [(i, (i + 1) % subset_count) for i in range(subset_count)])

    halves = images.reshape(CORES, half, voxels)
    mine = lax.dynamic_index_in_dim(halves, core, 0, keepdims=False)
    theirs = lax.dynamic_index_in_dim(halves, 1 - core, 0, keepdims=False)
    rows = jnp.concatenate([tile_vox, tile_ray, jnp.broadcast_to(live_blocks, tile_vox.shape)], axis=0)
    own_index = jnp.pad(rows, ((0, 5), (0, -slots % LANES)))
    tiles = (own_tiles, swap_cores(own_tiles))
    held = ((mine, swap_cores(theirs)),)
    index = (own_index, swap_cores(own_index))

    dealt = counts[0].astype(bf16).reshape(subset_count, CORES, half, rb_dev, size).transpose(1, 3, 0, 2, 4)
    kept = lax.dynamic_index_in_dim(dealt, core, 0, keepdims=False)
    got = swap_cores(lax.dynamic_index_in_dim(dealt, 1 - core, 0, keepdims=False))
    all_counts = joined(core, kept, got)
    step = 1
    while step < chips:
        side = lax.axis_index("tile") // CORES // step % 2
        all_counts = joined(side, all_counts, swap_chips(all_counts, step))
        step *= 2

    def counts_of(panel):
        return lax.dynamic_index_in_dim(all_counts, panel % subset_count, 1, keepdims=False)

    def sensitivity(index, tiles):
        return call(sensitivity_kernel, {"index": index, "tiles": tiles},
                    {"inverse": shaped((both, 8, size), f32)},
                    [pltpu.VMEM((both, 8, size), f32)])["inverse"]

    inverse = sensitivity(index, tiles)
    sets = [(index, tiles, inverse)] * ROUNDS
    moves = [True] * (ROUNDS - 1)
    now = [counts_of(position - r) for r in range(ROUNDS)]
    if subset_count == 2:
        far_index, far_tiles, far_counts = shift(own_index), shift(own_tiles), shift(now[0])
        far_index, far_tiles = (far_index, swap_cores(far_index)), (far_tiles, swap_cores(far_tiles))
        far = (far_index, far_tiles, sensitivity(far_index, far_tiles))
        for r in range(2, ROUNDS, 2):
            sets[r], now[r] = far, far_counts
        moves = [r == 0 for r in range(ROUNDS - 1)]
        if ROUNDS % 2:
            moves[-1] = True

    sums = {"wide": shaped((ray_blocks, half, size), f32), "sent": shaped((ray_blocks, half, size), bf16)}
    sum_scratch = [pltpu.VMEM((both, half, size), bf16), pltpu.VMEM((ray_blocks, half, size), f32)]

    def project(held, r):
        return call(project_kernel, {"held": held, "index": sets[r][0], "tiles": sets[r][1]},
                    sums, sum_scratch)

    out = project(held[0], 0)
    for r in range(ROUNDS):
        wide, sent = out["wide"], out["sent"]
        step = 1
        while step < chips:
            got = swap_chips(sent, step)
            step *= 2
            if step < chips:
                wide = wide + got.astype(f32)
                sent = wide.astype(bf16)
        ins = {"wide": wide, "got": got, "counts": now[r], "held": held,
               "index": sets[r][0], "tiles": sets[r][1], "inverse": sets[r][2]}
        scratch = [pltpu.VMEM((ray_blocks, half, size), bf16), pltpu.VMEM((both, half, size), f32)]
        panel = (CORES, half, voxels)
        if r + 1 == ROUNDS:
            held = call(update_kernel, ins, {"held": shaped(panel, f32)}, scratch)["held"]
        elif moves[r]:
            out = call(update_kernel, ins, {"high": shaped(panel, bf16), "low": shaped(panel, bf16)}, scratch)
            high = shift(out["high"])
            low, _ = lax.optimization_barrier((out["low"], high))
            held = (high, shift(low))
            out = project(high, r + 1)
        else:
            ins.update(next_index=sets[r + 1][0], next_tiles=sets[r + 1][1])
            out = call(update_kernel, ins, {"held": shaped(panel, f32), **sums}, scratch + sum_scratch)
            held = (out["held"],)
    return joined(core, held[0], swap_cores(held[1]))


def solution(mesh):
    in_specs = (
        P("subset", "tile"),
        P("subset", "tile", None, None),
        P("subset", "tile"),
        P("subset", "tile"),
        P("subset", "tile"),
        P("subset", None, "tile"),
    )
    return jax.shard_map(shards, mesh=mesh, in_specs=in_specs, out_specs=P("subset", "tile"),
                         check_vma=False)
```

time: 131 us -> 96.1 us (0.73)
  blocking collectives: 42.1 us -> 0 us
  starting transfers between devices: 22.6 us -> 35.9 us
  waiting for transfers between devices: 49.7 us -> 42 us
    all_to_all x4 -> x0, blocking collectives: 42.1 us -> none  [shards(): lax.all_to_all(spread.reshape(ray_blocks, frames, size), 'tile', 0, 0, ti...]
    all_to_all x4 -> x0, waiting for transfers between devices: 31.5 us -> none  [shards(): got = lax.all_to_all(partial, 'tile', 0, 0, tiled=True)]
    ppermute x3 -> x27, starting transfers between devices: 4.66 us -> 35.9 us  [the longest x15 26.2 us: swap_chips(): return lax.ppermute(array, 'tile', pairs)]
    ppermute x3 -> x27, waiting for transfers between devices: 18.2 us -> 42 us  [the longest x15 26.6 us: swap_chips(): return lax.ppermute(array, 'tile', pairs)]
    all_to_all x4 -> x0, starting transfers between devices: 17.9 us -> none  [shards(): got = lax.all_to_all(partial, 'tile', 0, 0, tiled=True)]
    unnamed x14 -> x10, local copies, waits for them, and re-layouts: 2.85 us -> 1.54 us
  transfers between devices with their start and end apart: 7 -> 27, of which waited for: 7 -> 18; matrix products, arithmetic and copies ran while one was open for 0% -> 1% of each run, Pallas kernels for 0% -> 7%
where the time goes in v3:
time: 96.1 us; the launch traced here: 95.8 us
  waiting for transfers between devices  42 us (44%)
  starting transfers between devices  35.9 us (37%)
  Pallas kernels  13.2 us (14%)
  local copies, waits for them, and re-layouts  2.65 us (3%)
  other arithmetic  1.02 us (1%)
  between operations  1.01 us (1%)
    ppermute x15, waiting for transfers between devices, swap_chips(): return lax.ppermute(array, 'tile', pairs)  26.6 us
    ppermute x15, starting transfers between devices, swap_chips(): return lax.ppermute(array, 'tile', pairs)  26.2 us
    pallas_call x8, Pallas kernels, call(): pl.pallas_call(kernel, out_shape=outs, in_specs=[jax.tree_util.tree_map_w...  13.2 us
    ppermute x5, waiting for transfers between devices, shift(): lax.ppermute(array, 'subset', [(i, (i + 1) % subset_count) for i in range...  11.8 us
    ppermute x5, starting transfers between devices, shift(): lax.ppermute(array, 'subset', [(i, (i + 1) % subset_count) for i in range...  8.63 us
    ppermute x7, waiting for transfers between devices, swap_cores(): return lax.ppermute(array, 'tile', [(i, i ^ 1) for i in range(tile_devs)])  3.54 us
  transfers between devices with their start and end apart: 27, of which 18 were waited for; matrix products, arithmetic and copies ran while one was open for 1% of the time, Pallas kernels for 7%

profile of v3, /device:TPU:0, one launch (start us, length us, event | category | flops | bytes accessed | tf_op | source)
XLA Modules:
  0.0 95.8 jit_solution(15278915105132929217)
XLA Ops:
  0.8 0.5 collective-permute-start
  1.3 2.6 %collective-permute-start.18 = (bf16[32,128,128]{2,1,0:T(8,128)(2,1)}, bf16[32,128,128]{2,1,0:T(8,128)(2,1)S(1)}, u32[]{:S(2)}, u32[]{:S(2)}) collective-permute-start(bf16[32,128,128]{2,1,0:T(8,128)(2,1)} %bitcast.26), channel_id=1, source_target_pairs={{0,16},{16,0},{1,17},{17,1},{2,18},{18,2},{3,19},{19,3},{4,20},{20... | collective-permute-start | bytes 3145736 | tf_op jit(solution)/shard_map/ppermute | solution.py:150
  3.9 1.8 %collective-permute-start.1 = (bf16[2,2,16,128]{3,2,0,1:T(8,128)(2,1)S(1)}, bf16[2,2,16,128]{3,2,0,1:T(8,128)(2,1)S(1)}, u32[]{:S(2)}, u32[]{:S(2)}) collective-permute-start(bf16[2,2,16,128]{3,2,0,1:T(8,128)(2,1)S(1)} %maximum_select_fusion.4), channel_id=1, source_target_pairs={{0,2},{1,3},{2,0},{3,1},{4,6},{5,7},{6,4},{7,5},{8,10},{9,11},{10,... | collective-permute-start | bytes 49160 | tf_op jit(solution)/shard_map/ppermute | solution.py:144
  5.6 1.0 %dynamic-slice_bitcast_fusion = (f32[16,2048]{1,0:T(8,128)S(1)}, f32[16,2048]{1,0:T(8,128)S(1)}) fusion(f32[2,16,2048]{2,1,0:T(8,128)} %bitcast.34, s32[]{:T(128)S(6)} %select_n.117, s32[]{:T(128)S(6)} %select_n.116), kind=kLoop, calls=%fused_computation.12 | loop fusion | bytes 524296 | tf_op jit(solution)/shard_map/jit(dynamic_index_in_dim)/squeeze | solution.py:154
  7.7 1.8 %collective-permute-start.2 = (bf16[4,2,16,128]{3,2,0,1:T(8,128)(2,1)S(1)}, bf16[4,2,16,128]{3,2,0,1:T(8,128)(2,1)S(1)}, u32[]{:S(2)}, u32[]{:S(2)}) collective-permute-start(bf16[4,2,16,128]{3,2,0,1:T(8,128)(2,1)S(1)} %maximum_select_fusion.3), channel_id=1, source_target_pairs={{0,4},{1,5},{2,6},{3,7},{4,0},{5,1},{6,2},{7,3},{8,12},{9,13},{10,... | collective-permute-start | bytes 98312 | tf_op jit(solution)/shard_map/ppermute | solution.py:144
  9.7 1.0 %collective-permute-done.6.ins__index___1_.ins__next_index___1_ = s32[8,128]{1,0:T(8,128)S(1)} collective-permute-done((s32[8,128]{1,0:T(8,128)S(1)}, s32[8,128]{1,0:T(8,128)S(1)}, u32[]{:S(2)}, u32[]{:S(2)}) %collective-permute-start.6) | collective-permute-done | bytes 4128 | tf_op jit(solution)/shard_map/ppermute | solution.py:140
  10.8 1.2 %copy-done = bf16[1,32,128,128]{3,2,1,0:T(8,128)(2,1)S(1)} copy-done((bf16[1,32,128,128]{3,2,1,0:T(8,128)(2,1)S(1)}, bf16[1,32,128,128]{3,2,1,0:T(8,128)(2,1)}, u32[]{:S(2)}) %copy-start) | copy-done | bytes 1048600
  12.0 1.6 %shard_map.64 = (bf16[16,16,128]{2,1,0:T(8,128)(2,1)S(1)}, f32[16,16,128]{2,1,0:T(8,128)S(1)}) custom-call(f32[16,2048]{1,0:T(8,128)S(1)} %get-tuple-element.42.ins__held___0_.ins__held___0__0_, f32[16,2048]{1,0:T(8,128)S(1)} %collective-permute-done.5.ins__held___1_.ins__held___0__1_, s32[8,128]{1,0:T(8,128)S(1)} %pad.4.ins__index___0_.ins__next_index___0_, ...), custom_call_target="tpu_custom_call" | custom-call | tf_op jit(solution)/shard_map/pallas_call | solution.py:112
  13.7 1.6 %collective-permute-start.8 = (bf16[16,16,128]{2,1,0:T(8,128)(2,1)S(1)}, bf16[16,16,128]{2,1,0:T(8,128)(2,1)S(1)}, u32[]{:S(2)}, u32[]{:S(2)}) collective-permute-start(bf16[16,16,128]{2,1,0:T(8,128)(2,1)S(1)} %get-tuple-element.19), channel_id=1, source_target_pairs={{0,2},{1,3},{2,0},{3,1},{4,6},{5,7},{6,4},{7,5},{8,10},{9,11},{10,... | collective-permute-start | bytes 196616 | tf_op jit(solution)/shard_map/ppermute | solution.py:144
  15.3 2.7 %collective-permute-start.3 = (bf16[8,2,16,128]{3,2,0,1:T(8,128)(2,1)S(1)}, bf16[8,2,16,128]{3,2,0,1:T(8,128)(2,1)S(1)}, u32[]{:S(2)}, u32[]{:S(2)}) collective-permute-start(bf16[8,2,16,128]{3,2,0,1:T(8,128)(2,1)S(1)} %maximum_select_fusion.2), channel_id=1, source_target_pairs={{0,8},{1,9},{2,10},{3,11},{4,12},{5,13},{6,14},{7,15},{8,0},{9,1},... | collective-permute-start | bytes 196616 | tf_op jit(solution)/shard_map/ppermute | solution.py:144
  18.0 0.5 collective-permute-start.9
  18.5 3.0 %collective-permute-done.3 = bf16[8,2,16,128]{3,2,0,1:T(8,128)(2,1)S(1)} collective-permute-done((bf16[8,2,16,128]{3,2,0,1:T(8,128)(2,1)S(1)}, bf16[8,2,16,128]{3,2,0,1:T(8,128)(2,1)S(1)}, u32[]{:S(2)}, u32[]{:S(2)}) %collective-permute-start.3) | collective-permute-done | bytes 65568 | tf_op jit(solution)/shard_map/ppermute | solution.py:144
  21.5 6.3 %collective-permute-done.18.ins__next_tiles___0_.ins__tiles___0_ = bf16[32,128,128]{2,1,0:T(8,128)(2,1)S(1)} collective-permute-done((bf16[32,128,128]{2,1,0:T(8,128)(2,1)}, bf16[32,128,128]{2,1,0:T(8,128)(2,1)S(1)}, u32[]{:S(2)}, u32[]{:S(2)}) %collective-permute-start.18) | collective-permute-done | bytes 1048608 | tf_op jit(solution)/shard_map/ppermute | solution.py:150
  27.8 2.9 %collective-permute-start.10 = (bf16[16,16,128]{2,1,0:T(8,128)(2,1)S(1)}, bf16[16,16,128]{2,1,0:T(8,128)(2,1)S(1)}, u32[]{:S(2)}, u32[]{:S(2)}) collective-permute-start(bf16[16,16,128]{2,1,0:T(8,128)(2,1)S(1)} %get-tuple-element.37), channel_id=1, source_target_pairs={{0,8},{1,9},{2,10},{3,11},{4,12},{5,13},{6,14},{7,15},{8,0},{9,1},... | collective-permute-start | bytes 196616 | tf_op jit(solution)/shard_map/ppermute | solution.py:144
  30.8 1.3 %shard_map.65.ins__inverse__ = f32[32,8,128]{2,1,0:T(8,128)S(1)} custom-call(s32[8,128]{1,0:T(8,128)S(1)} %pad.4.ins__index___0_.ins__next_index___0_, s32[8,128]{1,0:T(8,128)S(1)} %collective-permute-done.6.ins__index___1_.ins__next_index___1_, bf16[32,128,128]{2,1,0:T(8,128)(2,1)S(1)} %bitcast.28, ...), custom_call_target="tpu_custom_call" | custom-call | tf_op jit(solution)/shard_map/pallas_call | solution.py:112
  32.1 2.9 %collective-permute-done.10.ins__got__ = bf16[16,16,128]{2,1,0:T(8,128)(2,1)S(1)} collective-permute-done((bf16[16,16,128]{2,1,0:T(8,128)(2,1)S(1)}, bf16[16,16,128]{2,1,0:T(8,128)(2,1)S(1)}, u32[]{:S(2)}, u32[]{:S(2)}) %collective-permute-start.10) | collective-permute-done | bytes 65568 | tf_op jit(solution)/shard_map/ppermute | solution.py:144
  34.9 1.3 %shard_map.66 = (bf16[2,16,2048]{2,1,0:T(8,128)(2,1)S(1)}, bf16[2,16,2048]{2,1,0:T(8,128)(2,1)S(1)}) custom-call(bf16[16,16,128]{2,1,0:T(8,128)(2,1)S(1)} %get-tuple-element.44.ins__counts__, bf16[16,16,128]{2,1,0:T(8,128)(2,1)S(1)} %collective-permute-done.10.ins__got__, f32[16,2048]{1,0:T(8,128)S(1)} %get-tuple-element.42.ins__held___0_.ins__held___0__0_, ...), custom_call_target="tpu_custom_call" | custom-call | tf_op jit(solution)/shard_map/pallas_call | solution.py:112
  36.3 1.6 %collective-permute-start.11 = (bf16[2,16,2048]{2,1,0:T(8,128)(2,1)S(1)}, bf16[2,16,2048]{2,1,0:T(8,128)(2,1)S(1)}, u32[]{:S(2)}, u32[]{:S(2)}) collective-permute-start(bf16[2,16,2048]{2,1,0:T(8,128)(2,1)S(1)} %get-tuple-element.20), channel_id=1, source_target_pairs={{0,16},{16,0},{1,17},{17,1},{2,18},{18,2},{3,19},{19,3},{4,20},{20... | collective-permute-start | bytes 393224 | tf_op jit(solution)/shard_map/ppermute | solution.py:150
  37.9 3.4 %collective-permute-done.11.ins__held__.ins__held___0_ = bf16[2,16,2048]{2,1,0:T(8,128)(2,1)S(1)} collective-permute-done((bf16[2,16,2048]{2,1,0:T(8,128)(2,1)S(1)}, bf16[2,16,2048]{2,1,0:T(8,128)(2,1)S(1)}, u32[]{:S(2)}, u32[]{:S(2)}) %collective-permute-start.11) | collective-permute-done | bytes 131104 | tf_op jit(solution)/shard_map/ppermute | solution.py:150
  41.3 1.6 %shard_map.67 = (bf16[16,16,128]{2,1,0:T(8,128)(2,1)S(1)}, f32[16,16,128]{2,1,0:T(8,128)S(1)}) custom-call(bf16[2,16,2048]{2,1,0:T(8,128)(2,1)S(1)} %collective-permute-done.11.ins__held__.ins__held___0_, s32[8,128]{1,0:T(8,128)S(1)} %pad.4.ins__index___0_.ins__next_index___0_, s32[8,128]{1,0:T(8,128)S(1)} %collective-permute-done.6.ins__index___1_.ins__next_index___1_, ...), custom_call_target="tpu_custom_call" | custom-call | tf_op jit(solution)/shard_map/pallas_call | solution.py:112
  42.9 1.6 %collective-permute-start.12 = (bf16[16,16,128]{2,1,0:T(8,128)(2,1)S(1)}, bf16[16,16,128]{2,1,0:T(8,128)(2,1)S(1)}, u32[]{:S(2)}, u32[]{:S(2)}) collective-permute-start(bf16[16,16,128]{2,1,0:T(8,128)(2,1)S(1)} %get-tuple-element.22), channel_id=1, source_target_pairs={{0,2},{1,3},{2,0},{3,1},{4,6},{5,7},{6,4},{7,5},{8,10},{9,11},{10,... | collective-permute-start | bytes 196616 | tf_op jit(solution)/shard_map/ppermute | solution.py:144
  44.6 2.7 %collective-permute-done.12 = bf16[16,16,128]{2,1,0:T(8,128)(2,1)S(1)} collective-permute-done((bf16[16,16,128]{2,1,0:T(8,128)(2,1)S(1)}, bf16[16,16,128]{2,1,0:T(8,128)(2,1)S(1)}, u32[]{:S(2)}, u32[]{:S(2)}) %collective-permute-start.12) | collective-permute-done | bytes 65568 | tf_op jit(solution)/shard_map/ppermute | solution.py:144
  47.3 1.3 %collective-permute-start.13 = (bf16[16,16,128]{2,1,0:T(8,128)(2,1)S(1)}, bf16[16,16,128]{2,1,0:T(8,128)(2,1)S(1)}, u32[]{:S(2)}, u32[]{:S(2)}) collective-permute-start(bf16[16,16,128]{2,1,0:T(8,128)(2,1)S(1)} %fusion.1), channel_id=1, source_target_pairs={{0,4},{1,5},{2,6},{3,7},{4,0},{5,1},{6,2},{7,3},{8,12},{9,13},{10,... | collective-permute-start | bytes 196616 | tf_op jit(solution)/shard_map/ppermute | solution.py:144
  48.6 1.5 %collective-permute-start.15 = (bf16[2,16,2048]{2,1,0:T(8,128)(2,1)S(1)}, bf16[2,16,2048]{2,1,0:T(8,128)(2,1)S(1)}, u32[]{:S(2)}, u32[]{:S(2)}) collective-permute-start(bf16[2,16,2048]{2,1,0:T(8,128)(2,1)S(1)} %get-tuple-element.24), channel_id=1, source_target_pairs={{0,16},{16,0},{1,17},{17,1},{2,18},{18,2},{3,19},{19,3},{4,20},{20... | collective-permute-start | bytes 393224 | tf_op jit(solution)/shard_map/ppermute | solution.py:150
  50.1 1.5 %collective-permute-done.13 = bf16[16,16,128]{2,1,0:T(8,128)(2,1)S(1)} collective-permute-done((bf16[16,16,128]{2,1,0:T(8,128)(2,1)S(1)}, bf16[16,16,128]{2,1,0:T(8,128)(2,1)S(1)}, u32[]{:S(2)}, u32[]{:S(2)}) %collective-permute-start.13) | collective-permute-done | bytes 65568 | tf_op jit(solution)/shard_map/ppermute | solution.py:144
  51.7 2.8 %collective-permute-start.14 = (bf16[16,16,128]{2,1,0:T(8,128)(2,1)S(1)}, bf16[16,16,128]{2,1,0:T(8,128)(2,1)S(1)}, u32[]{:S(2)}, u32[]{:S(2)}) collective-permute-start(bf16[16,16,128]{2,1,0:T(8,128)(2,1)S(1)} %get-tuple-element.35), channel_id=1, source_target_pairs={{0,8},{1,9},{2,10},{3,11},{4,12},{5,13},{6,14},{7,15},{8,0},{9,1},... | collective-permute-start | bytes 196616 | tf_op jit(solution)/shard_map/ppermute | solution.py:144
  54.5 1.5 %collective-permute-start.16 = (s32[8,128]{1,0:T(8,128)S(1)}, s32[8,128]{1,0:T(8,128)S(1)}, u32[]{:S(2)}, u32[]{:S(2)}) collective-permute-start(s32[8,128]{1,0:T(8,128)S(1)} %pad.4.ins__index___0_.ins__next_index___0_), channel_id=1, source_target_pairs={{0,16},{16,0},{1,17},{17,1},{2,18},{18,2},{3,19},{19,3},{4,20},{20... | collective-permute-start | bytes 12296 | tf_op jit(solution)/shard_map/ppermute | solution.py:150
  55.9 2.1 %collective-permute-done.16.ins__next_index___0_.ins__index___0_ = s32[8,128]{1,0:T(8,128)S(1)} collective-permute-done((s32[8,128]{1,0:T(8,128)S(1)}, s32[8,128]{1,0:T(8,128)S(1)}, u32[]{:S(2)}, u32[]{:S(2)}) %collective-permute-start.16) | collective-permute-done | bytes 4128 | tf_op jit(solution)/shard_map/ppermute | solution.py:150
  58.1 1.2 %collective-permute-done.17.ins__next_index___1_.ins__index___1_ = s32[8,128]{1,0:T(8,128)S(1)} collective-permute-done((s32[8,128]{1,0:T(8,128)S(1)}, s32[8,128]{1,0:T(8,128)S(1)}, u32[]{:S(2)}, u32[]{:S(2)}) %collective-permute-start.17) | collective-permute-done | bytes 4128 | tf_op jit(solution)/shard_map/ppermute | solution.py:140
  59.2 2.4 %shard_map.68 = (f32[2,16,2048]{2,1,0:T(8,128)S(1)}, bf16[16,16,128]{2,1,0:T(8,128)(2,1)S(1)}, f32[16,16,128]{2,1,0:T(8,128)S(1)}) custom-call(bf16[16,16,128]{2,1,0:T(8,128)(2,1)S(1)} %get-tuple-element.43.ins__counts__, bf16[16,16,128]{2,1,0:T(8,128)(2,1)S(1)} %collective-permute-done.14.ins__got__, ...), custom_call_target="tpu_custom_call" | custom-call | tf_op jit(solution)/shard_map/pallas_call | solution.py:112
  61.7 1.6 %collective-permute-start.20 = (bf16[16,16,128]{2,1,0:T(8,128)(2,1)S(1)}, bf16[16,16,128]{2,1,0:T(8,128)(2,1)S(1)}, u32[]{:S(2)}, u32[]{:S(2)}) collective-permute-start(bf16[16,16,128]{2,1,0:T(8,128)(2,1)S(1)} %get-tuple-element.26), channel_id=1, source_target_pairs={{0,2},{1,3},{2,0},{3,1},{4,6},{5,7},{6,4},{7,5},{8,10},{9,11},{10,... | collective-permute-start | bytes 196616 | tf_op jit(solution)/shard_map/ppermute | solution.py:144
  63.3 2.7 %collective-permute-done.20 = bf16[16,16,128]{2,1,0:T(8,128)(2,1)S(1)} collective-permute-done((bf16[16,16,128]{2,1,0:T(8,128)(2,1)S(1)}, bf16[16,16,128]{2,1,0:T(8,128)(2,1)S(1)}, u32[]{:S(2)}, u32[]{:S(2)}) %collective-permute-start.20) | collective-permute-done | bytes 65568 | tf_op jit(solution)/shard_map/ppermute | solution.py:144
  66.0 1.9 %collective-permute-start.21 = (bf16[16,16,128]{2,1,0:T(8,128)(2,1)S(1)}, bf16[16,16,128]{2,1,0:T(8,128)(2,1)S(1)}, u32[]{:S(2)}, u32[]{:S(2)}) collective-permute-start(bf16[16,16,128]{2,1,0:T(8,128)(2,1)S(1)} %fusion.2), channel_id=1, source_target_pairs={{0,4},{1,5},{2,6},{3,7},{4,0},{5,1},{6,2},{7,3},{8,12},{9,13},{10,... | collective-permute-start | bytes 196616 | tf_op jit(solution)/shard_map/ppermute | solution.py:144
  68.0 1.5 %collective-permute-start.4 = (bf16[16,16,128]{2,1,0:T(8,128)(2,1)S(1)}, bf16[16,16,128]{2,1,0:T(8,128)(2,1)S(1)}, u32[]{:S(2)}, u32[]{:S(2)}) collective-permute-start(bf16[16,16,128]{2,1,0:T(8,128)(2,1)S(1)} %get-tuple-element.44.ins__counts__), channel_id=1, source_target_pairs={{0,16},{16,0},{1,17},{17,1},{2,18},{18,2},{3,19},{19,3},{4,20},{20... | collective-permute-start | bytes 196616 | tf_op jit(solution)/shard_map/ppermute | solution.py:150
  69.5 0.9 collective-permute-done.21
  70.4 0.6 collective-permute-start.22
  71.0 1.3 %shard_map.69.ins__inverse__ = f32[32,8,128]{2,1,0:T(8,128)S(1)} custom-call(s32[8,128]{1,0:T(8,128)S(1)} %collective-permute-done.16.ins__next_index___0_.ins__index___0_, s32[8,128]{1,0:T(8,128)S(1)} %collective-permute-done.17.ins__next_index___1_.ins__index___1_, bf16[32,128,128]{2,1,0:T(8,128)(2,1)S(1)} %collective-permute-done.18.ins__next_tiles___0_.ins__tiles___0_, ...), custom_call_target="tpu_custom_call" | custom-call | tf_op jit(solution)/shard_map/pallas_call | solution.py:112
  72.3 3.4 %collective-permute-done.22.ins__got__ = bf16[16,16,128]{2,1,0:T(8,128)(2,1)S(1)} collective-permute-done((bf16[16,16,128]{2,1,0:T(8,128)(2,1)S(1)}, bf16[16,16,128]{2,1,0:T(8,128)(2,1)S(1)}, u32[]{:S(2)}, u32[]{:S(2)}) %collective-permute-start.22) | collective-permute-done | bytes 65568 | tf_op jit(solution)/shard_map/ppermute | solution.py:144
  75.6 2.4 %shard_map.70 = (f32[2,16,2048]{2,1,0:T(8,128)S(1)}, bf16[16,16,128]{2,1,0:T(8,128)(2,1)S(1)}, f32[16,16,128]{2,1,0:T(8,128)S(1)}) custom-call(bf16[16,16,128]{2,1,0:T(8,128)(2,1)S(1)} %collective-permute-done.4.ins__counts__, bf16[16,16,128]{2,1,0:T(8,128)(2,1)S(1)} %collective-permute-done.22.ins__got__, ...), custom_call_target="tpu_custom_call" | custom-call | tf_op jit(solution)/shard_map/pallas_call | solution.py:112
  78.0 1.6 %collective-permute-start.23 = (bf16[16,16,128]{2,1,0:T(8,128)(2,1)S(1)}, bf16[16,16,128]{2,1,0:T(8,128)(2,1)S(1)}, u32[]{:S(2)}, u32[]{:S(2)}) collective-permute-start(bf16[16,16,128]{2,1,0:T(8,128)(2,1)S(1)} %get-tuple-element.29), channel_id=1, source_target_pairs={{0,2},{1,3},{2,0},{3,1},{4,6},{5,7},{6,4},{7,5},{8,10},{9,11},{10,... | collective-permute-start | bytes 196616 | tf_op jit(solution)/shard_map/ppermute | solution.py:144
  79.6 2.7 %collective-permute-done.23 = bf16[16,16,128]{2,1,0:T(8,128)(2,1)S(1)} collective-permute-done((bf16[16,16,128]{2,1,0:T(8,128)(2,1)S(1)}, bf16[16,16,128]{2,1,0:T(8,128)(2,1)S(1)}, u32[]{:S(2)}, u32[]{:S(2)}) %collective-permute-start.23) | collective-permute-done | bytes 65568 | tf_op jit(solution)/shard_map/ppermute | solution.py:144
  82.4 2.5 %collective-permute-start.24 = (bf16[16,16,128]{2,1,0:T(8,128)(2,1)S(1)}, bf16[16,16,128]{2,1,0:T(8,128)(2,1)S(1)}, u32[]{:S(2)}, u32[]{:S(2)}) collective-permute-start(bf16[16,16,128]{2,1,0:T(8,128)(2,1)S(1)} %fusion.3), channel_id=1, source_target_pairs={{0,4},{1,5},{2,6},{3,7},{4,0},{5,1},{6,2},{7,3},{8,12},{9,13},{10,... | collective-permute-start | bytes 196616 | tf_op jit(solution)/shard_map/ppermute | solution.py:144
  84.8 2.2 %collective-permute-done.24 = bf16[16,16,128]{2,1,0:T(8,128)(2,1)S(1)} collective-permute-done((bf16[16,16,128]{2,1,0:T(8,128)(2,1)S(1)}, bf16[16,16,128]{2,1,0:T(8,128)(2,1)S(1)}, u32[]{:S(2)}, u32[]{:S(2)}) %collective-permute-start.24) | collective-permute-done | bytes 65568 | tf_op jit(solution)/shard_map/ppermute | solution.py:144
  87.1 1.0 %collective-permute-start.25 = (bf16[16,16,128]{2,1,0:T(8,128)(2,1)S(1)}, bf16[16,16,128]{2,1,0:T(8,128)(2,1)S(1)}, u32[]{:S(2)}, u32[]{:S(2)}) collective-permute-start(bf16[16,16,128]{2,1,0:T(8,128)(2,1)S(1)} %get-tuple-element.31), channel_id=1, source_target_pairs={{0,8},{1,9},{2,10},{3,11},{4,12},{5,13},{6,14},{7,15},{8,0},{9,1},... | collective-permute-start | bytes 196616 | tf_op jit(solution)/shard_map/ppermute | solution.py:144
  88.1 4.2 %collective-permute-done.25.ins__got__ = bf16[16,16,128]{2,1,0:T(8,128)(2,1)S(1)} collective-permute-done((bf16[16,16,128]{2,1,0:T(8,128)(2,1)S(1)}, bf16[16,16,128]{2,1,0:T(8,128)(2,1)S(1)}, u32[]{:S(2)}, u32[]{:S(2)}) %collective-permute-start.25) | collective-permute-done | bytes 65568 | tf_op jit(solution)/shard_map/ppermute | solution.py:144
  92.3 1.3 %shard_map.71 = f32[2,16,2048]{2,1,0:T(8,128)S(1)} custom-call(bf16[16,16,128]{2,1,0:T(8,128)(2,1)S(1)} %get-tuple-element.45.ins__counts__, bf16[16,16,128]{2,1,0:T(8,128)(2,1)S(1)} %collective-permute-done.25.ins__got__, f32[2,16,2048]{2,1,0:T(8,128)S(1)} %get-tuple-element.30.ins__held___0_, s32[8,128]{1,0:T(8,128)S(1)} %pad.4.ins__index___0_.ins__next_index___0_, ...), custom_call_target="tpu_custom_call" | custom-call | tf_op jit(solution)/shard_map/pallas_call | solution.py:112
  93.8 1.3 %collective-permute-done.26 = f32[16,2048]{1,0:T(8,128)S(1)} collective-permute-done((f32[16,2048]{1,0:T(8,128)S(1)}, f32[16,2048]{1,0:T(8,128)S(1)}, u32[]{:S(2)}, u32[]{:S(2)}) %collective-permute-start.26) | collective-permute-done | bytes 131104 | tf_op jit(solution)/shard_map/ppermute | solution.py:140
  95.1 0.7 maximum_select_fusion
  (45 shorter events, 1.6 us)
Async XLA Ops:
  0.0 0.8 copy-start.2
  0.0 10.8 %collective-permute-start.7 = (bf16[32,128,128]{2,1,0:T(8,128)(2,1)}, bf16[32,128,128]{2,1,0:T(8,128)(2,1)S(1)}, u32[]{:S(2)}, u32[]{:S(2)}) collective-permute-start(bf16[32,128,128]{2,1,0:T(8,128)(2,1)} %bitcast.25), channel_id=1, source_target_pairs={{0,1},{1,0},{2,3},{3,2},{4,5},{5,4},{6,7},{7,6},{8,9},{9,8},{10,11... | collective-permute-start | bytes 3145736 | tf_op jit(solution)/shard_map/ppermute | solution.py:140
  0.8 3.1 %collective-permute-start = (bf16[1,2,16,128]{3,2,0,1:T(8,128)(2,1)S(1)}, bf16[1,2,16,128]{3,2,0,1:T(8,128)(2,1)S(1)}, u32[]{:S(2)}, u32[]{:S(2)}) collective-permute-start(bf16[1,2,16,128]{3,2,0,1:T(8,128)(2,1)S(1)} %get-tuple-element.47), channel_id=1, source_target_pairs={{0,1},{1,0},{2,3},{3,2},{4,5},{5,4},{6,7},{7,6},{8,9},{9,8},{10,11... | collective-permute-start | bytes 24584 | tf_op jit(solution)/shard_map/ppermute | solution.py:140
  1.3 26.5 %collective-permute-start.18 = (bf16[32,128,128]{2,1,0:T(8,128)(2,1)}, bf16[32,128,128]{2,1,0:T(8,128)(2,1)S(1)}, u32[]{:S(2)}, u32[]{:S(2)}) collective-permute-start(bf16[32,128,128]{2,1,0:T(8,128)(2,1)} %bitcast.26), channel_id=1, source_target_pairs={{0,16},{16,0},{1,17},{17,1},{2,18},{18,2},{3,19},{19,3},{4,20},{20... | collective-permute-start | bytes 3145736 | tf_op jit(solution)/shard_map/ppermute | solution.py:150
  3.9 3.8 %collective-permute-start.1 = (bf16[2,2,16,128]{3,2,0,1:T(8,128)(2,1)S(1)}, bf16[2,2,16,128]{3,2,0,1:T(8,128)(2,1)S(1)}, u32[]{:S(2)}, u32[]{:S(2)}) collective-permute-start(bf16[2,2,16,128]{3,2,0,1:T(8,128)(2,1)S(1)} %maximum_select_fusion.4), channel_id=1, source_target_pairs={{0,2},{1,3},{2,0},{3,1},{4,6},{5,7},{6,4},{7,5},{8,10},{9,11},{10,... | collective-permute-start | bytes 49160 | tf_op jit(solution)/shard_map/ppermute | solution.py:144
  6.6 4.1 %collective-permute-start.5 = (f32[16,2048]{1,0:T(8,128)S(1)}, f32[16,2048]{1,0:T(8,128)S(1)}, u32[]{:S(2)}, u32[]{:S(2)}) collective-permute-start(f32[16,2048]{1,0:T(8,128)S(1)} %get-tuple-element.41), channel_id=1, source_target_pairs={{0,1},{1,0},{2,3},{3,2},{4,5},{5,4},{6,7},{7,6},{8,9},{9,8},{10,11... | collective-permute-start | bytes 393224 | tf_op jit(solution)/shard_map/ppermute | solution.py:140
  7.5 2.0 %copy-start.3 = (s32[1,32]{1,0:T(1,128)S(1)}, s32[1,32]{1,0:T(1,128)}, u32[]{:S(2)}) copy-start(s32[1,32]{1,0:T(1,128)} %param.9) | copy-start | bytes 388
  7.5 2.0 %copy-start.4 = (s32[1,32]{1,0:T(1,128)S(1)}, s32[1,32]{1,0:T(1,128)}, u32[]{:S(2)}) copy-start(s32[1,32]{1,0:T(1,128)} %param.8) | copy-start | bytes 388
  7.7 7.6 %collective-permute-start.2 = (bf16[4,2,16,128]{3,2,0,1:T(8,128)(2,1)S(1)}, bf16[4,2,16,128]{3,2,0,1:T(8,128)(2,1)S(1)}, u32[]{:S(2)}, u32[]{:S(2)}) collective-permute-start(bf16[4,2,16,128]{3,2,0,1:T(8,128)(2,1)S(1)} %maximum_select_fusion.3), channel_id=1, source_target_pairs={{0,4},{1,5},{2,6},{3,7},{4,0},{5,1},{6,2},{7,3},{8,12},{9,13},{10,... | collective-permute-start | bytes 98312 | tf_op jit(solution)/shard_map/ppermute | solution.py:144
  9.6 1.2 %collective-permute-start.6 = (s32[8,128]{1,0:T(8,128)S(1)}, s32[8,128]{1,0:T(8,128)S(1)}, u32[]{:S(2)}, u32[]{:S(2)}) collective-permute-start(s32[8,128]{1,0:T(8,128)S(1)} %pad.4.ins__index___0_.ins__next_index___0_), channel_id=1, source_target_pairs={{0,1},{1,0},{2,3},{3,2},{4,5},{5,4},{6,7},{7,6},{8,9},{9,8},{10,11... | collective-permute-start | bytes 12296 | tf_op jit(solution)/shard_map/ppermute | solution.py:140
  10.8 1.2 %copy-start = (bf16[1,32,128,128]{3,2,1,0:T(8,128)(2,1)S(1)}, bf16[1,32,128,128]{3,2,1,0:T(8,128)(2,1)}, u32[]{:S(2)}) copy-start(bf16[1,32,128,128]{3,2,1,0:T(8,128)(2,1)} %param.7) | copy-start | bytes 3145732
  13.6 17.1 %copy-start.1 = (bf16[1,32,128,128]{3,2,1,0:T(8,128)(2,1)S(1)}, bf16[1,32,128,128]{3,2,1,0:T(8,128)(2,1)}, u32[]{:S(2)}) copy-start(bf16[1,32,128,128]{3,2,1,0:T(8,128)(2,1)} %param.7) | copy-start | bytes 3145732
  13.7 4.3 %collective-permute-start.8 = (bf16[16,16,128]{2,1,0:T(8,128)(2,1)S(1)}, bf16[16,16,128]{2,1,0:T(8,128)(2,1)S(1)}, u32[]{:S(2)}, u32[]{:S(2)}) collective-permute-start(bf16[16,16,128]{2,1,0:T(8,128)(2,1)S(1)} %get-tuple-element.19), channel_id=1, source_target_pairs={{0,2},{1,3},{2,0},{3,1},{4,6},{5,7},{6,4},{7,5},{8,10},{9,11},{10,... | collective-permute-start | bytes 196616 | tf_op jit(solution)/shard_map/ppermute | solution.py:144
  15.3 6.2 %collective-permute-start.3 = (bf16[8,2,16,128]{3,2,0,1:T(8,128)(2,1)S(1)}, bf16[8,2,16,128]{3,2,0,1:T(8,128)(2,1)S(1)}, u32[]{:S(2)}, u32[]{:S(2)}) collective-permute-start(bf16[8,2,16,128]{3,2,0,1:T(8,128)(2,1)S(1)} %maximum_select_fusion.2), channel_id=1, source_target_pairs={{0,8},{1,9},{2,10},{3,11},{4,12},{5,13},{6,14},{7,15},{8,0},{9,1},... | collective-permute-start | bytes 196616 | tf_op jit(solution)/shard_map/ppermute | solution.py:144
  18.0 9.8 %collective-permute-start.9 = (bf16[16,16,128]{2,1,0:T(8,128)(2,1)S(1)}, bf16[16,16,128]{2,1,0:T(8,128)(2,1)S(1)}, u32[]{:S(2)}, u32[]{:S(2)}) collective-permute-start(bf16[16,16,128]{2,1,0:T(8,128)(2,1)S(1)} %fusion), channel_id=1, source_target_pairs={{0,4},{1,5},{2,6},{3,7},{4,0},{5,1},{6,2},{7,3},{8,12},{9,13},{10,... | collective-permute-start | bytes 196616 | tf_op jit(solution)/shard_map/ppermute | solution.py:144
  27.8 31.4 %collective-permute-start.19 = (bf16[32,128,128]{2,1,0:T(8,128)(2,1)S(1)}, bf16[32,128,128]{2,1,0:T(8,128)(2,1)S(1)}, u32[]{:S(2)}, u32[]{:S(2)}) collective-permute-start(bf16[32,128,128]{2,1,0:T(8,128)(2,1)S(1)} %collective-permute-done.18.ins__next_tiles___0_.ins__tiles___0_), channel_id=1, source_target_pairs={{0,1},{1,0},{2,3},{3,2},{4,5},{5,4},{6,7},{7,6},{8,9},{9,8},{10,11... | collective-permute-start | bytes 3145736 | tf_op jit(solution)/shard_map/ppermute | solution.py:140
  27.8 7.1 %collective-permute-start.10 = (bf16[16,16,128]{2,1,0:T(8,128)(2,1)S(1)}, bf16[16,16,128]{2,1,0:T(8,128)(2,1)S(1)}, u32[]{:S(2)}, u32[]{:S(2)}) collective-permute-start(bf16[16,16,128]{2,1,0:T(8,128)(2,1)S(1)} %get-tuple-element.37), channel_id=1, source_target_pairs={{0,8},{1,9},{2,10},{3,11},{4,12},{5,13},{6,14},{7,15},{8,0},{9,1},... | collective-permute-start | bytes 196616 | tf_op jit(solution)/shard_map/ppermute | solution.py:144
  36.3 5.0 %collective-permute-start.11 = (bf16[2,16,2048]{2,1,0:T(8,128)(2,1)S(1)}, bf16[2,16,2048]{2,1,0:T(8,128)(2,1)S(1)}, u32[]{:S(2)}, u32[]{:S(2)}) collective-permute-start(bf16[2,16,2048]{2,1,0:T(8,128)(2,1)S(1)} %get-tuple-element.20), channel_id=1, source_target_pairs={{0,16},{16,0},{1,17},{17,1},{2,18},{18,2},{3,19},{19,3},{4,20},{20... | collective-permute-start | bytes 393224 | tf_op jit(solution)/shard_map/ppermute | solution.py:150
  42.9 4.3 %collective-permute-start.12 = (bf16[16,16,128]{2,1,0:T(8,128)(2,1)S(1)}, bf16[16,16,128]{2,1,0:T(8,128)(2,1)S(1)}, u32[]{:S(2)}, u32[]{:S(2)}) collective-permute-start(bf16[16,16,128]{2,1,0:T(8,128)(2,1)S(1)} %get-tuple-element.22), channel_id=1, source_target_pairs={{0,2},{1,3},{2,0},{3,1},{4,6},{5,7},{6,4},{7,5},{8,10},{9,11},{10,... | collective-permute-start | bytes 196616 | tf_op jit(solution)/shard_map/ppermute | solution.py:144
  47.3 4.3 %collective-permute-start.13 = (bf16[16,16,128]{2,1,0:T(8,128)(2,1)S(1)}, bf16[16,16,128]{2,1,0:T(8,128)(2,1)S(1)}, u32[]{:S(2)}, u32[]{:S(2)}) collective-permute-start(bf16[16,16,128]{2,1,0:T(8,128)(2,1)S(1)} %fusion.1), channel_id=1, source_target_pairs={{0,4},{1,5},{2,6},{3,7},{4,0},{5,1},{6,2},{7,3},{8,12},{9,13},{10,... | collective-permute-start | bytes 196616 | tf_op jit(solution)/shard_map/ppermute | solution.py:144
  48.6 10.6 %collective-permute-start.15 = (bf16[2,16,2048]{2,1,0:T(8,128)(2,1)S(1)}, bf16[2,16,2048]{2,1,0:T(8,128)(2,1)S(1)}, u32[]{:S(2)}, u32[]{:S(2)}) collective-permute-start(bf16[2,16,2048]{2,1,0:T(8,128)(2,1)S(1)} %get-tuple-element.24), channel_id=1, source_target_pairs={{0,16},{16,0},{1,17},{17,1},{2,18},{18,2},{3,19},{19,3},{4,20},{20... | collective-permute-start | bytes 393224 | tf_op jit(solution)/shard_map/ppermute | solution.py:150
  51.7 7.6 %collective-permute-start.14 = (bf16[16,16,128]{2,1,0:T(8,128)(2,1)S(1)}, bf16[16,16,128]{2,1,0:T(8,128)(2,1)S(1)}, u32[]{:S(2)}, u32[]{:S(2)}) collective-permute-start(bf16[16,16,128]{2,1,0:T(8,128)(2,1)S(1)} %get-tuple-element.35), channel_id=1, source_target_pairs={{0,8},{1,9},{2,10},{3,11},{4,12},{5,13},{6,14},{7,15},{8,0},{9,1},... | collective-permute-start | bytes 196616 | tf_op jit(solution)/shard_map/ppermute | solution.py:144
  54.5 3.6 %collective-permute-start.16 = (s32[8,128]{1,0:T(8,128)S(1)}, s32[8,128]{1,0:T(8,128)S(1)}, u32[]{:S(2)}, u32[]{:S(2)}) collective-permute-start(s32[8,128]{1,0:T(8,128)S(1)} %pad.4.ins__index___0_.ins__next_index___0_), channel_id=1, source_target_pairs={{0,16},{16,0},{1,17},{17,1},{2,18},{18,2},{3,19},{19,3},{4,20},{20... | collective-permute-start | bytes 12296 | tf_op jit(solution)/shard_map/ppermute | solution.py:150
  58.1 1.2 %collective-permute-start.17 = (s32[8,128]{1,0:T(8,128)S(1)}, s32[8,128]{1,0:T(8,128)S(1)}, u32[]{:S(2)}, u32[]{:S(2)}) collective-permute-start(s32[8,128]{1,0:T(8,128)S(1)} %collective-permute-done.16.ins__next_index___0_.ins__index___0_), channel_id=1, source_target_pairs={{0,1},{1,0},{2,3},{3,2},{4,5},{5,4},{6,7},{7,6},{8,9},{9,8},{10,11... | collective-permute-start | bytes 12296 | tf_op jit(solution)/shard_map/ppermute | solution.py:140
  61.7 4.3 %collective-permute-start.20 = (bf16[16,16,128]{2,1,0:T(8,128)(2,1)S(1)}, bf16[16,16,128]{2,1,0:T(8,128)(2,1)S(1)}, u32[]{:S(2)}, u32[]{:S(2)}) collective-permute-start(bf16[16,16,128]{2,1,0:T(8,128)(2,1)S(1)} %get-tuple-element.26), channel_id=1, source_target_pairs={{0,2},{1,3},{2,0},{3,1},{4,6},{5,7},{6,4},{7,5},{8,10},{9,11},{10,... | collective-permute-start | bytes 196616 | tf_op jit(solution)/shard_map/ppermute | solution.py:144
  66.0 4.3 %collective-permute-start.21 = (bf16[16,16,128]{2,1,0:T(8,128)(2,1)S(1)}, bf16[16,16,128]{2,1,0:T(8,128)(2,1)S(1)}, u32[]{:S(2)}, u32[]{:S(2)}) collective-permute-start(bf16[16,16,128]{2,1,0:T(8,128)(2,1)S(1)} %fusion.2), channel_id=1, source_target_pairs={{0,4},{1,5},{2,6},{3,7},{4,0},{5,1},{6,2},{7,3},{8,12},{9,13},{10,... | collective-permute-start | bytes 196616 | tf_op jit(solution)/shard_map/ppermute | solution.py:144
  68.0 4.3 %collective-permute-start.4 = (bf16[16,16,128]{2,1,0:T(8,128)(2,1)S(1)}, bf16[16,16,128]{2,1,0:T(8,128)(2,1)S(1)}, u32[]{:S(2)}, u32[]{:S(2)}) collective-permute-start(bf16[16,16,128]{2,1,0:T(8,128)(2,1)S(1)} %get-tuple-element.44.ins__counts__), channel_id=1, source_target_pairs={{0,16},{16,0},{1,17},{17,1},{2,18},{18,2},{3,19},{19,3},{4,20},{20... | collective-permute-start | bytes 196616 | tf_op jit(solution)/shard_map/ppermute | solution.py:150
  70.4 5.2 %collective-permute-start.22 = (bf16[16,16,128]{2,1,0:T(8,128)(2,1)S(1)}, bf16[16,16,128]{2,1,0:T(8,128)(2,1)S(1)}, u32[]{:S(2)}, u32[]{:S(2)}) collective-permute-start(bf16[16,16,128]{2,1,0:T(8,128)(2,1)S(1)} %get-tuple-element.33), channel_id=1, source_target_pairs={{0,8},{1,9},{2,10},{3,11},{4,12},{5,13},{6,14},{7,15},{8,0},{9,1},... | collective-permute-start | bytes 196616 | tf_op jit(solution)/shard_map/ppermute | solution.py:144
  78.0 4.3 %collective-permute-start.23 = (bf16[16,16,128]{2,1,0:T(8,128)(2,1)S(1)}, bf16[16,16,128]{2,1,0:T(8,128)(2,1)S(1)}, u32[]{:S(2)}, u32[]{:S(2)}) collective-permute-start(bf16[16,16,128]{2,1,0:T(8,128)(2,1)S(1)} %get-tuple-element.29), channel_id=1, source_target_pairs={{0,2},{1,3},{2,0},{3,1},{4,6},{5,7},{6,4},{7,5},{8,10},{9,11},{10,... | collective-permute-start | bytes 196616 | tf_op jit(solution)/shard_map/ppermute | solution.py:144
  82.4 4.7 %collective-permute-start.24 = (bf16[16,16,128]{2,1,0:T(8,128)(2,1)S(1)}, bf16[16,16,128]{2,1,0:T(8,128)(2,1)S(1)}, u32[]{:S(2)}, u32[]{:S(2)}) collective-permute-start(bf16[16,16,128]{2,1,0:T(8,128)(2,1)S(1)} %fusion.3), channel_id=1, source_target_pairs={{0,4},{1,5},{2,6},{3,7},{4,0},{5,1},{6,2},{7,3},{8,12},{9,13},{10,... | collective-permute-start | bytes 196616 | tf_op jit(solution)/shard_map/ppermute | solution.py:144
  87.1 5.2 %collective-permute-start.25 = (bf16[16,16,128]{2,1,0:T(8,128)(2,1)S(1)}, bf16[16,16,128]{2,1,0:T(8,128)(2,1)S(1)}, u32[]{:S(2)}, u32[]{:S(2)}) collective-permute-start(bf16[16,16,128]{2,1,0:T(8,128)(2,1)S(1)} %get-tuple-element.31), channel_id=1, source_target_pairs={{0,8},{1,9},{2,10},{3,11},{4,12},{5,13},{6,14},{7,15},{8,0},{9,1},... | collective-permute-start | bytes 196616 | tf_op jit(solution)/shard_map/ppermute | solution.py:144
  93.7 1.4 %collective-permute-start.26 = (f32[16,2048]{1,0:T(8,128)S(1)}, f32[16,2048]{1,0:T(8,128)S(1)}, u32[]{:S(2)}, u32[]{:S(2)}) collective-permute-start(f32[16,2048]{1,0:T(8,128)S(1)} %get-tuple-element.40), channel_id=1, source_target_pairs={{0,1},{1,0},{2,3},{3,2},{4,5},{5,4},{6,7},{7,6},{8,9},{9,8},{10,11... | collective-permute-start | bytes 393224 | tf_op jit(solution)/shard_map/ppermute | solution.py:140

commit v4 on v3

v4 whole, which is shorter than its diff:
```python
import functools

import jax
import jax.numpy as jnp
from jax import lax
from jax.experimental import pallas as pl
from jax.experimental.pallas import tpu as pltpu
from jax.sharding import PartitionSpec as P

TILE_GROUP = 32
ROUNDS = 4
CORES = 2
LANES = 128
VMEM_LIMIT = 40 * 1024 * 1024


def each_live(index_ref, slots, body):
    live = index_ref[2, 0]
    for group in range(-(-slots // TILE_GROUP)):
        first, last = group * TILE_GROUP, min(slots, (group + 1) * TILE_GROUP)

        @pl.when(group < live)
        def _():
            for t in range(first, last, 2):
                body(tuple(range(t, min(t + 2, last))))


def add_products(acc, left_of, targets, wide, transposed):
    left = jnp.concatenate(left_of, axis=0)
    dims = (((1,), (1,)), ((), ())) if transposed else (((1,), (0,)), ((), ()))
    part = lax.dot_general(left, wide, dims, preferred_element_type=jnp.float32)
    rows, size = acc.shape[1:]
    for i, at in enumerate(targets):
        used = part[i * left_of[i].shape[0]:, i * size:(i + 1) * size][:rows]
        acc[at] = acc[at] + used


def tile_at(tile_refs, t):
    for ref in tile_refs:
        if t < ref.shape[0]:
            return ref[t]
        t -= ref.shape[0]


def slots_of(tile_refs):
    return sum(ref.shape[0] for ref in tile_refs)


def project_into(acc, low, index_refs, sets):
    blocks = low.shape[0] // CORES
    for k in range(CORES):
        if sets[k] is None:
            continue
        index_ref, tile_refs = index_refs[k], sets[k]

        def body(ts):
            wide = jnp.concatenate([tile_at(tile_refs, t) for t in ts], axis=0)
            add_products(acc, [low[k * blocks + index_ref[0, t]] for t in ts],
                         [index_ref[1, t] for t in ts], wide, True)

        each_live(index_ref, slots_of(tile_refs), body)


def back_into(acc, ratios, index_refs, sets):
    blocks = acc.shape[0] // CORES
    acc[...] = jnp.zeros_like(acc)
    for k in range(CORES):
        index_ref, tile_refs = index_refs[k], sets[k]

        def body(ts):
            wide = jnp.concatenate([tile_at(tile_refs, t) for t in ts], axis=1)
            add_products(acc, [ratios(index_ref[1, t]) for t in ts],
                         [k * blocks + index_ref[0, t] for t in ts], wide, False)

        each_live(index_ref, slots_of(tile_refs), body)


def columns(blocks, size):
    for k in range(CORES):
        for b in range(blocks):
            yield k, slice(b * size, (b + 1) * size), k * blocks + b


def piece_of(held, k, cols):
    return held[k][:, cols] if isinstance(held, tuple) else held[k, :, cols]


def write_sums(ins, outs, acc):
    blocks = acc.shape[0]
    outs["wide"][...] = acc[...]
    outs["sent"][:blocks] = acc[...].astype(jnp.bfloat16)
    if "dealt" in ins:
        outs["sent"][blocks:] = ins["dealt"][...]


def first_kernel(ins, outs, low, acc, own, arrived):
    copy = pltpu.make_async_copy(ins["own_hbm"], own, arrived)
    copy.start()
    blocks, size = low.shape[0] // CORES, low.shape[-1]
    for k, cols, at in columns(blocks, size):
        low[at] = piece_of(ins["held"], k, cols).astype(jnp.bfloat16)
    acc[...] = jnp.zeros_like(acc)
    project_into(acc, low, ins["index"], (None, ins["tiles"]))
    copy.wait()
    project_into(acc, low, ins["index"], ((own,), None))
    write_sums(ins, outs, acc)


def project_kernel(ins, outs, low, acc):
    blocks, size = low.shape[0] // CORES, low.shape[-1]
    acc[...] = jnp.zeros_like(acc)
    for k, cols, at in columns(blocks, size):
        low[at] = piece_of(ins["held"], k, cols).astype(jnp.bfloat16)
    project_into(acc, low, ins["index"], ins["tiles"])
    write_sums(ins, outs, acc)


def sensitivity_kernel(ins, outs, acc):
    ones = jnp.ones((16, ins["tiles"][0][0].shape[1]), jnp.bfloat16)
    back_into(acc, lambda ray: ones, ins["index"], ins["tiles"])
    outs["inverse"][...] = 1.0 / acc[...]


def update_kernel(masks, ins, outs, counts, ratios, back, *scratch):
    blocks, size = back.shape[0] // CORES, back.shape[-1]
    rays = ratios.shape[0]
    total = ins["wide"][...]
    for got in ins["got"]:
        total = total + got[:rays].astype(jnp.float32)
    if "counts" in ins:
        counts[...] = ins["counts"][...]
    else:
        place = ins["index"][0][3, 0]
        share = ins["sent"].shape[0] - rays
        for mask, part in zip((0,) + masks, (ins["sent"],) + tuple(ins["got"])):
            counts[pl.ds((place ^ mask) * share, share)] = part[rays:]
    if "counts" in outs:
        outs["counts"][...] = counts[...]
    ratios[...] = (counts[...].astype(jnp.float32) / total).astype(jnp.bfloat16)
    back_into(back, lambda ray: ratios[ray], ins["index"], ins["tiles"])
    for k, cols, at in columns(blocks, size):
        value = piece_of(ins["held"], k, cols) * back[at] * ins["inverse"][at, :1]
        outs["held"][k, :, cols] = value
        if "sent" in outs:
            scratch[0][at] = value.astype(jnp.bfloat16)
    if "sent" in outs:
        scratch[1][...] = jnp.zeros_like(scratch[1])
        project_into(scratch[1], scratch[0], ins["next_index"], ins["next_tiles"])
        write_sums(ins, outs, scratch[1])


def call(kernel, ins, outs, scratch):
    def spec(path, _):
        name = path[0].key
        space = pltpu.SMEM if name.endswith("index") else pltpu.HBM if name.endswith("hbm") else pltpu.VMEM
        return pl.BlockSpec(memory_space=space)

    return pl.pallas_call(
        kernel,
        out_shape=outs,
        in_specs=[jax.tree_util.tree_map_with_path(spec, ins)],
        out_specs=jax.tree_util.tree_map_with_path(spec, outs),
        scratch_shapes=scratch,
        compiler_params=pltpu.CompilerParams(vmem_limit_bytes=VMEM_LIMIT))(ins)


def shards(images, system_tiles, tile_vox, tile_ray, live_blocks, counts):
    frames, voxels = images.shape
    half = frames // CORES
    size = system_tiles.shape[-1]
    vox_blocks = voxels // size
    own_tiles = system_tiles[0]
    slots = own_tiles.shape[0]
    tile_devs = lax.axis_size("tile")
    chips = tile_devs // CORES
    rb_dev = counts.shape[2] // size
    ray_blocks = rb_dev * tile_devs
    subset_count = lax.axis_size("subset")
    position = lax.axis_index("subset")
    core = lax.axis_index("tile") % CORES
    chip = lax.axis_index("tile") // CORES
    both = CORES * vox_blocks
    f32, bf16 = jnp.float32, jnp.bfloat16
    shaped = jax.ShapeDtypeStruct

    steps, bit = [(1,)], 2
    while bit < chips:
        wide_step = bit * 4 <= chips
        steps.append((bit, 3 * bit, 2 * bit) if wide_step else (bit,))
        bit *= 4 if wide_step else 2

    def place(masks):
        return chip // min(masks) % (len(masks) + 1)

    def swap_cores(array):
        return lax.ppermute(array, "tile", [(i, i ^ 1) for i in range(tile_devs)])

    def swap_chips(array, mask):
        pairs = [(CORES * j + c, CORES * (j ^ mask) + c) for j in range(chips) for c in range(CORES)]
        return lax.ppermute(array, "tile", pairs)

    def joined(side, own, other):
        return jnp.where(side == 0, jnp.concatenate([own, other]), jnp.concatenate([other, own]))

    def shift(array):
        return lax.ppermute(array, "subset", [(i, (i + 1) % subset_count) for i in range(subset_count)])

    def after(array, value):
        return lax.optimization_barrier((array, value))[0]

    halves = images.reshape(CORES, half, voxels)
    mine = lax.dynamic_index_in_dim(halves, core, 0, keepdims=False)
    theirs = lax.dynamic_index_in_dim(halves, 1 - core, 0, keepdims=False)
    rows = jnp.concatenate([tile_vox, tile_ray, jnp.broadcast_to(live_blocks, tile_vox.shape),
                            jnp.broadcast_to(place(steps[-1]), tile_vox.shape)], axis=0)
    own_index = jnp.pad(rows, ((0, 4), (0, -slots % LANES)))
    tiles = ((own_tiles,), (swap_cores(own_tiles),))
    held = (mine, swap_cores(theirs))
    index = (own_index, swap_cores(own_index))

    dealt = counts[0].astype(bf16).reshape(subset_count, CORES, half, rb_dev, size).transpose(1, 3, 0, 2, 4)
    kept = lax.dynamic_index_in_dim(dealt, core, 0, keepdims=False)
    got = swap_cores(lax.dynamic_index_in_dim(dealt, 1 - core, 0, keepdims=False))
    dealt = joined(core, kept, got)

    def dealt_of(panel):
        return lax.dynamic_index_in_dim(dealt, panel % subset_count, 1, keepdims=False)

    def sensitivity(index, tiles):
        return call(sensitivity_kernel, {"index": index, "tiles": tiles},
                    {"inverse": shaped((both, 8, size), f32)},
                    [pltpu.VMEM((both, 8, size), f32)])["inverse"]

    sets = [(index, tiles, sensitivity(index, tiles))] * ROUNDS
    moves = [True] * (ROUNDS - 1)
    known = [None] * ROUNDS
    two = subset_count == 2
    if two:
        moves = [r == 0 for r in range(ROUNDS - 1)]

    scratch_sum = [pltpu.VMEM((both, half, size), bf16), pltpu.VMEM((ray_blocks, half, size), f32)]
    scratch = [pltpu.VMEM((ray_blocks, half, size), bf16)] * 2 + [pltpu.VMEM((both, half, size), f32)]

    def sums(r):
        fresh = known[r] is None
        sent = ray_blocks + fresh * rb_dev * CORES
        return ({"dealt": dealt_of(position - r)} if fresh else {},
                {"wide": shaped((ray_blocks, half, size), f32), "sent": shaped((sent, half, size), bf16)})

    def project(held, r):
        extra, outs = sums(r)
        return call(project_kernel, {"held": held, "index": sets[r][0], "tiles": sets[r][1], **extra},
                    outs, scratch_sum)

    extra, outs = sums(0)
    out = call(first_kernel, {"held": held, "index": index, "own_hbm": own_tiles, "tiles": tiles[1], **extra},
               outs, scratch_sum + [pltpu.VMEM(own_tiles.shape, bf16), pltpu.SemaphoreType.DMA])
    for r in range(ROUNDS):
        wide, sent = out["wide"], out["sent"]
        if two and r == 0:
            far_index = shift(after(own_index, sent))
            far_tiles = [shift(after(own_tiles[:slots * 5 // 8], sent))]
        if two and r == 1:
            far_index = (far_index, swap_cores(after(far_index, sent)))
            far_swapped = [swap_cores(after(far_tiles[0], sent))]
            far_tiles.append(shift(after(own_tiles[slots * 5 // 8:], sent)))
        for masks in steps:
            got = [swap_chips(sent, mask) for mask in masks]
            if masks is not steps[-1]:
                wide = wide + sum(part[:ray_blocks].astype(f32) for part in got)
                own, counted = place(masks), wide.astype(bf16)
                if sent.shape[0] > ray_blocks:
                    parts = dict(zip((0,) + masks, [sent] + got))
                    ordered = [parts[m * min(masks)][ray_blocks:] for m in range(len(parts))]
                    if len(ordered) == 2:
                        passed = joined(own, *ordered)
                    else:
                        passed = jnp.concatenate([lax.dynamic_index_in_dim(
                            jnp.stack(ordered), own ^ v, 0, keepdims=False) for v in range(len(ordered))])
                    counted = jnp.concatenate([counted, passed])
                sent = counted
        if two and r == 1:
            far_swapped.append(swap_cores(after(far_tiles[1], tuple(got))))
            far_tiles = (tuple(far_tiles), tuple(far_swapped))
            far = (far_index, far_tiles, sensitivity(far_index, far_tiles))
            sets = [far if later >= 2 and later % 2 == 0 else sets[later] for later in range(ROUNDS)]
        ins = {"wide": wide, "got": got, "held": held,
               "index": sets[r][0], "tiles": sets[r][1], "inverse": sets[r][2]}
        outs = {"held": shaped((CORES, half, voxels), f32)}
        if known[r] is None:
            ins["sent"] = sent
            if two:
                outs["counts"] = shaped((ray_blocks, half, size), bf16)
        else:
            ins["counts"] = known[r]
        kernel = functools.partial(update_kernel, tuple(m // min(masks) for m in masks))
        if r + 1 < ROUNDS and not moves[r] and not (two and r == 1):
            extra, more = sums(r + 1)
            ins.update(next_index=sets[r + 1][0], next_tiles=sets[r + 1][1], **extra)
            outs.update(more)
        out = call(kernel, ins, outs, scratch + (scratch_sum if "sent" in outs else []))
        held = out["held"]
        if two and r < 2:
            for later in range(r + 2, ROUNDS, 2):
                known[later] = out["counts"] if r == 1 else shift(out["counts"])
        if r + 1 < ROUNDS and "sent" not in out:
            if moves[r]:
                held = shift(held)
                if two:
                    held, far_index, far_tiles[0] = lax.optimization_barrier((held, far_index, far_tiles[0]))
            out = project(held, r + 1)
    return joined(core, held[0], swap_cores(held[1]))


def solution(mesh):
    in_specs = (
        P("subset", "tile"),
        P("subset", "tile", None, None),
        P("subset", "tile"),
        P("subset", "tile"),
        P("subset", "tile"),
        P("subset", None, "tile"),
    )
    return jax.shard_map(shards, mesh=mesh, in_specs=in_specs, out_specs=P("subset", "tile"),
                         check_vma=False)
```

time: 96.1 us -> 83.7 us (0.87)
  waiting for transfers between devices: 42 us -> 34.6 us
  starting transfers between devices: 35.9 us -> 29.9 us
    ppermute x5, waiting for transfers between devices: 11.8 us -> 6.51 us  [shift(): lax.ppermute(array, 'subset', [(i, (i + 1) % subset_count) for i in range...]
    ppermute x15 -> x16, starting transfers between devices: 26.2 us -> 21.4 us  [swap_chips(): return lax.ppermute(array, 'tile', pairs)]
    ppermute x5, starting transfers between devices: 8.63 us -> 6.81 us  [shift(): lax.ppermute(array, 'subset', [(i, (i + 1) % subset_count) for i in range...]
    ppermute x15 -> x16, waiting for transfers between devices: 26.6 us -> 25.5 us  [swap_chips(): return lax.ppermute(array, 'tile', pairs)]
    ppermute x7 -> x8, waiting for transfers between devices: 3.54 us -> 2.59 us  [swap_cores(): return lax.ppermute(array, 'tile', [(i, i ^ 1) for i in range(tile_devs)])]
    pallas_call x8 -> x9, Pallas kernels: 13.2 us -> 14 us  [call(): pl.pallas_call(kernel, out_shape=outs, in_specs=[jax.tree_util.tree_map_w...]
  transfers between devices with their start and end apart: 27 -> 29, of which waited for: 18 -> 19; matrix products, arithmetic and copies ran while one was open for 1% -> 2% of each run, Pallas kernels for 7% -> 6%
where the time goes in v4:
time: 83.7 us; the launch traced here: 83.4 us
  waiting for transfers between devices  34.6 us (41%)
  starting transfers between devices  29.9 us (36%)
  Pallas kernels  14 us (17%)
  local copies, waits for them, and re-layouts  3.09 us (4%)
  between operations  0.94 us (1%)
  other arithmetic  0.93 us (1%)
    ppermute x16, waiting for transfers between devices, swap_chips(): return lax.ppermute(array, 'tile', pairs)  25.5 us
    ppermute x16, starting transfers between devices, swap_chips(): return lax.ppermute(array, 'tile', pairs)  21.4 us
    pallas_call x9, Pallas kernels, call(): pl.pallas_call(kernel, out_shape=outs, in_specs=[jax.tree_util.tree_map_w...  14 us
    ppermute x5, starting transfers between devices, shift(): lax.ppermute(array, 'subset', [(i, (i + 1) % subset_count) for i in range...  6.81 us
    ppermute x5, waiting for transfers between devices, shift(): lax.ppermute(array, 'subset', [(i, (i + 1) % subset_count) for i in range...  6.51 us
    ppermute x8, waiting for transfers between devices, swap_cores(): return lax.ppermute(array, 'tile', [(i, i ^ 1) for i in range(tile_devs)])  2.59 us
    unnamed x10, local copies, waits for them, and re-layouts  1.83 us
    ppermute x8, starting transfers between devices, swap_cores(): return lax.ppermute(array, 'tile', [(i, i ^ 1) for i in range(tile_devs)])  1.74 us
  transfers between devices with their start and end apart: 29, of which 19 were waited for; matrix products, arithmetic and copies ran while one was open for 2% of the time, Pallas kernels for 6%

profile of v4, /device:TPU:0, one launch (start us, length us, event | category | flops | bytes accessed | tf_op | source)
XLA Modules:
  0.0 83.4 jit_solution(14073997675468996796)
XLA Ops:
  0.0 0.5 collective-permute-start.3
  1.3 0.6 copy-done.3
  2.0 0.5 collective-permute-start
  2.5 1.0 %dynamic-slice_bitcast_fusion = (f32[16,2048]{1,0:T(8,128)S(1)}, f32[16,2048]{1,0:T(8,128)S(1)}) fusion(f32[2,16,2048]{2,1,0:T(8,128)} %bitcast.36, s32[]{:T(128)S(6)} %select_n.83, s32[]{:T(128)S(6)} %select_n.82), kind=kLoop, calls=%fused_computation.9 | loop fusion | bytes 524296 | tf_op jit(solution)/shard_map/jit(dynamic_index_in_dim)/squeeze | solution.py:213
  3.7 1.2 %collective-permute-done.1.ins__held___1_ = f32[16,2048]{1,0:T(8,128)S(1)} collective-permute-done((f32[16,2048]{1,0:T(8,128)S(1)}, f32[16,2048]{1,0:T(8,128)S(1)}, u32[]{:S(2)}, u32[]{:S(2)}) %collective-permute-start.1) | collective-permute-done | bytes 131104 | tf_op jit(solution)/shard_map/ppermute | solution.py:196
  5.0 1.2 %copy-done = bf16[1,32,128,128]{3,2,1,0:T(8,128)(2,1)S(1)} copy-done((bf16[1,32,128,128]{3,2,1,0:T(8,128)(2,1)S(1)}, bf16[1,32,128,128]{3,2,1,0:T(8,128)(2,1)}, u32[]{:S(2)}) %copy-start) | copy-done | bytes 1048600
  6.2 1.7 %shard_map.64 = (bf16[18,16,128]{2,1,0:T(8,128)(2,1)S(1)}, f32[16,16,128]{2,1,0:T(8,128)S(1)}) custom-call(bf16[2,16,128]{2,1,0:T(8,128)(2,1)S(1)} %get-tuple-element.61.ins__dealt__, f32[16,2048]{1,0:T(8,128)S(1)} %get-tuple-element.60.ins__held___0_, f32[16,2048]{1,0:T(8,128)S(1)} %collective-permute-done.1.ins__held___1_, ...), custom_call_target="tpu_custom_call" | custom-call | tf_op jit(solution)/shard_map/pallas_call | solution.py:158
  7.9 2.7 %collective-permute-start.4 = (bf16[18,16,128]{2,1,0:T(8,128)(2,1)S(1)}, bf16[18,16,128]{2,1,0:T(8,128)(2,1)S(1)}, u32[]{:S(2)}, u32[]{:S(2)}) collective-permute-start(bf16[18,16,128]{2,1,0:T(8,128)(2,1)S(1)} %get-tuple-element.28), channel_id=1, source_target_pairs={{0,2},{1,3},{2,0},{3,1},{4,6},{5,7},{6,4},{7,5},{8,10},{9,11},{10,... | collective-permute-start | bytes 221192 | tf_op jit(solution)/shard_map/ppermute | solution.py:200
  10.7 1.5 %collective-permute-start.10 = (bf16[20,128,128]{2,1,0:T(8,128)(2,1)S(1)}, bf16[20,128,128]{2,1,0:T(8,128)(2,1)S(1)}, u32[]{:S(2)}, u32[]{:S(2)}) collective-permute-start(bf16[20,128,128]{2,1,0:T(8,128)(2,1)S(1)} %slice_bitcast_fusion), channel_id=1, source_target_pairs={{0,16},{16,0},{1,17},{17,1},{2,18},{18,2},{3,19},{19,3},{4,20},{20... | collective-permute-start | bytes 1966088 | tf_op jit(solution)/shard_map/ppermute | solution.py:206
  12.3 1.2 %collective-permute-done.4 = bf16[18,16,128]{2,1,0:T(8,128)(2,1)S(1)} collective-permute-done((bf16[18,16,128]{2,1,0:T(8,128)(2,1)S(1)}, bf16[18,16,128]{2,1,0:T(8,128)(2,1)S(1)}, u32[]{:S(2)}, u32[]{:S(2)}) %collective-permute-start.4) | collective-permute-done | bytes 73760 | tf_op jit(solution)/shard_map/ppermute | solution.py:200
  13.5 2.9 %collective-permute-start.7 = (bf16[20,16,128]{2,1,0:T(8,128)(2,1)S(1)}, bf16[20,16,128]{2,1,0:T(8,128)(2,1)S(1)}, u32[]{:S(2)}, u32[]{:S(2)}) collective-permute-start(bf16[20,16,128]{2,1,0:T(8,128)(2,1)S(1)} %pad_maximum_fusion.ins__sent__), channel_id=1, source_target_pairs={{0,8},{1,9},{2,10},{3,11},{4,12},{5,13},{6,14},{7,15},{8,0},{9,1},... | collective-permute-start | bytes 245768 | tf_op jit(solution)/shard_map/ppermute | solution.py:200
  16.4 1.4 %collective-permute-start.6 = (bf16[20,16,128]{2,1,0:T(8,128)(2,1)S(1)}, bf16[20,16,128]{2,1,0:T(8,128)(2,1)S(1)}, u32[]{:S(2)}, u32[]{:S(2)}) collective-permute-start(bf16[20,16,128]{2,1,0:T(8,128)(2,1)S(1)} %pad_maximum_fusion.ins__sent__), channel_id=1, source_target_pairs={{0,12},{1,13},{2,14},{3,15},{4,8},{5,9},{6,10},{7,11},{8,4},{9,5},... | collective-permute-start | bytes 245768 | tf_op jit(solution)/shard_map/ppermute | solution.py:200
  18.0 1.3 %shard_map.65.ins__inverse__ = f32[32,8,128]{2,1,0:T(8,128)S(1)} custom-call(s32[8,128]{1,0:T(8,128)S(1)} %pad.4.ins__index___0_.ins__next_index___0_, s32[8,128]{1,0:T(8,128)S(1)} %collective-permute-done.2.ins__index___1_.ins__next_index___1_, bf16[32,128,128]{2,1,0:T(8,128)(2,1)S(1)} %bitcast.30, ...), custom_call_target="tpu_custom_call" | custom-call | tf_op jit(solution)/shard_map/pallas_call | solution.py:158
  19.2 2.5 %collective-permute-done.7.ins__got___2_ = bf16[20,16,128]{2,1,0:T(8,128)(2,1)S(1)} collective-permute-done((bf16[20,16,128]{2,1,0:T(8,128)(2,1)S(1)}, bf16[20,16,128]{2,1,0:T(8,128)(2,1)S(1)}, u32[]{:S(2)}, u32[]{:S(2)}) %collective-permute-start.7) | collective-permute-done | bytes 81952 | tf_op jit(solution)/shard_map/ppermute | solution.py:200
  21.7 1.3 %collective-permute-done.6.ins__got___1_ = bf16[20,16,128]{2,1,0:T(8,128)(2,1)S(1)} collective-permute-done((bf16[20,16,128]{2,1,0:T(8,128)(2,1)S(1)}, bf16[20,16,128]{2,1,0:T(8,128)(2,1)S(1)}, u32[]{:S(2)}, u32[]{:S(2)}) %collective-permute-start.6) | collective-permute-done | bytes 81952 | tf_op jit(solution)/shard_map/ppermute | solution.py:200
  23.2 1.4 %shard_map.66 = (bf16[16,16,128]{2,1,0:T(8,128)(2,1)S(1)}, f32[2,16,2048]{2,1,0:T(8,128)S(1)}) custom-call(bf16[20,16,128]{2,1,0:T(8,128)(2,1)S(1)} %collective-permute-done.5.ins__got___0_, bf16[20,16,128]{2,1,0:T(8,128)(2,1)S(1)} %collective-permute-done.6.ins__got___1_, bf16[20,16,128]{2,1,0:T(8,128)(2,1)S(1)} %collective-permute-done.7.ins__got___2_, ...), custom_call_target="tpu_custom_call" | custom-call | tf_op jit(solution)/shard_map/pallas_call | solution.py:158
  24.6 1.6 %collective-permute-start.8 = (f32[2,16,2048]{2,1,0:T(8,128)S(1)}, f32[2,16,2048]{2,1,0:T(8,128)S(1)}, u32[]{:S(2)}, u32[]{:S(2)}) collective-permute-start(f32[2,16,2048]{2,1,0:T(8,128)S(1)} %get-tuple-element.29), channel_id=1, source_target_pairs={{0,16},{16,0},{1,17},{17,1},{2,18},{18,2},{3,19},{19,3},{4,20},{20... | collective-permute-start | bytes 786440 | tf_op jit(solution)/shard_map/ppermute | solution.py:206
  26.2 0.5 collective-permute-start.9
  26.7 6.5 %collective-permute-done.9.ins__index___0_ = s32[8,128]{1,0:T(8,128)S(1)} collective-permute-done((s32[8,128]{1,0:T(8,128)S(1)}, s32[8,128]{1,0:T(8,128)S(1)}, u32[]{:S(2)}, u32[]{:S(2)}) %collective-permute-start.9) | collective-permute-done | bytes 4128 | tf_op jit(solution)/shard_map/ppermute | solution.py:206
  33.2 1.6 %shard_map.67 = (bf16[18,16,128]{2,1,0:T(8,128)(2,1)S(1)}, f32[16,16,128]{2,1,0:T(8,128)S(1)}) custom-call(bf16[2,16,128]{2,1,0:T(8,128)(2,1)S(1)} %get-tuple-element.62.ins__dealt__, f32[2,16,2048]{2,1,0:T(8,128)S(1)} %collective-permute-done.8.ins__held__, s32[8,128]{1,0:T(8,128)S(1)} %pad.4.ins__index___0_.ins__next_index___0_, ...), custom_call_target="tpu_custom_call" | custom-call | tf_op jit(solution)/shard_map/pallas_call | solution.py:158
  35.2 1.8 %collective-permute-start.17 = (bf16[12,128,128]{2,1,0:T(8,128)(2,1)S(1)}, bf16[12,128,128]{2,1,0:T(8,128)(2,1)S(1)}, u32[]{:S(2)}, u32[]{:S(2)}) collective-permute-start(bf16[12,128,128]{2,1,0:T(8,128)(2,1)S(1)} %slice_bitcast_fusion.1), channel_id=1, source_target_pairs={{0,16},{16,0},{1,17},{17,1},{2,18},{18,2},{3,19},{19,3},{4,20},{20... | collective-permute-start | bytes 1179656 | tf_op jit(solution)/shard_map/ppermute | solution.py:206
  37.0 2.2 %collective-permute-done.11 = bf16[18,16,128]{2,1,0:T(8,128)(2,1)S(1)} collective-permute-done((bf16[18,16,128]{2,1,0:T(8,128)(2,1)S(1)}, bf16[18,16,128]{2,1,0:T(8,128)(2,1)S(1)}, u32[]{:S(2)}, u32[]{:S(2)}) %collective-permute-start.11) | collective-permute-done | bytes 73760 | tf_op jit(solution)/shard_map/ppermute | solution.py:200
  39.3 3.0 %collective-permute-start.14 = (bf16[20,16,128]{2,1,0:T(8,128)(2,1)S(1)}, bf16[20,16,128]{2,1,0:T(8,128)(2,1)S(1)}, u32[]{:S(2)}, u32[]{:S(2)}) collective-permute-start(bf16[20,16,128]{2,1,0:T(8,128)(2,1)S(1)} %pad_maximum_fusion.1.ins__sent__), channel_id=1, source_target_pairs={{0,8},{1,9},{2,10},{3,11},{4,12},{5,13},{6,14},{7,15},{8,0},{9,1},... | collective-permute-start | bytes 245768 | tf_op jit(solution)/shard_map/ppermute | solution.py:200
  42.3 1.1 %collective-permute-start.13 = (bf16[20,16,128]{2,1,0:T(8,128)(2,1)S(1)}, bf16[20,16,128]{2,1,0:T(8,128)(2,1)S(1)}, u32[]{:S(2)}, u32[]{:S(2)}) collective-permute-start(bf16[20,16,128]{2,1,0:T(8,128)(2,1)S(1)} %pad_maximum_fusion.1.ins__sent__), channel_id=1, source_target_pairs={{0,12},{1,13},{2,14},{3,15},{4,8},{5,9},{6,10},{7,11},{8,4},{9,5},... | collective-permute-start | bytes 245768 | tf_op jit(solution)/shard_map/ppermute | solution.py:200
  43.6 3.9 %collective-permute-done.14.ins__got___2_ = bf16[20,16,128]{2,1,0:T(8,128)(2,1)S(1)} collective-permute-done((bf16[20,16,128]{2,1,0:T(8,128)(2,1)S(1)}, bf16[20,16,128]{2,1,0:T(8,128)(2,1)S(1)}, u32[]{:S(2)}, u32[]{:S(2)}) %collective-permute-start.14) | collective-permute-done | bytes 81952 | tf_op jit(solution)/shard_map/ppermute | solution.py:200
  47.4 1.3 %collective-permute-done.13.ins__got___1_ = bf16[20,16,128]{2,1,0:T(8,128)(2,1)S(1)} collective-permute-done((bf16[20,16,128]{2,1,0:T(8,128)(2,1)S(1)}, bf16[20,16,128]{2,1,0:T(8,128)(2,1)S(1)}, u32[]{:S(2)}, u32[]{:S(2)}) %collective-permute-start.13) | collective-permute-done | bytes 81952 | tf_op jit(solution)/shard_map/ppermute | solution.py:200
  48.9 0.5 collective-permute-start.16
  49.4 1.4 %shard_map.68 = (bf16[16,16,128]{2,1,0:T(8,128)(2,1)S(1)}, f32[2,16,2048]{2,1,0:T(8,128)S(1)}) custom-call(bf16[20,16,128]{2,1,0:T(8,128)(2,1)S(1)} %collective-permute-done.12.ins__got___0_, bf16[20,16,128]{2,1,0:T(8,128)(2,1)S(1)} %collective-permute-done.13.ins__got___1_, bf16[20,16,128]{2,1,0:T(8,128)(2,1)S(1)} %collective-permute-done.14.ins__got___2_, ...), custom_call_target="tpu_custom_call" | custom-call | tf_op jit(solution)/shard_map/pallas_call | solution.py:158
  50.8 1.6 %shard_map.69 = (bf16[16,16,128]{2,1,0:T(8,128)(2,1)S(1)}, f32[16,16,128]{2,1,0:T(8,128)S(1)}) custom-call(f32[2,16,2048]{2,1,0:T(8,128)S(1)} %get-tuple-element.37.ins__held__, s32[8,128]{1,0:T(8,128)S(1)} %collective-permute-done.9.ins__index___0_, s32[8,128]{1,0:T(8,128)S(1)} %collective-permute-done.16.ins__index___1_, ...), custom_call_target="tpu_custom_call" | custom-call | tf_op jit(solution)/shard_map/pallas_call | solution.py:158
  52.5 1.3 %collective-permute-start.20 = (bf16[16,16,128]{2,1,0:T(8,128)(2,1)S(1)}, bf16[16,16,128]{2,1,0:T(8,128)(2,1)S(1)}, u32[]{:S(2)}, u32[]{:S(2)}) collective-permute-start(bf16[16,16,128]{2,1,0:T(8,128)(2,1)S(1)} %get-tuple-element.45), channel_id=1, source_target_pairs={{0,2},{1,3},{2,0},{3,1},{4,6},{5,7},{6,4},{7,5},{8,10},{9,11},{10,... | collective-permute-start | bytes 196616 | tf_op jit(solution)/shard_map/ppermute | solution.py:200
  53.8 1.4 %collective-permute-start.15 = (bf16[16,16,128]{2,1,0:T(8,128)(2,1)S(1)}, bf16[16,16,128]{2,1,0:T(8,128)(2,1)S(1)}, u32[]{:S(2)}, u32[]{:S(2)}) collective-permute-start(bf16[16,16,128]{2,1,0:T(8,128)(2,1)S(1)} %get-tuple-element.36), channel_id=1, source_target_pairs={{0,16},{16,0},{1,17},{17,1},{2,18},{18,2},{3,19},{19,3},{4,20},{20... | collective-permute-start | bytes 196616 | tf_op jit(solution)/shard_map/ppermute | solution.py:206
  55.2 1.6 %collective-permute-done.20 = bf16[16,16,128]{2,1,0:T(8,128)(2,1)S(1)} collective-permute-done((bf16[16,16,128]{2,1,0:T(8,128)(2,1)S(1)}, bf16[16,16,128]{2,1,0:T(8,128)(2,1)S(1)}, u32[]{:S(2)}, u32[]{:S(2)}) %collective-permute-start.20) | collective-permute-done | bytes 65568 | tf_op jit(solution)/shard_map/ppermute | solution.py:200
  56.8 2.0 %collective-permute-start.23 = (bf16[16,16,128]{2,1,0:T(8,128)(2,1)S(1)}, bf16[16,16,128]{2,1,0:T(8,128)(2,1)S(1)}, u32[]{:S(2)}, u32[]{:S(2)}) collective-permute-start(bf16[16,16,128]{2,1,0:T(8,128)(2,1)S(1)} %get-tuple-element.51), channel_id=1, source_target_pairs={{0,8},{1,9},{2,10},{3,11},{4,12},{5,13},{6,14},{7,15},{8,0},{9,1},... | collective-permute-start | bytes 196616 | tf_op jit(solution)/shard_map/ppermute | solution.py:200
  58.8 1.5 %collective-permute-start.22 = (bf16[16,16,128]{2,1,0:T(8,128)(2,1)S(1)}, bf16[16,16,128]{2,1,0:T(8,128)(2,1)S(1)}, u32[]{:S(2)}, u32[]{:S(2)}) collective-permute-start(bf16[16,16,128]{2,1,0:T(8,128)(2,1)S(1)} %get-tuple-element.51), channel_id=1, source_target_pairs={{0,12},{1,13},{2,14},{3,15},{4,8},{5,9},{6,10},{7,11},{8,4},{9,5},... | collective-permute-start | bytes 196616 | tf_op jit(solution)/shard_map/ppermute | solution.py:200
  60.4 1.3 %shard_map.70.ins__inverse__ = f32[32,8,128]{2,1,0:T(8,128)S(1)} custom-call(s32[8,128]{1,0:T(8,128)S(1)} %collective-permute-done.9.ins__index___0_, s32[8,128]{1,0:T(8,128)S(1)} %collective-permute-done.16.ins__index___1_, bf16[20,128,128]{2,1,0:T(8,128)(2,1)S(1)} %collective-permute-done.10.ins__tiles___0__0_, ...), custom_call_target="tpu_custom_call" | custom-call | tf_op jit(solution)/shard_map/pallas_call | solution.py:158
  61.7 2.1 %collective-permute-done.23.ins__got___2_ = bf16[16,16,128]{2,1,0:T(8,128)(2,1)S(1)} collective-permute-done((bf16[16,16,128]{2,1,0:T(8,128)(2,1)S(1)}, bf16[16,16,128]{2,1,0:T(8,128)(2,1)S(1)}, u32[]{:S(2)}, u32[]{:S(2)}) %collective-permute-start.23) | collective-permute-done | bytes 65568 | tf_op jit(solution)/shard_map/ppermute | solution.py:200
  63.7 1.4 %collective-permute-done.22.ins__got___1_ = bf16[16,16,128]{2,1,0:T(8,128)(2,1)S(1)} collective-permute-done((bf16[16,16,128]{2,1,0:T(8,128)(2,1)S(1)}, bf16[16,16,128]{2,1,0:T(8,128)(2,1)S(1)}, u32[]{:S(2)}, u32[]{:S(2)}) %collective-permute-start.22) | collective-permute-done | bytes 65568 | tf_op jit(solution)/shard_map/ppermute | solution.py:200
  65.3 2.5 %shard_map.71 = (f32[2,16,2048]{2,1,0:T(8,128)S(1)}, bf16[16,16,128]{2,1,0:T(8,128)(2,1)S(1)}, f32[16,16,128]{2,1,0:T(8,128)S(1)}) custom-call(bf16[16,16,128]{2,1,0:T(8,128)(2,1)S(1)} %collective-permute-done.15.ins__counts__, bf16[16,16,128]{2,1,0:T(8,128)(2,1)S(1)} %collective-permute-done.21.ins__got___0_, ...), custom_call_target="tpu_custom_call" | custom-call | tf_op jit(solution)/shard_map/pallas_call | solution.py:158
  67.8 1.2 %collective-permute-start.24 = (bf16[16,16,128]{2,1,0:T(8,128)(2,1)S(1)}, bf16[16,16,128]{2,1,0:T(8,128)(2,1)S(1)}, u32[]{:S(2)}, u32[]{:S(2)}) collective-permute-start(bf16[16,16,128]{2,1,0:T(8,128)(2,1)S(1)} %get-tuple-element.47), channel_id=1, source_target_pairs={{0,2},{1,3},{2,0},{3,1},{4,6},{5,7},{6,4},{7,5},{8,10},{9,11},{10,... | collective-permute-start | bytes 196616 | tf_op jit(solution)/shard_map/ppermute | solution.py:200
  69.0 3.2 %collective-permute-done.24 = bf16[16,16,128]{2,1,0:T(8,128)(2,1)S(1)} collective-permute-done((bf16[16,16,128]{2,1,0:T(8,128)(2,1)S(1)}, bf16[16,16,128]{2,1,0:T(8,128)(2,1)S(1)}, u32[]{:S(2)}, u32[]{:S(2)}) %collective-permute-start.24) | collective-permute-done | bytes 65568 | tf_op jit(solution)/shard_map/ppermute | solution.py:200
  72.1 1.6 %collective-permute-start.27 = (bf16[16,16,128]{2,1,0:T(8,128)(2,1)S(1)}, bf16[16,16,128]{2,1,0:T(8,128)(2,1)S(1)}, u32[]{:S(2)}, u32[]{:S(2)}) collective-permute-start(bf16[16,16,128]{2,1,0:T(8,128)(2,1)S(1)} %get-tuple-element.49), channel_id=1, source_target_pairs={{0,8},{1,9},{2,10},{3,11},{4,12},{5,13},{6,14},{7,15},{8,0},{9,1},... | collective-permute-start | bytes 196616 | tf_op jit(solution)/shard_map/ppermute | solution.py:200
  73.7 1.3 %collective-permute-start.26 = (bf16[16,16,128]{2,1,0:T(8,128)(2,1)S(1)}, bf16[16,16,128]{2,1,0:T(8,128)(2,1)S(1)}, u32[]{:S(2)}, u32[]{:S(2)}) collective-permute-start(bf16[16,16,128]{2,1,0:T(8,128)(2,1)S(1)} %get-tuple-element.49), channel_id=1, source_target_pairs={{0,12},{1,13},{2,14},{3,15},{4,8},{5,9},{6,10},{7,11},{8,4},{9,5},... | collective-permute-start | bytes 196616 | tf_op jit(solution)/shard_map/ppermute | solution.py:200
  74.9 0.7 collective-permute-start.25
  75.7 2.4 %collective-permute-done.27.ins__got___2_ = bf16[16,16,128]{2,1,0:T(8,128)(2,1)S(1)} collective-permute-done((bf16[16,16,128]{2,1,0:T(8,128)(2,1)S(1)}, bf16[16,16,128]{2,1,0:T(8,128)(2,1)S(1)}, u32[]{:S(2)}, u32[]{:S(2)}) %collective-permute-start.27) | collective-permute-done | bytes 65568 | tf_op jit(solution)/shard_map/ppermute | solution.py:200
  78.1 1.8 %collective-permute-done.26.ins__got___1_ = bf16[16,16,128]{2,1,0:T(8,128)(2,1)S(1)} collective-permute-done((bf16[16,16,128]{2,1,0:T(8,128)(2,1)S(1)}, bf16[16,16,128]{2,1,0:T(8,128)(2,1)S(1)}, u32[]{:S(2)}, u32[]{:S(2)}) %collective-permute-start.26) | collective-permute-done | bytes 65568 | tf_op jit(solution)/shard_map/ppermute | solution.py:200
  79.9 1.4 %shard_map.72 = f32[2,16,2048]{2,1,0:T(8,128)S(1)} custom-call(bf16[16,16,128]{2,1,0:T(8,128)(2,1)S(1)} %get-tuple-element.35.ins__counts__, bf16[16,16,128]{2,1,0:T(8,128)(2,1)S(1)} %collective-permute-done.25.ins__got___0_, bf16[16,16,128]{2,1,0:T(8,128)(2,1)S(1)} %collective-permute-done.26.ins__got___1_, ...), custom_call_target="tpu_custom_call" | custom-call | tf_op jit(solution)/shard_map/pallas_call | solution.py:158
  81.4 1.3 %collective-permute-done.28 = f32[16,2048]{1,0:T(8,128)S(1)} collective-permute-done((f32[16,2048]{1,0:T(8,128)S(1)}, f32[16,2048]{1,0:T(8,128)S(1)}, u32[]{:S(2)}, u32[]{:S(2)}) %collective-permute-start.28) | collective-permute-done | bytes 131104 | tf_op jit(solution)/shard_map/ppermute | solution.py:196
  82.7 0.7 maximum_select_fusion
  (54 shorter events, 2.4 us)
Async XLA Ops:
  0.0 5.0 %collective-permute-start.3 = (bf16[32,128,128]{2,1,0:T(8,128)(2,1)}, bf16[32,128,128]{2,1,0:T(8,128)(2,1)S(1)}, u32[]{:S(2)}, u32[]{:S(2)}) collective-permute-start(bf16[32,128,128]{2,1,0:T(8,128)(2,1)} %bitcast.28), channel_id=1, source_target_pairs={{0,1},{1,0},{2,3},{3,2},{4,5},{5,4},{6,7},{7,6},{8,9},{9,8},{10,11... | collective-permute-start | bytes 3145736 | tf_op jit(solution)/shard_map/ppermute | solution.py:196
  0.5 1.6 %copy-start.2 = (s32[1,64,128]{2,1,0:T(8,128)S(1)}, s32[1,64,128]{2,1,0:T(8,128)}, u32[]{:S(2)}) copy-start(s32[1,64,128]{2,1,0:T(8,128)} %param.11) | copy-start | bytes 98308
  1.2 0.7 copy-start.3
  1.2 0.7 copy-start.4
  1.9 1.8 %collective-permute-start.2 = (s32[8,128]{1,0:T(8,128)S(1)}, s32[8,128]{1,0:T(8,128)S(1)}, u32[]{:S(2)}, u32[]{:S(2)}) collective-permute-start(s32[8,128]{1,0:T(8,128)S(1)} %pad.4.ins__index___0_.ins__next_index___0_), channel_id=1, source_target_pairs={{0,1},{1,0},{2,3},{3,2},{4,5},{5,4},{6,7},{7,6},{8,9},{9,8},{10,11... | collective-permute-start | bytes 12296 | tf_op jit(solution)/shard_map/ppermute | solution.py:196
  2.0 1.6 %collective-permute-start = (bf16[1,2,16,128]{3,2,0,1:T(8,128)(2,1)S(1)}, bf16[1,2,16,128]{3,2,0,1:T(8,128)(2,1)S(1)}, u32[]{:S(2)}, u32[]{:S(2)}) collective-permute-start(bf16[1,2,16,128]{3,2,0,1:T(8,128)(2,1)S(1)} %get-tuple-element.64), channel_id=1, source_target_pairs={{0,1},{1,0},{2,3},{3,2},{4,5},{5,4},{6,7},{7,6},{8,9},{9,8},{10,11... | collective-permute-start | bytes 24584 | tf_op jit(solution)/shard_map/ppermute | solution.py:196
  3.5 1.4 %collective-permute-start.1 = (f32[16,2048]{1,0:T(8,128)S(1)}, f32[16,2048]{1,0:T(8,128)S(1)}, u32[]{:S(2)}, u32[]{:S(2)}) collective-permute-start(f32[16,2048]{1,0:T(8,128)S(1)} %get-tuple-element.59), channel_id=1, source_target_pairs={{0,1},{1,0},{2,3},{3,2},{4,5},{5,4},{6,7},{7,6},{8,9},{9,8},{10,11... | collective-permute-start | bytes 393224 | tf_op jit(solution)/shard_map/ppermute | solution.py:196
  5.0 1.2 %copy-start = (bf16[1,32,128,128]{3,2,1,0:T(8,128)(2,1)S(1)}, bf16[1,32,128,128]{3,2,1,0:T(8,128)(2,1)}, u32[]{:S(2)}) copy-start(bf16[1,32,128,128]{3,2,1,0:T(8,128)(2,1)} %param.7) | copy-start | bytes 3145732
  7.9 10.1 %copy-start.1 = (bf16[1,32,128,128]{3,2,1,0:T(8,128)(2,1)S(1)}, bf16[1,32,128,128]{3,2,1,0:T(8,128)(2,1)}, u32[]{:S(2)}) copy-start(bf16[1,32,128,128]{3,2,1,0:T(8,128)(2,1)} %param.7) | copy-start | bytes 3145732
  7.9 5.5 %collective-permute-start.4 = (bf16[18,16,128]{2,1,0:T(8,128)(2,1)S(1)}, bf16[18,16,128]{2,1,0:T(8,128)(2,1)S(1)}, u32[]{:S(2)}, u32[]{:S(2)}) collective-permute-start(bf16[18,16,128]{2,1,0:T(8,128)(2,1)S(1)} %get-tuple-element.28), channel_id=1, source_target_pairs={{0,2},{1,3},{2,0},{3,1},{4,6},{5,7},{6,4},{7,5},{8,10},{9,11},{10,... | collective-permute-start | bytes 221192 | tf_op jit(solution)/shard_map/ppermute | solution.py:200
  10.7 22.5 %collective-permute-start.10 = (bf16[20,128,128]{2,1,0:T(8,128)(2,1)S(1)}, bf16[20,128,128]{2,1,0:T(8,128)(2,1)S(1)}, u32[]{:S(2)}, u32[]{:S(2)}) collective-permute-start(bf16[20,128,128]{2,1,0:T(8,128)(2,1)S(1)} %slice_bitcast_fusion), channel_id=1, source_target_pairs={{0,16},{16,0},{1,17},{17,1},{2,18},{18,2},{3,19},{19,3},{4,20},{20... | collective-permute-start | bytes 1966088 | tf_op jit(solution)/shard_map/ppermute | solution.py:206
  13.5 8.2 %collective-permute-start.7 = (bf16[20,16,128]{2,1,0:T(8,128)(2,1)S(1)}, bf16[20,16,128]{2,1,0:T(8,128)(2,1)S(1)}, u32[]{:S(2)}, u32[]{:S(2)}) collective-permute-start(bf16[20,16,128]{2,1,0:T(8,128)(2,1)S(1)} %pad_maximum_fusion.ins__sent__), channel_id=1, source_target_pairs={{0,8},{1,9},{2,10},{3,11},{4,12},{5,13},{6,14},{7,15},{8,0},{9,1},... | collective-permute-start | bytes 245768 | tf_op jit(solution)/shard_map/ppermute | solution.py:200
  16.4 6.6 %collective-permute-start.6 = (bf16[20,16,128]{2,1,0:T(8,128)(2,1)S(1)}, bf16[20,16,128]{2,1,0:T(8,128)(2,1)S(1)}, u32[]{:S(2)}, u32[]{:S(2)}) collective-permute-start(bf16[20,16,128]{2,1,0:T(8,128)(2,1)S(1)} %pad_maximum_fusion.ins__sent__), channel_id=1, source_target_pairs={{0,12},{1,13},{2,14},{3,15},{4,8},{5,9},{6,10},{7,11},{8,4},{9,5},... | collective-permute-start | bytes 245768 | tf_op jit(solution)/shard_map/ppermute | solution.py:200
  17.7 5.5 %collective-permute-start.5 = (bf16[20,16,128]{2,1,0:T(8,128)(2,1)S(1)}, bf16[20,16,128]{2,1,0:T(8,128)(2,1)S(1)}, u32[]{:S(2)}, u32[]{:S(2)}) collective-permute-start(bf16[20,16,128]{2,1,0:T(8,128)(2,1)S(1)} %pad_maximum_fusion.ins__sent__), channel_id=1, source_target_pairs={{0,4},{1,5},{2,6},{3,7},{4,0},{5,1},{6,2},{7,3},{8,12},{9,13},{10,... | collective-permute-start | bytes 245768 | tf_op jit(solution)/shard_map/ppermute | solution.py:200
  24.6 8.6 %collective-permute-start.8 = (f32[2,16,2048]{2,1,0:T(8,128)S(1)}, f32[2,16,2048]{2,1,0:T(8,128)S(1)}, u32[]{:S(2)}, u32[]{:S(2)}) collective-permute-start(f32[2,16,2048]{2,1,0:T(8,128)S(1)} %get-tuple-element.29), channel_id=1, source_target_pairs={{0,16},{16,0},{1,17},{17,1},{2,18},{18,2},{3,19},{19,3},{4,20},{20... | collective-permute-start | bytes 786440 | tf_op jit(solution)/shard_map/ppermute | solution.py:206
  26.2 7.0 %collective-permute-start.9 = (s32[8,128]{1,0:T(8,128)S(1)}, s32[8,128]{1,0:T(8,128)S(1)}, u32[]{:S(2)}, u32[]{:S(2)}) collective-permute-start(s32[8,128]{1,0:T(8,128)S(1)} %pad.4.ins__index___0_.ins__next_index___0_), channel_id=1, source_target_pairs={{0,16},{16,0},{1,17},{17,1},{2,18},{18,2},{3,19},{19,3},{4,20},{20... | collective-permute-start | bytes 12296 | tf_op jit(solution)/shard_map/ppermute | solution.py:206
  34.8 4.4 %collective-permute-start.11 = (bf16[18,16,128]{2,1,0:T(8,128)(2,1)S(1)}, bf16[18,16,128]{2,1,0:T(8,128)(2,1)S(1)}, u32[]{:S(2)}, u32[]{:S(2)}) collective-permute-start(bf16[18,16,128]{2,1,0:T(8,128)(2,1)S(1)} %get-tuple-element.34), channel_id=1, source_target_pairs={{0,2},{1,3},{2,0},{3,1},{4,6},{5,7},{6,4},{7,5},{8,10},{9,11},{10,... | collective-permute-start | bytes 221192 | tf_op jit(solution)/shard_map/ppermute | solution.py:200
  35.2 13.7 %collective-permute-start.17 = (bf16[12,128,128]{2,1,0:T(8,128)(2,1)S(1)}, bf16[12,128,128]{2,1,0:T(8,128)(2,1)S(1)}, u32[]{:S(2)}, u32[]{:S(2)}) collective-permute-start(bf16[12,128,128]{2,1,0:T(8,128)(2,1)S(1)} %slice_bitcast_fusion.1), channel_id=1, source_target_pairs={{0,16},{16,0},{1,17},{17,1},{2,18},{18,2},{3,19},{19,3},{4,20},{20... | collective-permute-start | bytes 1179656 | tf_op jit(solution)/shard_map/ppermute | solution.py:206
  37.0 13.8 %collective-permute-start.18 = (bf16[20,128,128]{2,1,0:T(8,128)(2,1)S(1)}, bf16[20,128,128]{2,1,0:T(8,128)(2,1)S(1)}, u32[]{:S(2)}, u32[]{:S(2)}) collective-permute-start(bf16[20,128,128]{2,1,0:T(8,128)(2,1)S(1)} %collective-permute-done.10.ins__tiles___0__0_), channel_id=1, source_target_pairs={{0,1},{1,0},{2,3},{3,2},{4,5},{5,4},{6,7},{7,6},{8,9},{9,8},{10,11... | collective-permute-start | bytes 1966088 | tf_op jit(solution)/shard_map/ppermute | solution.py:196
  39.3 8.1 %collective-permute-start.14 = (bf16[20,16,128]{2,1,0:T(8,128)(2,1)S(1)}, bf16[20,16,128]{2,1,0:T(8,128)(2,1)S(1)}, u32[]{:S(2)}, u32[]{:S(2)}) collective-permute-start(bf16[20,16,128]{2,1,0:T(8,128)(2,1)S(1)} %pad_maximum_fusion.1.ins__sent__), channel_id=1, source_target_pairs={{0,8},{1,9},{2,10},{3,11},{4,12},{5,13},{6,14},{7,15},{8,0},{9,1},... | collective-permute-start | bytes 245768 | tf_op jit(solution)/shard_map/ppermute | solution.py:200
  42.3 6.4 %collective-permute-start.13 = (bf16[20,16,128]{2,1,0:T(8,128)(2,1)S(1)}, bf16[20,16,128]{2,1,0:T(8,128)(2,1)S(1)}, u32[]{:S(2)}, u32[]{:S(2)}) collective-permute-start(bf16[20,16,128]{2,1,0:T(8,128)(2,1)S(1)} %pad_maximum_fusion.1.ins__sent__), channel_id=1, source_target_pairs={{0,12},{1,13},{2,14},{3,15},{4,8},{5,9},{6,10},{7,11},{8,4},{9,5},... | collective-permute-start | bytes 245768 | tf_op jit(solution)/shard_map/ppermute | solution.py:200
  43.3 5.6 %collective-permute-start.12 = (bf16[20,16,128]{2,1,0:T(8,128)(2,1)S(1)}, bf16[20,16,128]{2,1,0:T(8,128)(2,1)S(1)}, u32[]{:S(2)}, u32[]{:S(2)}) collective-permute-start(bf16[20,16,128]{2,1,0:T(8,128)(2,1)S(1)} %pad_maximum_fusion.1.ins__sent__), channel_id=1, source_target_pairs={{0,4},{1,5},{2,6},{3,7},{4,0},{5,1},{6,2},{7,3},{8,12},{9,13},{10,... | collective-permute-start | bytes 245768 | tf_op jit(solution)/shard_map/ppermute | solution.py:200
  48.9 1.9 %collective-permute-start.19 = (bf16[12,128,128]{2,1,0:T(8,128)(2,1)S(1)}, bf16[12,128,128]{2,1,0:T(8,128)(2,1)S(1)}, u32[]{:S(2)}, u32[]{:S(2)}) collective-permute-start(bf16[12,128,128]{2,1,0:T(8,128)(2,1)S(1)} %collective-permute-done.17.ins__tiles___0__1_), channel_id=1, source_target_pairs={{0,1},{1,0},{2,3},{3,2},{4,5},{5,4},{6,7},{7,6},{8,9},{9,8},{10,11... | collective-permute-start | bytes 1179656 | tf_op jit(solution)/shard_map/ppermute | solution.py:196
  48.9 1.9 %collective-permute-start.16 = (s32[8,128]{1,0:T(8,128)S(1)}, s32[8,128]{1,0:T(8,128)S(1)}, u32[]{:S(2)}, u32[]{:S(2)}) collective-permute-start(s32[8,128]{1,0:T(8,128)S(1)} %collective-permute-done.9.ins__index___0_), channel_id=1, source_target_pairs={{0,1},{1,0},{2,3},{3,2},{4,5},{5,4},{6,7},{7,6},{8,9},{9,8},{10,11... | collective-permute-start | bytes 12296 | tf_op jit(solution)/shard_map/ppermute | solution.py:196
  52.5 4.3 %collective-permute-start.20 = (bf16[16,16,128]{2,1,0:T(8,128)(2,1)S(1)}, bf16[16,16,128]{2,1,0:T(8,128)(2,1)S(1)}, u32[]{:S(2)}, u32[]{:S(2)}) collective-permute-start(bf16[16,16,128]{2,1,0:T(8,128)(2,1)S(1)} %get-tuple-element.45), channel_id=1, source_target_pairs={{0,2},{1,3},{2,0},{3,1},{4,6},{5,7},{6,4},{7,5},{8,10},{9,11},{10,... | collective-permute-start | bytes 196616 | tf_op jit(solution)/shard_map/ppermute | solution.py:200
  53.8 7.9 %collective-permute-start.15 = (bf16[16,16,128]{2,1,0:T(8,128)(2,1)S(1)}, bf16[16,16,128]{2,1,0:T(8,128)(2,1)S(1)}, u32[]{:S(2)}, u32[]{:S(2)}) collective-permute-start(bf16[16,16,128]{2,1,0:T(8,128)(2,1)S(1)} %get-tuple-element.36), channel_id=1, source_target_pairs={{0,16},{16,0},{1,17},{17,1},{2,18},{18,2},{3,19},{19,3},{4,20},{20... | collective-permute-start | bytes 196616 | tf_op jit(solution)/shard_map/ppermute | solution.py:206
  56.8 6.9 %collective-permute-start.23 = (bf16[16,16,128]{2,1,0:T(8,128)(2,1)S(1)}, bf16[16,16,128]{2,1,0:T(8,128)(2,1)S(1)}, u32[]{:S(2)}, u32[]{:S(2)}) collective-permute-start(bf16[16,16,128]{2,1,0:T(8,128)(2,1)S(1)} %get-tuple-element.51), channel_id=1, source_target_pairs={{0,8},{1,9},{2,10},{3,11},{4,12},{5,13},{6,14},{7,15},{8,0},{9,1},... | collective-permute-start | bytes 196616 | tf_op jit(solution)/shard_map/ppermute | solution.py:200
  58.8 6.2 %collective-permute-start.22 = (bf16[16,16,128]{2,1,0:T(8,128)(2,1)S(1)}, bf16[16,16,128]{2,1,0:T(8,128)(2,1)S(1)}, u32[]{:S(2)}, u32[]{:S(2)}) collective-permute-start(bf16[16,16,128]{2,1,0:T(8,128)(2,1)S(1)} %get-tuple-element.51), channel_id=1, source_target_pairs={{0,12},{1,13},{2,14},{3,15},{4,8},{5,9},{6,10},{7,11},{8,4},{9,5},... | collective-permute-start | bytes 196616 | tf_op jit(solution)/shard_map/ppermute | solution.py:200
  60.3 5.0 %collective-permute-start.21 = (bf16[16,16,128]{2,1,0:T(8,128)(2,1)S(1)}, bf16[16,16,128]{2,1,0:T(8,128)(2,1)S(1)}, u32[]{:S(2)}, u32[]{:S(2)}) collective-permute-start(bf16[16,16,128]{2,1,0:T(8,128)(2,1)S(1)} %get-tuple-element.51), channel_id=1, source_target_pairs={{0,4},{1,5},{2,6},{3,7},{4,0},{5,1},{6,2},{7,3},{8,12},{9,13},{10,... | collective-permute-start | bytes 196616 | tf_op jit(solution)/shard_map/ppermute | solution.py:200
  67.8 4.3 %collective-permute-start.24 = (bf16[16,16,128]{2,1,0:T(8,128)(2,1)S(1)}, bf16[16,16,128]{2,1,0:T(8,128)(2,1)S(1)}, u32[]{:S(2)}, u32[]{:S(2)}) collective-permute-start(bf16[16,16,128]{2,1,0:T(8,128)(2,1)S(1)} %get-tuple-element.47), channel_id=1, source_target_pairs={{0,2},{1,3},{2,0},{3,1},{4,6},{5,7},{6,4},{7,5},{8,10},{9,11},{10,... | collective-permute-start | bytes 196616 | tf_op jit(solution)/shard_map/ppermute | solution.py:200
  72.1 6.0 %collective-permute-start.27 = (bf16[16,16,128]{2,1,0:T(8,128)(2,1)S(1)}, bf16[16,16,128]{2,1,0:T(8,128)(2,1)S(1)}, u32[]{:S(2)}, u32[]{:S(2)}) collective-permute-start(bf16[16,16,128]{2,1,0:T(8,128)(2,1)S(1)} %get-tuple-element.49), channel_id=1, source_target_pairs={{0,8},{1,9},{2,10},{3,11},{4,12},{5,13},{6,14},{7,15},{8,0},{9,1},... | collective-permute-start | bytes 196616 | tf_op jit(solution)/shard_map/ppermute | solution.py:200
  73.7 6.2 %collective-permute-start.26 = (bf16[16,16,128]{2,1,0:T(8,128)(2,1)S(1)}, bf16[16,16,128]{2,1,0:T(8,128)(2,1)S(1)}, u32[]{:S(2)}, u32[]{:S(2)}) collective-permute-start(bf16[16,16,128]{2,1,0:T(8,128)(2,1)S(1)} %get-tuple-element.49), channel_id=1, source_target_pairs={{0,12},{1,13},{2,14},{3,15},{4,8},{5,9},{6,10},{7,11},{8,4},{9,5},... | collective-permute-start | bytes 196616 | tf_op jit(solution)/shard_map/ppermute | solution.py:200
  74.9 5.0 %collective-permute-start.25 = (bf16[16,16,128]{2,1,0:T(8,128)(2,1)S(1)}, bf16[16,16,128]{2,1,0:T(8,128)(2,1)S(1)}, u32[]{:S(2)}, u32[]{:S(2)}) collective-permute-start(bf16[16,16,128]{2,1,0:T(8,128)(2,1)S(1)} %get-tuple-element.49), channel_id=1, source_target_pairs={{0,4},{1,5},{2,6},{3,7},{4,0},{5,1},{6,2},{7,3},{8,12},{9,13},{10,... | collective-permute-start | bytes 196616 | tf_op jit(solution)/shard_map/ppermute | solution.py:200
  81.3 1.4 %collective-permute-start.28 = (f32[16,2048]{1,0:T(8,128)S(1)}, f32[16,2048]{1,0:T(8,128)S(1)}, u32[]{:S(2)}, u32[]{:S(2)}) collective-permute-start(f32[16,2048]{1,0:T(8,128)S(1)} %get-tuple-element.58), channel_id=1, source_target_pairs={{0,1},{1,0},{2,3},{3,2},{4,5},{5,4},{6,7},{7,6},{8,9},{9,8},{10,11... | collective-permute-start | bytes 393224 | tf_op jit(solution)/shard_map/ppermute | solution.py:196

commit v5 on v4

--- a/solution.py
+++ b/solution.py
@@ -183,10 +183,10 @@
     f32, bf16 = jnp.float32, jnp.bfloat16
     shaped = jax.ShapeDtypeStruct
 
-    steps, bit = [(1,)], 2
+    steps, bit = [], 1
     while bit < chips:
         wide_step = bit * 4 <= chips
-        steps.append((bit, 3 * bit, 2 * bit) if wide_step else (bit,))
+        steps.append((bit, 2 * bit, 3 * bit) if wide_step else (bit,))
         bit *= 4 if wide_step else 2
 
     def place(masks):

time: 83.7 us -> 82.9 us (level)
  waiting for transfers between devices: 34.6 us -> 29.2 us
  starting transfers between devices: 29.9 us -> 34.5 us
    ppermute x16, waiting for transfers between devices: 25.5 us -> 20.5 us  [swap_chips(): return lax.ppermute(array, 'tile', pairs)]
    ppermute x16, starting transfers between devices: 21.4 us -> 25.8 us  [swap_chips(): return lax.ppermute(array, 'tile', pairs)]
    ppermute x8, waiting for transfers between devices: 2.59 us -> 1.35 us  [swap_cores(): return lax.ppermute(array, 'tile', [(i, i ^ 1) for i in range(tile_devs)])]
    unnamed x10 -> x14, local copies, waits for them, and re-layouts: 1.83 us -> 0.7 us
    slice x1, local copies, waits for them, and re-layouts: 0.04 us -> 1.13 us  [shards(): far_tiles = [shift(after(own_tiles[:slots * 5 // 8], sent))]]
  transfers between devices with their start and end apart: 29 -> 29, of which waited for: 19 -> 18; matrix products, arithmetic and copies ran while one was open for 2% -> 3% of each run, Pallas kernels for 6% -> 6%
where the time goes in v5:
time: 82.9 us; the launch traced here: 82.6 us
  starting transfers between devices  34.5 us (42%)
  waiting for transfers between devices  29.2 us (35%)
  Pallas kernels  13.9 us (17%)
  local copies, waits for them, and re-layouts  3.08 us (4%)
  between operations  1.01 us (1%)
  other arithmetic  0.98 us (1%)
    ppermute x16, starting transfers between devices, swap_chips(): return lax.ppermute(array, 'tile', pairs)  25.8 us
    ppermute x16, waiting for transfers between devices, swap_chips(): return lax.ppermute(array, 'tile', pairs)  20.5 us
    pallas_call x9, Pallas kernels, call(): pl.pallas_call(kernel, out_shape=outs, in_specs=[jax.tree_util.tree_map_w...  13.9 us
    ppermute x5, waiting for transfers between devices, shift(): lax.ppermute(array, 'subset', [(i, (i + 1) % subset_count) for i in range...  7.29 us
    ppermute x5, starting transfers between devices, shift(): lax.ppermute(array, 'subset', [(i, (i + 1) % subset_count) for i in range...  6.89 us
    ppermute x8, starting transfers between devices, swap_cores(): return lax.ppermute(array, 'tile', [(i, i ^ 1) for i in range(tile_devs)])  1.83 us
  transfers between devices with their start and end apart: 29, of which 18 were waited for; matrix products, arithmetic and copies ran while one was open for 3% of the time, Pallas kernels for 6%

profile of v5, /device:TPU:0, one launch (start us, length us, event | category | flops | bytes accessed | tf_op | source)
XLA Modules:
  0.0 82.6 jit_solution(465884560076057691)
XLA Ops:
  0.0 0.5 collective-permute-start.3
  1.3 0.6 copy-done.2
  2.1 0.5 collective-permute-start
  2.6 1.0 %dynamic-slice_bitcast_fusion = (f32[16,2048]{1,0:T(8,128)S(1)}, f32[16,2048]{1,0:T(8,128)S(1)}) fusion(f32[2,16,2048]{2,1,0:T(8,128)} %bitcast.68, s32[]{:T(128)S(6)} %select_n.88, s32[]{:T(128)S(6)} %select_n.87), kind=kLoop, calls=%fused_computation.9 | loop fusion | bytes 524296 | tf_op jit(solution)/shard_map/jit(dynamic_index_in_dim)/squeeze | solution.py:213
  3.8 1.1 %slice_bitcast_fusion = bf16[20,128,128]{2,1,0:T(8,128)(2,1)S(1)} fusion(bf16[1,32,128,128]{3,2,1,0:T(8,128)(2,1)} %param.7), kind=kLoop, calls=%fused_computation | loop fusion | bytes 1310720 | tf_op jit(solution)/shard_map/slice | solution.py:262
  5.1 1.7 %shard_map.64 = (bf16[18,16,128]{2,1,0:T(8,128)(2,1)S(1)}, f32[16,16,128]{2,1,0:T(8,128)S(1)}) custom-call(bf16[2,16,128]{2,1,0:T(8,128)(2,1)S(1)} %get-tuple-element.61.ins__dealt__, f32[16,2048]{1,0:T(8,128)S(1)} %get-tuple-element.60.ins__held___0_, f32[16,2048]{1,0:T(8,128)S(1)} %collective-permute-done.1.ins__held___1_, ...), custom_call_target="tpu_custom_call" | custom-call | tf_op jit(solution)/shard_map/pallas_call | solution.py:158
  6.8 4.0 %collective-permute-start.6 = (bf16[18,16,128]{2,1,0:T(8,128)(2,1)S(1)}, bf16[18,16,128]{2,1,0:T(8,128)(2,1)S(1)}, u32[]{:S(2)}, u32[]{:S(2)}) collective-permute-start(bf16[18,16,128]{2,1,0:T(8,128)(2,1)S(1)} %get-tuple-element.28), channel_id=1, source_target_pairs={{0,6},{1,7},{2,4},{3,5},{4,2},{5,3},{6,0},{7,1},{8,14},{9,15},{10,... | collective-permute-start | bytes 221192 | tf_op jit(solution)/shard_map/ppermute | solution.py:200
  10.7 0.4 collective-permute-start.5
  11.4 1.8 %collective-permute-start.10 = (bf16[20,128,128]{2,1,0:T(8,128)(2,1)S(1)}, bf16[20,128,128]{2,1,0:T(8,128)(2,1)S(1)}, u32[]{:S(2)}, u32[]{:S(2)}) collective-permute-start(bf16[20,128,128]{2,1,0:T(8,128)(2,1)S(1)} %slice_bitcast_fusion), channel_id=1, source_target_pairs={{0,16},{16,0},{1,17},{17,1},{2,18},{18,2},{3,19},{19,3},{4,20},{20... | collective-permute-start | bytes 1966088 | tf_op jit(solution)/shard_map/ppermute | solution.py:206
  13.5 1.6 %collective-permute-done.5 = bf16[18,16,128]{2,1,0:T(8,128)(2,1)S(1)} collective-permute-done((bf16[18,16,128]{2,1,0:T(8,128)(2,1)S(1)}, bf16[18,16,128]{2,1,0:T(8,128)(2,1)S(1)}, u32[]{:S(2)}, u32[]{:S(2)}) %collective-permute-start.5) | collective-permute-done | bytes 73760 | tf_op jit(solution)/shard_map/ppermute | solution.py:200
  15.1 0.4 collective-permute-done.4
  15.7 2.6 %collective-permute-start.7 = (bf16[24,16,128]{2,1,0:T(8,128)(2,1)S(1)}, bf16[24,16,128]{2,1,0:T(8,128)(2,1)S(1)}, u32[]{:S(2)}, u32[]{:S(2)}) collective-permute-start(bf16[24,16,128]{2,1,0:T(8,128)(2,1)S(1)} %constant_dynamic-update-slice_fusion.ins__sent__), channel_id=1, source_target_pairs={{0,8},{1,9},{2,10},{3,11},{4,12},{5,13},{6,14},{7,15},{8,0},{9,1},... | collective-permute-start | bytes 294920 | tf_op jit(solution)/shard_map/ppermute | solution.py:200
  18.3 1.3 %shard_map.65.ins__inverse__ = f32[32,8,128]{2,1,0:T(8,128)S(1)} custom-call(s32[8,128]{1,0:T(8,128)S(1)} %pad.4.ins__index___0_.ins__next_index___0_, s32[8,128]{1,0:T(8,128)S(1)} %collective-permute-done.2.ins__index___1_.ins__next_index___1_, bf16[32,128,128]{2,1,0:T(8,128)(2,1)S(1)} %bitcast.62, ...), custom_call_target="tpu_custom_call" | custom-call | tf_op jit(solution)/shard_map/pallas_call | solution.py:158
  19.6 3.0 %collective-permute-done.7.ins__got___0_ = bf16[24,16,128]{2,1,0:T(8,128)(2,1)S(1)} collective-permute-done((bf16[24,16,128]{2,1,0:T(8,128)(2,1)S(1)}, bf16[24,16,128]{2,1,0:T(8,128)(2,1)S(1)}, u32[]{:S(2)}, u32[]{:S(2)}) %collective-permute-start.7) | collective-permute-done | bytes 98336 | tf_op jit(solution)/shard_map/ppermute | solution.py:200
  22.6 1.3 %shard_map.66 = (bf16[16,16,128]{2,1,0:T(8,128)(2,1)S(1)}, f32[2,16,2048]{2,1,0:T(8,128)S(1)}) custom-call(bf16[24,16,128]{2,1,0:T(8,128)(2,1)S(1)} %collective-permute-done.7.ins__got___0_, f32[16,2048]{1,0:T(8,128)S(1)} %get-tuple-element.60.ins__held___0_, f32[16,2048]{1,0:T(8,128)S(1)} %collective-permute-done.1.ins__held___1_, ...), custom_call_target="tpu_custom_call" | custom-call | tf_op jit(solution)/shard_map/pallas_call | solution.py:158
  23.9 1.5 %collective-permute-start.8 = (f32[2,16,2048]{2,1,0:T(8,128)S(1)}, f32[2,16,2048]{2,1,0:T(8,128)S(1)}, u32[]{:S(2)}, u32[]{:S(2)}) collective-permute-start(f32[2,16,2048]{2,1,0:T(8,128)S(1)} %get-tuple-element.29), channel_id=1, source_target_pairs={{0,16},{16,0},{1,17},{17,1},{2,18},{18,2},{3,19},{19,3},{4,20},{20... | collective-permute-start | bytes 786440 | tf_op jit(solution)/shard_map/ppermute | solution.py:206
  25.5 0.5 collective-permute-start.9
  26.0 7.3 %collective-permute-done.9.ins__index___0_ = s32[8,128]{1,0:T(8,128)S(1)} collective-permute-done((s32[8,128]{1,0:T(8,128)S(1)}, s32[8,128]{1,0:T(8,128)S(1)}, u32[]{:S(2)}, u32[]{:S(2)}) %collective-permute-start.9) | collective-permute-done | bytes 4128 | tf_op jit(solution)/shard_map/ppermute | solution.py:206
  33.3 1.6 %shard_map.67 = (bf16[18,16,128]{2,1,0:T(8,128)(2,1)S(1)}, f32[16,16,128]{2,1,0:T(8,128)S(1)}) custom-call(bf16[2,16,128]{2,1,0:T(8,128)(2,1)S(1)} %get-tuple-element.62.ins__dealt__, f32[2,16,2048]{2,1,0:T(8,128)S(1)} %collective-permute-done.8.ins__held__, s32[8,128]{1,0:T(8,128)S(1)} %pad.4.ins__index___0_.ins__next_index___0_, ...), custom_call_target="tpu_custom_call" | custom-call | tf_op jit(solution)/shard_map/pallas_call | solution.py:158
  34.9 2.6 %collective-permute-start.13 = (bf16[18,16,128]{2,1,0:T(8,128)(2,1)S(1)}, bf16[18,16,128]{2,1,0:T(8,128)(2,1)S(1)}, u32[]{:S(2)}, u32[]{:S(2)}) collective-permute-start(bf16[18,16,128]{2,1,0:T(8,128)(2,1)S(1)} %get-tuple-element.34), channel_id=1, source_target_pairs={{0,6},{1,7},{2,4},{3,5},{4,2},{5,3},{6,0},{7,1},{8,14},{9,15},{10,... | collective-permute-start | bytes 221192 | tf_op jit(solution)/shard_map/ppermute | solution.py:200
  38.0 0.5 collective-permute-start.11
  38.5 1.5 %collective-permute-start.17 = (bf16[12,128,128]{2,1,0:T(8,128)(2,1)S(1)}, bf16[12,128,128]{2,1,0:T(8,128)(2,1)S(1)}, u32[]{:S(2)}, u32[]{:S(2)}) collective-permute-start(bf16[12,128,128]{2,1,0:T(8,128)(2,1)S(1)} %slice_bitcast_fusion.1), channel_id=1, source_target_pairs={{0,16},{16,0},{1,17},{17,1},{2,18},{18,2},{3,19},{19,3},{4,20},{20... | collective-permute-start | bytes 1179656 | tf_op jit(solution)/shard_map/ppermute | solution.py:206
  40.3 1.6 %collective-permute-done.12 = bf16[18,16,128]{2,1,0:T(8,128)(2,1)S(1)} collective-permute-done((bf16[18,16,128]{2,1,0:T(8,128)(2,1)S(1)}, bf16[18,16,128]{2,1,0:T(8,128)(2,1)S(1)}, u32[]{:S(2)}, u32[]{:S(2)}) %collective-permute-start.12) | collective-permute-done | bytes 73760 | tf_op jit(solution)/shard_map/ppermute | solution.py:200
  42.5 2.7 %collective-permute-start.14 = (bf16[24,16,128]{2,1,0:T(8,128)(2,1)S(1)}, bf16[24,16,128]{2,1,0:T(8,128)(2,1)S(1)}, u32[]{:S(2)}, u32[]{:S(2)}) collective-permute-start(bf16[24,16,128]{2,1,0:T(8,128)(2,1)S(1)} %constant_dynamic-update-slice_fusion.4.ins__sent__), channel_id=1, source_target_pairs={{0,8},{1,9},{2,10},{3,11},{4,12},{5,13},{6,14},{7,15},{8,0},{9,1},... | collective-permute-start | bytes 294920 | tf_op jit(solution)/shard_map/ppermute | solution.py:200
  45.2 2.9 %collective-permute-done.14.ins__got___0_ = bf16[24,16,128]{2,1,0:T(8,128)(2,1)S(1)} collective-permute-done((bf16[24,16,128]{2,1,0:T(8,128)(2,1)S(1)}, bf16[24,16,128]{2,1,0:T(8,128)(2,1)S(1)}, u32[]{:S(2)}, u32[]{:S(2)}) %collective-permute-start.14) | collective-permute-done | bytes 98336 | tf_op jit(solution)/shard_map/ppermute | solution.py:200
  48.1 0.5 collective-permute-start.16
  48.6 1.3 %shard_map.68 = (bf16[16,16,128]{2,1,0:T(8,128)(2,1)S(1)}, f32[2,16,2048]{2,1,0:T(8,128)S(1)}) custom-call(bf16[24,16,128]{2,1,0:T(8,128)(2,1)S(1)} %collective-permute-done.14.ins__got___0_, f32[2,16,2048]{2,1,0:T(8,128)S(1)} %collective-permute-done.8.ins__held__, s32[8,128]{1,0:T(8,128)S(1)} %pad.4.ins__index___0_.ins__next_index___0_, ...), custom_call_target="tpu_custom_call" | custom-call | tf_op jit(solution)/shard_map/pallas_call | solution.py:158
  50.0 1.6 %shard_map.69 = (bf16[16,16,128]{2,1,0:T(8,128)(2,1)S(1)}, f32[16,16,128]{2,1,0:T(8,128)S(1)}) custom-call(f32[2,16,2048]{2,1,0:T(8,128)S(1)} %get-tuple-element.37.ins__held__, s32[8,128]{1,0:T(8,128)S(1)} %collective-permute-done.9.ins__index___0_, s32[8,128]{1,0:T(8,128)S(1)} %collective-permute-done.16.ins__index___1_, ...), custom_call_target="tpu_custom_call" | custom-call | tf_op jit(solution)/shard_map/pallas_call | solution.py:158
  51.6 2.1 %collective-permute-start.22 = (bf16[16,16,128]{2,1,0:T(8,128)(2,1)S(1)}, bf16[16,16,128]{2,1,0:T(8,128)(2,1)S(1)}, u32[]{:S(2)}, u32[]{:S(2)}) collective-permute-start(bf16[16,16,128]{2,1,0:T(8,128)(2,1)S(1)} %get-tuple-element.45), channel_id=1, source_target_pairs={{0,6},{1,7},{2,4},{3,5},{4,2},{5,3},{6,0},{7,1},{8,14},{9,15},{10,... | collective-permute-start | bytes 196616 | tf_op jit(solution)/shard_map/ppermute | solution.py:200
  53.7 1.4 %collective-permute-start.21 = (bf16[16,16,128]{2,1,0:T(8,128)(2,1)S(1)}, bf16[16,16,128]{2,1,0:T(8,128)(2,1)S(1)}, u32[]{:S(2)}, u32[]{:S(2)}) collective-permute-start(bf16[16,16,128]{2,1,0:T(8,128)(2,1)S(1)} %get-tuple-element.45), channel_id=1, source_target_pairs={{0,4},{1,5},{2,6},{3,7},{4,0},{5,1},{6,2},{7,3},{8,12},{9,13},{10,... | collective-permute-start | bytes 196616 | tf_op jit(solution)/shard_map/ppermute | solution.py:200
  55.2 1.5 %collective-permute-start.15 = (bf16[16,16,128]{2,1,0:T(8,128)(2,1)S(1)}, bf16[16,16,128]{2,1,0:T(8,128)(2,1)S(1)}, u32[]{:S(2)}, u32[]{:S(2)}) collective-permute-start(bf16[16,16,128]{2,1,0:T(8,128)(2,1)S(1)} %get-tuple-element.36), channel_id=1, source_target_pairs={{0,16},{16,0},{1,17},{17,1},{2,18},{18,2},{3,19},{19,3},{4,20},{20... | collective-permute-start | bytes 196616 | tf_op jit(solution)/shard_map/ppermute | solution.py:206
  56.7 0.5 collective-permute-done.22
  57.2 1.3 %collective-permute-done.21 = bf16[16,16,128]{2,1,0:T(8,128)(2,1)S(1)} collective-permute-done((bf16[16,16,128]{2,1,0:T(8,128)(2,1)S(1)}, bf16[16,16,128]{2,1,0:T(8,128)(2,1)S(1)}, u32[]{:S(2)}, u32[]{:S(2)}) %collective-permute-start.21) | collective-permute-done | bytes 65568 | tf_op jit(solution)/shard_map/ppermute | solution.py:200
  58.4 0.9 %collective-permute-done.20 = bf16[16,16,128]{2,1,0:T(8,128)(2,1)S(1)} collective-permute-done((bf16[16,16,128]{2,1,0:T(8,128)(2,1)S(1)}, bf16[16,16,128]{2,1,0:T(8,128)(2,1)S(1)}, u32[]{:S(2)}, u32[]{:S(2)}) %collective-permute-start.20) | collective-permute-done | bytes 65568 | tf_op jit(solution)/shard_map/ppermute | solution.py:200
  59.4 2.1 %collective-permute-start.23 = (bf16[16,16,128]{2,1,0:T(8,128)(2,1)S(1)}, bf16[16,16,128]{2,1,0:T(8,128)(2,1)S(1)}, u32[]{:S(2)}, u32[]{:S(2)}) collective-permute-start(bf16[16,16,128]{2,1,0:T(8,128)(2,1)S(1)} %get-tuple-element.51), channel_id=1, source_target_pairs={{0,8},{1,9},{2,10},{3,11},{4,12},{5,13},{6,14},{7,15},{8,0},{9,1},... | collective-permute-start | bytes 196616 | tf_op jit(solution)/shard_map/ppermute | solution.py:200
  61.5 1.3 %shard_map.70.ins__inverse__ = f32[32,8,128]{2,1,0:T(8,128)S(1)} custom-call(s32[8,128]{1,0:T(8,128)S(1)} %collective-permute-done.9.ins__index___0_, s32[8,128]{1,0:T(8,128)S(1)} %collective-permute-done.16.ins__index___1_, bf16[20,128,128]{2,1,0:T(8,128)(2,1)S(1)} %collective-permute-done.10.ins__tiles___0__0_, ...), custom_call_target="tpu_custom_call" | custom-call | tf_op jit(solution)/shard_map/pallas_call | solution.py:158
  62.8 2.6 %collective-permute-done.23.ins__got___0_ = bf16[16,16,128]{2,1,0:T(8,128)(2,1)S(1)} collective-permute-done((bf16[16,16,128]{2,1,0:T(8,128)(2,1)S(1)}, bf16[16,16,128]{2,1,0:T(8,128)(2,1)S(1)}, u32[]{:S(2)}, u32[]{:S(2)}) %collective-permute-start.23) | collective-permute-done | bytes 65568 | tf_op jit(solution)/shard_map/ppermute | solution.py:200
  65.3 2.4 %shard_map.71 = (f32[2,16,2048]{2,1,0:T(8,128)S(1)}, bf16[16,16,128]{2,1,0:T(8,128)(2,1)S(1)}, f32[16,16,128]{2,1,0:T(8,128)S(1)}) custom-call(bf16[16,16,128]{2,1,0:T(8,128)(2,1)S(1)} %collective-permute-done.15.ins__counts__, bf16[16,16,128]{2,1,0:T(8,128)(2,1)S(1)} %collective-permute-done.23.ins__got___0_, ...), custom_call_target="tpu_custom_call" | custom-call | tf_op jit(solution)/shard_map/pallas_call | solution.py:158
  67.7 1.1 %collective-permute-start.26 = (bf16[16,16,128]{2,1,0:T(8,128)(2,1)S(1)}, bf16[16,16,128]{2,1,0:T(8,128)(2,1)S(1)}, u32[]{:S(2)}, u32[]{:S(2)}) collective-permute-start(bf16[16,16,128]{2,1,0:T(8,128)(2,1)S(1)} %get-tuple-element.47), channel_id=1, source_target_pairs={{0,6},{1,7},{2,4},{3,5},{4,2},{5,3},{6,0},{7,1},{8,14},{9,15},{10,... | collective-permute-start | bytes 196616 | tf_op jit(solution)/shard_map/ppermute | solution.py:200
  68.9 0.7 collective-permute-start.25
  69.5 1.8 %collective-permute-start.24 = (bf16[16,16,128]{2,1,0:T(8,128)(2,1)S(1)}, bf16[16,16,128]{2,1,0:T(8,128)(2,1)S(1)}, u32[]{:S(2)}, u32[]{:S(2)}) collective-permute-start(bf16[16,16,128]{2,1,0:T(8,128)(2,1)S(1)} %get-tuple-element.47), channel_id=1, source_target_pairs={{0,2},{1,3},{2,0},{3,1},{4,6},{5,7},{6,4},{7,5},{8,10},{9,11},{10,... | collective-permute-start | bytes 196616 | tf_op jit(solution)/shard_map/ppermute | solution.py:200
  71.3 1.7 %collective-permute-done.26 = bf16[16,16,128]{2,1,0:T(8,128)(2,1)S(1)} collective-permute-done((bf16[16,16,128]{2,1,0:T(8,128)(2,1)S(1)}, bf16[16,16,128]{2,1,0:T(8,128)(2,1)S(1)}, u32[]{:S(2)}, u32[]{:S(2)}) %collective-permute-start.26) | collective-permute-done | bytes 65568 | tf_op jit(solution)/shard_map/ppermute | solution.py:200
  73.1 0.7 collective-permute-done.24
  73.8 3.1 %collective-permute-start.27 = (bf16[16,16,128]{2,1,0:T(8,128)(2,1)S(1)}, bf16[16,16,128]{2,1,0:T(8,128)(2,1)S(1)}, u32[]{:S(2)}, u32[]{:S(2)}) collective-permute-start(bf16[16,16,128]{2,1,0:T(8,128)(2,1)S(1)} %get-tuple-element.49), channel_id=1, source_target_pairs={{0,8},{1,9},{2,10},{3,11},{4,12},{5,13},{6,14},{7,15},{8,0},{9,1},... | collective-permute-start | bytes 196616 | tf_op jit(solution)/shard_map/ppermute | solution.py:200
  76.9 2.2 %collective-permute-done.27.ins__got___0_ = bf16[16,16,128]{2,1,0:T(8,128)(2,1)S(1)} collective-permute-done((bf16[16,16,128]{2,1,0:T(8,128)(2,1)S(1)}, bf16[16,16,128]{2,1,0:T(8,128)(2,1)S(1)}, u32[]{:S(2)}, u32[]{:S(2)}) %collective-permute-start.27) | collective-permute-done | bytes 65568 | tf_op jit(solution)/shard_map/ppermute | solution.py:200
  79.1 1.3 %shard_map.72 = f32[2,16,2048]{2,1,0:T(8,128)S(1)} custom-call(bf16[16,16,128]{2,1,0:T(8,128)(2,1)S(1)} %get-tuple-element.35.ins__counts__, bf16[16,16,128]{2,1,0:T(8,128)(2,1)S(1)} %collective-permute-done.27.ins__got___0_, f32[2,16,2048]{2,1,0:T(8,128)S(1)} %get-tuple-element.48.ins__held__, s32[8,128]{1,0:T(8,128)S(1)} %pad.4.ins__index___0_.ins__next_index___0_, ...), custom_call_target="tpu_custom_call" | custom-call | tf_op jit(solution)/shard_map/pallas_call | solution.py:158
  80.6 1.3 %collective-permute-done.28 = f32[16,2048]{1,0:T(8,128)S(1)} collective-permute-done((f32[16,2048]{1,0:T(8,128)S(1)}, f32[16,2048]{1,0:T(8,128)S(1)}, u32[]{:S(2)}, u32[]{:S(2)}) %collective-permute-start.28) | collective-permute-done | bytes 131104 | tf_op jit(solution)/shard_map/ppermute | solution.py:196
  81.9 0.7 maximum_select_fusion
  (62 shorter events, 3.0 us)
Async XLA Ops:
  0.0 5.0 %collective-permute-start.3 = (bf16[32,128,128]{2,1,0:T(8,128)(2,1)}, bf16[32,128,128]{2,1,0:T(8,128)(2,1)S(1)}, u32[]{:S(2)}, u32[]{:S(2)}) collective-permute-start(bf16[32,128,128]{2,1,0:T(8,128)(2,1)} %bitcast.60), channel_id=1, source_target_pairs={{0,1},{1,0},{2,3},{3,2},{4,5},{5,4},{6,7},{7,6},{8,9},{9,8},{10,11... | collective-permute-start | bytes 3145736 | tf_op jit(solution)/shard_map/ppermute | solution.py:196
  0.5 1.6 %copy-start.1 = (s32[1,64,128]{2,1,0:T(8,128)S(1)}, s32[1,64,128]{2,1,0:T(8,128)}, u32[]{:S(2)}) copy-start(s32[1,64,128]{2,1,0:T(8,128)} %param.11) | copy-start | bytes 98308
  1.2 0.7 copy-start.2
  1.2 0.7 copy-start.3
  1.9 3.1 %collective-permute-start.2 = (s32[8,128]{1,0:T(8,128)S(1)}, s32[8,128]{1,0:T(8,128)S(1)}, u32[]{:S(2)}, u32[]{:S(2)}) collective-permute-start(s32[8,128]{1,0:T(8,128)S(1)} %pad.4.ins__index___0_.ins__next_index___0_), channel_id=1, source_target_pairs={{0,1},{1,0},{2,3},{3,2},{4,5},{5,4},{6,7},{7,6},{8,9},{9,8},{10,11... | collective-permute-start | bytes 12296 | tf_op jit(solution)/shard_map/ppermute | solution.py:196
  2.0 3.0 %copy-start = (bf16[1,32,128,128]{3,2,1,0:T(8,128)(2,1)S(1)}, bf16[1,32,128,128]{3,2,1,0:T(8,128)(2,1)}, u32[]{:S(2)}) copy-start(bf16[1,32,128,128]{3,2,1,0:T(8,128)(2,1)} %param.7) | copy-start | bytes 3145732
  2.1 2.9 %collective-permute-start = (bf16[1,2,16,128]{3,2,0,1:T(8,128)(2,1)S(1)}, bf16[1,2,16,128]{3,2,0,1:T(8,128)(2,1)S(1)}, u32[]{:S(2)}, u32[]{:S(2)}) collective-permute-start(bf16[1,2,16,128]{3,2,0,1:T(8,128)(2,1)S(1)} %get-tuple-element.64), channel_id=1, source_target_pairs={{0,1},{1,0},{2,3},{3,2},{4,5},{5,4},{6,7},{7,6},{8,9},{9,8},{10,11... | collective-permute-start | bytes 24584 | tf_op jit(solution)/shard_map/ppermute | solution.py:196
  3.6 1.5 %collective-permute-start.1 = (f32[16,2048]{1,0:T(8,128)S(1)}, f32[16,2048]{1,0:T(8,128)S(1)}, u32[]{:S(2)}, u32[]{:S(2)}) collective-permute-start(f32[16,2048]{1,0:T(8,128)S(1)} %get-tuple-element.59), channel_id=1, source_target_pairs={{0,1},{1,0},{2,3},{3,2},{4,5},{5,4},{6,7},{7,6},{8,9},{9,8},{10,11... | collective-permute-start | bytes 393224 | tf_op jit(solution)/shard_map/ppermute | solution.py:196
  6.8 6.7 %collective-permute-start.6 = (bf16[18,16,128]{2,1,0:T(8,128)(2,1)S(1)}, bf16[18,16,128]{2,1,0:T(8,128)(2,1)S(1)}, u32[]{:S(2)}, u32[]{:S(2)}) collective-permute-start(bf16[18,16,128]{2,1,0:T(8,128)(2,1)S(1)} %get-tuple-element.28), channel_id=1, source_target_pairs={{0,6},{1,7},{2,4},{3,5},{4,2},{5,3},{6,0},{7,1},{8,14},{9,15},{10,... | collective-permute-start | bytes 221192 | tf_op jit(solution)/shard_map/ppermute | solution.py:200
  10.7 4.4 %collective-permute-start.5 = (bf16[18,16,128]{2,1,0:T(8,128)(2,1)S(1)}, bf16[18,16,128]{2,1,0:T(8,128)(2,1)S(1)}, u32[]{:S(2)}, u32[]{:S(2)}) collective-permute-start(bf16[18,16,128]{2,1,0:T(8,128)(2,1)S(1)} %get-tuple-element.28), channel_id=1, source_target_pairs={{0,4},{1,5},{2,6},{3,7},{4,0},{5,1},{6,2},{7,3},{8,12},{9,13},{10,... | collective-permute-start | bytes 221192 | tf_op jit(solution)/shard_map/ppermute | solution.py:200
  11.2 4.4 %collective-permute-start.4 = (bf16[18,16,128]{2,1,0:T(8,128)(2,1)S(1)}, bf16[18,16,128]{2,1,0:T(8,128)(2,1)S(1)}, u32[]{:S(2)}, u32[]{:S(2)}) collective-permute-start(bf16[18,16,128]{2,1,0:T(8,128)(2,1)S(1)} %get-tuple-element.28), channel_id=1, source_target_pairs={{0,2},{1,3},{2,0},{3,1},{4,6},{5,7},{6,4},{7,5},{8,10},{9,11},{10,... | collective-permute-start | bytes 221192 | tf_op jit(solution)/shard_map/ppermute | solution.py:200
  11.4 21.9 %collective-permute-start.10 = (bf16[20,128,128]{2,1,0:T(8,128)(2,1)S(1)}, bf16[20,128,128]{2,1,0:T(8,128)(2,1)S(1)}, u32[]{:S(2)}, u32[]{:S(2)}) collective-permute-start(bf16[20,128,128]{2,1,0:T(8,128)(2,1)S(1)} %slice_bitcast_fusion), channel_id=1, source_target_pairs={{0,16},{16,0},{1,17},{17,1},{2,18},{18,2},{3,19},{19,3},{4,20},{20... | collective-permute-start | bytes 1966088 | tf_op jit(solution)/shard_map/ppermute | solution.py:206
  15.7 6.9 %collective-permute-start.7 = (bf16[24,16,128]{2,1,0:T(8,128)(2,1)S(1)}, bf16[24,16,128]{2,1,0:T(8,128)(2,1)S(1)}, u32[]{:S(2)}, u32[]{:S(2)}) collective-permute-start(bf16[24,16,128]{2,1,0:T(8,128)(2,1)S(1)} %constant_dynamic-update-slice_fusion.ins__sent__), channel_id=1, source_target_pairs={{0,8},{1,9},{2,10},{3,11},{4,12},{5,13},{6,14},{7,15},{8,0},{9,1},... | collective-permute-start | bytes 294920 | tf_op jit(solution)/shard_map/ppermute | solution.py:200
  23.9 9.4 %collective-permute-start.8 = (f32[2,16,2048]{2,1,0:T(8,128)S(1)}, f32[2,16,2048]{2,1,0:T(8,128)S(1)}, u32[]{:S(2)}, u32[]{:S(2)}) collective-permute-start(f32[2,16,2048]{2,1,0:T(8,128)S(1)} %get-tuple-element.29), channel_id=1, source_target_pairs={{0,16},{16,0},{1,17},{17,1},{2,18},{18,2},{3,19},{19,3},{4,20},{20... | collective-permute-start | bytes 786440 | tf_op jit(solution)/shard_map/ppermute | solution.py:206
  25.5 7.9 %collective-permute-start.9 = (s32[8,128]{1,0:T(8,128)S(1)}, s32[8,128]{1,0:T(8,128)S(1)}, u32[]{:S(2)}, u32[]{:S(2)}) collective-permute-start(s32[8,128]{1,0:T(8,128)S(1)} %pad.4.ins__index___0_.ins__next_index___0_), channel_id=1, source_target_pairs={{0,16},{16,0},{1,17},{17,1},{2,18},{18,2},{3,19},{19,3},{4,20},{20... | collective-permute-start | bytes 12296 | tf_op jit(solution)/shard_map/ppermute | solution.py:206
  34.9 5.4 %collective-permute-start.13 = (bf16[18,16,128]{2,1,0:T(8,128)(2,1)S(1)}, bf16[18,16,128]{2,1,0:T(8,128)(2,1)S(1)}, u32[]{:S(2)}, u32[]{:S(2)}) collective-permute-start(bf16[18,16,128]{2,1,0:T(8,128)(2,1)S(1)} %get-tuple-element.34), channel_id=1, source_target_pairs={{0,6},{1,7},{2,4},{3,5},{4,2},{5,3},{6,0},{7,1},{8,14},{9,15},{10,... | collective-permute-start | bytes 221192 | tf_op jit(solution)/shard_map/ppermute | solution.py:200
  37.6 4.4 %collective-permute-start.12 = (bf16[18,16,128]{2,1,0:T(8,128)(2,1)S(1)}, bf16[18,16,128]{2,1,0:T(8,128)(2,1)S(1)}, u32[]{:S(2)}, u32[]{:S(2)}) collective-permute-start(bf16[18,16,128]{2,1,0:T(8,128)(2,1)S(1)} %get-tuple-element.34), channel_id=1, source_target_pairs={{0,4},{1,5},{2,6},{3,7},{4,0},{5,1},{6,2},{7,3},{8,12},{9,13},{10,... | collective-permute-start | bytes 221192 | tf_op jit(solution)/shard_map/ppermute | solution.py:200
  38.0 4.4 %collective-permute-start.11 = (bf16[18,16,128]{2,1,0:T(8,128)(2,1)S(1)}, bf16[18,16,128]{2,1,0:T(8,128)(2,1)S(1)}, u32[]{:S(2)}, u32[]{:S(2)}) collective-permute-start(bf16[18,16,128]{2,1,0:T(8,128)(2,1)S(1)} %get-tuple-element.34), channel_id=1, source_target_pairs={{0,2},{1,3},{2,0},{3,1},{4,6},{5,7},{6,4},{7,5},{8,10},{9,11},{10,... | collective-permute-start | bytes 221192 | tf_op jit(solution)/shard_map/ppermute | solution.py:200
  38.5 9.6 %collective-permute-start.17 = (bf16[12,128,128]{2,1,0:T(8,128)(2,1)S(1)}, bf16[12,128,128]{2,1,0:T(8,128)(2,1)S(1)}, u32[]{:S(2)}, u32[]{:S(2)}) collective-permute-start(bf16[12,128,128]{2,1,0:T(8,128)(2,1)S(1)} %slice_bitcast_fusion.1), channel_id=1, source_target_pairs={{0,16},{16,0},{1,17},{17,1},{2,18},{18,2},{3,19},{19,3},{4,20},{20... | collective-permute-start | bytes 1179656 | tf_op jit(solution)/shard_map/ppermute | solution.py:206
  40.0 10.0 %collective-permute-start.18 = (bf16[20,128,128]{2,1,0:T(8,128)(2,1)S(1)}, bf16[20,128,128]{2,1,0:T(8,128)(2,1)S(1)}, u32[]{:S(2)}, u32[]{:S(2)}) collective-permute-start(bf16[20,128,128]{2,1,0:T(8,128)(2,1)S(1)} %collective-permute-done.10.ins__tiles___0__0_), channel_id=1, source_target_pairs={{0,1},{1,0},{2,3},{3,2},{4,5},{5,4},{6,7},{7,6},{8,9},{9,8},{10,11... | collective-permute-start | bytes 1966088 | tf_op jit(solution)/shard_map/ppermute | solution.py:196
  42.5 5.6 %collective-permute-start.14 = (bf16[24,16,128]{2,1,0:T(8,128)(2,1)S(1)}, bf16[24,16,128]{2,1,0:T(8,128)(2,1)S(1)}, u32[]{:S(2)}, u32[]{:S(2)}) collective-permute-start(bf16[24,16,128]{2,1,0:T(8,128)(2,1)S(1)} %constant_dynamic-update-slice_fusion.4.ins__sent__), channel_id=1, source_target_pairs={{0,8},{1,9},{2,10},{3,11},{4,12},{5,13},{6,14},{7,15},{8,0},{9,1},... | collective-permute-start | bytes 294920 | tf_op jit(solution)/shard_map/ppermute | solution.py:200
  48.1 1.9 %collective-permute-start.19 = (bf16[12,128,128]{2,1,0:T(8,128)(2,1)S(1)}, bf16[12,128,128]{2,1,0:T(8,128)(2,1)S(1)}, u32[]{:S(2)}, u32[]{:S(2)}) collective-permute-start(bf16[12,128,128]{2,1,0:T(8,128)(2,1)S(1)} %collective-permute-done.17.ins__tiles___0__1_), channel_id=1, source_target_pairs={{0,1},{1,0},{2,3},{3,2},{4,5},{5,4},{6,7},{7,6},{8,9},{9,8},{10,11... | collective-permute-start | bytes 1179656 | tf_op jit(solution)/shard_map/ppermute | solution.py:196
  48.1 1.9 %collective-permute-start.16 = (s32[8,128]{1,0:T(8,128)S(1)}, s32[8,128]{1,0:T(8,128)S(1)}, u32[]{:S(2)}, u32[]{:S(2)}) collective-permute-start(s32[8,128]{1,0:T(8,128)S(1)} %collective-permute-done.9.ins__index___0_), channel_id=1, source_target_pairs={{0,1},{1,0},{2,3},{3,2},{4,5},{5,4},{6,7},{7,6},{8,9},{9,8},{10,11... | collective-permute-start | bytes 12296 | tf_op jit(solution)/shard_map/ppermute | solution.py:196
  51.6 5.5 %collective-permute-start.22 = (bf16[16,16,128]{2,1,0:T(8,128)(2,1)S(1)}, bf16[16,16,128]{2,1,0:T(8,128)(2,1)S(1)}, u32[]{:S(2)}, u32[]{:S(2)}) collective-permute-start(bf16[16,16,128]{2,1,0:T(8,128)(2,1)S(1)} %get-tuple-element.45), channel_id=1, source_target_pairs={{0,6},{1,7},{2,4},{3,5},{4,2},{5,3},{6,0},{7,1},{8,14},{9,15},{10,... | collective-permute-start | bytes 196616 | tf_op jit(solution)/shard_map/ppermute | solution.py:200
  53.7 4.7 %collective-permute-start.21 = (bf16[16,16,128]{2,1,0:T(8,128)(2,1)S(1)}, bf16[16,16,128]{2,1,0:T(8,128)(2,1)S(1)}, u32[]{:S(2)}, u32[]{:S(2)}) collective-permute-start(bf16[16,16,128]{2,1,0:T(8,128)(2,1)S(1)} %get-tuple-element.45), channel_id=1, source_target_pairs={{0,4},{1,5},{2,6},{3,7},{4,0},{5,1},{6,2},{7,3},{8,12},{9,13},{10,... | collective-permute-start | bytes 196616 | tf_op jit(solution)/shard_map/ppermute | solution.py:200
  55.1 4.3 %collective-permute-start.20 = (bf16[16,16,128]{2,1,0:T(8,128)(2,1)S(1)}, bf16[16,16,128]{2,1,0:T(8,128)(2,1)S(1)}, u32[]{:S(2)}, u32[]{:S(2)}) collective-permute-start(bf16[16,16,128]{2,1,0:T(8,128)(2,1)S(1)} %get-tuple-element.45), channel_id=1, source_target_pairs={{0,2},{1,3},{2,0},{3,1},{4,6},{5,7},{6,4},{7,5},{8,10},{9,11},{10,... | collective-permute-start | bytes 196616 | tf_op jit(solution)/shard_map/ppermute | solution.py:200
  55.2 7.5 %collective-permute-start.15 = (bf16[16,16,128]{2,1,0:T(8,128)(2,1)S(1)}, bf16[16,16,128]{2,1,0:T(8,128)(2,1)S(1)}, u32[]{:S(2)}, u32[]{:S(2)}) collective-permute-start(bf16[16,16,128]{2,1,0:T(8,128)(2,1)S(1)} %get-tuple-element.36), channel_id=1, source_target_pairs={{0,16},{16,0},{1,17},{17,1},{2,18},{18,2},{3,19},{19,3},{4,20},{20... | collective-permute-start | bytes 196616 | tf_op jit(solution)/shard_map/ppermute | solution.py:206
  59.4 5.9 %collective-permute-start.23 = (bf16[16,16,128]{2,1,0:T(8,128)(2,1)S(1)}, bf16[16,16,128]{2,1,0:T(8,128)(2,1)S(1)}, u32[]{:S(2)}, u32[]{:S(2)}) collective-permute-start(bf16[16,16,128]{2,1,0:T(8,128)(2,1)S(1)} %get-tuple-element.51), channel_id=1, source_target_pairs={{0,8},{1,9},{2,10},{3,11},{4,12},{5,13},{6,14},{7,15},{8,0},{9,1},... | collective-permute-start | bytes 196616 | tf_op jit(solution)/shard_map/ppermute | solution.py:200
  67.7 5.2 %collective-permute-start.26 = (bf16[16,16,128]{2,1,0:T(8,128)(2,1)S(1)}, bf16[16,16,128]{2,1,0:T(8,128)(2,1)S(1)}, u32[]{:S(2)}, u32[]{:S(2)}) collective-permute-start(bf16[16,16,128]{2,1,0:T(8,128)(2,1)S(1)} %get-tuple-element.47), channel_id=1, source_target_pairs={{0,6},{1,7},{2,4},{3,5},{4,2},{5,3},{6,0},{7,1},{8,14},{9,15},{10,... | collective-permute-start | bytes 196616 | tf_op jit(solution)/shard_map/ppermute | solution.py:200
  68.9 4.3 %collective-permute-start.25 = (bf16[16,16,128]{2,1,0:T(8,128)(2,1)S(1)}, bf16[16,16,128]{2,1,0:T(8,128)(2,1)S(1)}, u32[]{:S(2)}, u32[]{:S(2)}) collective-permute-start(bf16[16,16,128]{2,1,0:T(8,128)(2,1)S(1)} %get-tuple-element.47), channel_id=1, source_target_pairs={{0,4},{1,5},{2,6},{3,7},{4,0},{5,1},{6,2},{7,3},{8,12},{9,13},{10,... | collective-permute-start | bytes 196616 | tf_op jit(solution)/shard_map/ppermute | solution.py:200
  69.5 4.3 %collective-permute-start.24 = (bf16[16,16,128]{2,1,0:T(8,128)(2,1)S(1)}, bf16[16,16,128]{2,1,0:T(8,128)(2,1)S(1)}, u32[]{:S(2)}, u32[]{:S(2)}) collective-permute-start(bf16[16,16,128]{2,1,0:T(8,128)(2,1)S(1)} %get-tuple-element.47), channel_id=1, source_target_pairs={{0,2},{1,3},{2,0},{3,1},{4,6},{5,7},{6,4},{7,5},{8,10},{9,11},{10,... | collective-permute-start | bytes 196616 | tf_op jit(solution)/shard_map/ppermute | solution.py:200
  73.8 5.3 %collective-permute-start.27 = (bf16[16,16,128]{2,1,0:T(8,128)(2,1)S(1)}, bf16[16,16,128]{2,1,0:T(8,128)(2,1)S(1)}, u32[]{:S(2)}, u32[]{:S(2)}) collective-permute-start(bf16[16,16,128]{2,1,0:T(8,128)(2,1)S(1)} %get-tuple-element.49), channel_id=1, source_target_pairs={{0,8},{1,9},{2,10},{3,11},{4,12},{5,13},{6,14},{7,15},{8,0},{9,1},... | collective-permute-start | bytes 196616 | tf_op jit(solution)/shard_map/ppermute | solution.py:200
  80.5 1.4 %collective-permute-start.28 = (f32[16,2048]{1,0:T(8,128)S(1)}, f32[16,2048]{1,0:T(8,128)S(1)}, u32[]{:S(2)}, u32[]{:S(2)}) collective-permute-start(f32[16,2048]{1,0:T(8,128)S(1)} %get-tuple-element.58), channel_id=1, source_target_pairs={{0,1},{1,0},{2,3},{3,2},{4,5},{5,4},{6,7},{7,6},{8,9},{9,8},{10,11... | collective-permute-start | bytes 393224 | tf_op jit(solution)/shard_map/ppermute | solution.py:196

commit v6 on v5

--- a/solution.py
+++ b/solution.py
@@ -65,6 +65,8 @@
     blocks = acc.shape[0] // CORES
     acc[...] = jnp.zeros_like(acc)
     for k in range(CORES):
+        if sets[k] is None:
+            continue
         index_ref, tile_refs = index_refs[k], sets[k]
 
         def body(ts):
@@ -75,30 +77,28 @@
         each_live(index_ref, slots_of(tile_refs), body)
 
 
-def columns(blocks, size):
+def columns(held, size):
     for k in range(CORES):
-        for b in range(blocks):
-            yield k, slice(b * size, (b + 1) * size), k * blocks + b
-
-
-def piece_of(held, k, cols):
-    return held[k][:, cols] if isinstance(held, tuple) else held[k, :, cols]
+        if held[k] is not None:
+            blocks = held[k].shape[1] // size
+            for b in range(blocks):
+                yield k, slice(b * size, (b + 1) * size), k * blocks + b
 
 
 def write_sums(ins, outs, acc):
     blocks = acc.shape[0]
     outs["wide"][...] = acc[...]
-    outs["sent"][:blocks] = acc[...].astype(jnp.bfloat16)
-    if "dealt" in ins:
-        outs["sent"][blocks:] = ins["dealt"][...]
+    if "sent" in outs:
+        outs["sent"][:blocks] = acc[...].astype(jnp.bfloat16)
+        if "dealt" in ins:
+            outs["sent"][blocks:] = ins["dealt"][...]
 
 
 def first_kernel(ins, outs, low, acc, own, arrived):
     copy = pltpu.make_async_copy(ins["own_hbm"], own, arrived)
     copy.start()
-    blocks, size = low.shape[0] // CORES, low.shape[-1]
-    for k, cols, at in columns(blocks, size):
-        low[at] = piece_of(ins["held"], k, cols).astype(jnp.bfloat16)
+    for k, cols, at in columns(ins["held"], low.shape[-1]):
+        low[at] = ins["held"][k][:, cols].astype(jnp.bfloat16)
     acc[...] = jnp.zeros_like(acc)
     project_into(acc, low, ins["index"], (None, ins["tiles"]))
     copy.wait()
@@ -107,10 +107,9 @@
 
 
 def project_kernel(ins, outs, low, acc):
-    blocks, size = low.shape[0] // CORES, low.shape[-1]
-    acc[...] = jnp.zeros_like(acc)
-    for k, cols, at in columns(blocks, size):
-        low[at] = piece_of(ins["held"], k, cols).astype(jnp.bfloat16)
+    acc[...] = ins["begun"][...] if "begun" in ins else jnp.zeros_like(acc)
+    for k, cols, at in columns(ins["held"], low.shape[-1]):
+        low[at] = ins["held"][k][:, cols].astype(jnp.bfloat16)
     project_into(acc, low, ins["index"], ins["tiles"])
     write_sums(ins, outs, acc)
 
@@ -121,8 +120,7 @@
     outs["inverse"][...] = 1.0 / acc[...]
 
 
-def update_kernel(masks, ins, outs, counts, ratios, back, *scratch):
-    blocks, size = back.shape[0] // CORES, back.shape[-1]
+def form_ratios(masks, ins, outs, counts, ratios):
     rays = ratios.shape[0]
     total = ins["wide"][...]
     for got in ins["got"]:
@@ -137,10 +135,20 @@
     if "counts" in outs:
         outs["counts"][...] = counts[...]
     ratios[...] = (counts[...].astype(jnp.float32) / total).astype(jnp.bfloat16)
+    if "ratios" in outs:
+        outs["ratios"][...] = ratios[...]
+
+
+def update_kernel(masks, ins, outs, back, *scratch):
+    if "ratios" in ins:
+        ratios = ins["ratios"]
+    else:
+        counts, ratios, *scratch = scratch
+        form_ratios(masks, ins, outs, counts, ratios)
     back_into(back, lambda ray: ratios[ray], ins["index"], ins["tiles"])
-    for k, cols, at in columns(blocks, size):
-        value = piece_of(ins["held"], k, cols) * back[at] * ins["inverse"][at, :1]
-        outs["held"][k, :, cols] = value
+    for k, cols, at in columns(ins["held"], back.shape[-1]):
+        value = ins["held"][k][:, cols] * back[at] * ins["inverse"][at, :1]
+        outs["held"][k][:, cols] = value
         if "sent" in outs:
             scratch[0][at] = value.astype(jnp.bfloat16)
     if "sent" in outs:
@@ -236,34 +244,36 @@
     known = [None] * ROUNDS
     two = subset_count == 2
     if two:
+        far_tiles = shift(after(own_tiles, (theirs, own_index)))
+    if two:
         moves = [r == 0 for r in range(ROUNDS - 1)]
 
-    scratch_sum = [pltpu.VMEM((both, half, size), bf16), pltpu.VMEM((ray_blocks, half, size), f32)]
-    scratch = [pltpu.VMEM((ray_blocks, half, size), bf16)] * 2 + [pltpu.VMEM((both, half, size), f32)]
+    low_scratch, back_scratch = pltpu.VMEM((both, half, size), bf16), pltpu.VMEM((both, half, size), f32)
+    ray_scratch, sum_scratch = (pltpu.VMEM((ray_blocks, half, size), kind) for kind in (bf16, f32))
+    piece = shaped((half, voxels), f32)
+    summed = shaped((ray_blocks, half, size), f32)
+
+    def only(k, pair):
+        return tuple(value if i == k else None for i, value in enumerate(pair))
 
     def sums(r):
         fresh = known[r] is None
         sent = ray_blocks + fresh * rb_dev * CORES
         return ({"dealt": dealt_of(position - r)} if fresh else {},
-                {"wide": shaped((ray_blocks, half, size), f32), "sent": shaped((sent, half, size), bf16)})
-
-    def project(held, r):
-        extra, outs = sums(r)
-        return call(project_kernel, {"held": held, "index": sets[r][0], "tiles": sets[r][1], **extra},
-                    outs, scratch_sum)
+                {"wide": summed, "sent": shaped((sent, half, size), bf16)})
 
     extra, outs = sums(0)
     out = call(first_kernel, {"held": held, "index": index, "own_hbm": own_tiles, "tiles": tiles[1], **extra},
-               outs, scratch_sum + [pltpu.VMEM(own_tiles.shape, bf16), pltpu.SemaphoreType.DMA])
+               outs, [low_scratch, sum_scratch, pltpu.VMEM(own_tiles.shape, bf16), pltpu.SemaphoreType.DMA])
     for r in range(ROUNDS):
         wide, sent = out["wide"], out["sent"]
         if two and r == 0:
             far_index = shift(after(own_index, sent))
-            far_tiles = [shift(after(own_tiles[:slots * 5 // 8], sent))]
         if two and r == 1:
             far_index = (far_index, swap_cores(after(far_index, sent)))
-            far_swapped = [swap_cores(after(far_tiles[0], sent))]
-            far_tiles.append(shift(after(own_tiles[slots * 5 // 8:], sent)))
+            far_tiles = ((far_tiles,), (swap_cores(after(far_tiles, sent)),))
+            far = (far_index, far_tiles, sensitivity(far_index, far_tiles))
+            sets = [far if later >= 2 and later % 2 == 0 else sets[later] for later in range(ROUNDS)]
         for masks in steps:
             got = [swap_chips(sent, mask) for mask in masks]
             if masks is not steps[-1]:
@@ -279,37 +289,61 @@
                             jnp.stack(ordered), own ^ v, 0, keepdims=False) for v in range(len(ordered))])
                     counted = jnp.concatenate([counted, passed])
                 sent = counted
-        if two and r == 1:
-            far_swapped.append(swap_cores(after(far_tiles[1], tuple(got))))
-            far_tiles = (tuple(far_tiles), tuple(far_swapped))
-            far = (far_index, far_tiles, sensitivity(far_index, far_tiles))
-            sets = [far if later >= 2 and later % 2 == 0 else sets[later] for later in range(ROUNDS)]
-        ins = {"wide": wide, "got": got, "held": held,
-               "index": sets[r][0], "tiles": sets[r][1], "inverse": sets[r][2]}
-        outs = {"held": shaped((CORES, half, voxels), f32)}
+        if two and r == 0:
+            wide, far_index = lax.optimization_barrier((wide, far_index))
+        now_index, now_tiles, now_inverse = sets[r]
+        base = {"index": now_index, "inverse": now_inverse}
+        ins = {"wide": wide, "got": got, **base}
+        outs = {}
         if known[r] is None:
             ins["sent"] = sent
             if two:
-                outs["counts"] = shaped((ray_blocks, half, size), bf16)
+                outs["counts"] = summed.update(dtype=bf16)
         else:
             ins["counts"] = known[r]
         kernel = functools.partial(update_kernel, tuple(m // min(masks) for m in masks))
-        if r + 1 < ROUNDS and not moves[r] and not (two and r == 1):
+        last = r + 1 == ROUNDS
+        if last or moves[r]:
+            order = (1, 0) if last else (0, 1)
+            moved, ratios = {}, None
+            for k in order:
+                if ratios is None:
+                    out = call(kernel, {**ins, "held": only(k, held), "tiles": only(k, now_tiles)},
+                               {"held": only(k, (piece,) * CORES), "ratios": summed.update(dtype=bf16), **outs},
+                               [back_scratch, ray_scratch, ray_scratch])
+                    ratios = out["ratios"]
+                    if two and r == 0:
+                        far_counts = shift(out["counts"])
+                else:
+                    out = {**out, **call(kernel, {**base, "ratios": ratios, "held": only(k, held),
+                                                  "tiles": only(k, now_tiles)},
+                                         {"held": only(k, (piece,) * CORES)}, [back_scratch])}
+                moved[k] = out["held"][k]
+                if not last:
+                    moved[k] = shift(moved[k])
+                elif k == 1:
+                    moved[k] = swap_cores(moved[k])
+            held = (moved[0], moved[1])
+            if not last:
+                extra, more = sums(r + 1)
+                begun = call(project_kernel, {"held": only(0, held), "index": sets[r + 1][0],
+                                              "tiles": only(0, sets[r + 1][1])},
+                             {"wide": summed}, [low_scratch, sum_scratch])["wide"]
+                out = call(project_kernel, {"held": only(1, held), "index": sets[r + 1][0], "begun": begun,
+                                            "tiles": only(1, sets[r + 1][1]), **extra},
+                           more, [low_scratch, sum_scratch])
+        else:
+            if two and r == 1:
+                known[r + 1] = far_counts
             extra, more = sums(r + 1)
-            ins.update(next_index=sets[r + 1][0], next_tiles=sets[r + 1][1], **extra)
-            outs.update(more)
-        out = call(kernel, ins, outs, scratch + (scratch_sum if "sent" in outs else []))
-        held = out["held"]
-        if two and r < 2:
-            for later in range(r + 2, ROUNDS, 2):
-                known[later] = out["counts"] if r == 1 else shift(out["counts"])
-        if r + 1 < ROUNDS and "sent" not in out:
-            if moves[r]:
-                held = shift(held)
-                if two:
-                    held, far_index, far_tiles[0] = lax.optimization_barrier((held, far_index, far_tiles[0]))
-            out = project(held, r + 1)
-    return joined(core, held[0], swap_cores(held[1]))
+            ins.update(held=held, tiles=now_tiles, next_index=sets[r + 1][0], next_tiles=sets[r + 1][1], **extra)
+            outs.update(held=(piece,) * CORES, **more)
+            out = call(kernel, ins, outs, [back_scratch, ray_scratch, ray_scratch, low_scratch, sum_scratch])
+            held = out["held"]
+            if two and r == 1:
+                known = [known[later] if later < 2 else far_counts if later % 2 == 0 else out["counts"]
+                         for later in range(ROUNDS)]
+    return joined(core, held[0], held[1])
 
 
 def solution(mesh):

time: 82.9 us -> 86.7 us (1.046)
  waiting for transfers between devices: 29.2 us -> 31.2 us
  Pallas kernels: 13.9 us -> 15.4 us
    ppermute x5, waiting for transfers between devices: 7.29 us -> 11.8 us  [shift(): lax.ppermute(array, 'subset', [(i, (i + 1) % subset_count) for i in range...]
    ppermute x16, waiting for transfers between devices: 20.5 us -> 17.9 us  [swap_chips(): return lax.ppermute(array, 'tile', pairs)]
    pallas_call x9 -> x11, Pallas kernels: 13.9 us -> 15.4 us  [call(): pl.pallas_call(kernel, out_shape=outs, in_specs=[jax.tree_util.tree_map_w...]
    unnamed x14 -> x16, local copies, waits for them, and re-layouts: 0.7 us -> 1.92 us
    slice x2 -> x0, local copies, waits for them, and re-layouts: 1.16 us -> none  [the longest x1 1.13 us: shards(): far_tiles = [shift(after(own_tiles[:slots * 5 // 8], sent))]]
    ppermute x8 -> x7, starting transfers between devices: 1.83 us -> 1.24 us  [swap_cores(): return lax.ppermute(array, 'tile', [(i, i ^ 1) for i in range(tile_devs)])]
  transfers between devices with their start and end apart: 29 -> 28, of which waited for: 18 -> 20; matrix products, arithmetic and copies ran while one was open for 3% -> 2% of each run, Pallas kernels for 6% -> 11%
where the time goes in v6:
time: 86.7 us; the launch traced here: 86.5 us
  starting transfers between devices  34.9 us (40%)
  waiting for transfers between devices  31.2 us (36%)
  Pallas kernels  15.4 us (18%)
  local copies, waits for them, and re-layouts  3.13 us (4%)
  other arithmetic  0.98 us (1%)
  between operations  0.91 us (1%)
    ppermute x16, starting transfers between devices, swap_chips(): return lax.ppermute(array, 'tile', pairs)  26.5 us
    ppermute x16, waiting for transfers between devices, swap_chips(): return lax.ppermute(array, 'tile', pairs)  17.9 us
    pallas_call x11, Pallas kernels, call(): pl.pallas_call(kernel, out_shape=outs, in_specs=[jax.tree_util.tree_map_w...  15.4 us
    ppermute x5, waiting for transfers between devices, shift(): lax.ppermute(array, 'subset', [(i, (i + 1) % subset_count) for i in range...  11.8 us
    ppermute x5, starting transfers between devices, shift(): lax.ppermute(array, 'subset', [(i, (i + 1) % subset_count) for i in range...  7.16 us
    unnamed x16, local copies, waits for them, and re-layouts  1.92 us
  transfers between devices with their start and end apart: 28, of which 20 were waited for; matrix products, arithmetic and copies ran while one was open for 2% of the time, Pallas kernels for 11%

profile of v6, /device:TPU:0, one launch (start us, length us, event | category | flops | bytes accessed | tf_op | source)
XLA Modules:
  0.0 86.5 jit_solution(3649337956594191071)
XLA Ops:
  0.0 0.5 collective-permute-start.3
  1.3 0.6 copy-done.3
  2.0 0.5 collective-permute-start
  2.5 1.0 %dynamic-slice_bitcast_fusion = (f32[16,2048]{1,0:T(8,128)S(1)}, f32[16,2048]{1,0:T(8,128)S(1)}) fusion(f32[2,16,2048]{2,1,0:T(8,128)} %bitcast.61, s32[]{:T(128)S(6)} %select_n.88, s32[]{:T(128)S(6)} %select_n.87), kind=kLoop, calls=%fused_computation.5 | loop fusion | bytes 524296 | tf_op jit(solution)/shard_map/jit(dynamic_index_in_dim)/squeeze | solution.py:221
  3.7 2.9 %collective-permute-start.17 = (bf16[32,128,128]{2,1,0:T(8,128)(2,1)}, bf16[32,128,128]{2,1,0:T(8,128)(2,1)S(1)}, u32[]{:S(2)}, u32[]{:S(2)}) collective-permute-start(bf16[32,128,128]{2,1,0:T(8,128)(2,1)} %bitcast.53), channel_id=1, source_target_pairs={{0,16},{16,0},{1,17},{17,1},{2,18},{18,2},{3,19},{19,3},{4,20},{20... | collective-permute-start | bytes 3145736 | tf_op jit(solution)/shard_map/ppermute | solution.py:214
  6.7 1.2 %copy-done = bf16[1,32,128,128]{3,2,1,0:T(8,128)(2,1)S(1)} copy-done((bf16[1,32,128,128]{3,2,1,0:T(8,128)(2,1)S(1)}, bf16[1,32,128,128]{3,2,1,0:T(8,128)(2,1)}, u32[]{:S(2)}) %copy-start) | copy-done | bytes 1048600
  7.9 1.7 %shard_map.64 = (bf16[18,16,128]{2,1,0:T(8,128)(2,1)S(1)}, f32[16,16,128]{2,1,0:T(8,128)S(1)}) custom-call(bf16[2,16,128]{2,1,0:T(8,128)(2,1)S(1)} %get-tuple-element.64.ins__dealt__, f32[16,2048]{1,0:T(8,128)S(1)} %get-tuple-element.62.ins__held___0_, f32[16,2048]{1,0:T(8,128)S(1)} %collective-permute-done.1.ins__held___1_, ...), custom_call_target="tpu_custom_call" | custom-call | tf_op jit(solution)/shard_map/pallas_call | solution.py:166
  9.6 2.6 %collective-permute-start.6 = (bf16[18,16,128]{2,1,0:T(8,128)(2,1)S(1)}, bf16[18,16,128]{2,1,0:T(8,128)(2,1)S(1)}, u32[]{:S(2)}, u32[]{:S(2)}) collective-permute-start(bf16[18,16,128]{2,1,0:T(8,128)(2,1)S(1)} %get-tuple-element.30), channel_id=1, source_target_pairs={{0,6},{1,7},{2,4},{3,5},{4,2},{5,3},{6,0},{7,1},{8,14},{9,15},{10,... | collective-permute-start | bytes 221192 | tf_op jit(solution)/shard_map/ppermute | solution.py:208
  12.2 0.4 collective-permute-start.5
  12.7 0.5 collective-permute-start.4
  13.2 2.4 %collective-permute-done.6 = bf16[18,16,128]{2,1,0:T(8,128)(2,1)S(1)} collective-permute-done((bf16[18,16,128]{2,1,0:T(8,128)(2,1)S(1)}, bf16[18,16,128]{2,1,0:T(8,128)(2,1)S(1)}, u32[]{:S(2)}, u32[]{:S(2)}) %collective-permute-start.6) | collective-permute-done | bytes 73760 | tf_op jit(solution)/shard_map/ppermute | solution.py:208
  15.6 1.0 %collective-permute-done.5 = bf16[18,16,128]{2,1,0:T(8,128)(2,1)S(1)} collective-permute-done((bf16[18,16,128]{2,1,0:T(8,128)(2,1)S(1)}, bf16[18,16,128]{2,1,0:T(8,128)(2,1)S(1)}, u32[]{:S(2)}, u32[]{:S(2)}) %collective-permute-start.5) | collective-permute-done | bytes 73760 | tf_op jit(solution)/shard_map/ppermute | solution.py:208
  17.2 2.7 %collective-permute-start.7 = (bf16[24,16,128]{2,1,0:T(8,128)(2,1)S(1)}, bf16[24,16,128]{2,1,0:T(8,128)(2,1)S(1)}, u32[]{:S(2)}, u32[]{:S(2)}) collective-permute-start(bf16[24,16,128]{2,1,0:T(8,128)(2,1)S(1)} %constant_dynamic-update-slice_fusion.ins__sent__), channel_id=1, source_target_pairs={{0,8},{1,9},{2,10},{3,11},{4,12},{5,13},{6,14},{7,15},{8,0},{9,1},... | collective-permute-start | bytes 294920 | tf_op jit(solution)/shard_map/ppermute | solution.py:208
  19.8 0.9 %collective-permute-start.8 = (s32[8,128]{1,0:T(8,128)S(1)}, s32[8,128]{1,0:T(8,128)S(1)}, u32[]{:S(2)}, u32[]{:S(2)}) collective-permute-start(s32[8,128]{1,0:T(8,128)S(1)} %pad.4.ins__index___0_.ins__next_index___0_), channel_id=1, source_target_pairs={{0,16},{16,0},{1,17},{17,1},{2,18},{18,2},{3,19},{19,3},{4,20},{20... | collective-permute-start | bytes 12296 | tf_op jit(solution)/shard_map/ppermute | solution.py:214
  20.7 1.3 %shard_map.65.ins__inverse__ = f32[32,8,128]{2,1,0:T(8,128)S(1)} custom-call(s32[8,128]{1,0:T(8,128)S(1)} %pad.4.ins__index___0_.ins__next_index___0_, s32[8,128]{1,0:T(8,128)S(1)} %collective-permute-done.2.ins__index___1_.ins__next_index___1_, bf16[32,128,128]{2,1,0:T(8,128)(2,1)S(1)} %bitcast.55, ...), custom_call_target="tpu_custom_call" | custom-call | tf_op jit(solution)/shard_map/pallas_call | solution.py:166
  22.0 8.3 %collective-permute-done.8.ins__next_index___0_.ins__index___0_ = s32[8,128]{1,0:T(8,128)S(1)} collective-permute-done((s32[8,128]{1,0:T(8,128)S(1)}, s32[8,128]{1,0:T(8,128)S(1)}, u32[]{:S(2)}, u32[]{:S(2)}) %collective-permute-start.8) | collective-permute-done | bytes 4128 | tf_op jit(solution)/shard_map/ppermute | solution.py:214
  30.3 1.0 %shard_map.66 = (bf16[16,16,128]{2,1,0:T(8,128)(2,1)S(1)}, f32[16,2048]{1,0:T(8,128)S(1)}, bf16[16,16,128]{2,1,0:T(8,128)(2,1)S(1)}) custom-call(bf16[24,16,128]{2,1,0:T(8,128)(2,1)S(1)} %collective-permute-done.7.ins__got___0_, f32[16,2048]{1,0:T(8,128)S(1)} %get-tuple-element.62.ins__held___0_, s32[8,128]{1,0:T(8,128)S(1)} %pad.4.ins__index___0_.ins__next_index___0_, ...), custom_call_target="tpu_custom_call" | custom-call | tf_op jit(solution)/shard_map/pallas_call | solution.py:166
  31.3 1.8 %collective-permute-start.10 = (f32[16,2048]{1,0:T(8,128)S(1)}, f32[16,2048]{1,0:T(8,128)S(1)}, u32[]{:S(2)}, u32[]{:S(2)}) collective-permute-start(f32[16,2048]{1,0:T(8,128)S(1)} %get-tuple-element.34), channel_id=1, source_target_pairs={{0,16},{16,0},{1,17},{17,1},{2,18},{18,2},{3,19},{19,3},{4,20},{20... | collective-permute-start | bytes 393224 | tf_op jit(solution)/shard_map/ppermute | solution.py:214
  33.1 1.0 %shard_map.68 = f32[16,2048]{1,0:T(8,128)S(1)} custom-call(f32[16,2048]{1,0:T(8,128)S(1)} %collective-permute-done.1.ins__held___1_, s32[8,128]{1,0:T(8,128)S(1)} %pad.4.ins__index___0_.ins__next_index___0_, s32[8,128]{1,0:T(8,128)S(1)} %collective-permute-done.2.ins__index___1_.ins__next_index___1_, f32[32,8,128]{2,1,0:T(8,128)S(1)} %shard_map.65.ins__inverse__, ...), custom_call_target="tpu_custom_call" | custom-call | tf_op jit(solution)/shard_map/pallas_call | solution.py:166
  34.5 2.6 %collective-permute-done.10.ins__held___0_ = f32[16,2048]{1,0:T(8,128)S(1)} collective-permute-done((f32[16,2048]{1,0:T(8,128)S(1)}, f32[16,2048]{1,0:T(8,128)S(1)}, u32[]{:S(2)}, u32[]{:S(2)}) %collective-permute-start.10) | collective-permute-done | bytes 131104 | tf_op jit(solution)/shard_map/ppermute | solution.py:214
  37.0 1.1 %shard_map.67.ins__begun__ = f32[16,16,128]{2,1,0:T(8,128)S(1)} custom-call(f32[16,2048]{1,0:T(8,128)S(1)} %collective-permute-done.10.ins__held___0_, s32[8,128]{1,0:T(8,128)S(1)} %pad.4.ins__index___0_.ins__next_index___0_, s32[8,128]{1,0:T(8,128)S(1)} %collective-permute-done.2.ins__index___1_.ins__next_index___1_, bf16[32,128,128]{2,1,0:T(8,128)(2,1)S(1)} %bitcast.57), custom_call_target="tpu_custom_call" | custom-call | tf_op jit(solution)/shard_map/pallas_call | solution.py:166
  38.2 1.0 %collective-permute-done.11.ins__held___1_ = f32[16,2048]{1,0:T(8,128)S(1)} collective-permute-done((f32[16,2048]{1,0:T(8,128)S(1)}, f32[16,2048]{1,0:T(8,128)S(1)}, u32[]{:S(2)}, u32[]{:S(2)}) %collective-permute-start.11) | collective-permute-done | bytes 131104 | tf_op jit(solution)/shard_map/ppermute | solution.py:214
  39.2 1.2 %shard_map.69 = (bf16[18,16,128]{2,1,0:T(8,128)(2,1)S(1)}, f32[16,16,128]{2,1,0:T(8,128)S(1)}) custom-call(f32[16,16,128]{2,1,0:T(8,128)S(1)} %shard_map.67.ins__begun__, bf16[2,16,128]{2,1,0:T(8,128)(2,1)S(1)} %get-tuple-element.63.ins__dealt__, f32[16,2048]{1,0:T(8,128)S(1)} %collective-permute-done.11.ins__held___1_, ...), custom_call_target="tpu_custom_call" | custom-call | tf_op jit(solution)/shard_map/pallas_call | solution.py:166
  40.4 2.8 %collective-permute-start.14 = (bf16[18,16,128]{2,1,0:T(8,128)(2,1)S(1)}, bf16[18,16,128]{2,1,0:T(8,128)(2,1)S(1)}, u32[]{:S(2)}, u32[]{:S(2)}) collective-permute-start(bf16[18,16,128]{2,1,0:T(8,128)(2,1)S(1)} %get-tuple-element.37), channel_id=1, source_target_pairs={{0,6},{1,7},{2,4},{3,5},{4,2},{5,3},{6,0},{7,1},{8,14},{9,15},{10,... | collective-permute-start | bytes 221192 | tf_op jit(solution)/shard_map/ppermute | solution.py:208
  43.9 2.1 %collective-permute-done.14 = bf16[18,16,128]{2,1,0:T(8,128)(2,1)S(1)} collective-permute-done((bf16[18,16,128]{2,1,0:T(8,128)(2,1)S(1)}, bf16[18,16,128]{2,1,0:T(8,128)(2,1)S(1)}, u32[]{:S(2)}, u32[]{:S(2)}) %collective-permute-start.14) | collective-permute-done | bytes 73760 | tf_op jit(solution)/shard_map/ppermute | solution.py:208
  46.0 1.5 %collective-permute-done.13 = bf16[18,16,128]{2,1,0:T(8,128)(2,1)S(1)} collective-permute-done((bf16[18,16,128]{2,1,0:T(8,128)(2,1)S(1)}, bf16[18,16,128]{2,1,0:T(8,128)(2,1)S(1)}, u32[]{:S(2)}, u32[]{:S(2)}) %collective-permute-start.13) | collective-permute-done | bytes 73760 | tf_op jit(solution)/shard_map/ppermute | solution.py:208
  48.1 2.7 %collective-permute-start.15 = (bf16[24,16,128]{2,1,0:T(8,128)(2,1)S(1)}, bf16[24,16,128]{2,1,0:T(8,128)(2,1)S(1)}, u32[]{:S(2)}, u32[]{:S(2)}) collective-permute-start(bf16[24,16,128]{2,1,0:T(8,128)(2,1)S(1)} %constant_dynamic-update-slice_fusion.4.ins__sent__), channel_id=1, source_target_pairs={{0,8},{1,9},{2,10},{3,11},{4,12},{5,13},{6,14},{7,15},{8,0},{9,1},... | collective-permute-start | bytes 294920 | tf_op jit(solution)/shard_map/ppermute | solution.py:208
  50.8 1.2 %collective-permute-done.16.ins__next_index___1_.ins__index___1_ = s32[8,128]{1,0:T(8,128)S(1)} collective-permute-done((s32[8,128]{1,0:T(8,128)S(1)}, s32[8,128]{1,0:T(8,128)S(1)}, u32[]{:S(2)}, u32[]{:S(2)}) %collective-permute-start.16) | collective-permute-done | bytes 4128 | tf_op jit(solution)/shard_map/ppermute | solution.py:204
  51.9 1.8 %collective-permute-done.15.ins__got___0_ = bf16[24,16,128]{2,1,0:T(8,128)(2,1)S(1)} collective-permute-done((bf16[24,16,128]{2,1,0:T(8,128)(2,1)S(1)}, bf16[24,16,128]{2,1,0:T(8,128)(2,1)S(1)}, u32[]{:S(2)}, u32[]{:S(2)}) %collective-permute-start.15) | collective-permute-done | bytes 98336 | tf_op jit(solution)/shard_map/ppermute | solution.py:208
  53.7 2.4 %shard_map.70 = (bf16[16,16,128]{2,1,0:T(8,128)(2,1)S(1)}, f32[16,2048]{1,0:T(8,128)S(1)}, f32[16,2048]{1,0:T(8,128)S(1)}, bf16[16,16,128]{2,1,0:T(8,128)(2,1)S(1)}, f32[16,16,128]{2,1,0:T(8,128)S(1)}) custom-call(bf16[24,16,128]{2,1,0:T(8,128)(2,1)S(1)} %collective-permute-done.15.ins__got___0_, f32[16,2048]{1,0:T(8,128)S(1)} %collective-permute-done.10.ins__held___0_, ...), custom_call_target="tpu_custom_call" | custom-call | tf_op jit(solution)/shard_map/pallas_call | solution.py:166
  56.2 1.7 %collective-permute-start.21 = (bf16[16,16,128]{2,1,0:T(8,128)(2,1)S(1)}, bf16[16,16,128]{2,1,0:T(8,128)(2,1)S(1)}, u32[]{:S(2)}, u32[]{:S(2)}) collective-permute-start(bf16[16,16,128]{2,1,0:T(8,128)(2,1)S(1)} %get-tuple-element.43), channel_id=1, source_target_pairs={{0,6},{1,7},{2,4},{3,5},{4,2},{5,3},{6,0},{7,1},{8,14},{9,15},{10,... | collective-permute-start | bytes 196616 | tf_op jit(solution)/shard_map/ppermute | solution.py:208
  58.0 1.7 %collective-permute-start.19 = (bf16[16,16,128]{2,1,0:T(8,128)(2,1)S(1)}, bf16[16,16,128]{2,1,0:T(8,128)(2,1)S(1)}, u32[]{:S(2)}, u32[]{:S(2)}) collective-permute-start(bf16[16,16,128]{2,1,0:T(8,128)(2,1)S(1)} %get-tuple-element.43), channel_id=1, source_target_pairs={{0,2},{1,3},{2,0},{3,1},{4,6},{5,7},{6,4},{7,5},{8,10},{9,11},{10,... | collective-permute-start | bytes 196616 | tf_op jit(solution)/shard_map/ppermute | solution.py:208
  59.7 1.2 %collective-permute-start.9 = (bf16[16,16,128]{2,1,0:T(8,128)(2,1)S(1)}, bf16[16,16,128]{2,1,0:T(8,128)(2,1)S(1)}, u32[]{:S(2)}, u32[]{:S(2)}) collective-permute-start(bf16[16,16,128]{2,1,0:T(8,128)(2,1)S(1)} %get-tuple-element.33), channel_id=1, source_target_pairs={{0,16},{16,0},{1,17},{17,1},{2,18},{18,2},{3,19},{19,3},{4,20},{20... | collective-permute-start | bytes 196616 | tf_op jit(solution)/shard_map/ppermute | solution.py:214
  60.9 0.5 collective-permute-done.21
  61.4 0.8 collective-permute-done.20
  62.3 3.7 %collective-permute-start.22 = (bf16[16,16,128]{2,1,0:T(8,128)(2,1)S(1)}, bf16[16,16,128]{2,1,0:T(8,128)(2,1)S(1)}, u32[]{:S(2)}, u32[]{:S(2)}) collective-permute-start(bf16[16,16,128]{2,1,0:T(8,128)(2,1)S(1)} %get-tuple-element.55), channel_id=1, source_target_pairs={{0,8},{1,9},{2,10},{3,11},{4,12},{5,13},{6,14},{7,15},{8,0},{9,1},... | collective-permute-start | bytes 196616 | tf_op jit(solution)/shard_map/ppermute | solution.py:208
  66.0 1.3 %shard_map.71.ins__inverse__ = f32[32,8,128]{2,1,0:T(8,128)S(1)} custom-call(s32[8,128]{1,0:T(8,128)S(1)} %collective-permute-done.8.ins__next_index___0_.ins__index___0_, s32[8,128]{1,0:T(8,128)S(1)} %collective-permute-done.16.ins__next_index___1_.ins__index___1_, ...), custom_call_target="tpu_custom_call" | custom-call | tf_op jit(solution)/shard_map/pallas_call | solution.py:166
  67.3 1.0 %collective-permute-done.22.ins__got___0_ = bf16[16,16,128]{2,1,0:T(8,128)(2,1)S(1)} collective-permute-done((bf16[16,16,128]{2,1,0:T(8,128)(2,1)S(1)}, bf16[16,16,128]{2,1,0:T(8,128)(2,1)S(1)}, u32[]{:S(2)}, u32[]{:S(2)}) %collective-permute-start.22) | collective-permute-done | bytes 65568 | tf_op jit(solution)/shard_map/ppermute | solution.py:208
  68.3 2.4 %shard_map.72 = (f32[16,2048]{1,0:T(8,128)S(1)}, f32[16,2048]{1,0:T(8,128)S(1)}, bf16[16,16,128]{2,1,0:T(8,128)(2,1)S(1)}, f32[16,16,128]{2,1,0:T(8,128)S(1)}) custom-call(bf16[16,16,128]{2,1,0:T(8,128)(2,1)S(1)} %collective-permute-done.9.ins__counts__, bf16[16,16,128]{2,1,0:T(8,128)(2,1)S(1)} %collective-permute-done.22.ins__got___0_, ...), custom_call_target="tpu_custom_call" | custom-call | tf_op jit(solution)/shard_map/pallas_call | solution.py:166
  70.7 2.6 %collective-permute-start.25 = (bf16[16,16,128]{2,1,0:T(8,128)(2,1)S(1)}, bf16[16,16,128]{2,1,0:T(8,128)(2,1)S(1)}, u32[]{:S(2)}, u32[]{:S(2)}) collective-permute-start(bf16[16,16,128]{2,1,0:T(8,128)(2,1)S(1)} %get-tuple-element.49), channel_id=1, source_target_pairs={{0,6},{1,7},{2,4},{3,5},{4,2},{5,3},{6,0},{7,1},{8,14},{9,15},{10,... | collective-permute-start | bytes 196616 | tf_op jit(solution)/shard_map/ppermute | solution.py:208
  73.6 0.7 collective-permute-start.23
  74.3 2.4 %collective-permute-done.25 = bf16[16,16,128]{2,1,0:T(8,128)(2,1)S(1)} collective-permute-done((bf16[16,16,128]{2,1,0:T(8,128)(2,1)S(1)}, bf16[16,16,128]{2,1,0:T(8,128)(2,1)S(1)}, u32[]{:S(2)}, u32[]{:S(2)}) %collective-permute-start.25) | collective-permute-done | bytes 65568 | tf_op jit(solution)/shard_map/ppermute | solution.py:208
  76.7 1.0 %collective-permute-done.24 = bf16[16,16,128]{2,1,0:T(8,128)(2,1)S(1)} collective-permute-done((bf16[16,16,128]{2,1,0:T(8,128)(2,1)S(1)}, bf16[16,16,128]{2,1,0:T(8,128)(2,1)S(1)}, u32[]{:S(2)}, u32[]{:S(2)}) %collective-permute-start.24) | collective-permute-done | bytes 65568 | tf_op jit(solution)/shard_map/ppermute | solution.py:208
  77.9 3.2 %collective-permute-start.26 = (bf16[16,16,128]{2,1,0:T(8,128)(2,1)S(1)}, bf16[16,16,128]{2,1,0:T(8,128)(2,1)S(1)}, u32[]{:S(2)}, u32[]{:S(2)}) collective-permute-start(bf16[16,16,128]{2,1,0:T(8,128)(2,1)S(1)} %get-tuple-element.53), channel_id=1, source_target_pairs={{0,8},{1,9},{2,10},{3,11},{4,12},{5,13},{6,14},{7,15},{8,0},{9,1},... | collective-permute-start | bytes 196616 | tf_op jit(solution)/shard_map/ppermute | solution.py:208
  81.1 2.2 %collective-permute-done.26.ins__got___0_ = bf16[16,16,128]{2,1,0:T(8,128)(2,1)S(1)} collective-permute-done((bf16[16,16,128]{2,1,0:T(8,128)(2,1)S(1)}, bf16[16,16,128]{2,1,0:T(8,128)(2,1)S(1)}, u32[]{:S(2)}, u32[]{:S(2)}) %collective-permute-start.26) | collective-permute-done | bytes 65568 | tf_op jit(solution)/shard_map/ppermute | solution.py:208
  83.3 1.0 %shard_map.73 = (f32[16,2048]{1,0:T(8,128)S(1)}, bf16[16,16,128]{2,1,0:T(8,128)(2,1)S(1)}) custom-call(bf16[16,16,128]{2,1,0:T(8,128)(2,1)S(1)} %get-tuple-element.47.ins__counts__, bf16[16,16,128]{2,1,0:T(8,128)(2,1)S(1)} %collective-permute-done.26.ins__got___0_, f32[16,2048]{1,0:T(8,128)S(1)} %get-tuple-element.50.ins__held___1_, ...), custom_call_target="tpu_custom_call" | custom-call | tf_op jit(solution)/shard_map/pallas_call | solution.py:166
  84.5 1.0 %shard_map.74 = f32[16,2048]{1,0:T(8,128)S(1)} custom-call(f32[16,2048]{1,0:T(8,128)S(1)} %get-tuple-element.46.ins__held___0_, s32[8,128]{1,0:T(8,128)S(1)} %pad.4.ins__index___0_.ins__next_index___0_, s32[8,128]{1,0:T(8,128)S(1)} %collective-permute-done.2.ins__index___1_.ins__next_index___1_, f32[32,8,128]{2,1,0:T(8,128)S(1)} %shard_map.65.ins__inverse__, ...), custom_call_target="tpu_custom_call" | custom-call | tf_op jit(solution)/shard_map/pallas_call | solution.py:166
  85.8 0.7 maximum_select_fusion
  (61 shorter events, 3.9 us)
Async XLA Ops:
  0.0 6.7 %collective-permute-start.3 = (bf16[32,128,128]{2,1,0:T(8,128)(2,1)}, bf16[32,128,128]{2,1,0:T(8,128)(2,1)S(1)}, u32[]{:S(2)}, u32[]{:S(2)}) collective-permute-start(bf16[32,128,128]{2,1,0:T(8,128)(2,1)} %bitcast.52), channel_id=1, source_target_pairs={{0,1},{1,0},{2,3},{3,2},{4,5},{5,4},{6,7},{7,6},{8,9},{9,8},{10,11... | collective-permute-start | bytes 3145736 | tf_op jit(solution)/shard_map/ppermute | solution.py:204
  0.5 1.6 %copy-start.2 = (s32[1,64,128]{2,1,0:T(8,128)S(1)}, s32[1,64,128]{2,1,0:T(8,128)}, u32[]{:S(2)}) copy-start(s32[1,64,128]{2,1,0:T(8,128)} %param.11) | copy-start | bytes 98308
  1.2 0.7 copy-start.3
  1.2 0.7 copy-start.4
  1.9 4.7 %collective-permute-start.2 = (s32[8,128]{1,0:T(8,128)S(1)}, s32[8,128]{1,0:T(8,128)S(1)}, u32[]{:S(2)}, u32[]{:S(2)}) collective-permute-start(s32[8,128]{1,0:T(8,128)S(1)} %pad.4.ins__index___0_.ins__next_index___0_), channel_id=1, source_target_pairs={{0,1},{1,0},{2,3},{3,2},{4,5},{5,4},{6,7},{7,6},{8,9},{9,8},{10,11... | collective-permute-start | bytes 12296 | tf_op jit(solution)/shard_map/ppermute | solution.py:204
  2.0 4.6 %collective-permute-start = (bf16[1,2,16,128]{3,2,0,1:T(8,128)(2,1)S(1)}, bf16[1,2,16,128]{3,2,0,1:T(8,128)(2,1)S(1)}, u32[]{:S(2)}, u32[]{:S(2)}) collective-permute-start(bf16[1,2,16,128]{3,2,0,1:T(8,128)(2,1)S(1)} %get-tuple-element.66), channel_id=1, source_target_pairs={{0,1},{1,0},{2,3},{3,2},{4,5},{5,4},{6,7},{7,6},{8,9},{9,8},{10,11... | collective-permute-start | bytes 24584 | tf_op jit(solution)/shard_map/ppermute | solution.py:204
  3.5 3.1 %collective-permute-start.1 = (f32[16,2048]{1,0:T(8,128)S(1)}, f32[16,2048]{1,0:T(8,128)S(1)}, u32[]{:S(2)}, u32[]{:S(2)}) collective-permute-start(f32[16,2048]{1,0:T(8,128)S(1)} %get-tuple-element.61), channel_id=1, source_target_pairs={{0,1},{1,0},{2,3},{3,2},{4,5},{5,4},{6,7},{7,6},{8,9},{9,8},{10,11... | collective-permute-start | bytes 393224 | tf_op jit(solution)/shard_map/ppermute | solution.py:204
  3.7 40.2 %collective-permute-start.17 = (bf16[32,128,128]{2,1,0:T(8,128)(2,1)}, bf16[32,128,128]{2,1,0:T(8,128)(2,1)S(1)}, u32[]{:S(2)}, u32[]{:S(2)}) collective-permute-start(bf16[32,128,128]{2,1,0:T(8,128)(2,1)} %bitcast.53), channel_id=1, source_target_pairs={{0,16},{16,0},{1,17},{17,1},{2,18},{18,2},{3,19},{19,3},{4,20},{20... | collective-permute-start | bytes 3145736 | tf_op jit(solution)/shard_map/ppermute | solution.py:214
  6.7 1.2 %copy-start = (bf16[1,32,128,128]{3,2,1,0:T(8,128)(2,1)S(1)}, bf16[1,32,128,128]{3,2,1,0:T(8,128)(2,1)}, u32[]{:S(2)}) copy-start(bf16[1,32,128,128]{3,2,1,0:T(8,128)(2,1)} %param.7) | copy-start | bytes 3145732
  7.9 12.9 %copy-start.1 = (bf16[1,32,128,128]{3,2,1,0:T(8,128)(2,1)S(1)}, bf16[1,32,128,128]{3,2,1,0:T(8,128)(2,1)}, u32[]{:S(2)}) copy-start(bf16[1,32,128,128]{3,2,1,0:T(8,128)(2,1)} %param.7) | copy-start | bytes 3145732
  9.6 6.0 %collective-permute-start.6 = (bf16[18,16,128]{2,1,0:T(8,128)(2,1)S(1)}, bf16[18,16,128]{2,1,0:T(8,128)(2,1)S(1)}, u32[]{:S(2)}, u32[]{:S(2)}) collective-permute-start(bf16[18,16,128]{2,1,0:T(8,128)(2,1)S(1)} %get-tuple-element.30), channel_id=1, source_target_pairs={{0,6},{1,7},{2,4},{3,5},{4,2},{5,3},{6,0},{7,1},{8,14},{9,15},{10,... | collective-permute-start | bytes 221192 | tf_op jit(solution)/shard_map/ppermute | solution.py:208
  12.2 4.4 %collective-permute-start.5 = (bf16[18,16,128]{2,1,0:T(8,128)(2,1)S(1)}, bf16[18,16,128]{2,1,0:T(8,128)(2,1)S(1)}, u32[]{:S(2)}, u32[]{:S(2)}) collective-permute-start(bf16[18,16,128]{2,1,0:T(8,128)(2,1)S(1)} %get-tuple-element.30), channel_id=1, source_target_pairs={{0,4},{1,5},{2,6},{3,7},{4,0},{5,1},{6,2},{7,3},{8,12},{9,13},{10,... | collective-permute-start | bytes 221192 | tf_op jit(solution)/shard_map/ppermute | solution.py:208
  12.7 4.4 %collective-permute-start.4 = (bf16[18,16,128]{2,1,0:T(8,128)(2,1)S(1)}, bf16[18,16,128]{2,1,0:T(8,128)(2,1)S(1)}, u32[]{:S(2)}, u32[]{:S(2)}) collective-permute-start(bf16[18,16,128]{2,1,0:T(8,128)(2,1)S(1)} %get-tuple-element.30), channel_id=1, source_target_pairs={{0,2},{1,3},{2,0},{3,1},{4,6},{5,7},{6,4},{7,5},{8,10},{9,11},{10,... | collective-permute-start | bytes 221192 | tf_op jit(solution)/shard_map/ppermute | solution.py:208
  17.2 13.2 %collective-permute-start.7 = (bf16[24,16,128]{2,1,0:T(8,128)(2,1)S(1)}, bf16[24,16,128]{2,1,0:T(8,128)(2,1)S(1)}, u32[]{:S(2)}, u32[]{:S(2)}) collective-permute-start(bf16[24,16,128]{2,1,0:T(8,128)(2,1)S(1)} %constant_dynamic-update-slice_fusion.ins__sent__), channel_id=1, source_target_pairs={{0,8},{1,9},{2,10},{3,11},{4,12},{5,13},{6,14},{7,15},{8,0},{9,1},... | collective-permute-start | bytes 294920 | tf_op jit(solution)/shard_map/ppermute | solution.py:208
  19.8 10.5 %collective-permute-start.8 = (s32[8,128]{1,0:T(8,128)S(1)}, s32[8,128]{1,0:T(8,128)S(1)}, u32[]{:S(2)}, u32[]{:S(2)}) collective-permute-start(s32[8,128]{1,0:T(8,128)S(1)} %pad.4.ins__index___0_.ins__next_index___0_), channel_id=1, source_target_pairs={{0,16},{16,0},{1,17},{17,1},{2,18},{18,2},{3,19},{19,3},{4,20},{20... | collective-permute-start | bytes 12296 | tf_op jit(solution)/shard_map/ppermute | solution.py:214
  31.3 5.7 %collective-permute-start.10 = (f32[16,2048]{1,0:T(8,128)S(1)}, f32[16,2048]{1,0:T(8,128)S(1)}, u32[]{:S(2)}, u32[]{:S(2)}) collective-permute-start(f32[16,2048]{1,0:T(8,128)S(1)} %get-tuple-element.34), channel_id=1, source_target_pairs={{0,16},{16,0},{1,17},{17,1},{2,18},{18,2},{3,19},{19,3},{4,20},{20... | collective-permute-start | bytes 393224 | tf_op jit(solution)/shard_map/ppermute | solution.py:214
  34.1 5.1 %collective-permute-start.11 = (f32[16,2048]{1,0:T(8,128)S(1)}, f32[16,2048]{1,0:T(8,128)S(1)}, u32[]{:S(2)}, u32[]{:S(2)}) collective-permute-start(f32[16,2048]{1,0:T(8,128)S(1)} %shard_map.68), channel_id=1, source_target_pairs={{0,16},{16,0},{1,17},{17,1},{2,18},{18,2},{3,19},{19,3},{4,20},{20... | collective-permute-start | bytes 393224 | tf_op jit(solution)/shard_map/ppermute | solution.py:214
  40.4 5.7 %collective-permute-start.14 = (bf16[18,16,128]{2,1,0:T(8,128)(2,1)S(1)}, bf16[18,16,128]{2,1,0:T(8,128)(2,1)S(1)}, u32[]{:S(2)}, u32[]{:S(2)}) collective-permute-start(bf16[18,16,128]{2,1,0:T(8,128)(2,1)S(1)} %get-tuple-element.37), channel_id=1, source_target_pairs={{0,6},{1,7},{2,4},{3,5},{4,2},{5,3},{6,0},{7,1},{8,14},{9,15},{10,... | collective-permute-start | bytes 221192 | tf_op jit(solution)/shard_map/ppermute | solution.py:208
  43.2 4.4 %collective-permute-start.13 = (bf16[18,16,128]{2,1,0:T(8,128)(2,1)S(1)}, bf16[18,16,128]{2,1,0:T(8,128)(2,1)S(1)}, u32[]{:S(2)}, u32[]{:S(2)}) collective-permute-start(bf16[18,16,128]{2,1,0:T(8,128)(2,1)S(1)} %get-tuple-element.37), channel_id=1, source_target_pairs={{0,4},{1,5},{2,6},{3,7},{4,0},{5,1},{6,2},{7,3},{8,12},{9,13},{10,... | collective-permute-start | bytes 221192 | tf_op jit(solution)/shard_map/ppermute | solution.py:208
  43.6 4.4 %collective-permute-start.12 = (bf16[18,16,128]{2,1,0:T(8,128)(2,1)S(1)}, bf16[18,16,128]{2,1,0:T(8,128)(2,1)S(1)}, u32[]{:S(2)}, u32[]{:S(2)}) collective-permute-start(bf16[18,16,128]{2,1,0:T(8,128)(2,1)S(1)} %get-tuple-element.37), channel_id=1, source_target_pairs={{0,2},{1,3},{2,0},{3,1},{4,6},{5,7},{6,4},{7,5},{8,10},{9,11},{10,... | collective-permute-start | bytes 221192 | tf_op jit(solution)/shard_map/ppermute | solution.py:208
  43.9 9.8 %collective-permute-start.18 = (bf16[32,128,128]{2,1,0:T(8,128)(2,1)S(1)}, bf16[32,128,128]{2,1,0:T(8,128)(2,1)S(1)}, u32[]{:S(2)}, u32[]{:S(2)}) collective-permute-start(bf16[32,128,128]{2,1,0:T(8,128)(2,1)S(1)} %collective-permute-done.17.ins__next_tiles___0__0_.ins__tiles___0__0_), channel_id=1, source_target_pairs={{0,1},{1,0},{2,3},{3,2},{4,5},{5,4},{6,7},{7,6},{8,9},{9,8},{10,11... | collective-permute-start | bytes 3145736 | tf_op jit(solution)/shard_map/ppermute | solution.py:204
  48.1 5.6 %collective-permute-start.15 = (bf16[24,16,128]{2,1,0:T(8,128)(2,1)S(1)}, bf16[24,16,128]{2,1,0:T(8,128)(2,1)S(1)}, u32[]{:S(2)}, u32[]{:S(2)}) collective-permute-start(bf16[24,16,128]{2,1,0:T(8,128)(2,1)S(1)} %constant_dynamic-update-slice_fusion.4.ins__sent__), channel_id=1, source_target_pairs={{0,8},{1,9},{2,10},{3,11},{4,12},{5,13},{6,14},{7,15},{8,0},{9,1},... | collective-permute-start | bytes 294920 | tf_op jit(solution)/shard_map/ppermute | solution.py:208
  50.8 1.2 %collective-permute-start.16 = (s32[8,128]{1,0:T(8,128)S(1)}, s32[8,128]{1,0:T(8,128)S(1)}, u32[]{:S(2)}, u32[]{:S(2)}) collective-permute-start(s32[8,128]{1,0:T(8,128)S(1)} %collective-permute-done.8.ins__next_index___0_.ins__index___0_), channel_id=1, source_target_pairs={{0,1},{1,0},{2,3},{3,2},{4,5},{5,4},{6,7},{7,6},{8,9},{9,8},{10,11... | collective-permute-start | bytes 12296 | tf_op jit(solution)/shard_map/ppermute | solution.py:204
  56.2 5.2 %collective-permute-start.21 = (bf16[16,16,128]{2,1,0:T(8,128)(2,1)S(1)}, bf16[16,16,128]{2,1,0:T(8,128)(2,1)S(1)}, u32[]{:S(2)}, u32[]{:S(2)}) collective-permute-start(bf16[16,16,128]{2,1,0:T(8,128)(2,1)S(1)} %get-tuple-element.43), channel_id=1, source_target_pairs={{0,6},{1,7},{2,4},{3,5},{4,2},{5,3},{6,0},{7,1},{8,14},{9,15},{10,... | collective-permute-start | bytes 196616 | tf_op jit(solution)/shard_map/ppermute | solution.py:208
  57.9 4.3 %collective-permute-start.20 = (bf16[16,16,128]{2,1,0:T(8,128)(2,1)S(1)}, bf16[16,16,128]{2,1,0:T(8,128)(2,1)S(1)}, u32[]{:S(2)}, u32[]{:S(2)}) collective-permute-start(bf16[16,16,128]{2,1,0:T(8,128)(2,1)S(1)} %get-tuple-element.43), channel_id=1, source_target_pairs={{0,4},{1,5},{2,6},{3,7},{4,0},{5,1},{6,2},{7,3},{8,12},{9,13},{10,... | collective-permute-start | bytes 196616 | tf_op jit(solution)/shard_map/ppermute | solution.py:208
  58.0 4.3 %collective-permute-start.19 = (bf16[16,16,128]{2,1,0:T(8,128)(2,1)S(1)}, bf16[16,16,128]{2,1,0:T(8,128)(2,1)S(1)}, u32[]{:S(2)}, u32[]{:S(2)}) collective-permute-start(bf16[16,16,128]{2,1,0:T(8,128)(2,1)S(1)} %get-tuple-element.43), channel_id=1, source_target_pairs={{0,2},{1,3},{2,0},{3,1},{4,6},{5,7},{6,4},{7,5},{8,10},{9,11},{10,... | collective-permute-start | bytes 196616 | tf_op jit(solution)/shard_map/ppermute | solution.py:208
  59.7 7.6 %collective-permute-start.9 = (bf16[16,16,128]{2,1,0:T(8,128)(2,1)S(1)}, bf16[16,16,128]{2,1,0:T(8,128)(2,1)S(1)}, u32[]{:S(2)}, u32[]{:S(2)}) collective-permute-start(bf16[16,16,128]{2,1,0:T(8,128)(2,1)S(1)} %get-tuple-element.33), channel_id=1, source_target_pairs={{0,16},{16,0},{1,17},{17,1},{2,18},{18,2},{3,19},{19,3},{4,20},{20... | collective-permute-start | bytes 196616 | tf_op jit(solution)/shard_map/ppermute | solution.py:214
  62.3 6.0 %collective-permute-start.22 = (bf16[16,16,128]{2,1,0:T(8,128)(2,1)S(1)}, bf16[16,16,128]{2,1,0:T(8,128)(2,1)S(1)}, u32[]{:S(2)}, u32[]{:S(2)}) collective-permute-start(bf16[16,16,128]{2,1,0:T(8,128)(2,1)S(1)} %get-tuple-element.55), channel_id=1, source_target_pairs={{0,8},{1,9},{2,10},{3,11},{4,12},{5,13},{6,14},{7,15},{8,0},{9,1},... | collective-permute-start | bytes 196616 | tf_op jit(solution)/shard_map/ppermute | solution.py:208
  70.7 5.9 %collective-permute-start.25 = (bf16[16,16,128]{2,1,0:T(8,128)(2,1)S(1)}, bf16[16,16,128]{2,1,0:T(8,128)(2,1)S(1)}, u32[]{:S(2)}, u32[]{:S(2)}) collective-permute-start(bf16[16,16,128]{2,1,0:T(8,128)(2,1)S(1)} %get-tuple-element.49), channel_id=1, source_target_pairs={{0,6},{1,7},{2,4},{3,5},{4,2},{5,3},{6,0},{7,1},{8,14},{9,15},{10,... | collective-permute-start | bytes 196616 | tf_op jit(solution)/shard_map/ppermute | solution.py:208
  73.4 4.3 %collective-permute-start.24 = (bf16[16,16,128]{2,1,0:T(8,128)(2,1)S(1)}, bf16[16,16,128]{2,1,0:T(8,128)(2,1)S(1)}, u32[]{:S(2)}, u32[]{:S(2)}) collective-permute-start(bf16[16,16,128]{2,1,0:T(8,128)(2,1)S(1)} %get-tuple-element.49), channel_id=1, source_target_pairs={{0,4},{1,5},{2,6},{3,7},{4,0},{5,1},{6,2},{7,3},{8,12},{9,13},{10,... | collective-permute-start | bytes 196616 | tf_op jit(solution)/shard_map/ppermute | solution.py:208
  73.6 4.3 %collective-permute-start.23 = (bf16[16,16,128]{2,1,0:T(8,128)(2,1)S(1)}, bf16[16,16,128]{2,1,0:T(8,128)(2,1)S(1)}, u32[]{:S(2)}, u32[]{:S(2)}) collective-permute-start(bf16[16,16,128]{2,1,0:T(8,128)(2,1)S(1)} %get-tuple-element.49), channel_id=1, source_target_pairs={{0,2},{1,3},{2,0},{3,1},{4,6},{5,7},{6,4},{7,5},{8,10},{9,11},{10,... | collective-permute-start | bytes 196616 | tf_op jit(solution)/shard_map/ppermute | solution.py:208
  77.9 5.5 %collective-permute-start.26 = (bf16[16,16,128]{2,1,0:T(8,128)(2,1)S(1)}, bf16[16,16,128]{2,1,0:T(8,128)(2,1)S(1)}, u32[]{:S(2)}, u32[]{:S(2)}) collective-permute-start(bf16[16,16,128]{2,1,0:T(8,128)(2,1)S(1)} %get-tuple-element.53), channel_id=1, source_target_pairs={{0,8},{1,9},{2,10},{3,11},{4,12},{5,13},{6,14},{7,15},{8,0},{9,1},... | collective-permute-start | bytes 196616 | tf_op jit(solution)/shard_map/ppermute | solution.py:208
  84.4 1.4 %collective-permute-start.27 = (f32[16,2048]{1,0:T(8,128)S(1)}, f32[16,2048]{1,0:T(8,128)S(1)}, u32[]{:S(2)}, u32[]{:S(2)}) collective-permute-start(f32[16,2048]{1,0:T(8,128)S(1)} %get-tuple-element.52), channel_id=1, source_target_pairs={{0,1},{1,0},{2,3},{3,2},{4,5},{5,4},{6,7},{7,6},{8,9},{9,8},{10,11... | collective-permute-start | bytes 393224 | tf_op jit(solution)/shard_map/ppermute | solution.py:204

commit v7 on v6

--- a/solution.py
+++ b/solution.py
@@ -244,8 +244,6 @@
     known = [None] * ROUNDS
     two = subset_count == 2
     if two:
-        far_tiles = shift(after(own_tiles, (theirs, own_index)))
-    if two:
         moves = [r == 0 for r in range(ROUNDS - 1)]
 
     low_scratch, back_scratch = pltpu.VMEM((both, half, size), bf16), pltpu.VMEM((both, half, size), f32)
@@ -268,12 +266,10 @@
     for r in range(ROUNDS):
         wide, sent = out["wide"], out["sent"]
         if two and r == 0:
-            far_index = shift(after(own_index, sent))
+            far_tiles = [shift(after(own_tiles[:slots // 2], sent))]
         if two and r == 1:
             far_index = (far_index, swap_cores(after(far_index, sent)))
-            far_tiles = ((far_tiles,), (swap_cores(after(far_tiles, sent)),))
-            far = (far_index, far_tiles, sensitivity(far_index, far_tiles))
-            sets = [far if later >= 2 and later % 2 == 0 else sets[later] for later in range(ROUNDS)]
+            far_swapped = [swap_cores(after(far_tiles[0], sent))]
         for masks in steps:
             got = [swap_chips(sent, mask) for mask in masks]
             if masks is not steps[-1]:
@@ -289,8 +285,11 @@
                             jnp.stack(ordered), own ^ v, 0, keepdims=False) for v in range(len(ordered))])
                     counted = jnp.concatenate([counted, passed])
                 sent = counted
-        if two and r == 0:
-            wide, far_index = lax.optimization_barrier((wide, far_index))
+        if two and r == 1:
+            far_swapped.append(swap_cores(after(far_tiles[1], wide)))
+            far_tiles = (tuple(far_tiles), tuple(far_swapped))
+            far = (far_index, far_tiles, sensitivity(far_index, far_tiles))
+            sets = [far if later >= 2 and later % 2 == 0 else sets[later] for later in range(ROUNDS)]
         now_index, now_tiles, now_inverse = sets[r]
         base = {"index": now_index, "inverse": now_inverse}
         ins = {"wide": wide, "got": got, **base}
@@ -319,10 +318,15 @@
                                                   "tiles": only(k, now_tiles)},
                                          {"held": only(k, (piece,) * CORES)}, [back_scratch])}
                 moved[k] = out["held"][k]
+                if two and r == 0 and k == 1:
+                    far_index = shift(after(own_index, moved[k]))
+                    far_tiles.append(shift(after(own_tiles[slots // 2:], moved[k])))
                 if not last:
                     moved[k] = shift(moved[k])
                 elif k == 1:
                     moved[k] = swap_cores(moved[k])
+            if two and r == 0:
+                moved[1], far_index, far_tiles[0] = lax.optimization_barrier((moved[1], far_index, far_tiles[0]))
             held = (moved[0], moved[1])
             if not last:
                 extra, more = sums(r + 1)

time: 86.7 us -> 85.5 us (0.986)
  starting transfers between devices: 34.9 us -> 32.3 us
    ppermute x5 -> x6, waiting for transfers between devices: 11.8 us -> 3.09 us  [shift(): lax.ppermute(array, 'subset', [(i, (i + 1) % subset_count) for i in range...]
    ppermute x16, waiting for transfers between devices: 17.9 us -> 26.6 us  [swap_chips(): return lax.ppermute(array, 'tile', pairs)]
    ppermute x16, starting transfers between devices: 26.5 us -> 23.5 us  [swap_chips(): return lax.ppermute(array, 'tile', pairs)]
    slice x0 -> x1, local copies, waits for them, and re-layouts: none -> 1.34 us  [shards(): far_tiles.append(shift(after(own_tiles[slots // 2:], moved[k])))]
    unnamed x16 -> x14, local copies, waits for them, and re-layouts: 1.92 us -> 0.7 us
    ppermute x5 -> x6, starting transfers between devices: 7.16 us -> 7.37 us  [shift(): lax.ppermute(array, 'subset', [(i, (i + 1) % subset_count) for i in range...]
  transfers between devices with their start and end apart: 28 -> 30, of which waited for: 20 -> 19; matrix products, arithmetic and copies ran while one was open for 2% -> 5% of each run, Pallas kernels for 11% -> 9%
where the time goes in v7:
time: 85.5 us; the launch traced here: 85.2 us
  starting transfers between devices  32.3 us (38%)
  waiting for transfers between devices  31 us (36%)
  Pallas kernels  15.4 us (18%)
  local copies, waits for them, and re-layouts  3.84 us (4%)
  other arithmetic  1.75 us (2%)
  between operations  0.98 us (1%)
    ppermute x16, waiting for transfers between devices, swap_chips(): return lax.ppermute(array, 'tile', pairs)  26.6 us
    ppermute x16, starting transfers between devices, swap_chips(): return lax.ppermute(array, 'tile', pairs)  23.5 us
    pallas_call x11, Pallas kernels, call(): pl.pallas_call(kernel, out_shape=outs, in_specs=[jax.tree_util.tree_map_w...  15.4 us
    ppermute x6, starting transfers between devices, shift(): lax.ppermute(array, 'subset', [(i, (i + 1) % subset_count) for i in range...  7.37 us
    ppermute x6, waiting for transfers between devices, shift(): lax.ppermute(array, 'subset', [(i, (i + 1) % subset_count) for i in range...  3.09 us
  transfers between devices with their start and end apart: 30, of which 19 were waited for; matrix products, arithmetic and copies ran while one was open for 5% of the time, Pallas kernels for 9%

profile of v7, /device:TPU:0, one launch (start us, length us, event | category | flops | bytes accessed | tf_op | source)
XLA Modules:
  0.0 85.2 jit_solution(13290657955895958224)
XLA Ops:
  1.3 0.6 copy-done.2
  2.0 0.6 dynamic-slice_bitcast_fusion.5
  3.1 1.0 %dynamic-slice_bitcast_fusion = (f32[16,2048]{1,0:T(8,128)S(1)}, f32[16,2048]{1,0:T(8,128)S(1)}) fusion(f32[2,16,2048]{2,1,0:T(8,128)} %bitcast.64, s32[]{:T(128)S(6)} %select_n.88, s32[]{:T(128)S(6)} %select_n.87), kind=kLoop, calls=%fused_computation.7 | loop fusion | bytes 524296 | tf_op jit(solution)/shard_map/jit(dynamic_index_in_dim)/squeeze | solution.py:221
  4.2 1.3 %slice_bitcast_fusion = (bf16[16,128,128]{2,1,0:T(8,128)(2,1)S(1)}, bf16[16,128,128]{2,1,0:T(8,128)(2,1)S(1)}) fusion(bf16[1,32,128,128]{3,2,1,0:T(8,128)(2,1)} %param.7), kind=kLoop, calls=%fused_computation | loop fusion | bytes 2097152 | tf_op jit(solution)/shard_map/slice | solution.py:323
  5.6 0.8 maximum_select_fusion.1
  6.5 1.7 %shard_map.64 = (bf16[18,16,128]{2,1,0:T(8,128)(2,1)S(1)}, f32[16,16,128]{2,1,0:T(8,128)S(1)}) custom-call(bf16[2,16,128]{2,1,0:T(8,128)(2,1)S(1)} %get-tuple-element.72.ins__dealt__, f32[16,2048]{1,0:T(8,128)S(1)} %get-tuple-element.70.ins__held___0_, f32[16,2048]{1,0:T(8,128)S(1)} %collective-permute-done.1.ins__held___1_, ...), custom_call_target="tpu_custom_call" | custom-call | tf_op jit(solution)/shard_map/pallas_call | solution.py:166
  8.2 4.0 %collective-permute-start.6 = (bf16[18,16,128]{2,1,0:T(8,128)(2,1)S(1)}, bf16[18,16,128]{2,1,0:T(8,128)(2,1)S(1)}, u32[]{:S(2)}, u32[]{:S(2)}) collective-permute-start(bf16[18,16,128]{2,1,0:T(8,128)(2,1)S(1)} %get-tuple-element.33), channel_id=1, source_target_pairs={{0,6},{1,7},{2,4},{3,5},{4,2},{5,3},{6,0},{7,1},{8,14},{9,15},{10,... | collective-permute-start | bytes 221192 | tf_op jit(solution)/shard_map/ppermute | solution.py:208
  12.8 1.8 %collective-permute-start.12 = (bf16[16,128,128]{2,1,0:T(8,128)(2,1)S(1)}, bf16[16,128,128]{2,1,0:T(8,128)(2,1)S(1)}, u32[]{:S(2)}, u32[]{:S(2)}) collective-permute-start(bf16[16,128,128]{2,1,0:T(8,128)(2,1)S(1)} %get-tuple-element.38), channel_id=1, source_target_pairs={{0,16},{16,0},{1,17},{17,1},{2,18},{18,2},{3,19},{19,3},{4,20},{20... | collective-permute-start | bytes 1572872 | tf_op jit(solution)/shard_map/ppermute | solution.py:214
  14.9 1.6 %collective-permute-done.5 = bf16[18,16,128]{2,1,0:T(8,128)(2,1)S(1)} collective-permute-done((bf16[18,16,128]{2,1,0:T(8,128)(2,1)S(1)}, bf16[18,16,128]{2,1,0:T(8,128)(2,1)S(1)}, u32[]{:S(2)}, u32[]{:S(2)}) %collective-permute-start.5) | collective-permute-done | bytes 73760 | tf_op jit(solution)/shard_map/ppermute | solution.py:208
  17.1 2.7 %collective-permute-start.7 = (bf16[24,16,128]{2,1,0:T(8,128)(2,1)S(1)}, bf16[24,16,128]{2,1,0:T(8,128)(2,1)S(1)}, u32[]{:S(2)}, u32[]{:S(2)}) collective-permute-start(bf16[24,16,128]{2,1,0:T(8,128)(2,1)S(1)} %constant_dynamic-update-slice_fusion.ins__sent__), channel_id=1, source_target_pairs={{0,8},{1,9},{2,10},{3,11},{4,12},{5,13},{6,14},{7,15},{8,0},{9,1},... | collective-permute-start | bytes 294920 | tf_op jit(solution)/shard_map/ppermute | solution.py:208
  19.7 1.3 %shard_map.65.ins__inverse__ = f32[32,8,128]{2,1,0:T(8,128)S(1)} custom-call(s32[8,128]{1,0:T(8,128)S(1)} %pad.4.ins__index___0_.ins__next_index___0_, s32[8,128]{1,0:T(8,128)S(1)} %collective-permute-done.2.ins__index___1_.ins__next_index___1_, bf16[32,128,128]{2,1,0:T(8,128)(2,1)S(1)} %bitcast.58, ...), custom_call_target="tpu_custom_call" | custom-call | tf_op jit(solution)/shard_map/pallas_call | solution.py:166
  21.0 3.0 %collective-permute-done.7.ins__got___0_ = bf16[24,16,128]{2,1,0:T(8,128)(2,1)S(1)} collective-permute-done((bf16[24,16,128]{2,1,0:T(8,128)(2,1)S(1)}, bf16[24,16,128]{2,1,0:T(8,128)(2,1)S(1)}, u32[]{:S(2)}, u32[]{:S(2)}) %collective-permute-start.7) | collective-permute-done | bytes 98336 | tf_op jit(solution)/shard_map/ppermute | solution.py:208
  24.0 1.0 %shard_map.66 = (bf16[16,16,128]{2,1,0:T(8,128)(2,1)S(1)}, f32[16,2048]{1,0:T(8,128)S(1)}, bf16[16,16,128]{2,1,0:T(8,128)(2,1)S(1)}) custom-call(bf16[24,16,128]{2,1,0:T(8,128)(2,1)S(1)} %collective-permute-done.7.ins__got___0_, f32[16,2048]{1,0:T(8,128)S(1)} %get-tuple-element.70.ins__held___0_, s32[8,128]{1,0:T(8,128)S(1)} %pad.4.ins__index___0_.ins__next_index___0_, ...), custom_call_target="tpu_custom_call" | custom-call | tf_op jit(solution)/shard_map/pallas_call | solution.py:166
  25.0 1.5 %collective-permute-start.9 = (f32[16,2048]{1,0:T(8,128)S(1)}, f32[16,2048]{1,0:T(8,128)S(1)}, u32[]{:S(2)}, u32[]{:S(2)}) collective-permute-start(f32[16,2048]{1,0:T(8,128)S(1)} %get-tuple-element.35), channel_id=1, source_target_pairs={{0,16},{16,0},{1,17},{17,1},{2,18},{18,2},{3,19},{19,3},{4,20},{20... | collective-permute-start | bytes 393224 | tf_op jit(solution)/shard_map/ppermute | solution.py:214
  26.6 1.0 %shard_map.68 = f32[16,2048]{1,0:T(8,128)S(1)} custom-call(f32[16,2048]{1,0:T(8,128)S(1)} %collective-permute-done.1.ins__held___1_, s32[8,128]{1,0:T(8,128)S(1)} %pad.4.ins__index___0_.ins__next_index___0_, s32[8,128]{1,0:T(8,128)S(1)} %collective-permute-done.2.ins__index___1_.ins__next_index___1_, f32[32,8,128]{2,1,0:T(8,128)S(1)} %shard_map.65.ins__inverse__, ...), custom_call_target="tpu_custom_call" | custom-call | tf_op jit(solution)/shard_map/pallas_call | solution.py:166
  27.5 0.6 collective-permute-start.10
  28.1 1.5 %collective-permute-start.11 = (s32[8,128]{1,0:T(8,128)S(1)}, s32[8,128]{1,0:T(8,128)S(1)}, u32[]{:S(2)}, u32[]{:S(2)}) collective-permute-start(s32[8,128]{1,0:T(8,128)S(1)} %pad.4.ins__index___0_.ins__next_index___0_), channel_id=1, source_target_pairs={{0,16},{16,0},{1,17},{17,1},{2,18},{18,2},{3,19},{19,3},{4,20},{20... | collective-permute-start | bytes 12296 | tf_op jit(solution)/shard_map/ppermute | solution.py:214
  30.2 1.3 %collective-permute-done.9.ins__held___0_ = f32[16,2048]{1,0:T(8,128)S(1)} collective-permute-done((f32[16,2048]{1,0:T(8,128)S(1)}, f32[16,2048]{1,0:T(8,128)S(1)}, u32[]{:S(2)}, u32[]{:S(2)}) %collective-permute-start.9) | collective-permute-done | bytes 131104 | tf_op jit(solution)/shard_map/ppermute | solution.py:214
  31.5 1.1 %shard_map.67.ins__begun__ = f32[16,16,128]{2,1,0:T(8,128)S(1)} custom-call(f32[16,2048]{1,0:T(8,128)S(1)} %collective-permute-done.9.ins__held___0_, s32[8,128]{1,0:T(8,128)S(1)} %pad.4.ins__index___0_.ins__next_index___0_, s32[8,128]{1,0:T(8,128)S(1)} %collective-permute-done.2.ins__index___1_.ins__next_index___1_, bf16[32,128,128]{2,1,0:T(8,128)(2,1)S(1)} %bitcast.60), custom_call_target="tpu_custom_call" | custom-call | tf_op jit(solution)/shard_map/pallas_call | solution.py:166
  32.7 1.7 %collective-permute-done.11.ins__next_index___0_.ins__index___0_ = s32[8,128]{1,0:T(8,128)S(1)} collective-permute-done((s32[8,128]{1,0:T(8,128)S(1)}, s32[8,128]{1,0:T(8,128)S(1)}, u32[]{:S(2)}, u32[]{:S(2)}) %collective-permute-start.11) | collective-permute-done | bytes 4128 | tf_op jit(solution)/shard_map/ppermute | solution.py:214
  34.4 1.2 %shard_map.69 = (bf16[18,16,128]{2,1,0:T(8,128)(2,1)S(1)}, f32[16,16,128]{2,1,0:T(8,128)S(1)}) custom-call(f32[16,16,128]{2,1,0:T(8,128)S(1)} %shard_map.67.ins__begun__, bf16[2,16,128]{2,1,0:T(8,128)(2,1)S(1)} %get-tuple-element.71.ins__dealt__, f32[16,2048]{1,0:T(8,128)S(1)} %collective-permute-done.10.ins__held___1_, ...), custom_call_target="tpu_custom_call" | custom-call | tf_op jit(solution)/shard_map/pallas_call | solution.py:166
  35.6 1.4 %collective-permute-start.15 = (bf16[18,16,128]{2,1,0:T(8,128)(2,1)S(1)}, bf16[18,16,128]{2,1,0:T(8,128)(2,1)S(1)}, u32[]{:S(2)}, u32[]{:S(2)}) collective-permute-start(bf16[18,16,128]{2,1,0:T(8,128)(2,1)S(1)} %get-tuple-element.41), channel_id=1, source_target_pairs={{0,6},{1,7},{2,4},{3,5},{4,2},{5,3},{6,0},{7,1},{8,14},{9,15},{10,... | collective-permute-start | bytes 221192 | tf_op jit(solution)/shard_map/ppermute | solution.py:208
  36.9 1.9 %collective-permute-start.14 = (bf16[18,16,128]{2,1,0:T(8,128)(2,1)S(1)}, bf16[18,16,128]{2,1,0:T(8,128)(2,1)S(1)}, u32[]{:S(2)}, u32[]{:S(2)}) collective-permute-start(bf16[18,16,128]{2,1,0:T(8,128)(2,1)S(1)} %get-tuple-element.41), channel_id=1, source_target_pairs={{0,4},{1,5},{2,6},{3,7},{4,0},{5,1},{6,2},{7,3},{8,12},{9,13},{10,... | collective-permute-start | bytes 221192 | tf_op jit(solution)/shard_map/ppermute | solution.py:208
  39.1 1.8 %collective-permute-done.15 = bf16[18,16,128]{2,1,0:T(8,128)(2,1)S(1)} collective-permute-done((bf16[18,16,128]{2,1,0:T(8,128)(2,1)S(1)}, bf16[18,16,128]{2,1,0:T(8,128)(2,1)S(1)}, u32[]{:S(2)}, u32[]{:S(2)}) %collective-permute-start.15) | collective-permute-done | bytes 73760 | tf_op jit(solution)/shard_map/ppermute | solution.py:208
  40.9 1.1 %collective-permute-done.14 = bf16[18,16,128]{2,1,0:T(8,128)(2,1)S(1)} collective-permute-done((bf16[18,16,128]{2,1,0:T(8,128)(2,1)S(1)}, bf16[18,16,128]{2,1,0:T(8,128)(2,1)S(1)}, u32[]{:S(2)}, u32[]{:S(2)}) %collective-permute-start.14) | collective-permute-done | bytes 73760 | tf_op jit(solution)/shard_map/ppermute | solution.py:208
  42.0 1.2 %collective-permute-done.13 = bf16[18,16,128]{2,1,0:T(8,128)(2,1)S(1)} collective-permute-done((bf16[18,16,128]{2,1,0:T(8,128)(2,1)S(1)}, bf16[18,16,128]{2,1,0:T(8,128)(2,1)S(1)}, u32[]{:S(2)}, u32[]{:S(2)}) %collective-permute-start.13) | collective-permute-done | bytes 73760 | tf_op jit(solution)/shard_map/ppermute | solution.py:208
  43.4 2.5 %collective-permute-start.16 = (bf16[24,16,128]{2,1,0:T(8,128)(2,1)S(1)}, bf16[24,16,128]{2,1,0:T(8,128)(2,1)S(1)}, u32[]{:S(2)}, u32[]{:S(2)}) collective-permute-start(bf16[24,16,128]{2,1,0:T(8,128)(2,1)S(1)} %constant_dynamic-update-slice_fusion.4.ins__sent__), channel_id=1, source_target_pairs={{0,8},{1,9},{2,10},{3,11},{4,12},{5,13},{6,14},{7,15},{8,0},{9,1},... | collective-permute-start | bytes 294920 | tf_op jit(solution)/shard_map/ppermute | solution.py:208
  46.1 1.0 %collective-permute-done.17.ins__next_index___1_.ins__index___1_ = s32[8,128]{1,0:T(8,128)S(1)} collective-permute-done((s32[8,128]{1,0:T(8,128)S(1)}, s32[8,128]{1,0:T(8,128)S(1)}, u32[]{:S(2)}, u32[]{:S(2)}) %collective-permute-start.17) | collective-permute-done | bytes 4128 | tf_op jit(solution)/shard_map/ppermute | solution.py:204
  47.0 4.6 %collective-permute-done.16.ins__got___0_ = bf16[24,16,128]{2,1,0:T(8,128)(2,1)S(1)} collective-permute-done((bf16[24,16,128]{2,1,0:T(8,128)(2,1)S(1)}, bf16[24,16,128]{2,1,0:T(8,128)(2,1)S(1)}, u32[]{:S(2)}, u32[]{:S(2)}) %collective-permute-start.16) | collective-permute-done | bytes 98336 | tf_op jit(solution)/shard_map/ppermute | solution.py:208
  51.6 2.4 %shard_map.70 = (bf16[16,16,128]{2,1,0:T(8,128)(2,1)S(1)}, f32[16,2048]{1,0:T(8,128)S(1)}, f32[16,2048]{1,0:T(8,128)S(1)}, bf16[16,16,128]{2,1,0:T(8,128)(2,1)S(1)}, f32[16,16,128]{2,1,0:T(8,128)S(1)}) custom-call(bf16[24,16,128]{2,1,0:T(8,128)(2,1)S(1)} %collective-permute-done.16.ins__got___0_, f32[16,2048]{1,0:T(8,128)S(1)} %collective-permute-done.9.ins__held___0_, ...), custom_call_target="tpu_custom_call" | custom-call | tf_op jit(solution)/shard_map/pallas_call | solution.py:166
  54.1 1.6 %collective-permute-start.23 = (bf16[16,16,128]{2,1,0:T(8,128)(2,1)S(1)}, bf16[16,16,128]{2,1,0:T(8,128)(2,1)S(1)}, u32[]{:S(2)}, u32[]{:S(2)}) collective-permute-start(bf16[16,16,128]{2,1,0:T(8,128)(2,1)S(1)} %get-tuple-element.49), channel_id=1, source_target_pairs={{0,6},{1,7},{2,4},{3,5},{4,2},{5,3},{6,0},{7,1},{8,14},{9,15},{10,... | collective-permute-start | bytes 196616 | tf_op jit(solution)/shard_map/ppermute | solution.py:208
  55.6 2.4 %collective-permute-start.22 = (bf16[16,16,128]{2,1,0:T(8,128)(2,1)S(1)}, bf16[16,16,128]{2,1,0:T(8,128)(2,1)S(1)}, u32[]{:S(2)}, u32[]{:S(2)}) collective-permute-start(bf16[16,16,128]{2,1,0:T(8,128)(2,1)S(1)} %get-tuple-element.49), channel_id=1, source_target_pairs={{0,4},{1,5},{2,6},{3,7},{4,0},{5,1},{6,2},{7,3},{8,12},{9,13},{10,... | collective-permute-start | bytes 196616 | tf_op jit(solution)/shard_map/ppermute | solution.py:208
  58.0 1.4 %collective-permute-start.8 = (bf16[16,16,128]{2,1,0:T(8,128)(2,1)S(1)}, bf16[16,16,128]{2,1,0:T(8,128)(2,1)S(1)}, u32[]{:S(2)}, u32[]{:S(2)}) collective-permute-start(bf16[16,16,128]{2,1,0:T(8,128)(2,1)S(1)} %get-tuple-element.34), channel_id=1, source_target_pairs={{0,16},{16,0},{1,17},{17,1},{2,18},{18,2},{3,19},{19,3},{4,20},{20... | collective-permute-start | bytes 196616 | tf_op jit(solution)/shard_map/ppermute | solution.py:214
  59.8 1.3 %collective-permute-done.22 = bf16[16,16,128]{2,1,0:T(8,128)(2,1)S(1)} collective-permute-done((bf16[16,16,128]{2,1,0:T(8,128)(2,1)S(1)}, bf16[16,16,128]{2,1,0:T(8,128)(2,1)S(1)}, u32[]{:S(2)}, u32[]{:S(2)}) %collective-permute-start.22) | collective-permute-done | bytes 65568 | tf_op jit(solution)/shard_map/ppermute | solution.py:208
  61.1 1.2 %collective-permute-done.21 = bf16[16,16,128]{2,1,0:T(8,128)(2,1)S(1)} collective-permute-done((bf16[16,16,128]{2,1,0:T(8,128)(2,1)S(1)}, bf16[16,16,128]{2,1,0:T(8,128)(2,1)S(1)}, u32[]{:S(2)}, u32[]{:S(2)}) %collective-permute-start.21) | collective-permute-done | bytes 65568 | tf_op jit(solution)/shard_map/ppermute | solution.py:208
  62.3 1.1 %collective-permute-start.24 = (bf16[16,16,128]{2,1,0:T(8,128)(2,1)S(1)}, bf16[16,16,128]{2,1,0:T(8,128)(2,1)S(1)}, u32[]{:S(2)}, u32[]{:S(2)}) collective-permute-start(bf16[16,16,128]{2,1,0:T(8,128)(2,1)S(1)} %get-tuple-element.61), channel_id=1, source_target_pairs={{0,8},{1,9},{2,10},{3,11},{4,12},{5,13},{6,14},{7,15},{8,0},{9,1},... | collective-permute-start | bytes 196616 | tf_op jit(solution)/shard_map/ppermute | solution.py:208
  63.4 1.3 %shard_map.71.ins__inverse__ = f32[32,8,128]{2,1,0:T(8,128)S(1)} custom-call(s32[8,128]{1,0:T(8,128)S(1)} %collective-permute-done.11.ins__next_index___0_.ins__index___0_, s32[8,128]{1,0:T(8,128)S(1)} %collective-permute-done.17.ins__next_index___1_.ins__index___1_, ...), custom_call_target="tpu_custom_call" | custom-call | tf_op jit(solution)/shard_map/pallas_call | solution.py:166
  64.7 3.1 %collective-permute-done.24.ins__got___0_ = bf16[16,16,128]{2,1,0:T(8,128)(2,1)S(1)} collective-permute-done((bf16[16,16,128]{2,1,0:T(8,128)(2,1)S(1)}, bf16[16,16,128]{2,1,0:T(8,128)(2,1)S(1)}, u32[]{:S(2)}, u32[]{:S(2)}) %collective-permute-start.24) | collective-permute-done | bytes 65568 | tf_op jit(solution)/shard_map/ppermute | solution.py:208
  67.8 2.4 %shard_map.72 = (f32[16,2048]{1,0:T(8,128)S(1)}, f32[16,2048]{1,0:T(8,128)S(1)}, bf16[16,16,128]{2,1,0:T(8,128)(2,1)S(1)}, f32[16,16,128]{2,1,0:T(8,128)S(1)}) custom-call(bf16[16,16,128]{2,1,0:T(8,128)(2,1)S(1)} %collective-permute-done.8.ins__counts__, bf16[16,16,128]{2,1,0:T(8,128)(2,1)S(1)} %collective-permute-done.24.ins__got___0_, ...), custom_call_target="tpu_custom_call" | custom-call | tf_op jit(solution)/shard_map/pallas_call | solution.py:166
  70.3 2.1 %collective-permute-start.26 = (bf16[16,16,128]{2,1,0:T(8,128)(2,1)S(1)}, bf16[16,16,128]{2,1,0:T(8,128)(2,1)S(1)}, u32[]{:S(2)}, u32[]{:S(2)}) collective-permute-start(bf16[16,16,128]{2,1,0:T(8,128)(2,1)S(1)} %get-tuple-element.55), channel_id=1, source_target_pairs={{0,4},{1,5},{2,6},{3,7},{4,0},{5,1},{6,2},{7,3},{8,12},{9,13},{10,... | collective-permute-start | bytes 196616 | tf_op jit(solution)/shard_map/ppermute | solution.py:208
  72.4 1.4 %collective-permute-start.25 = (bf16[16,16,128]{2,1,0:T(8,128)(2,1)S(1)}, bf16[16,16,128]{2,1,0:T(8,128)(2,1)S(1)}, u32[]{:S(2)}, u32[]{:S(2)}) collective-permute-start(bf16[16,16,128]{2,1,0:T(8,128)(2,1)S(1)} %get-tuple-element.55), channel_id=1, source_target_pairs={{0,2},{1,3},{2,0},{3,1},{4,6},{5,7},{6,4},{7,5},{8,10},{9,11},{10,... | collective-permute-start | bytes 196616 | tf_op jit(solution)/shard_map/ppermute | solution.py:208
  73.8 1.7 %collective-permute-done.27 = bf16[16,16,128]{2,1,0:T(8,128)(2,1)S(1)} collective-permute-done((bf16[16,16,128]{2,1,0:T(8,128)(2,1)S(1)}, bf16[16,16,128]{2,1,0:T(8,128)(2,1)S(1)}, u32[]{:S(2)}, u32[]{:S(2)}) %collective-permute-start.27) | collective-permute-done | bytes 65568 | tf_op jit(solution)/shard_map/ppermute | solution.py:208
  75.4 1.2 %collective-permute-done.25 = bf16[16,16,128]{2,1,0:T(8,128)(2,1)S(1)} collective-permute-done((bf16[16,16,128]{2,1,0:T(8,128)(2,1)S(1)}, bf16[16,16,128]{2,1,0:T(8,128)(2,1)S(1)}, u32[]{:S(2)}, u32[]{:S(2)}) %collective-permute-start.25) | collective-permute-done | bytes 65568 | tf_op jit(solution)/shard_map/ppermute | solution.py:208
  76.7 1.6 %collective-permute-start.28 = (bf16[16,16,128]{2,1,0:T(8,128)(2,1)S(1)}, bf16[16,16,128]{2,1,0:T(8,128)(2,1)S(1)}, u32[]{:S(2)}, u32[]{:S(2)}) collective-permute-start(bf16[16,16,128]{2,1,0:T(8,128)(2,1)S(1)} %get-tuple-element.59), channel_id=1, source_target_pairs={{0,8},{1,9},{2,10},{3,11},{4,12},{5,13},{6,14},{7,15},{8,0},{9,1},... | collective-permute-start | bytes 196616 | tf_op jit(solution)/shard_map/ppermute | solution.py:208
  78.3 3.7 %collective-permute-done.28.ins__got___0_ = bf16[16,16,128]{2,1,0:T(8,128)(2,1)S(1)} collective-permute-done((bf16[16,16,128]{2,1,0:T(8,128)(2,1)S(1)}, bf16[16,16,128]{2,1,0:T(8,128)(2,1)S(1)}, u32[]{:S(2)}, u32[]{:S(2)}) %collective-permute-start.28) | collective-permute-done | bytes 65568 | tf_op jit(solution)/shard_map/ppermute | solution.py:208
  82.1 1.0 %shard_map.73 = (f32[16,2048]{1,0:T(8,128)S(1)}, bf16[16,16,128]{2,1,0:T(8,128)(2,1)S(1)}) custom-call(bf16[16,16,128]{2,1,0:T(8,128)(2,1)S(1)} %get-tuple-element.53.ins__counts__, bf16[16,16,128]{2,1,0:T(8,128)(2,1)S(1)} %collective-permute-done.28.ins__got___0_, f32[16,2048]{1,0:T(8,128)S(1)} %get-tuple-element.56.ins__held___1_, ...), custom_call_target="tpu_custom_call" | custom-call | tf_op jit(solution)/shard_map/pallas_call | solution.py:166
  83.2 1.0 %shard_map.74 = f32[16,2048]{1,0:T(8,128)S(1)} custom-call(f32[16,2048]{1,0:T(8,128)S(1)} %get-tuple-element.52.ins__held___0_, s32[8,128]{1,0:T(8,128)S(1)} %pad.4.ins__index___0_.ins__next_index___0_, s32[8,128]{1,0:T(8,128)S(1)} %collective-permute-done.2.ins__index___1_.ins__next_index___1_, f32[32,8,128]{2,1,0:T(8,128)S(1)} %shard_map.65.ins__inverse__, ...), custom_call_target="tpu_custom_call" | custom-call | tf_op jit(solution)/shard_map/pallas_call | solution.py:166
  84.5 0.7 maximum_select_fusion
  (64 shorter events, 5.1 us)
Async XLA Ops:
  0.0 6.4 %collective-permute-start.3 = (bf16[32,128,128]{2,1,0:T(8,128)(2,1)}, bf16[32,128,128]{2,1,0:T(8,128)(2,1)S(1)}, u32[]{:S(2)}, u32[]{:S(2)}) collective-permute-start(bf16[32,128,128]{2,1,0:T(8,128)(2,1)} %bitcast.56), channel_id=1, source_target_pairs={{0,1},{1,0},{2,3},{3,2},{4,5},{5,4},{6,7},{7,6},{8,9},{9,8},{10,11... | collective-permute-start | bytes 3145736 | tf_op jit(solution)/shard_map/ppermute | solution.py:204
  0.5 1.6 %copy-start.1 = (s32[1,64,128]{2,1,0:T(8,128)S(1)}, s32[1,64,128]{2,1,0:T(8,128)}, u32[]{:S(2)}) copy-start(s32[1,64,128]{2,1,0:T(8,128)} %param.11) | copy-start | bytes 98308
  1.2 0.7 copy-start.2
  1.2 0.7 copy-start.3
  1.9 4.5 %collective-permute-start.2 = (s32[8,128]{1,0:T(8,128)S(1)}, s32[8,128]{1,0:T(8,128)S(1)}, u32[]{:S(2)}, u32[]{:S(2)}) collective-permute-start(s32[8,128]{1,0:T(8,128)S(1)} %pad.4.ins__index___0_.ins__next_index___0_), channel_id=1, source_target_pairs={{0,1},{1,0},{2,3},{3,2},{4,5},{5,4},{6,7},{7,6},{8,9},{9,8},{10,11... | collective-permute-start | bytes 12296 | tf_op jit(solution)/shard_map/ppermute | solution.py:204
  2.6 3.0 %collective-permute-start = (bf16[1,2,16,128]{3,2,0,1:T(8,128)(2,1)}, bf16[1,2,16,128]{3,2,0,1:T(8,128)(2,1)}, u32[]{:S(2)}, u32[]{:S(2)}) collective-permute-start(bf16[1,2,16,128]{3,2,0,1:T(8,128)(2,1)} %get-tuple-element.74), channel_id=1, source_target_pairs={{0,1},{1,0},{2,3},{3,2},{4,5},{5,4},{6,7},{7,6},{8,9},{9,8},{10,11... | collective-permute-start | bytes 24584 | tf_op jit(solution)/shard_map/ppermute | solution.py:204
  4.1 2.4 %copy-start = (bf16[1,32,128,128]{3,2,1,0:T(8,128)(2,1)S(1)}, bf16[1,32,128,128]{3,2,1,0:T(8,128)(2,1)}, u32[]{:S(2)}) copy-start(bf16[1,32,128,128]{3,2,1,0:T(8,128)(2,1)} %param.7) | copy-start | bytes 3145732
  4.1 2.4 %collective-permute-start.1 = (f32[16,2048]{1,0:T(8,128)S(1)}, f32[16,2048]{1,0:T(8,128)S(1)}, u32[]{:S(2)}, u32[]{:S(2)}) collective-permute-start(f32[16,2048]{1,0:T(8,128)S(1)} %get-tuple-element.69), channel_id=1, source_target_pairs={{0,1},{1,0},{2,3},{3,2},{4,5},{5,4},{6,7},{7,6},{8,9},{9,8},{10,11... | collective-permute-start | bytes 393224 | tf_op jit(solution)/shard_map/ppermute | solution.py:204
  8.2 6.7 %collective-permute-start.6 = (bf16[18,16,128]{2,1,0:T(8,128)(2,1)S(1)}, bf16[18,16,128]{2,1,0:T(8,128)(2,1)S(1)}, u32[]{:S(2)}, u32[]{:S(2)}) collective-permute-start(bf16[18,16,128]{2,1,0:T(8,128)(2,1)S(1)} %get-tuple-element.33), channel_id=1, source_target_pairs={{0,6},{1,7},{2,4},{3,5},{4,2},{5,3},{6,0},{7,1},{8,14},{9,15},{10,... | collective-permute-start | bytes 221192 | tf_op jit(solution)/shard_map/ppermute | solution.py:208
  12.1 4.4 %collective-permute-start.5 = (bf16[18,16,128]{2,1,0:T(8,128)(2,1)S(1)}, bf16[18,16,128]{2,1,0:T(8,128)(2,1)S(1)}, u32[]{:S(2)}, u32[]{:S(2)}) collective-permute-start(bf16[18,16,128]{2,1,0:T(8,128)(2,1)S(1)} %get-tuple-element.33), channel_id=1, source_target_pairs={{0,4},{1,5},{2,6},{3,7},{4,0},{5,1},{6,2},{7,3},{8,12},{9,13},{10,... | collective-permute-start | bytes 221192 | tf_op jit(solution)/shard_map/ppermute | solution.py:208
  12.6 4.4 %collective-permute-start.4 = (bf16[18,16,128]{2,1,0:T(8,128)(2,1)S(1)}, bf16[18,16,128]{2,1,0:T(8,128)(2,1)S(1)}, u32[]{:S(2)}, u32[]{:S(2)}) collective-permute-start(bf16[18,16,128]{2,1,0:T(8,128)(2,1)S(1)} %get-tuple-element.33), channel_id=1, source_target_pairs={{0,2},{1,3},{2,0},{3,1},{4,6},{5,7},{6,4},{7,5},{8,10},{9,11},{10,... | collective-permute-start | bytes 221192 | tf_op jit(solution)/shard_map/ppermute | solution.py:208
  12.8 21.6 %collective-permute-start.12 = (bf16[16,128,128]{2,1,0:T(8,128)(2,1)S(1)}, bf16[16,128,128]{2,1,0:T(8,128)(2,1)S(1)}, u32[]{:S(2)}, u32[]{:S(2)}) collective-permute-start(bf16[16,128,128]{2,1,0:T(8,128)(2,1)S(1)} %get-tuple-element.38), channel_id=1, source_target_pairs={{0,16},{16,0},{1,17},{17,1},{2,18},{18,2},{3,19},{19,3},{4,20},{20... | collective-permute-start | bytes 1572872 | tf_op jit(solution)/shard_map/ppermute | solution.py:214
  17.1 6.9 %collective-permute-start.7 = (bf16[24,16,128]{2,1,0:T(8,128)(2,1)S(1)}, bf16[24,16,128]{2,1,0:T(8,128)(2,1)S(1)}, u32[]{:S(2)}, u32[]{:S(2)}) collective-permute-start(bf16[24,16,128]{2,1,0:T(8,128)(2,1)S(1)} %constant_dynamic-update-slice_fusion.ins__sent__), channel_id=1, source_target_pairs={{0,8},{1,9},{2,10},{3,11},{4,12},{5,13},{6,14},{7,15},{8,0},{9,1},... | collective-permute-start | bytes 294920 | tf_op jit(solution)/shard_map/ppermute | solution.py:208
  25.0 6.5 %collective-permute-start.9 = (f32[16,2048]{1,0:T(8,128)S(1)}, f32[16,2048]{1,0:T(8,128)S(1)}, u32[]{:S(2)}, u32[]{:S(2)}) collective-permute-start(f32[16,2048]{1,0:T(8,128)S(1)} %get-tuple-element.35), channel_id=1, source_target_pairs={{0,16},{16,0},{1,17},{17,1},{2,18},{18,2},{3,19},{19,3},{4,20},{20... | collective-permute-start | bytes 393224 | tf_op jit(solution)/shard_map/ppermute | solution.py:214
  27.5 6.9 %collective-permute-start.10 = (f32[16,2048]{1,0:T(8,128)S(1)}, f32[16,2048]{1,0:T(8,128)S(1)}, u32[]{:S(2)}, u32[]{:S(2)}) collective-permute-start(f32[16,2048]{1,0:T(8,128)S(1)} %shard_map.68), channel_id=1, source_target_pairs={{0,16},{16,0},{1,17},{17,1},{2,18},{18,2},{3,19},{19,3},{4,20},{20... | collective-permute-start | bytes 393224 | tf_op jit(solution)/shard_map/ppermute | solution.py:214
  28.1 6.3 %collective-permute-start.11 = (s32[8,128]{1,0:T(8,128)S(1)}, s32[8,128]{1,0:T(8,128)S(1)}, u32[]{:S(2)}, u32[]{:S(2)}) collective-permute-start(s32[8,128]{1,0:T(8,128)S(1)} %pad.4.ins__index___0_.ins__next_index___0_), channel_id=1, source_target_pairs={{0,16},{16,0},{1,17},{17,1},{2,18},{18,2},{3,19},{19,3},{4,20},{20... | collective-permute-start | bytes 12296 | tf_op jit(solution)/shard_map/ppermute | solution.py:214
  29.6 13.6 %collective-permute-start.18 = (bf16[16,128,128]{2,1,0:T(8,128)(2,1)S(1)}, bf16[16,128,128]{2,1,0:T(8,128)(2,1)S(1)}, u32[]{:S(2)}, u32[]{:S(2)}) collective-permute-start(bf16[16,128,128]{2,1,0:T(8,128)(2,1)S(1)} %get-tuple-element.45), channel_id=1, source_target_pairs={{0,16},{16,0},{1,17},{17,1},{2,18},{18,2},{3,19},{19,3},{4,20},{20... | collective-permute-start | bytes 1572872 | tf_op jit(solution)/shard_map/ppermute | solution.py:214
  35.6 5.3 %collective-permute-start.15 = (bf16[18,16,128]{2,1,0:T(8,128)(2,1)S(1)}, bf16[18,16,128]{2,1,0:T(8,128)(2,1)S(1)}, u32[]{:S(2)}, u32[]{:S(2)}) collective-permute-start(bf16[18,16,128]{2,1,0:T(8,128)(2,1)S(1)} %get-tuple-element.41), channel_id=1, source_target_pairs={{0,6},{1,7},{2,4},{3,5},{4,2},{5,3},{6,0},{7,1},{8,14},{9,15},{10,... | collective-permute-start | bytes 221192 | tf_op jit(solution)/shard_map/ppermute | solution.py:208
  36.9 5.0 %collective-permute-start.14 = (bf16[18,16,128]{2,1,0:T(8,128)(2,1)S(1)}, bf16[18,16,128]{2,1,0:T(8,128)(2,1)S(1)}, u32[]{:S(2)}, u32[]{:S(2)}) collective-permute-start(bf16[18,16,128]{2,1,0:T(8,128)(2,1)S(1)} %get-tuple-element.41), channel_id=1, source_target_pairs={{0,4},{1,5},{2,6},{3,7},{4,0},{5,1},{6,2},{7,3},{8,12},{9,13},{10,... | collective-permute-start | bytes 221192 | tf_op jit(solution)/shard_map/ppermute | solution.py:208
  38.8 4.4 %collective-permute-start.13 = (bf16[18,16,128]{2,1,0:T(8,128)(2,1)S(1)}, bf16[18,16,128]{2,1,0:T(8,128)(2,1)S(1)}, u32[]{:S(2)}, u32[]{:S(2)}) collective-permute-start(bf16[18,16,128]{2,1,0:T(8,128)(2,1)S(1)} %get-tuple-element.41), channel_id=1, source_target_pairs={{0,2},{1,3},{2,0},{3,1},{4,6},{5,7},{6,4},{7,5},{8,10},{9,11},{10,... | collective-permute-start | bytes 221192 | tf_op jit(solution)/shard_map/ppermute | solution.py:208
  39.1 12.5 %collective-permute-start.19 = (bf16[16,128,128]{2,1,0:T(8,128)(2,1)S(1)}, bf16[16,128,128]{2,1,0:T(8,128)(2,1)S(1)}, u32[]{:S(2)}, u32[]{:S(2)}) collective-permute-start(bf16[16,128,128]{2,1,0:T(8,128)(2,1)S(1)} %collective-permute-done.12.ins__next_tiles___0__0_.ins__tiles___0__0_), channel_id=1, source_target_pairs={{0,1},{1,0},{2,3},{3,2},{4,5},{5,4},{6,7},{7,6},{8,9},{9,8},{10,11... | collective-permute-start | bytes 1572872 | tf_op jit(solution)/shard_map/ppermute | solution.py:204
  43.3 8.4 %collective-permute-start.20 = (bf16[16,128,128]{2,1,0:T(8,128)(2,1)S(1)}, bf16[16,128,128]{2,1,0:T(8,128)(2,1)S(1)}, u32[]{:S(2)}, u32[]{:S(2)}) collective-permute-start(bf16[16,128,128]{2,1,0:T(8,128)(2,1)S(1)} %collective-permute-done.18.ins__next_tiles___0__1_.ins__tiles___0__1_), channel_id=1, source_target_pairs={{0,1},{1,0},{2,3},{3,2},{4,5},{5,4},{6,7},{7,6},{8,9},{9,8},{10,11... | collective-permute-start | bytes 1572872 | tf_op jit(solution)/shard_map/ppermute | solution.py:204
  43.4 8.2 %collective-permute-start.16 = (bf16[24,16,128]{2,1,0:T(8,128)(2,1)S(1)}, bf16[24,16,128]{2,1,0:T(8,128)(2,1)S(1)}, u32[]{:S(2)}, u32[]{:S(2)}) collective-permute-start(bf16[24,16,128]{2,1,0:T(8,128)(2,1)S(1)} %constant_dynamic-update-slice_fusion.4.ins__sent__), channel_id=1, source_target_pairs={{0,8},{1,9},{2,10},{3,11},{4,12},{5,13},{6,14},{7,15},{8,0},{9,1},... | collective-permute-start | bytes 294920 | tf_op jit(solution)/shard_map/ppermute | solution.py:208
  45.9 1.2 %collective-permute-start.17 = (s32[8,128]{1,0:T(8,128)S(1)}, s32[8,128]{1,0:T(8,128)S(1)}, u32[]{:S(2)}, u32[]{:S(2)}) collective-permute-start(s32[8,128]{1,0:T(8,128)S(1)} %collective-permute-done.11.ins__next_index___0_.ins__index___0_), channel_id=1, source_target_pairs={{0,1},{1,0},{2,3},{3,2},{4,5},{5,4},{6,7},{7,6},{8,9},{9,8},{10,11... | collective-permute-start | bytes 12296 | tf_op jit(solution)/shard_map/ppermute | solution.py:204
  54.1 5.7 %collective-permute-start.23 = (bf16[16,16,128]{2,1,0:T(8,128)(2,1)S(1)}, bf16[16,16,128]{2,1,0:T(8,128)(2,1)S(1)}, u32[]{:S(2)}, u32[]{:S(2)}) collective-permute-start(bf16[16,16,128]{2,1,0:T(8,128)(2,1)S(1)} %get-tuple-element.49), channel_id=1, source_target_pairs={{0,6},{1,7},{2,4},{3,5},{4,2},{5,3},{6,0},{7,1},{8,14},{9,15},{10,... | collective-permute-start | bytes 196616 | tf_op jit(solution)/shard_map/ppermute | solution.py:208
  55.6 5.4 %collective-permute-start.22 = (bf16[16,16,128]{2,1,0:T(8,128)(2,1)S(1)}, bf16[16,16,128]{2,1,0:T(8,128)(2,1)S(1)}, u32[]{:S(2)}, u32[]{:S(2)}) collective-permute-start(bf16[16,16,128]{2,1,0:T(8,128)(2,1)S(1)} %get-tuple-element.49), channel_id=1, source_target_pairs={{0,4},{1,5},{2,6},{3,7},{4,0},{5,1},{6,2},{7,3},{8,12},{9,13},{10,... | collective-permute-start | bytes 196616 | tf_op jit(solution)/shard_map/ppermute | solution.py:208
  58.0 4.3 %collective-permute-start.21 = (bf16[16,16,128]{2,1,0:T(8,128)(2,1)S(1)}, bf16[16,16,128]{2,1,0:T(8,128)(2,1)S(1)}, u32[]{:S(2)}, u32[]{:S(2)}) collective-permute-start(bf16[16,16,128]{2,1,0:T(8,128)(2,1)S(1)} %get-tuple-element.49), channel_id=1, source_target_pairs={{0,2},{1,3},{2,0},{3,1},{4,6},{5,7},{6,4},{7,5},{8,10},{9,11},{10,... | collective-permute-start | bytes 196616 | tf_op jit(solution)/shard_map/ppermute | solution.py:208
  58.0 6.6 %collective-permute-start.8 = (bf16[16,16,128]{2,1,0:T(8,128)(2,1)S(1)}, bf16[16,16,128]{2,1,0:T(8,128)(2,1)S(1)}, u32[]{:S(2)}, u32[]{:S(2)}) collective-permute-start(bf16[16,16,128]{2,1,0:T(8,128)(2,1)S(1)} %get-tuple-element.34), channel_id=1, source_target_pairs={{0,16},{16,0},{1,17},{17,1},{2,18},{18,2},{3,19},{19,3},{4,20},{20... | collective-permute-start | bytes 196616 | tf_op jit(solution)/shard_map/ppermute | solution.py:214
  62.3 5.5 %collective-permute-start.24 = (bf16[16,16,128]{2,1,0:T(8,128)(2,1)S(1)}, bf16[16,16,128]{2,1,0:T(8,128)(2,1)S(1)}, u32[]{:S(2)}, u32[]{:S(2)}) collective-permute-start(bf16[16,16,128]{2,1,0:T(8,128)(2,1)S(1)} %get-tuple-element.61), channel_id=1, source_target_pairs={{0,8},{1,9},{2,10},{3,11},{4,12},{5,13},{6,14},{7,15},{8,0},{9,1},... | collective-permute-start | bytes 196616 | tf_op jit(solution)/shard_map/ppermute | solution.py:208
  70.2 5.2 %collective-permute-start.27 = (bf16[16,16,128]{2,1,0:T(8,128)(2,1)S(1)}, bf16[16,16,128]{2,1,0:T(8,128)(2,1)S(1)}, u32[]{:S(2)}, u32[]{:S(2)}) collective-permute-start(bf16[16,16,128]{2,1,0:T(8,128)(2,1)S(1)} %get-tuple-element.55), channel_id=1, source_target_pairs={{0,6},{1,7},{2,4},{3,5},{4,2},{5,3},{6,0},{7,1},{8,14},{9,15},{10,... | collective-permute-start | bytes 196616 | tf_op jit(solution)/shard_map/ppermute | solution.py:208
  70.3 5.2 %collective-permute-start.26 = (bf16[16,16,128]{2,1,0:T(8,128)(2,1)S(1)}, bf16[16,16,128]{2,1,0:T(8,128)(2,1)S(1)}, u32[]{:S(2)}, u32[]{:S(2)}) collective-permute-start(bf16[16,16,128]{2,1,0:T(8,128)(2,1)S(1)} %get-tuple-element.55), channel_id=1, source_target_pairs={{0,4},{1,5},{2,6},{3,7},{4,0},{5,1},{6,2},{7,3},{8,12},{9,13},{10,... | collective-permute-start | bytes 196616 | tf_op jit(solution)/shard_map/ppermute | solution.py:208
  72.4 4.3 %collective-permute-start.25 = (bf16[16,16,128]{2,1,0:T(8,128)(2,1)S(1)}, bf16[16,16,128]{2,1,0:T(8,128)(2,1)S(1)}, u32[]{:S(2)}, u32[]{:S(2)}) collective-permute-start(bf16[16,16,128]{2,1,0:T(8,128)(2,1)S(1)} %get-tuple-element.55), channel_id=1, source_target_pairs={{0,2},{1,3},{2,0},{3,1},{4,6},{5,7},{6,4},{7,5},{8,10},{9,11},{10,... | collective-permute-start | bytes 196616 | tf_op jit(solution)/shard_map/ppermute | solution.py:208
  76.7 5.4 %collective-permute-start.28 = (bf16[16,16,128]{2,1,0:T(8,128)(2,1)S(1)}, bf16[16,16,128]{2,1,0:T(8,128)(2,1)S(1)}, u32[]{:S(2)}, u32[]{:S(2)}) collective-permute-start(bf16[16,16,128]{2,1,0:T(8,128)(2,1)S(1)} %get-tuple-element.59), channel_id=1, source_target_pairs={{0,8},{1,9},{2,10},{3,11},{4,12},{5,13},{6,14},{7,15},{8,0},{9,1},... | collective-permute-start | bytes 196616 | tf_op jit(solution)/shard_map/ppermute | solution.py:208
  83.1 1.4 %collective-permute-start.29 = (f32[16,2048]{1,0:T(8,128)S(1)}, f32[16,2048]{1,0:T(8,128)S(1)}, u32[]{:S(2)}, u32[]{:S(2)}) collective-permute-start(f32[16,2048]{1,0:T(8,128)S(1)} %get-tuple-element.58), channel_id=1, source_target_pairs={{0,1},{1,0},{2,3},{3,2},{4,5},{5,4},{6,7},{7,6},{8,9},{9,8},{10,11... | collective-permute-start | bytes 393224 | tf_op jit(solution)/shard_map/ppermute | solution.py:204

commit v8 on v7

--- a/solution.py
+++ b/solution.py
@@ -14,8 +14,19 @@
 VMEM_LIMIT = 40 * 1024 * 1024
 
 
-def each_live(index_ref, slots, body):
-    live = index_ref[2, 0]
+VOX, RAY, LIVE = range(3)
+
+
+def entry(index, row, t):
+    return index[row][0, t] if isinstance(index, tuple) else index[row, t]
+
+
+def core_here():
+    return lax.rem(lax.axis_index("tile"), CORES)
+
+
+def each_live(index, slots, body):
+    live = entry(index, LIVE, 0)
     for group in range(-(-slots // TILE_GROUP)):
         first, last = group * TILE_GROUP, min(slots, (group + 1) * TILE_GROUP)
 
@@ -43,7 +54,7 @@
 
 
 def slots_of(tile_refs):
-    return sum(ref.shape[0] for ref in tile_refs)
+    return sum(ref.shape[0] for ref in tile_refs) // TILE_GROUP * TILE_GROUP
 
 
 def project_into(acc, low, index_refs, sets):
@@ -55,8 +66,8 @@
 
         def body(ts):
             wide = jnp.concatenate([tile_at(tile_refs, t) for t in ts], axis=0)
-            add_products(acc, [low[k * blocks + index_ref[0, t]] for t in ts],
-                         [index_ref[1, t] for t in ts], wide, True)
+            add_products(acc, [low[k * blocks + entry(index_ref, VOX, t)] for t in ts],
+                         [entry(index_ref, RAY, t) for t in ts], wide, True)
 
         each_live(index_ref, slots_of(tile_refs), body)
 
@@ -71,8 +82,8 @@
 
         def body(ts):
             wide = jnp.concatenate([tile_at(tile_refs, t) for t in ts], axis=1)
-            add_products(acc, [ratios(index_ref[1, t]) for t in ts],
-                         [k * blocks + index_ref[0, t] for t in ts], wide, False)
+            add_products(acc, [ratios(entry(index_ref, RAY, t)) for t in ts],
+                         [k * blocks + entry(index_ref, VOX, t) for t in ts], wide, False)
 
         each_live(index_ref, slots_of(tile_refs), body)
 
@@ -85,33 +96,47 @@
                 yield k, slice(b * size, (b + 1) * size), k * blocks + b
 
 
-def write_sums(ins, outs, acc):
-    blocks = acc.shape[0]
+def frames_of(held, half, cols):
+    if held.shape[0] == half:
+        return held[:, cols]
+    return held[pl.ds(pl.multiple_of(core_here() * half, half), half), cols]
+
+
+def write_sums(r, ins, outs, acc):
+    rays, half, size = acc.shape
     outs["wide"][...] = acc[...]
     if "sent" in outs:
-        outs["sent"][:blocks] = acc[...].astype(jnp.bfloat16)
-        if "dealt" in ins:
-            outs["sent"][blocks:] = ins["dealt"][...]
+        outs["sent"][:rays] = acc[...].astype(jnp.bfloat16)
+    if "dealt" in ins:
+        core, frames = core_here(), CORES * half
+        subsets = ins["dealt"][0].shape[0] // frames
+        panel = lax.rem(lax.axis_index("subset") - r + subsets * ROUNDS, subsets)
+        rows = pl.ds(pl.multiple_of(panel * frames + core * half, half), half)
+        for side, ref in zip((core, 1 - core), ins["dealt"]):
+            held = ref.shape[1] // size
+            for b in range(held):
+                block = ref[rows, b * size:(b + 1) * size].astype(jnp.float32)
+                outs["sent"][rays + side * held + b] = block.astype(jnp.bfloat16)
 
 
 def first_kernel(ins, outs, low, acc, own, arrived):
     copy = pltpu.make_async_copy(ins["own_hbm"], own, arrived)
     copy.start()
     for k, cols, at in columns(ins["held"], low.shape[-1]):
-        low[at] = ins["held"][k][:, cols].astype(jnp.bfloat16)
+        low[at] = frames_of(ins["held"][k], low.shape[1], cols).astype(jnp.bfloat16)
     acc[...] = jnp.zeros_like(acc)
     project_into(acc, low, ins["index"], (None, ins["tiles"]))
     copy.wait()
     project_into(acc, low, ins["index"], ((own,), None))
-    write_sums(ins, outs, acc)
-
-
-def project_kernel(ins, outs, low, acc):
+    write_sums(0, ins, outs, acc)
+
+
+def project_kernel(r, ins, outs, low, acc):
     acc[...] = ins["begun"][...] if "begun" in ins else jnp.zeros_like(acc)
     for k, cols, at in columns(ins["held"], low.shape[-1]):
         low[at] = ins["held"][k][:, cols].astype(jnp.bfloat16)
     project_into(acc, low, ins["index"], ins["tiles"])
-    write_sums(ins, outs, acc)
+    write_sums(r, ins, outs, acc)
 
 
 def sensitivity_kernel(ins, outs, acc):
@@ -128,10 +153,11 @@
     if "counts" in ins:
         counts[...] = ins["counts"][...]
     else:
-        place = ins["index"][0][3, 0]
+        unit = min(masks)
+        place = lax.rem(lax.div(lax.axis_index("tile"), CORES * unit), len(masks) + 1)
         share = ins["sent"].shape[0] - rays
         for mask, part in zip((0,) + masks, (ins["sent"],) + tuple(ins["got"])):
-            counts[pl.ds((place ^ mask) * share, share)] = part[rays:]
+            counts[pl.ds((place ^ mask // unit) * share, share)] = part[rays:]
     if "counts" in outs:
         outs["counts"][...] = counts[...]
     ratios[...] = (counts[...].astype(jnp.float32) / total).astype(jnp.bfloat16)
@@ -139,7 +165,7 @@
         outs["ratios"][...] = ratios[...]
 
 
-def update_kernel(masks, ins, outs, back, *scratch):
+def update_kernel(masks, r, ins, outs, back, *scratch):
     if "ratios" in ins:
         ratios = ins["ratios"]
     else:
@@ -147,17 +173,19 @@
         form_ratios(masks, ins, outs, counts, ratios)
     back_into(back, lambda ray: ratios[ray], ins["index"], ins["tiles"])
     for k, cols, at in columns(ins["held"], back.shape[-1]):
-        value = ins["held"][k][:, cols] * back[at] * ins["inverse"][at, :1]
+        value = frames_of(ins["held"][k], back.shape[1], cols) * back[at] * ins["inverse"][at, :1]
         outs["held"][k][:, cols] = value
         if "sent" in outs:
             scratch[0][at] = value.astype(jnp.bfloat16)
     if "sent" in outs:
         scratch[1][...] = jnp.zeros_like(scratch[1])
         project_into(scratch[1], scratch[0], ins["next_index"], ins["next_tiles"])
-        write_sums(ins, outs, scratch[1])
+        write_sums(r + 1, ins, outs, scratch[1])
 
 
 def call(kernel, ins, outs, scratch):
+    work = 2 * 256 * 256 * 128 * 32
+
     def spec(path, _):
         name = path[0].key
         space = pltpu.SMEM if name.endswith("index") else pltpu.HBM if name.endswith("hbm") else pltpu.VMEM
@@ -169,6 +197,8 @@
         in_specs=[jax.tree_util.tree_map_with_path(spec, ins)],
         out_specs=jax.tree_util.tree_map_with_path(spec, outs),
         scratch_shapes=scratch,
+        cost_estimate=pl.CostEstimate(flops=work * len(jax.tree.leaves(ins.get("tiles"))), transcendentals=0,
+                                      bytes_accessed=0),
         compiler_params=pltpu.CompilerParams(vmem_limit_bytes=VMEM_LIMIT))(ins)
 
 
@@ -179,12 +209,12 @@
     vox_blocks = voxels // size
     own_tiles = system_tiles[0]
     slots = own_tiles.shape[0]
+    assert slots % TILE_GROUP == 0
     tile_devs = lax.axis_size("tile")
     chips = tile_devs // CORES
     rb_dev = counts.shape[2] // size
     ray_blocks = rb_dev * tile_devs
     subset_count = lax.axis_size("subset")
-    position = lax.axis_index("subset")
     core = lax.axis_index("tile") % CORES
     chip = lax.axis_index("tile") // CORES
     both = CORES * vox_blocks
@@ -216,23 +246,11 @@
     def after(array, value):
         return lax.optimization_barrier((array, value))[0]
 
-    halves = images.reshape(CORES, half, voxels)
-    mine = lax.dynamic_index_in_dim(halves, core, 0, keepdims=False)
-    theirs = lax.dynamic_index_in_dim(halves, 1 - core, 0, keepdims=False)
-    rows = jnp.concatenate([tile_vox, tile_ray, jnp.broadcast_to(live_blocks, tile_vox.shape),
-                            jnp.broadcast_to(place(steps[-1]), tile_vox.shape)], axis=0)
-    own_index = jnp.pad(rows, ((0, 4), (0, -slots % LANES)))
+    rows = (tile_vox, tile_ray, live_blocks)
     tiles = ((own_tiles,), (swap_cores(own_tiles),))
-    held = (mine, swap_cores(theirs))
-    index = (own_index, swap_cores(own_index))
-
-    dealt = counts[0].astype(bf16).reshape(subset_count, CORES, half, rb_dev, size).transpose(1, 3, 0, 2, 4)
-    kept = lax.dynamic_index_in_dim(dealt, core, 0, keepdims=False)
-    got = swap_cores(lax.dynamic_index_in_dim(dealt, 1 - core, 0, keepdims=False))
-    dealt = joined(core, kept, got)
-
-    def dealt_of(panel):
-        return lax.dynamic_index_in_dim(dealt, panel % subset_count, 1, keepdims=False)
+    held = (images, swap_cores(images))
+    index = (rows, tuple(swap_cores(row) for row in rows))
+    dealt = (counts[0], swap_cores(counts[0]))
 
     def sensitivity(index, tiles):
         return call(sensitivity_kernel, {"index": index, "tiles": tiles},
@@ -242,7 +260,17 @@
     sets = [(index, tiles, sensitivity(index, tiles))] * ROUNDS
     moves = [True] * (ROUNDS - 1)
     known = [None] * ROUNDS
-    two = subset_count == 2
+    two = subset_count == 2 and ray_blocks <= 256 and slots <= size and size == LANES
+    early = slots * 11 // 16
+    def packed(rows):
+        rows = jnp.concatenate([jnp.broadcast_to(row, (1, slots)) for row in rows], axis=0)
+        return jnp.pad(rows.astype(bf16), ((0, size - 3), (0, size - slots)))[None]
+
+    def index_of(pieces):
+        return pieces[-1][-1, :8].astype(jnp.int32)
+
+    if two:
+        far_tiles = [shift(own_tiles[:early])]
     if two:
         moves = [r == 0 for r in range(ROUNDS - 1)]
 
@@ -257,7 +285,7 @@
     def sums(r):
         fresh = known[r] is None
         sent = ray_blocks + fresh * rb_dev * CORES
-        return ({"dealt": dealt_of(position - r)} if fresh else {},
+        return ({"dealt": dealt} if fresh else {},
                 {"wide": summed, "sent": shaped((sent, half, size), bf16)})
 
     extra, outs = sums(0)
@@ -265,10 +293,7 @@
                outs, [low_scratch, sum_scratch, pltpu.VMEM(own_tiles.shape, bf16), pltpu.SemaphoreType.DMA])
     for r in range(ROUNDS):
         wide, sent = out["wide"], out["sent"]
-        if two and r == 0:
-            far_tiles = [shift(after(own_tiles[:slots // 2], sent))]
         if two and r == 1:
-            far_index = (far_index, swap_cores(after(far_index, sent)))
             far_swapped = [swap_cores(after(far_tiles[0], sent))]
         for masks in steps:
             got = [swap_chips(sent, mask) for mask in masks]
@@ -288,6 +313,7 @@
         if two and r == 1:
             far_swapped.append(swap_cores(after(far_tiles[1], wide)))
             far_tiles = (tuple(far_tiles), tuple(far_swapped))
+            far_index = tuple(index_of(pieces) for pieces in far_tiles)
             far = (far_index, far_tiles, sensitivity(far_index, far_tiles))
             sets = [far if later >= 2 and later % 2 == 0 else sets[later] for later in range(ROUNDS)]
         now_index, now_tiles, now_inverse = sets[r]
@@ -300,7 +326,7 @@
                 outs["counts"] = summed.update(dtype=bf16)
         else:
             ins["counts"] = known[r]
-        kernel = functools.partial(update_kernel, tuple(m // min(masks) for m in masks))
+        kernel = functools.partial(update_kernel, masks, r)
         last = r + 1 == ROUNDS
         if last or moves[r]:
             order = (1, 0) if last else (0, 1)
@@ -319,21 +345,18 @@
                                          {"held": only(k, (piece,) * CORES)}, [back_scratch])}
                 moved[k] = out["held"][k]
                 if two and r == 0 and k == 1:
-                    far_index = shift(after(own_index, moved[k]))
-                    far_tiles.append(shift(after(own_tiles[slots // 2:], moved[k])))
+                    far_tiles.append(shift(after(jnp.concatenate([own_tiles[early:], packed(after(rows, sent))]), moved[k])))
                 if not last:
                     moved[k] = shift(moved[k])
                 elif k == 1:
                     moved[k] = swap_cores(moved[k])
-            if two and r == 0:
-                moved[1], far_index, far_tiles[0] = lax.optimization_barrier((moved[1], far_index, far_tiles[0]))
             held = (moved[0], moved[1])
             if not last:
                 extra, more = sums(r + 1)
-                begun = call(project_kernel, {"held": only(0, held), "index": sets[r + 1][0],
+                begun = call(functools.partial(project_kernel, r + 1), {"held": only(0, held), "index": sets[r + 1][0],
                                               "tiles": only(0, sets[r + 1][1])},
                              {"wide": summed}, [low_scratch, sum_scratch])["wide"]
-                out = call(project_kernel, {"held": only(1, held), "index": sets[r + 1][0], "begun": begun,
+                out = call(functools.partial(project_kernel, r + 1), {"held": only(1, held), "index": sets[r + 1][0], "begun": begun,
                                             "tiles": only(1, sets[r + 1][1]), **extra},
                            more, [low_scratch, sum_scratch])
         else:

time: 85.5 us -> 88.2 us (1.032)
  Pallas kernels: 15.4 us -> 20.7 us
  starting transfers between devices: 32.3 us -> 31.2 us
  local copies, waits for them, and re-layouts: 3.84 us -> 2.88 us
    pallas_call x11, Pallas kernels: 15.4 us -> 20.7 us  [call(): pl.pallas_call(kernel, out_shape=outs, in_specs=[jax.tree_util.tree_map_w...]
    ppermute x16, waiting for transfers between devices: 26.6 us -> 28.2 us  [swap_chips(): return lax.ppermute(array, 'tile', pairs)]
    squeeze x3 -> x0, local copies, waits for them, and re-layouts: 1.6 us -> none  [the longest x1 0.99 us: shards(): theirs = lax.dynamic_index_in_dim(halves, 1 - core, 0, keepdims=False)]
    ppermute x16, starting transfers between devices: 23.5 us -> 22.2 us  [swap_chips(): return lax.ppermute(array, 'tile', pairs)]
    ppermute x8 -> x9, waiting for transfers between devices: 1.32 us -> 0.02 us  [swap_cores(): return lax.ppermute(array, 'tile', [(i, i ^ 1) for i in range(tile_devs)])]
    slice x1 -> x2, local copies, waits for them, and re-layouts: 1.34 us -> 2.07 us  [the longest x1 2.05 us: shards(): far_tiles = [shift(own_tiles[:early])]]
    ppermute x6 -> x5, waiting for transfers between devices: 3.09 us -> 2.83 us  [shift(): lax.ppermute(array, 'subset', [(i, (i + 1) % subset_count) for i in range...]
    ppermute x6 -> x5, starting transfers between devices: 7.37 us -> 7.36 us  [shift(): lax.ppermute(array, 'subset', [(i, (i + 1) % subset_count) for i in range...]
  transfers between devices with their start and end apart: 30 -> 30, of which waited for: 19 -> 17; matrix products, arithmetic and copies ran while one was open for 5% -> 3% of each run, Pallas kernels for 9% -> 15%
where the time goes in v8:
time: 88.2 us; the launch traced here: 87.9 us
  starting transfers between devices  31.2 us (35%)
  waiting for transfers between devices  31 us (35%)
  Pallas kernels  20.7 us (23%)
  local copies, waits for them, and re-layouts  2.88 us (3%)
  between operations  1.03 us (1%)
  other arithmetic  1.01 us (1%)
    ppermute x16, waiting for transfers between devices, swap_chips(): return lax.ppermute(array, 'tile', pairs)  28.2 us
    ppermute x16, starting transfers between devices, swap_chips(): return lax.ppermute(array, 'tile', pairs)  22.2 us
    pallas_call x11, Pallas kernels, call(): pl.pallas_call(kernel, out_shape=outs, in_specs=[jax.tree_util.tree_map_w...  20.7 us
    ppermute x5, starting transfers between devices, shift(): lax.ppermute(array, 'subset', [(i, (i + 1) % subset_count) for i in range...  7.36 us
    ppermute x5, waiting for transfers between devices, shift(): lax.ppermute(array, 'subset', [(i, (i + 1) % subset_count) for i in range...  2.83 us
    slice x1, local copies, waits for them, and re-layouts, shards(): far_tiles = [shift(own_tiles[:early])]  2.05 us
  transfers between devices with their start and end apart: 30, of which 17 were waited for; matrix products, arithmetic and copies ran while one was open for 3% of the time, Pallas kernels for 15%

profile of v8, /device:TPU:0, one launch (start us, length us, event | category | flops | bytes accessed | tf_op | source)
XLA Modules:
  0.0 87.9 jit_solution(6126515118541246468)
XLA Ops:
  1.5 2.0 %slice_bitcast_fusion = bf16[22,128,128]{2,1,0:T(8,128)(2,1)} fusion(bf16[1,32,128,128]{3,2,1,0:T(8,128)(2,1)} %param.7), kind=kLoop, calls=%fused_computation | loop fusion | bytes 1441792 | tf_op jit(solution)/shard_map/slice | solution.py:273
  4.4 0.6 copy-done.4
  5.0 2.9 %collective-permute-start.19 = (bf16[22,128,128]{2,1,0:T(8,128)(2,1)}, bf16[22,128,128]{2,1,0:T(8,128)(2,1)S(1)}, u32[]{:S(2)}, u32[]{:S(2)}) collective-permute-start(bf16[22,128,128]{2,1,0:T(8,128)(2,1)} %slice_bitcast_fusion), channel_id=1, source_target_pairs={{0,16},{16,0},{1,17},{17,1},{2,18},{18,2},{3,19},{19,3},{4,20},{20... | collective-permute-start | bytes 2162696 | tf_op jit(solution)/shard_map/ppermute | solution.py:244
  8.0 2.3 %shard_map.64 = (bf16[18,16,128]{2,1,0:T(8,128)(2,1)S(1)}, f32[16,16,128]{2,1,0:T(8,128)S(1)}) custom-call(s32[64,128]{1,0:T(8,128)S(1)} %bitcast.62, s32[64,128]{1,0:T(8,128)S(1)} %collective-permute-done.ins__dealt___1_, f32[32,2048]{1,0:T(8,128)S(1)} %copy-done.1, f32[32,2048]{1,0:T(8,128)S(1)} %collective-permute-done.1.ins__held___1_, ...), custom_call_target="tpu_custom_call" | custom-call | flops 536870912 | tf_op jit(solution)/shard_map/pallas_call | solution.py:194
  10.3 2.6 %collective-permute-start.8 = (bf16[18,16,128]{2,1,0:T(8,128)(2,1)S(1)}, bf16[18,16,128]{2,1,0:T(8,128)(2,1)S(1)}, u32[]{:S(2)}, u32[]{:S(2)}) collective-permute-start(bf16[18,16,128]{2,1,0:T(8,128)(2,1)S(1)} %get-tuple-element.30), channel_id=1, source_target_pairs={{0,6},{1,7},{2,4},{3,5},{4,2},{5,3},{6,0},{7,1},{8,14},{9,15},{10,... | collective-permute-start | bytes 221192 | tf_op jit(solution)/shard_map/ppermute | solution.py:238
  13.3 0.5 collective-permute-start.6
  13.8 1.8 %shard_map.65.ins__inverse__ = f32[32,8,128]{2,1,0:T(8,128)S(1)} custom-call(s32[1,32]{1,0:T(1,128)S(1)} %copy-done.3, s32[1,32]{1,0:T(1,128)S(1)} %copy-done.4, s32[1,1]{1,0:T(1,128)S(6)} %copy.15.ins__index___0__2_.ins__next_index___0__2_, s32[1,32]{1,0:T(1,128)S(1)} %collective-permute-done.2.ins__index___1__0_.ins__next_index___1__0_, ...), custom_call_target="tpu_custom_call" | custom-call | flops 1073741824 | tf_op jit(solution)/shard_map/pallas_call | solution.py:194
  15.6 0.6 collective-permute-done.8
  16.3 1.0 %collective-permute-done.7 = bf16[18,16,128]{2,1,0:T(8,128)(2,1)S(1)} collective-permute-done((bf16[18,16,128]{2,1,0:T(8,128)(2,1)S(1)}, bf16[18,16,128]{2,1,0:T(8,128)(2,1)S(1)}, u32[]{:S(2)}, u32[]{:S(2)}) %collective-permute-start.7) | collective-permute-done | bytes 73760 | tf_op jit(solution)/shard_map/ppermute | solution.py:238
  17.8 2.7 %collective-permute-start.9 = (bf16[24,16,128]{2,1,0:T(8,128)(2,1)S(1)}, bf16[24,16,128]{2,1,0:T(8,128)(2,1)S(1)}, u32[]{:S(2)}, u32[]{:S(2)}) collective-permute-start(bf16[24,16,128]{2,1,0:T(8,128)(2,1)S(1)} %constant_dynamic-update-slice_fusion.ins__sent__), channel_id=1, source_target_pairs={{0,8},{1,9},{2,10},{3,11},{4,12},{5,13},{6,14},{7,15},{8,0},{9,1},... | collective-permute-start | bytes 294920 | tf_op jit(solution)/shard_map/ppermute | solution.py:238
  20.6 4.0 %collective-permute-done.9.ins__got___0_ = bf16[24,16,128]{2,1,0:T(8,128)(2,1)S(1)} collective-permute-done((bf16[24,16,128]{2,1,0:T(8,128)(2,1)S(1)}, bf16[24,16,128]{2,1,0:T(8,128)(2,1)S(1)}, u32[]{:S(2)}, u32[]{:S(2)}) %collective-permute-start.9) | collective-permute-done | bytes 98336 | tf_op jit(solution)/shard_map/ppermute | solution.py:238
  24.6 1.6 %shard_map.66 = (bf16[16,16,128]{2,1,0:T(8,128)(2,1)S(1)}, f32[16,2048]{1,0:T(8,128)S(1)}, bf16[16,16,128]{2,1,0:T(8,128)(2,1)S(1)}) custom-call(bf16[24,16,128]{2,1,0:T(8,128)(2,1)S(1)} %collective-permute-done.9.ins__got___0_, f32[32,2048]{1,0:T(8,128)S(1)} %copy-done.1, s32[1,32]{1,0:T(1,128)S(1)} %copy-done.3, s32[1,32]{1,0:T(1,128)S(1)} %copy-done.4, ...), custom_call_target="tpu_custom_call" | custom-call | flops 536870912 | tf_op jit(solution)/shard_map/pallas_call | solution.py:194
  26.1 1.1 %collective-permute-start.11 = (f32[16,2048]{1,0:T(8,128)S(1)}, f32[16,2048]{1,0:T(8,128)S(1)}, u32[]{:S(2)}, u32[]{:S(2)}) collective-permute-start(f32[16,2048]{1,0:T(8,128)S(1)} %get-tuple-element.32), channel_id=1, source_target_pairs={{0,16},{16,0},{1,17},{17,1},{2,18},{18,2},{3,19},{19,3},{4,20},{20... | collective-permute-start | bytes 393224 | tf_op jit(solution)/shard_map/ppermute | solution.py:244
  27.2 1.5 %shard_map.68 = f32[16,2048]{1,0:T(8,128)S(1)} custom-call(f32[32,2048]{1,0:T(8,128)S(1)} %collective-permute-done.1.ins__held___1_, s32[1,32]{1,0:T(1,128)S(1)} %copy-done.3, s32[1,32]{1,0:T(1,128)S(1)} %copy-done.4, s32[1,1]{1,0:T(1,128)S(6)} %copy.15.ins__index___0__2_.ins__next_index___0__2_, ...), custom_call_target="tpu_custom_call" | custom-call | flops 536870912 | tf_op jit(solution)/shard_map/pallas_call | solution.py:194
  28.7 1.1 %collective-permute-start.12 = (f32[16,2048]{1,0:T(8,128)S(1)}, f32[16,2048]{1,0:T(8,128)S(1)}, u32[]{:S(2)}, u32[]{:S(2)}) collective-permute-start(f32[16,2048]{1,0:T(8,128)S(1)} %shard_map.68), channel_id=1, source_target_pairs={{0,16},{16,0},{1,17},{17,1},{2,18},{18,2},{3,19},{19,3},{4,20},{20... | collective-permute-start | bytes 393224 | tf_op jit(solution)/shard_map/ppermute | solution.py:244
  29.8 1.1 %collective-permute-start.17 = (bf16[11,128,128]{2,1,0:T(8,128)(2,1)S(1)}, bf16[11,128,128]{2,1,0:T(8,128)(2,1)S(1)}, u32[]{:S(2)}, u32[]{:S(2)}) collective-permute-start(bf16[11,128,128]{2,1,0:T(8,128)(2,1)S(1)} %pad_maximum_fusion), channel_id=1, source_target_pairs={{0,16},{16,0},{1,17},{17,1},{2,18},{18,2},{3,19},{19,3},{4,20},{20... | collective-permute-start | bytes 1081352 | tf_op jit(solution)/shard_map/ppermute | solution.py:244
  30.9 1.7 %collective-permute-done.11.ins__held___0_ = f32[16,2048]{1,0:T(8,128)S(1)} collective-permute-done((f32[16,2048]{1,0:T(8,128)S(1)}, f32[16,2048]{1,0:T(8,128)S(1)}, u32[]{:S(2)}, u32[]{:S(2)}) %collective-permute-start.11) | collective-permute-done | bytes 131104 | tf_op jit(solution)/shard_map/ppermute | solution.py:244
  32.6 1.7 %shard_map.67.ins__begun__ = f32[16,16,128]{2,1,0:T(8,128)S(1)} custom-call(f32[16,2048]{1,0:T(8,128)S(1)} %collective-permute-done.11.ins__held___0_, s32[1,32]{1,0:T(1,128)S(1)} %copy-done.3, s32[1,32]{1,0:T(1,128)S(1)} %copy-done.4, s32[1,1]{1,0:T(1,128)S(6)} %copy.15.ins__index___0__2_.ins__next_index___0__2_, ...), custom_call_target="tpu_custom_call" | custom-call | flops 536870912 | tf_op jit(solution)/shard_map/pallas_call | solution.py:194
  34.3 1.1 %collective-permute-done.12.ins__held___1_ = f32[16,2048]{1,0:T(8,128)S(1)} collective-permute-done((f32[16,2048]{1,0:T(8,128)S(1)}, f32[16,2048]{1,0:T(8,128)S(1)}, u32[]{:S(2)}, u32[]{:S(2)}) %collective-permute-start.12) | collective-permute-done | bytes 131104 | tf_op jit(solution)/shard_map/ppermute | solution.py:244
  35.4 1.7 %shard_map.69 = (bf16[18,16,128]{2,1,0:T(8,128)(2,1)S(1)}, f32[16,16,128]{2,1,0:T(8,128)S(1)}) custom-call(f32[16,16,128]{2,1,0:T(8,128)S(1)} %shard_map.67.ins__begun__, s32[64,128]{1,0:T(8,128)S(1)} %bitcast.63, s32[64,128]{1,0:T(8,128)S(1)} %collective-permute-done.ins__dealt___1_, f32[16,2048]{1,0:T(8,128)S(1)} %collective-permute-done.12.ins__held___1_, ...), custom_call_target="tpu_custom_call" | custom-call | flops 536870912 | tf_op jit(solution)/shard_map/pallas_call | solution.py:194
  37.1 1.7 %collective-permute-start.15 = (bf16[18,16,128]{2,1,0:T(8,128)(2,1)S(1)}, bf16[18,16,128]{2,1,0:T(8,128)(2,1)S(1)}, u32[]{:S(2)}, u32[]{:S(2)}) collective-permute-start(bf16[18,16,128]{2,1,0:T(8,128)(2,1)S(1)} %get-tuple-element.35), channel_id=1, source_target_pairs={{0,6},{1,7},{2,4},{3,5},{4,2},{5,3},{6,0},{7,1},{8,14},{9,15},{10,... | collective-permute-start | bytes 221192 | tf_op jit(solution)/shard_map/ppermute | solution.py:238
  38.8 1.4 %collective-permute-start.14 = (bf16[18,16,128]{2,1,0:T(8,128)(2,1)S(1)}, bf16[18,16,128]{2,1,0:T(8,128)(2,1)S(1)}, u32[]{:S(2)}, u32[]{:S(2)}) collective-permute-start(bf16[18,16,128]{2,1,0:T(8,128)(2,1)S(1)} %get-tuple-element.35), channel_id=1, source_target_pairs={{0,4},{1,5},{2,6},{3,7},{4,0},{5,1},{6,2},{7,3},{8,12},{9,13},{10,... | collective-permute-start | bytes 221192 | tf_op jit(solution)/shard_map/ppermute | solution.py:238
  40.7 1.8 %collective-permute-done.15 = bf16[18,16,128]{2,1,0:T(8,128)(2,1)S(1)} collective-permute-done((bf16[18,16,128]{2,1,0:T(8,128)(2,1)S(1)}, bf16[18,16,128]{2,1,0:T(8,128)(2,1)S(1)}, u32[]{:S(2)}, u32[]{:S(2)}) %collective-permute-start.15) | collective-permute-done | bytes 73760 | tf_op jit(solution)/shard_map/ppermute | solution.py:238
  42.4 0.9 %collective-permute-done.14 = bf16[18,16,128]{2,1,0:T(8,128)(2,1)S(1)} collective-permute-done((bf16[18,16,128]{2,1,0:T(8,128)(2,1)S(1)}, bf16[18,16,128]{2,1,0:T(8,128)(2,1)S(1)}, u32[]{:S(2)}, u32[]{:S(2)}) %collective-permute-start.14) | collective-permute-done | bytes 73760 | tf_op jit(solution)/shard_map/ppermute | solution.py:238
  43.4 1.2 %collective-permute-done.13 = bf16[18,16,128]{2,1,0:T(8,128)(2,1)S(1)} collective-permute-done((bf16[18,16,128]{2,1,0:T(8,128)(2,1)S(1)}, bf16[18,16,128]{2,1,0:T(8,128)(2,1)S(1)}, u32[]{:S(2)}, u32[]{:S(2)}) %collective-permute-start.13) | collective-permute-done | bytes 73760 | tf_op jit(solution)/shard_map/ppermute | solution.py:238
  44.8 2.0 %collective-permute-start.16 = (bf16[24,16,128]{2,1,0:T(8,128)(2,1)S(1)}, bf16[24,16,128]{2,1,0:T(8,128)(2,1)S(1)}, u32[]{:S(2)}, u32[]{:S(2)}) collective-permute-start(bf16[24,16,128]{2,1,0:T(8,128)(2,1)S(1)} %constant_dynamic-update-slice_fusion.4.ins__sent__), channel_id=1, source_target_pairs={{0,8},{1,9},{2,10},{3,11},{4,12},{5,13},{6,14},{7,15},{8,0},{9,1},... | collective-permute-start | bytes 294920 | tf_op jit(solution)/shard_map/ppermute | solution.py:238
  46.9 6.2 %collective-permute-done.16.ins__got___0_ = bf16[24,16,128]{2,1,0:T(8,128)(2,1)S(1)} collective-permute-done((bf16[24,16,128]{2,1,0:T(8,128)(2,1)S(1)}, bf16[24,16,128]{2,1,0:T(8,128)(2,1)S(1)}, u32[]{:S(2)}, u32[]{:S(2)}) %collective-permute-start.16) | collective-permute-done | bytes 98336 | tf_op jit(solution)/shard_map/ppermute | solution.py:238
  53.1 3.0 %shard_map.70 = (bf16[16,16,128]{2,1,0:T(8,128)(2,1)S(1)}, f32[16,2048]{1,0:T(8,128)S(1)}, f32[16,2048]{1,0:T(8,128)S(1)}, bf16[16,16,128]{2,1,0:T(8,128)(2,1)S(1)}, f32[16,16,128]{2,1,0:T(8,128)S(1)}) custom-call(bf16[24,16,128]{2,1,0:T(8,128)(2,1)S(1)} %collective-permute-done.16.ins__got___0_, f32[16,2048]{1,0:T(8,128)S(1)} %collective-permute-done.11.ins__held___0_, ...), custom_call_target="tpu_custom_call" | custom-call | flops 1073741824 | tf_op jit(solution)/shard_map/pallas_call | solution.py:194
  56.2 1.7 %collective-permute-start.22 = (bf16[16,16,128]{2,1,0:T(8,128)(2,1)S(1)}, bf16[16,16,128]{2,1,0:T(8,128)(2,1)S(1)}, u32[]{:S(2)}, u32[]{:S(2)}) collective-permute-start(bf16[16,16,128]{2,1,0:T(8,128)(2,1)S(1)} %get-tuple-element.43), channel_id=1, source_target_pairs={{0,4},{1,5},{2,6},{3,7},{4,0},{5,1},{6,2},{7,3},{8,12},{9,13},{10,... | collective-permute-start | bytes 196616 | tf_op jit(solution)/shard_map/ppermute | solution.py:238
  58.0 1.6 %collective-permute-start.21 = (bf16[16,16,128]{2,1,0:T(8,128)(2,1)S(1)}, bf16[16,16,128]{2,1,0:T(8,128)(2,1)S(1)}, u32[]{:S(2)}, u32[]{:S(2)}) collective-permute-start(bf16[16,16,128]{2,1,0:T(8,128)(2,1)S(1)} %get-tuple-element.43), channel_id=1, source_target_pairs={{0,2},{1,3},{2,0},{3,1},{4,6},{5,7},{6,4},{7,5},{8,10},{9,11},{10,... | collective-permute-start | bytes 196616 | tf_op jit(solution)/shard_map/ppermute | solution.py:238
  59.6 1.2 %collective-permute-start.10 = (bf16[16,16,128]{2,1,0:T(8,128)(2,1)S(1)}, bf16[16,16,128]{2,1,0:T(8,128)(2,1)S(1)}, u32[]{:S(2)}, u32[]{:S(2)}) collective-permute-start(bf16[16,16,128]{2,1,0:T(8,128)(2,1)S(1)} %get-tuple-element.31), channel_id=1, source_target_pairs={{0,16},{16,0},{1,17},{17,1},{2,18},{18,2},{3,19},{19,3},{4,20},{20... | collective-permute-start | bytes 196616 | tf_op jit(solution)/shard_map/ppermute | solution.py:244
  60.8 0.6 collective-permute-done.23
  61.3 0.9 %collective-permute-done.21 = bf16[16,16,128]{2,1,0:T(8,128)(2,1)S(1)} collective-permute-done((bf16[16,16,128]{2,1,0:T(8,128)(2,1)S(1)}, bf16[16,16,128]{2,1,0:T(8,128)(2,1)S(1)}, u32[]{:S(2)}, u32[]{:S(2)}) %collective-permute-start.21) | collective-permute-done | bytes 65568 | tf_op jit(solution)/shard_map/ppermute | solution.py:238
  62.3 1.7 %collective-permute-start.24 = (bf16[16,16,128]{2,1,0:T(8,128)(2,1)S(1)}, bf16[16,16,128]{2,1,0:T(8,128)(2,1)S(1)}, u32[]{:S(2)}, u32[]{:S(2)}) collective-permute-start(bf16[16,16,128]{2,1,0:T(8,128)(2,1)S(1)} %get-tuple-element.55), channel_id=1, source_target_pairs={{0,8},{1,9},{2,10},{3,11},{4,12},{5,13},{6,14},{7,15},{8,0},{9,1},... | collective-permute-start | bytes 196616 | tf_op jit(solution)/shard_map/ppermute | solution.py:238
  64.0 1.3 %shard_map.71.ins__inverse__ = f32[32,8,128]{2,1,0:T(8,128)S(1)} custom-call(s32[8,128]{1,0:T(8,128)S(1)} %fusion.1.ins__next_index___0_.ins__index___0_, s32[8,128]{1,0:T(8,128)S(1)} %fusion.ins__next_index___1_.ins__index___1_, bf16[22,128,128]{2,1,0:T(8,128)(2,1)S(1)} %collective-permute-done.19.ins__next_tiles___0__0_.ins__tiles___0__0_, ...), custom_call_target="tpu_custom_call" | custom-call | flops 2147483648 | tf_op jit(solution)/shard_map/pallas_call | solution.py:194
  65.3 2.9 %collective-permute-done.24.ins__got___0_ = bf16[16,16,128]{2,1,0:T(8,128)(2,1)S(1)} collective-permute-done((bf16[16,16,128]{2,1,0:T(8,128)(2,1)S(1)}, bf16[16,16,128]{2,1,0:T(8,128)(2,1)S(1)}, u32[]{:S(2)}, u32[]{:S(2)}) %collective-permute-start.24) | collective-permute-done | bytes 65568 | tf_op jit(solution)/shard_map/ppermute | solution.py:238
  68.2 3.0 %shard_map.72 = (f32[16,2048]{1,0:T(8,128)S(1)}, f32[16,2048]{1,0:T(8,128)S(1)}, bf16[16,16,128]{2,1,0:T(8,128)(2,1)S(1)}, f32[16,16,128]{2,1,0:T(8,128)S(1)}) custom-call(bf16[16,16,128]{2,1,0:T(8,128)(2,1)S(1)} %collective-permute-done.10.ins__counts__, bf16[16,16,128]{2,1,0:T(8,128)(2,1)S(1)} %collective-permute-done.24.ins__got___0_, ...), custom_call_target="tpu_custom_call" | custom-call | flops 2147483648 | tf_op jit(solution)/shard_map/pallas_call | solution.py:194
  71.2 1.0 %collective-permute-start.27 = (bf16[16,16,128]{2,1,0:T(8,128)(2,1)S(1)}, bf16[16,16,128]{2,1,0:T(8,128)(2,1)S(1)}, u32[]{:S(2)}, u32[]{:S(2)}) collective-permute-start(bf16[16,16,128]{2,1,0:T(8,128)(2,1)S(1)} %get-tuple-element.49), channel_id=1, source_target_pairs={{0,6},{1,7},{2,4},{3,5},{4,2},{5,3},{6,0},{7,1},{8,14},{9,15},{10,... | collective-permute-start | bytes 196616 | tf_op jit(solution)/shard_map/ppermute | solution.py:238
  72.2 2.1 %collective-permute-start.26 = (bf16[16,16,128]{2,1,0:T(8,128)(2,1)S(1)}, bf16[16,16,128]{2,1,0:T(8,128)(2,1)S(1)}, u32[]{:S(2)}, u32[]{:S(2)}) collective-permute-start(bf16[16,16,128]{2,1,0:T(8,128)(2,1)S(1)} %get-tuple-element.49), channel_id=1, source_target_pairs={{0,4},{1,5},{2,6},{3,7},{4,0},{5,1},{6,2},{7,3},{8,12},{9,13},{10,... | collective-permute-start | bytes 196616 | tf_op jit(solution)/shard_map/ppermute | solution.py:238
  74.2 0.5 collective-permute-start.25
  74.7 1.7 %collective-permute-done.27 = bf16[16,16,128]{2,1,0:T(8,128)(2,1)S(1)} collective-permute-done((bf16[16,16,128]{2,1,0:T(8,128)(2,1)S(1)}, bf16[16,16,128]{2,1,0:T(8,128)(2,1)S(1)}, u32[]{:S(2)}, u32[]{:S(2)}) %collective-permute-start.27) | collective-permute-done | bytes 65568 | tf_op jit(solution)/shard_map/ppermute | solution.py:238
  76.4 0.8 collective-permute-done.26
  77.2 1.3 %collective-permute-done.25 = bf16[16,16,128]{2,1,0:T(8,128)(2,1)S(1)} collective-permute-done((bf16[16,16,128]{2,1,0:T(8,128)(2,1)S(1)}, bf16[16,16,128]{2,1,0:T(8,128)(2,1)S(1)}, u32[]{:S(2)}, u32[]{:S(2)}) %collective-permute-start.25) | collective-permute-done | bytes 65568 | tf_op jit(solution)/shard_map/ppermute | solution.py:238
  78.6 1.6 %collective-permute-start.28 = (bf16[16,16,128]{2,1,0:T(8,128)(2,1)S(1)}, bf16[16,16,128]{2,1,0:T(8,128)(2,1)S(1)}, u32[]{:S(2)}, u32[]{:S(2)}) collective-permute-start(bf16[16,16,128]{2,1,0:T(8,128)(2,1)S(1)} %get-tuple-element.53), channel_id=1, source_target_pairs={{0,8},{1,9},{2,10},{3,11},{4,12},{5,13},{6,14},{7,15},{8,0},{9,1},... | collective-permute-start | bytes 196616 | tf_op jit(solution)/shard_map/ppermute | solution.py:238
  80.1 3.9 %collective-permute-done.28.ins__got___0_ = bf16[16,16,128]{2,1,0:T(8,128)(2,1)S(1)} collective-permute-done((bf16[16,16,128]{2,1,0:T(8,128)(2,1)S(1)}, bf16[16,16,128]{2,1,0:T(8,128)(2,1)S(1)}, u32[]{:S(2)}, u32[]{:S(2)}) %collective-permute-start.28) | collective-permute-done | bytes 65568 | tf_op jit(solution)/shard_map/ppermute | solution.py:238
  84.0 1.6 %shard_map.73 = (f32[16,2048]{1,0:T(8,128)S(1)}, bf16[16,16,128]{2,1,0:T(8,128)(2,1)S(1)}) custom-call(bf16[16,16,128]{2,1,0:T(8,128)(2,1)S(1)} %get-tuple-element.47.ins__counts__, bf16[16,16,128]{2,1,0:T(8,128)(2,1)S(1)} %collective-permute-done.28.ins__got___0_, f32[16,2048]{1,0:T(8,128)S(1)} %get-tuple-element.50.ins__held___1_, s32[1,32]{1,0:T(1,128)S(1)} %copy-done.3, ...), custom_call_target="tpu_custom_call" | custom-call | flops 536870912 | tf_op jit(solution)/shard_map/pallas_call | solution.py:194
  85.6 1.5 %shard_map.74 = f32[16,2048]{1,0:T(8,128)S(1)} custom-call(f32[16,2048]{1,0:T(8,128)S(1)} %get-tuple-element.46.ins__held___0_, s32[1,32]{1,0:T(1,128)S(1)} %copy-done.3, s32[1,32]{1,0:T(1,128)S(1)} %copy-done.4, s32[1,1]{1,0:T(1,128)S(6)} %copy.15.ins__index___0__2_.ins__next_index___0__2_, ...), custom_call_target="tpu_custom_call" | custom-call | flops 536870912 | tf_op jit(solution)/shard_map/pallas_call | solution.py:194
  87.2 0.7 maximum_select_fusion
  (66 shorter events, 3.8 us)
Async XLA Ops:
  0.0 3.5 %copy-start = (bf16[1,32,128,128]{3,2,1,0:T(8,128)(2,1)S(1)}, bf16[1,32,128,128]{3,2,1,0:T(8,128)(2,1)}, u32[]{:S(2)}) copy-start(bf16[1,32,128,128]{3,2,1,0:T(8,128)(2,1)} %param.7) | copy-start | bytes 3145732
  0.0 8.0 %collective-permute-start.5 = (bf16[32,128,128]{2,1,0:T(8,128)(2,1)}, bf16[32,128,128]{2,1,0:T(8,128)(2,1)S(1)}, u32[]{:S(2)}, u32[]{:S(2)}) collective-permute-start(bf16[32,128,128]{2,1,0:T(8,128)(2,1)} %bitcast.53), channel_id=1, source_target_pairs={{0,1},{1,0},{2,3},{3,2},{4,5},{5,4},{6,7},{7,6},{8,9},{9,8},{10,11... | collective-permute-start | bytes 3145736 | tf_op jit(solution)/shard_map/ppermute | solution.py:234
  0.5 4.6 %collective-permute-start.2 = (s32[1,32]{1,0:T(1,128)}, s32[1,32]{1,0:T(1,128)S(1)}, u32[]{:S(2)}, u32[]{:S(2)}) collective-permute-start(s32[1,32]{1,0:T(1,128)} %ins__index___0__0_.17), channel_id=1, source_target_pairs={{0,1},{1,0},{2,3},{3,2},{4,5},{5,4},{6,7},{7,6},{8,9},{9,8},{10,11... | collective-permute-start | bytes 392 | tf_op jit(solution)/shard_map/ppermute | solution.py:234
  0.5 3.9 %collective-permute-start.4 = (s32[1,1]{1,0:T(1,128)}, s32[1,1]{1,0:T(1,128)}, u32[]{:S(2)}, u32[]{:S(2)}) collective-permute-start(s32[1,1]{1,0:T(1,128)} %param.10), channel_id=1, source_target_pairs={{0,1},{1,0},{2,3},{3,2},{4,5},{5,4},{6,7},{7,6},{8,9},{9,8},{10,11... | collective-permute-start | bytes 20 | tf_op jit(solution)/shard_map/ppermute | solution.py:234
  1.0 7.0 %collective-permute-start = (s32[64,128]{1,0:T(8,128)}, s32[64,128]{1,0:T(8,128)S(1)}, u32[]{:S(2)}, u32[]{:S(2)}) collective-permute-start(s32[64,128]{1,0:T(8,128)} %bitcast.61), channel_id=1, source_target_pairs={{0,1},{1,0},{2,3},{3,2},{4,5},{5,4},{6,7},{7,6},{8,9},{9,8},{10,11... | collective-permute-start | bytes 98312 | tf_op jit(solution)/shard_map/ppermute | solution.py:234
  1.0 6.9 %collective-permute-start.1 = (f32[32,2048]{1,0:T(8,128)}, f32[32,2048]{1,0:T(8,128)S(1)}, u32[]{:S(2)}, u32[]{:S(2)}) collective-permute-start(f32[32,2048]{1,0:T(8,128)} %ins__held___0_.3), channel_id=1, source_target_pairs={{0,1},{1,0},{2,3},{3,2},{4,5},{5,4},{6,7},{7,6},{8,9},{9,8},{10,11... | collective-permute-start | bytes 786440 | tf_op jit(solution)/shard_map/ppermute | solution.py:234
  3.5 4.5 %copy-start.1 = (f32[32,2048]{1,0:T(8,128)S(1)}, f32[32,2048]{1,0:T(8,128)}, u32[]{:S(2)}) copy-start(f32[32,2048]{1,0:T(8,128)} %ins__held___0_.3) | copy-start | bytes 786436
  3.6 4.4 %copy-start.2 = (s32[1,64,128]{2,1,0:T(8,128)S(1)}, s32[1,64,128]{2,1,0:T(8,128)}, u32[]{:S(2)}) copy-start(s32[1,64,128]{2,1,0:T(8,128)} %param.11) | copy-start | bytes 98308
  4.3 0.7 copy-start.4
  4.3 3.7 %copy-start.3 = (s32[1,32]{1,0:T(1,128)S(1)}, s32[1,32]{1,0:T(1,128)}, u32[]{:S(2)}) copy-start(s32[1,32]{1,0:T(1,128)} %ins__index___0__0_.17) | copy-start | bytes 388
  5.0 3.0 %collective-permute-start.3 = (s32[1,32]{1,0:T(1,128)S(1)}, s32[1,32]{1,0:T(1,128)S(1)}, u32[]{:S(2)}, u32[]{:S(2)}) collective-permute-start(s32[1,32]{1,0:T(1,128)S(1)} %copy-done.4), channel_id=1, source_target_pairs={{0,1},{1,0},{2,3},{3,2},{4,5},{5,4},{6,7},{7,6},{8,9},{9,8},{10,11... | collective-permute-start | bytes 392 | tf_op jit(solution)/shard_map/ppermute | solution.py:234
  5.0 35.7 %collective-permute-start.19 = (bf16[22,128,128]{2,1,0:T(8,128)(2,1)}, bf16[22,128,128]{2,1,0:T(8,128)(2,1)S(1)}, u32[]{:S(2)}, u32[]{:S(2)}) collective-permute-start(bf16[22,128,128]{2,1,0:T(8,128)(2,1)} %slice_bitcast_fusion), channel_id=1, source_target_pairs={{0,16},{16,0},{1,17},{17,1},{2,18},{18,2},{3,19},{19,3},{4,20},{20... | collective-permute-start | bytes 2162696 | tf_op jit(solution)/shard_map/ppermute | solution.py:244
  10.3 6.0 %collective-permute-start.8 = (bf16[18,16,128]{2,1,0:T(8,128)(2,1)S(1)}, bf16[18,16,128]{2,1,0:T(8,128)(2,1)S(1)}, u32[]{:S(2)}, u32[]{:S(2)}) collective-permute-start(bf16[18,16,128]{2,1,0:T(8,128)(2,1)S(1)} %get-tuple-element.30), channel_id=1, source_target_pairs={{0,6},{1,7},{2,4},{3,5},{4,2},{5,3},{6,0},{7,1},{8,14},{9,15},{10,... | collective-permute-start | bytes 221192 | tf_op jit(solution)/shard_map/ppermute | solution.py:238
  12.9 4.4 %collective-permute-start.7 = (bf16[18,16,128]{2,1,0:T(8,128)(2,1)S(1)}, bf16[18,16,128]{2,1,0:T(8,128)(2,1)S(1)}, u32[]{:S(2)}, u32[]{:S(2)}) collective-permute-start(bf16[18,16,128]{2,1,0:T(8,128)(2,1)S(1)} %get-tuple-element.30), channel_id=1, source_target_pairs={{0,4},{1,5},{2,6},{3,7},{4,0},{5,1},{6,2},{7,3},{8,12},{9,13},{10,... | collective-permute-start | bytes 221192 | tf_op jit(solution)/shard_map/ppermute | solution.py:238
  13.3 4.4 %collective-permute-start.6 = (bf16[18,16,128]{2,1,0:T(8,128)(2,1)S(1)}, bf16[18,16,128]{2,1,0:T(8,128)(2,1)S(1)}, u32[]{:S(2)}, u32[]{:S(2)}) collective-permute-start(bf16[18,16,128]{2,1,0:T(8,128)(2,1)S(1)} %get-tuple-element.30), channel_id=1, source_target_pairs={{0,2},{1,3},{2,0},{3,1},{4,6},{5,7},{6,4},{7,5},{8,10},{9,11},{10,... | collective-permute-start | bytes 221192 | tf_op jit(solution)/shard_map/ppermute | solution.py:238
  17.8 6.7 %collective-permute-start.9 = (bf16[24,16,128]{2,1,0:T(8,128)(2,1)S(1)}, bf16[24,16,128]{2,1,0:T(8,128)(2,1)S(1)}, u32[]{:S(2)}, u32[]{:S(2)}) collective-permute-start(bf16[24,16,128]{2,1,0:T(8,128)(2,1)S(1)} %constant_dynamic-update-slice_fusion.ins__sent__), channel_id=1, source_target_pairs={{0,8},{1,9},{2,10},{3,11},{4,12},{5,13},{6,14},{7,15},{8,0},{9,1},... | collective-permute-start | bytes 294920 | tf_op jit(solution)/shard_map/ppermute | solution.py:238
  26.1 6.5 %collective-permute-start.11 = (f32[16,2048]{1,0:T(8,128)S(1)}, f32[16,2048]{1,0:T(8,128)S(1)}, u32[]{:S(2)}, u32[]{:S(2)}) collective-permute-start(f32[16,2048]{1,0:T(8,128)S(1)} %get-tuple-element.32), channel_id=1, source_target_pairs={{0,16},{16,0},{1,17},{17,1},{2,18},{18,2},{3,19},{19,3},{4,20},{20... | collective-permute-start | bytes 393224 | tf_op jit(solution)/shard_map/ppermute | solution.py:244
  28.7 6.7 %collective-permute-start.12 = (f32[16,2048]{1,0:T(8,128)S(1)}, f32[16,2048]{1,0:T(8,128)S(1)}, u32[]{:S(2)}, u32[]{:S(2)}) collective-permute-start(f32[16,2048]{1,0:T(8,128)S(1)} %shard_map.68), channel_id=1, source_target_pairs={{0,16},{16,0},{1,17},{17,1},{2,18},{18,2},{3,19},{19,3},{4,20},{20... | collective-permute-start | bytes 393224 | tf_op jit(solution)/shard_map/ppermute | solution.py:244
  29.8 14.9 %collective-permute-start.17 = (bf16[11,128,128]{2,1,0:T(8,128)(2,1)S(1)}, bf16[11,128,128]{2,1,0:T(8,128)(2,1)S(1)}, u32[]{:S(2)}, u32[]{:S(2)}) collective-permute-start(bf16[11,128,128]{2,1,0:T(8,128)(2,1)S(1)} %pad_maximum_fusion), channel_id=1, source_target_pairs={{0,16},{16,0},{1,17},{17,1},{2,18},{18,2},{3,19},{19,3},{4,20},{20... | collective-permute-start | bytes 1081352 | tf_op jit(solution)/shard_map/ppermute | solution.py:244
  37.1 5.3 %collective-permute-start.15 = (bf16[18,16,128]{2,1,0:T(8,128)(2,1)S(1)}, bf16[18,16,128]{2,1,0:T(8,128)(2,1)S(1)}, u32[]{:S(2)}, u32[]{:S(2)}) collective-permute-start(bf16[18,16,128]{2,1,0:T(8,128)(2,1)S(1)} %get-tuple-element.35), channel_id=1, source_target_pairs={{0,6},{1,7},{2,4},{3,5},{4,2},{5,3},{6,0},{7,1},{8,14},{9,15},{10,... | collective-permute-start | bytes 221192 | tf_op jit(solution)/shard_map/ppermute | solution.py:238
  38.8 4.5 %collective-permute-start.14 = (bf16[18,16,128]{2,1,0:T(8,128)(2,1)S(1)}, bf16[18,16,128]{2,1,0:T(8,128)(2,1)S(1)}, u32[]{:S(2)}, u32[]{:S(2)}) collective-permute-start(bf16[18,16,128]{2,1,0:T(8,128)(2,1)S(1)} %get-tuple-element.35), channel_id=1, source_target_pairs={{0,4},{1,5},{2,6},{3,7},{4,0},{5,1},{6,2},{7,3},{8,12},{9,13},{10,... | collective-permute-start | bytes 221192 | tf_op jit(solution)/shard_map/ppermute | solution.py:238
  40.3 4.4 %collective-permute-start.13 = (bf16[18,16,128]{2,1,0:T(8,128)(2,1)S(1)}, bf16[18,16,128]{2,1,0:T(8,128)(2,1)S(1)}, u32[]{:S(2)}, u32[]{:S(2)}) collective-permute-start(bf16[18,16,128]{2,1,0:T(8,128)(2,1)S(1)} %get-tuple-element.35), channel_id=1, source_target_pairs={{0,2},{1,3},{2,0},{3,1},{4,6},{5,7},{6,4},{7,5},{8,10},{9,11},{10,... | collective-permute-start | bytes 221192 | tf_op jit(solution)/shard_map/ppermute | solution.py:238
  40.7 12.4 %collective-permute-start.20 = (bf16[22,128,128]{2,1,0:T(8,128)(2,1)S(1)}, bf16[22,128,128]{2,1,0:T(8,128)(2,1)S(1)}, u32[]{:S(2)}, u32[]{:S(2)}) collective-permute-start(bf16[22,128,128]{2,1,0:T(8,128)(2,1)S(1)} %collective-permute-done.19.ins__next_tiles___0__0_.ins__tiles___0__0_), channel_id=1, source_target_pairs={{0,1},{1,0},{2,3},{3,2},{4,5},{5,4},{6,7},{7,6},{8,9},{9,8},{10,11... | collective-permute-start | bytes 2162696 | tf_op jit(solution)/shard_map/ppermute | solution.py:234
  44.7 2.2 %collective-permute-start.18 = (bf16[11,128,128]{2,1,0:T(8,128)(2,1)S(1)}, bf16[11,128,128]{2,1,0:T(8,128)(2,1)S(1)}, u32[]{:S(2)}, u32[]{:S(2)}) collective-permute-start(bf16[11,128,128]{2,1,0:T(8,128)(2,1)S(1)} %collective-permute-done.17.ins__next_tiles___0__1_.ins__tiles___0__1_), channel_id=1, source_target_pairs={{0,1},{1,0},{2,3},{3,2},{4,5},{5,4},{6,7},{7,6},{8,9},{9,8},{10,11... | collective-permute-start | bytes 1081352 | tf_op jit(solution)/shard_map/ppermute | solution.py:234
  44.8 8.2 %collective-permute-start.16 = (bf16[24,16,128]{2,1,0:T(8,128)(2,1)S(1)}, bf16[24,16,128]{2,1,0:T(8,128)(2,1)S(1)}, u32[]{:S(2)}, u32[]{:S(2)}) collective-permute-start(bf16[24,16,128]{2,1,0:T(8,128)(2,1)S(1)} %constant_dynamic-update-slice_fusion.4.ins__sent__), channel_id=1, source_target_pairs={{0,8},{1,9},{2,10},{3,11},{4,12},{5,13},{6,14},{7,15},{8,0},{9,1},... | collective-permute-start | bytes 294920 | tf_op jit(solution)/shard_map/ppermute | solution.py:238
  56.0 5.3 %collective-permute-start.23 = (bf16[16,16,128]{2,1,0:T(8,128)(2,1)S(1)}, bf16[16,16,128]{2,1,0:T(8,128)(2,1)S(1)}, u32[]{:S(2)}, u32[]{:S(2)}) collective-permute-start(bf16[16,16,128]{2,1,0:T(8,128)(2,1)S(1)} %get-tuple-element.43), channel_id=1, source_target_pairs={{0,6},{1,7},{2,4},{3,5},{4,2},{5,3},{6,0},{7,1},{8,14},{9,15},{10,... | collective-permute-start | bytes 196616 | tf_op jit(solution)/shard_map/ppermute | solution.py:238
  56.2 5.1 %collective-permute-start.22 = (bf16[16,16,128]{2,1,0:T(8,128)(2,1)S(1)}, bf16[16,16,128]{2,1,0:T(8,128)(2,1)S(1)}, u32[]{:S(2)}, u32[]{:S(2)}) collective-permute-start(bf16[16,16,128]{2,1,0:T(8,128)(2,1)S(1)} %get-tuple-element.43), channel_id=1, source_target_pairs={{0,4},{1,5},{2,6},{3,7},{4,0},{5,1},{6,2},{7,3},{8,12},{9,13},{10,... | collective-permute-start | bytes 196616 | tf_op jit(solution)/shard_map/ppermute | solution.py:238
  58.0 4.3 %collective-permute-start.21 = (bf16[16,16,128]{2,1,0:T(8,128)(2,1)S(1)}, bf16[16,16,128]{2,1,0:T(8,128)(2,1)S(1)}, u32[]{:S(2)}, u32[]{:S(2)}) collective-permute-start(bf16[16,16,128]{2,1,0:T(8,128)(2,1)S(1)} %get-tuple-element.43), channel_id=1, source_target_pairs={{0,2},{1,3},{2,0},{3,1},{4,6},{5,7},{6,4},{7,5},{8,10},{9,11},{10,... | collective-permute-start | bytes 196616 | tf_op jit(solution)/shard_map/ppermute | solution.py:238
  59.6 5.7 %collective-permute-start.10 = (bf16[16,16,128]{2,1,0:T(8,128)(2,1)S(1)}, bf16[16,16,128]{2,1,0:T(8,128)(2,1)S(1)}, u32[]{:S(2)}, u32[]{:S(2)}) collective-permute-start(bf16[16,16,128]{2,1,0:T(8,128)(2,1)S(1)} %get-tuple-element.31), channel_id=1, source_target_pairs={{0,16},{16,0},{1,17},{17,1},{2,18},{18,2},{3,19},{19,3},{4,20},{20... | collective-permute-start | bytes 196616 | tf_op jit(solution)/shard_map/ppermute | solution.py:244
  62.3 5.9 %collective-permute-start.24 = (bf16[16,16,128]{2,1,0:T(8,128)(2,1)S(1)}, bf16[16,16,128]{2,1,0:T(8,128)(2,1)S(1)}, u32[]{:S(2)}, u32[]{:S(2)}) collective-permute-start(bf16[16,16,128]{2,1,0:T(8,128)(2,1)S(1)} %get-tuple-element.55), channel_id=1, source_target_pairs={{0,8},{1,9},{2,10},{3,11},{4,12},{5,13},{6,14},{7,15},{8,0},{9,1},... | collective-permute-start | bytes 196616 | tf_op jit(solution)/shard_map/ppermute | solution.py:238
  71.2 5.2 %collective-permute-start.27 = (bf16[16,16,128]{2,1,0:T(8,128)(2,1)S(1)}, bf16[16,16,128]{2,1,0:T(8,128)(2,1)S(1)}, u32[]{:S(2)}, u32[]{:S(2)}) collective-permute-start(bf16[16,16,128]{2,1,0:T(8,128)(2,1)S(1)} %get-tuple-element.49), channel_id=1, source_target_pairs={{0,6},{1,7},{2,4},{3,5},{4,2},{5,3},{6,0},{7,1},{8,14},{9,15},{10,... | collective-permute-start | bytes 196616 | tf_op jit(solution)/shard_map/ppermute | solution.py:238
  72.2 5.0 %collective-permute-start.26 = (bf16[16,16,128]{2,1,0:T(8,128)(2,1)S(1)}, bf16[16,16,128]{2,1,0:T(8,128)(2,1)S(1)}, u32[]{:S(2)}, u32[]{:S(2)}) collective-permute-start(bf16[16,16,128]{2,1,0:T(8,128)(2,1)S(1)} %get-tuple-element.49), channel_id=1, source_target_pairs={{0,4},{1,5},{2,6},{3,7},{4,0},{5,1},{6,2},{7,3},{8,12},{9,13},{10,... | collective-permute-start | bytes 196616 | tf_op jit(solution)/shard_map/ppermute | solution.py:238
  74.2 4.3 %collective-permute-start.25 = (bf16[16,16,128]{2,1,0:T(8,128)(2,1)S(1)}, bf16[16,16,128]{2,1,0:T(8,128)(2,1)S(1)}, u32[]{:S(2)}, u32[]{:S(2)}) collective-permute-start(bf16[16,16,128]{2,1,0:T(8,128)(2,1)S(1)} %get-tuple-element.49), channel_id=1, source_target_pairs={{0,2},{1,3},{2,0},{3,1},{4,6},{5,7},{6,4},{7,5},{8,10},{9,11},{10,... | collective-permute-start | bytes 196616 | tf_op jit(solution)/shard_map/ppermute | solution.py:238
  78.6 5.4 %collective-permute-start.28 = (bf16[16,16,128]{2,1,0:T(8,128)(2,1)S(1)}, bf16[16,16,128]{2,1,0:T(8,128)(2,1)S(1)}, u32[]{:S(2)}, u32[]{:S(2)}) collective-permute-start(bf16[16,16,128]{2,1,0:T(8,128)(2,1)S(1)} %get-tuple-element.53), channel_id=1, source_target_pairs={{0,8},{1,9},{2,10},{3,11},{4,12},{5,13},{6,14},{7,15},{8,0},{9,1},... | collective-permute-start | bytes 196616 | tf_op jit(solution)/shard_map/ppermute | solution.py:238
  85.5 1.6 %collective-permute-start.29 = (f32[16,2048]{1,0:T(8,128)S(1)}, f32[16,2048]{1,0:T(8,128)S(1)}, u32[]{:S(2)}, u32[]{:S(2)}) collective-permute-start(f32[16,2048]{1,0:T(8,128)S(1)} %get-tuple-element.52), channel_id=1, source_target_pairs={{0,1},{1,0},{2,3},{3,2},{4,5},{5,4},{6,7},{7,6},{8,9},{9,8},{10,11... | collective-permute-start | bytes 393224 | tf_op jit(solution)/shard_map/ppermute | solution.py:234

commit v9 on v8

--- a/solution.py
+++ b/solution.py
@@ -17,16 +17,16 @@
 VOX, RAY, LIVE = range(3)
 
 
-def entry(index, row, t):
-    return index[row][0, t] if isinstance(index, tuple) else index[row, t]
+def entry(index, k, row, t):
+    return index[k][row, t] if isinstance(index, tuple) else index[3 * k + row, t]
 
 
 def core_here():
     return lax.rem(lax.axis_index("tile"), CORES)
 
 
-def each_live(index, slots, body):
-    live = entry(index, LIVE, 0)
+def each_live(index, k, slots, body):
+    live = entry(index, k, LIVE, 0)
     for group in range(-(-slots // TILE_GROUP)):
         first, last = group * TILE_GROUP, min(slots, (group + 1) * TILE_GROUP)
 
@@ -57,35 +57,35 @@
     return sum(ref.shape[0] for ref in tile_refs) // TILE_GROUP * TILE_GROUP
 
 
-def project_into(acc, low, index_refs, sets):
+def project_into(acc, low, index, sets):
     blocks = low.shape[0] // CORES
     for k in range(CORES):
         if sets[k] is None:
             continue
-        index_ref, tile_refs = index_refs[k], sets[k]
-
-        def body(ts):
+        tile_refs = sets[k]
+
+        def body(ts, k=k, tile_refs=tile_refs):
             wide = jnp.concatenate([tile_at(tile_refs, t) for t in ts], axis=0)
-            add_products(acc, [low[k * blocks + entry(index_ref, VOX, t)] for t in ts],
-                         [entry(index_ref, RAY, t) for t in ts], wide, True)
-
-        each_live(index_ref, slots_of(tile_refs), body)
-
-
-def back_into(acc, ratios, index_refs, sets):
+            add_products(acc, [low[k * blocks + entry(index, k, VOX, t)] for t in ts],
+                         [entry(index, k, RAY, t) for t in ts], wide, True)
+
+        each_live(index, k, slots_of(tile_refs), body)
+
+
+def back_into(acc, ratios, index, sets):
     blocks = acc.shape[0] // CORES
     acc[...] = jnp.zeros_like(acc)
     for k in range(CORES):
         if sets[k] is None:
             continue
-        index_ref, tile_refs = index_refs[k], sets[k]
-
-        def body(ts):
+        tile_refs = sets[k]
+
+        def body(ts, k=k, tile_refs=tile_refs):
             wide = jnp.concatenate([tile_at(tile_refs, t) for t in ts], axis=1)
-            add_products(acc, [ratios(entry(index_ref, RAY, t)) for t in ts],
-                         [k * blocks + entry(index_ref, VOX, t) for t in ts], wide, False)
-
-        each_live(index_ref, slots_of(tile_refs), body)
+            add_products(acc, [ratios(entry(index, k, RAY, t)) for t in ts],
+                         [k * blocks + entry(index, k, VOX, t) for t in ts], wide, False)
+
+        each_live(index, k, slots_of(tile_refs), body)
 
 
 def columns(held, size):
@@ -246,10 +246,16 @@
     def after(array, value):
         return lax.optimization_barrier((array, value))[0]
 
-    rows = (tile_vox, tile_ray, live_blocks)
+    rows = jnp.concatenate([tile_vox, tile_ray, jnp.broadcast_to(live_blocks, tile_vox.shape)], axis=0)
+    own_index = jnp.pad(rows, ((0, 5), (0, -slots % LANES)))
     tiles = ((own_tiles,), (swap_cores(own_tiles),))
     held = (images, swap_cores(images))
-    index = (rows, tuple(swap_cores(row) for row in rows))
+    first_index = (own_index, swap_cores(own_index))
+
+    def merged(own, other):
+        return jnp.concatenate([own[:3], other[:3], jnp.zeros_like(own[:2])])
+
+    index = merged(*first_index)
     dealt = (counts[0], swap_cores(counts[0]))
 
     def sensitivity(index, tiles):
@@ -261,16 +267,7 @@
     moves = [True] * (ROUNDS - 1)
     known = [None] * ROUNDS
     two = subset_count == 2 and ray_blocks <= 256 and slots <= size and size == LANES
-    early = slots * 11 // 16
-    def packed(rows):
-        rows = jnp.concatenate([jnp.broadcast_to(row, (1, slots)) for row in rows], axis=0)
-        return jnp.pad(rows.astype(bf16), ((0, size - 3), (0, size - slots)))[None]
-
-    def index_of(pieces):
-        return pieces[-1][-1, :8].astype(jnp.int32)
-
-    if two:
-        far_tiles = [shift(own_tiles[:early])]
+    late = slots // 2
     if two:
         moves = [r == 0 for r in range(ROUNDS - 1)]
 
@@ -289,12 +286,16 @@
                 {"wide": summed, "sent": shaped((sent, half, size), bf16)})
 
     extra, outs = sums(0)
-    out = call(first_kernel, {"held": held, "index": index, "own_hbm": own_tiles, "tiles": tiles[1], **extra},
+    out = call(first_kernel, {"held": held, "index": first_index, "own_hbm": own_tiles, "tiles": tiles[1], **extra},
                outs, [low_scratch, sum_scratch, pltpu.VMEM(own_tiles.shape, bf16), pltpu.SemaphoreType.DMA])
     for r in range(ROUNDS):
         wide, sent = out["wide"], out["sent"]
+        if two and r == 0:
+            tiles_then, rows_then = after((own_tiles[late:], own_index), sent)
+            slot = jnp.pad(rows_then.astype(bf16), ((0, size - 8), (0, 0)))[None]
+            far_second = shift(jnp.concatenate([tiles_then, slot]))
         if two and r == 1:
-            far_swapped = [swap_cores(after(far_tiles[0], sent))]
+            other_second = swap_cores(after(far_second, sent))
         for masks in steps:
             got = [swap_chips(sent, mask) for mask in masks]
             if masks is not steps[-1]:
@@ -311,9 +312,9 @@
                     counted = jnp.concatenate([counted, passed])
                 sent = counted
         if two and r == 1:
-            far_swapped.append(swap_cores(after(far_tiles[1], wide)))
-            far_tiles = (tuple(far_tiles), tuple(far_swapped))
-            far_index = tuple(index_of(pieces) for pieces in far_tiles)
+            other_first = swap_cores(after(far_first, tuple(got)))
+            far_tiles = ((far_first, far_second), (other_first, other_second))
+            far_index = merged(*(piece[-1, :8].astype(jnp.int32) for piece in (far_second, other_second)))
             far = (far_index, far_tiles, sensitivity(far_index, far_tiles))
             sets = [far if later >= 2 and later % 2 == 0 else sets[later] for later in range(ROUNDS)]
         now_index, now_tiles, now_inverse = sets[r]
@@ -345,11 +346,13 @@
                                          {"held": only(k, (piece,) * CORES)}, [back_scratch])}
                 moved[k] = out["held"][k]
                 if two and r == 0 and k == 1:
-                    far_tiles.append(shift(after(jnp.concatenate([own_tiles[early:], packed(after(rows, sent))]), moved[k])))
+                    far_first = shift(after(own_tiles[:late], moved[k]))
                 if not last:
                     moved[k] = shift(moved[k])
                 elif k == 1:
                     moved[k] = swap_cores(moved[k])
+            if two and r == 0:
+                moved[1], far_second = lax.optimization_barrier((moved[1], far_second))
             held = (moved[0], moved[1])
             if not last:
                 extra, more = sums(r + 1)
@@ -363,9 +366,18 @@
             if two and r == 1:
                 known[r + 1] = far_counts
             extra, more = sums(r + 1)
-            ins.update(held=held, tiles=now_tiles, next_index=sets[r + 1][0], next_tiles=sets[r + 1][1], **extra)
-            outs.update(held=(piece,) * CORES, **more)
-            out = call(kernel, ins, outs, [back_scratch, ray_scratch, ray_scratch, low_scratch, sum_scratch])
+            ins.update(held=held, tiles=now_tiles)
+            outs.update(held=(piece,) * CORES)
+            if two and r == 1:
+                out = call(kernel, ins, outs, [back_scratch, ray_scratch, ray_scratch])
+                then = call(functools.partial(project_kernel, r + 1),
+                            {"held": out["held"], "index": sets[r + 1][0], "tiles": sets[r + 1][1], **extra},
+                            more, [low_scratch, sum_scratch])
+                out = {**out, **then}
+            else:
+                ins.update(next_index=sets[r + 1][0], next_tiles=sets[r + 1][1], **extra)
+                outs.update(more)
+                out = call(kernel, ins, outs, [back_scratch, ray_scratch, ray_scratch, low_scratch, sum_scratch])
             held = out["held"]
             if two and r == 1:
                 known = [known[later] if later < 2 else far_counts if later % 2 == 0 else out["counts"]

time: 88.2 us -> 83 us (0.941)
  Pallas kernels: 20.7 us -> 15.2 us
  waiting for transfers between devices: 31 us -> 29.4 us
  starting transfers between devices: 31.2 us -> 32.4 us
    pallas_call x11 -> x12, Pallas kernels: 20.7 us -> 15.2 us  [call(): pl.pallas_call(kernel, out_shape=outs, in_specs=[jax.tree_util.tree_map_w...]
    ppermute x16, waiting for transfers between devices: 28.2 us -> 24.8 us  [swap_chips(): return lax.ppermute(array, 'tile', pairs)]
    ppermute x16, starting transfers between devices: 22.2 us -> 24.5 us  [swap_chips(): return lax.ppermute(array, 'tile', pairs)]
    ppermute x9 -> x7, waiting for transfers between devices: 0.02 us -> 0.94 us  [swap_cores(): return lax.ppermute(array, 'tile', [(i, i ^ 1) for i in range(tile_devs)])]
    slice x2 -> x3, local copies, waits for them, and re-layouts: 2.07 us -> 2.15 us  [the longest x1 2.14 us: shards(): far_first = shift(after(own_tiles[:late], moved[k]))]
  transfers between devices with their start and end apart: 30 -> 28, of which waited for: 17 -> 19; matrix products, arithmetic and copies ran while one was open for 3% -> 3% of each run, Pallas kernels for 15% -> 10%
where the time goes in v9:
time: 83 us; the launch traced here: 82.7 us
  starting transfers between devices  32.4 us (39%)
  waiting for transfers between devices  29.4 us (35%)
  Pallas kernels  15.2 us (18%)
  local copies, waits for them, and re-layouts  3.61 us (4%)
  other arithmetic  1.18 us (1%)
  between operations  0.91 us (1%)
    ppermute x16, waiting for transfers between devices, swap_chips(): return lax.ppermute(array, 'tile', pairs)  24.8 us
    ppermute x16, starting transfers between devices, swap_chips(): return lax.ppermute(array, 'tile', pairs)  24.5 us
    pallas_call x12, Pallas kernels, call(): pl.pallas_call(kernel, out_shape=outs, in_specs=[jax.tree_util.tree_map_w...  15.2 us
    ppermute x5, starting transfers between devices, shift(): lax.ppermute(array, 'subset', [(i, (i + 1) % subset_count) for i in range...  6.8 us
    ppermute x5, waiting for transfers between devices, shift(): lax.ppermute(array, 'subset', [(i, (i + 1) % subset_count) for i in range...  3.63 us
    slice x1, local copies, waits for them, and re-layouts, shards(): far_first = shift(after(own_tiles[:late], moved[k]))  2.14 us
  transfers between devices with their start and end apart: 28, of which 19 were waited for; matrix products, arithmetic and copies ran while one was open for 3% of the time, Pallas kernels for 10%

profile of v9, /device:TPU:0, one launch (start us, length us, event | category | flops | bytes accessed | tf_op | source)
XLA Modules:
  0.0 82.7 jit_solution(7359291002516697597)
XLA Ops:
  1.2 0.6 copy-done.4
  2.5 2.1 %slice_bitcast_fusion = (bf16[16,128,128]{2,1,0:T(8,128)(2,1)}, bf16[16,128,128]{2,1,0:T(8,128)(2,1)S(1)}) fusion(bf16[1,32,128,128]{3,2,1,0:T(8,128)(2,1)} %param.7), kind=kLoop, calls=%fused_computation.1 | loop fusion | bytes 2097152 | tf_op jit(solution)/shard_map/slice | solution.py:349
  4.8 0.6 copy-done.2
  5.4 1.7 %shard_map.64 = (bf16[18,16,128]{2,1,0:T(8,128)(2,1)S(1)}, f32[16,16,128]{2,1,0:T(8,128)S(1)}) custom-call(s32[64,128]{1,0:T(8,128)S(1)} %bitcast.61, s32[64,128]{1,0:T(8,128)S(1)} %collective-permute-done.ins__dealt___1_, f32[32,2048]{1,0:T(8,128)S(1)} %copy-done.1, f32[32,2048]{1,0:T(8,128)S(1)} %collective-permute-done.1.ins__held___1_, ...), custom_call_target="tpu_custom_call" | custom-call | flops 536870912 | tf_op jit(solution)/shard_map/pallas_call | solution.py:194
  7.1 4.0 %collective-permute-start.6 = (bf16[18,16,128]{2,1,0:T(8,128)(2,1)S(1)}, bf16[18,16,128]{2,1,0:T(8,128)(2,1)S(1)}, u32[]{:S(2)}, u32[]{:S(2)}) collective-permute-start(bf16[18,16,128]{2,1,0:T(8,128)(2,1)S(1)} %get-tuple-element.31), channel_id=1, source_target_pairs={{0,6},{1,7},{2,4},{3,5},{4,2},{5,3},{6,0},{7,1},{8,14},{9,15},{10,... | collective-permute-start | bytes 221192 | tf_op jit(solution)/shard_map/ppermute | solution.py:238
  11.8 1.9 %collective-permute-start.11 = (bf16[17,128,128]{2,1,0:T(8,128)(2,1)S(1)}, bf16[17,128,128]{2,1,0:T(8,128)(2,1)S(1)}, u32[]{:S(2)}, u32[]{:S(2)}) collective-permute-start(bf16[17,128,128]{2,1,0:T(8,128)(2,1)S(1)} %pad_maximum_fusion), channel_id=1, source_target_pairs={{0,16},{16,0},{1,17},{17,1},{2,18},{18,2},{3,19},{19,3},{4,20},{20... | collective-permute-start | bytes 1671176 | tf_op jit(solution)/shard_map/ppermute | solution.py:244
  13.9 1.6 %collective-permute-done.5 = bf16[18,16,128]{2,1,0:T(8,128)(2,1)S(1)} collective-permute-done((bf16[18,16,128]{2,1,0:T(8,128)(2,1)S(1)}, bf16[18,16,128]{2,1,0:T(8,128)(2,1)S(1)}, u32[]{:S(2)}, u32[]{:S(2)}) %collective-permute-start.5) | collective-permute-done | bytes 73760 | tf_op jit(solution)/shard_map/ppermute | solution.py:238
  16.1 2.7 %collective-permute-start.7 = (bf16[24,16,128]{2,1,0:T(8,128)(2,1)S(1)}, bf16[24,16,128]{2,1,0:T(8,128)(2,1)S(1)}, u32[]{:S(2)}, u32[]{:S(2)}) collective-permute-start(bf16[24,16,128]{2,1,0:T(8,128)(2,1)S(1)} %constant_dynamic-update-slice_fusion.ins__sent__), channel_id=1, source_target_pairs={{0,8},{1,9},{2,10},{3,11},{4,12},{5,13},{6,14},{7,15},{8,0},{9,1},... | collective-permute-start | bytes 294920 | tf_op jit(solution)/shard_map/ppermute | solution.py:238
  18.7 1.2 %shard_map.65.ins__inverse__ = f32[32,8,128]{2,1,0:T(8,128)S(1)} custom-call(s32[8,128]{1,0:T(8,128)S(1)} %add_add_fusion.4.ins__index__.ins__next_index__, bf16[32,128,128]{2,1,0:T(8,128)(2,1)S(1)} %bitcast.54, bf16[32,128,128]{2,1,0:T(8,128)(2,1)S(1)} %collective-permute-done.3.ins__tiles___0_.ins__tiles___1__0_.ins__next_tiles___1__0_), custom_call_target="tpu_custom_call" | custom-call | flops 1073741824 | tf_op jit(solution)/shard_map/pallas_call | solution.py:194
  19.9 3.0 %collective-permute-done.7.ins__got___0_ = bf16[24,16,128]{2,1,0:T(8,128)(2,1)S(1)} collective-permute-done((bf16[24,16,128]{2,1,0:T(8,128)(2,1)S(1)}, bf16[24,16,128]{2,1,0:T(8,128)(2,1)S(1)}, u32[]{:S(2)}, u32[]{:S(2)}) %collective-permute-start.7) | collective-permute-done | bytes 98336 | tf_op jit(solution)/shard_map/ppermute | solution.py:238
  22.9 1.0 %shard_map.66 = (bf16[16,16,128]{2,1,0:T(8,128)(2,1)S(1)}, f32[16,2048]{1,0:T(8,128)S(1)}, bf16[16,16,128]{2,1,0:T(8,128)(2,1)S(1)}) custom-call(bf16[24,16,128]{2,1,0:T(8,128)(2,1)S(1)} %collective-permute-done.7.ins__got___0_, f32[32,2048]{1,0:T(8,128)S(1)} %copy-done.1, s32[8,128]{1,0:T(8,128)S(1)} %add_add_fusion.4.ins__index__.ins__next_index__, ...), custom_call_target="tpu_custom_call" | custom-call | flops 536870912 | tf_op jit(solution)/shard_map/pallas_call | solution.py:194
  23.9 1.6 %collective-permute-start.9 = (f32[16,2048]{1,0:T(8,128)S(1)}, f32[16,2048]{1,0:T(8,128)S(1)}, u32[]{:S(2)}, u32[]{:S(2)}) collective-permute-start(f32[16,2048]{1,0:T(8,128)S(1)} %get-tuple-element.33), channel_id=1, source_target_pairs={{0,16},{16,0},{1,17},{17,1},{2,18},{18,2},{3,19},{19,3},{4,20},{20... | collective-permute-start | bytes 393224 | tf_op jit(solution)/shard_map/ppermute | solution.py:244
  25.5 0.9 %shard_map.68 = f32[16,2048]{1,0:T(8,128)S(1)} custom-call(f32[32,2048]{1,0:T(8,128)S(1)} %collective-permute-done.1.ins__held___1_, s32[8,128]{1,0:T(8,128)S(1)} %add_add_fusion.4.ins__index__.ins__next_index__, f32[32,8,128]{2,1,0:T(8,128)S(1)} %shard_map.65.ins__inverse__, bf16[16,16,128]{2,1,0:T(8,128)(2,1)S(1)} %get-tuple-element.34.ins__ratios__, ...), custom_call_target="tpu_custom_call" | custom-call | flops 536870912 | tf_op jit(solution)/shard_map/pallas_call | solution.py:194
  26.4 0.6 collective-permute-start.10
  27.0 1.5 %collective-permute-start.17 = (bf16[16,128,128]{2,1,0:T(8,128)(2,1)S(1)}, bf16[16,128,128]{2,1,0:T(8,128)(2,1)S(1)}, u32[]{:S(2)}, u32[]{:S(2)}) collective-permute-start(bf16[16,128,128]{2,1,0:T(8,128)(2,1)S(1)} %copy-done.3), channel_id=1, source_target_pairs={{0,16},{16,0},{1,17},{17,1},{2,18},{18,2},{3,19},{19,3},{4,20},{20... | collective-permute-start | bytes 1572872 | tf_op jit(solution)/shard_map/ppermute | solution.py:244
  28.5 1.9 %collective-permute-done.9.ins__held___0_ = f32[16,2048]{1,0:T(8,128)S(1)} collective-permute-done((f32[16,2048]{1,0:T(8,128)S(1)}, f32[16,2048]{1,0:T(8,128)S(1)}, u32[]{:S(2)}, u32[]{:S(2)}) %collective-permute-start.9) | collective-permute-done | bytes 131104 | tf_op jit(solution)/shard_map/ppermute | solution.py:244
  30.4 1.1 %shard_map.67.ins__begun__ = f32[16,16,128]{2,1,0:T(8,128)S(1)} custom-call(f32[16,2048]{1,0:T(8,128)S(1)} %collective-permute-done.9.ins__held___0_, s32[8,128]{1,0:T(8,128)S(1)} %add_add_fusion.4.ins__index__.ins__next_index__, bf16[32,128,128]{2,1,0:T(8,128)(2,1)S(1)} %bitcast.56), custom_call_target="tpu_custom_call" | custom-call | flops 536870912 | tf_op jit(solution)/shard_map/pallas_call | solution.py:194
  31.5 1.7 %collective-permute-done.10.ins__held___1_ = f32[16,2048]{1,0:T(8,128)S(1)} collective-permute-done((f32[16,2048]{1,0:T(8,128)S(1)}, f32[16,2048]{1,0:T(8,128)S(1)}, u32[]{:S(2)}, u32[]{:S(2)}) %collective-permute-start.10) | collective-permute-done | bytes 131104 | tf_op jit(solution)/shard_map/ppermute | solution.py:244
  33.2 1.1 %shard_map.69 = (bf16[18,16,128]{2,1,0:T(8,128)(2,1)S(1)}, f32[16,16,128]{2,1,0:T(8,128)S(1)}) custom-call(f32[16,16,128]{2,1,0:T(8,128)S(1)} %shard_map.67.ins__begun__, s32[64,128]{1,0:T(8,128)S(1)} %bitcast.62, s32[64,128]{1,0:T(8,128)S(1)} %collective-permute-done.ins__dealt___1_, f32[16,2048]{1,0:T(8,128)S(1)} %collective-permute-done.10.ins__held___1_, ...), custom_call_target="tpu_custom_call" | custom-call | flops 536870912 | tf_op jit(solution)/shard_map/pallas_call | solution.py:194
  34.3 1.7 %collective-permute-start.14 = (bf16[18,16,128]{2,1,0:T(8,128)(2,1)S(1)}, bf16[18,16,128]{2,1,0:T(8,128)(2,1)S(1)}, u32[]{:S(2)}, u32[]{:S(2)}) collective-permute-start(bf16[18,16,128]{2,1,0:T(8,128)(2,1)S(1)} %get-tuple-element.39), channel_id=1, source_target_pairs={{0,6},{1,7},{2,4},{3,5},{4,2},{5,3},{6,0},{7,1},{8,14},{9,15},{10,... | collective-permute-start | bytes 221192 | tf_op jit(solution)/shard_map/ppermute | solution.py:238
  36.0 1.5 %collective-permute-start.13 = (bf16[18,16,128]{2,1,0:T(8,128)(2,1)S(1)}, bf16[18,16,128]{2,1,0:T(8,128)(2,1)S(1)}, u32[]{:S(2)}, u32[]{:S(2)}) collective-permute-start(bf16[18,16,128]{2,1,0:T(8,128)(2,1)S(1)} %get-tuple-element.39), channel_id=1, source_target_pairs={{0,4},{1,5},{2,6},{3,7},{4,0},{5,1},{6,2},{7,3},{8,12},{9,13},{10,... | collective-permute-start | bytes 221192 | tf_op jit(solution)/shard_map/ppermute | solution.py:238
  37.9 1.8 %collective-permute-done.14 = bf16[18,16,128]{2,1,0:T(8,128)(2,1)S(1)} collective-permute-done((bf16[18,16,128]{2,1,0:T(8,128)(2,1)S(1)}, bf16[18,16,128]{2,1,0:T(8,128)(2,1)S(1)}, u32[]{:S(2)}, u32[]{:S(2)}) %collective-permute-start.14) | collective-permute-done | bytes 73760 | tf_op jit(solution)/shard_map/ppermute | solution.py:238
  39.6 1.0 %collective-permute-done.13 = bf16[18,16,128]{2,1,0:T(8,128)(2,1)S(1)} collective-permute-done((bf16[18,16,128]{2,1,0:T(8,128)(2,1)S(1)}, bf16[18,16,128]{2,1,0:T(8,128)(2,1)S(1)}, u32[]{:S(2)}, u32[]{:S(2)}) %collective-permute-start.13) | collective-permute-done | bytes 73760 | tf_op jit(solution)/shard_map/ppermute | solution.py:238
  40.6 1.2 %collective-permute-done.12 = bf16[18,16,128]{2,1,0:T(8,128)(2,1)S(1)} collective-permute-done((bf16[18,16,128]{2,1,0:T(8,128)(2,1)S(1)}, bf16[18,16,128]{2,1,0:T(8,128)(2,1)S(1)}, u32[]{:S(2)}, u32[]{:S(2)}) %collective-permute-start.12) | collective-permute-done | bytes 73760 | tf_op jit(solution)/shard_map/ppermute | solution.py:238
  42.0 2.7 %collective-permute-start.15 = (bf16[24,16,128]{2,1,0:T(8,128)(2,1)S(1)}, bf16[24,16,128]{2,1,0:T(8,128)(2,1)S(1)}, u32[]{:S(2)}, u32[]{:S(2)}) collective-permute-start(bf16[24,16,128]{2,1,0:T(8,128)(2,1)S(1)} %constant_dynamic-update-slice_fusion.4.ins__sent__), channel_id=1, source_target_pairs={{0,8},{1,9},{2,10},{3,11},{4,12},{5,13},{6,14},{7,15},{8,0},{9,1},... | collective-permute-start | bytes 294920 | tf_op jit(solution)/shard_map/ppermute | solution.py:238
  44.7 3.9 %collective-permute-done.15.ins__got___0_ = bf16[24,16,128]{2,1,0:T(8,128)(2,1)S(1)} collective-permute-done((bf16[24,16,128]{2,1,0:T(8,128)(2,1)S(1)}, bf16[24,16,128]{2,1,0:T(8,128)(2,1)S(1)}, u32[]{:S(2)}, u32[]{:S(2)}) %collective-permute-start.15) | collective-permute-done | bytes 98336 | tf_op jit(solution)/shard_map/ppermute | solution.py:238
  48.6 1.3 %shard_map.70 = (bf16[16,16,128]{2,1,0:T(8,128)(2,1)S(1)}, f32[16,2048]{1,0:T(8,128)S(1)}, f32[16,2048]{1,0:T(8,128)S(1)}) custom-call(bf16[24,16,128]{2,1,0:T(8,128)(2,1)S(1)} %collective-permute-done.15.ins__got___0_, f32[16,2048]{1,0:T(8,128)S(1)} %collective-permute-done.9.ins__held___0_, f32[16,2048]{1,0:T(8,128)S(1)} %collective-permute-done.10.ins__held___1_, ...), custom_call_target="tpu_custom_call" | custom-call | flops 1073741824 | tf_op jit(solution)/shard_map/pallas_call | solution.py:194
  50.0 0.5 collective-permute-done.18.ins__tiles___1__0_
  50.5 1.6 %shard_map.71 = (bf16[16,16,128]{2,1,0:T(8,128)(2,1)S(1)}, f32[16,16,128]{2,1,0:T(8,128)S(1)}) custom-call(f32[16,2048]{1,0:T(8,128)S(1)} %get-tuple-element.40.ins__held___0_, f32[16,2048]{1,0:T(8,128)S(1)} %get-tuple-element.41.ins__held___1_, s32[8,128]{1,0:T(8,128)S(1)} %add_add_fusion.5.ins__index__, ...), custom_call_target="tpu_custom_call" | custom-call | flops 2147483648 | tf_op jit(solution)/shard_map/pallas_call | solution.py:194
  52.1 0.6 collective-permute-start.21
  52.9 2.7 %collective-permute-start.19 = (bf16[16,16,128]{2,1,0:T(8,128)(2,1)S(1)}, bf16[16,16,128]{2,1,0:T(8,128)(2,1)S(1)}, u32[]{:S(2)}, u32[]{:S(2)}) collective-permute-start(bf16[16,16,128]{2,1,0:T(8,128)(2,1)S(1)} %get-tuple-element.47), channel_id=1, source_target_pairs={{0,2},{1,3},{2,0},{3,1},{4,6},{5,7},{6,4},{7,5},{8,10},{9,11},{10,... | collective-permute-start | bytes 196616 | tf_op jit(solution)/shard_map/ppermute | solution.py:238
  55.6 1.3 %collective-permute-start.8 = (bf16[16,16,128]{2,1,0:T(8,128)(2,1)S(1)}, bf16[16,16,128]{2,1,0:T(8,128)(2,1)S(1)}, u32[]{:S(2)}, u32[]{:S(2)}) collective-permute-start(bf16[16,16,128]{2,1,0:T(8,128)(2,1)S(1)} %get-tuple-element.32), channel_id=1, source_target_pairs={{0,16},{16,0},{1,17},{17,1},{2,18},{18,2},{3,19},{19,3},{4,20},{20... | collective-permute-start | bytes 196616 | tf_op jit(solution)/shard_map/ppermute | solution.py:244
  56.9 1.0 %collective-permute-done.21 = bf16[16,16,128]{2,1,0:T(8,128)(2,1)S(1)} collective-permute-done((bf16[16,16,128]{2,1,0:T(8,128)(2,1)S(1)}, bf16[16,16,128]{2,1,0:T(8,128)(2,1)S(1)}, u32[]{:S(2)}, u32[]{:S(2)}) %collective-permute-start.21) | collective-permute-done | bytes 65568 | tf_op jit(solution)/shard_map/ppermute | solution.py:238
  57.9 0.7 collective-permute-done.19
  58.6 1.9 %collective-permute-start.22 = (bf16[16,16,128]{2,1,0:T(8,128)(2,1)S(1)}, bf16[16,16,128]{2,1,0:T(8,128)(2,1)S(1)}, u32[]{:S(2)}, u32[]{:S(2)}) collective-permute-start(bf16[16,16,128]{2,1,0:T(8,128)(2,1)S(1)} %get-tuple-element.57), channel_id=1, source_target_pairs={{0,8},{1,9},{2,10},{3,11},{4,12},{5,13},{6,14},{7,15},{8,0},{9,1},... | collective-permute-start | bytes 196616 | tf_op jit(solution)/shard_map/ppermute | solution.py:238
  60.5 1.2 %shard_map.72.ins__inverse__ = f32[32,8,128]{2,1,0:T(8,128)S(1)} custom-call(s32[8,128]{1,0:T(8,128)S(1)} %add_add_fusion.5.ins__index__, bf16[16,128,128]{2,1,0:T(8,128)(2,1)S(1)} %collective-permute-done.17.ins__tiles___0__0_, bf16[17,128,128]{2,1,0:T(8,128)(2,1)S(1)} %collective-permute-done.11.ins__tiles___0__1_, ...), custom_call_target="tpu_custom_call" | custom-call | flops 2147483648 | tf_op jit(solution)/shard_map/pallas_call | solution.py:194
  61.7 2.9 %collective-permute-done.22.ins__got___0_ = bf16[16,16,128]{2,1,0:T(8,128)(2,1)S(1)} collective-permute-done((bf16[16,16,128]{2,1,0:T(8,128)(2,1)S(1)}, bf16[16,16,128]{2,1,0:T(8,128)(2,1)S(1)}, u32[]{:S(2)}, u32[]{:S(2)}) %collective-permute-start.22) | collective-permute-done | bytes 65568 | tf_op jit(solution)/shard_map/ppermute | solution.py:238
  64.7 2.3 %shard_map.73 = (f32[16,2048]{1,0:T(8,128)S(1)}, f32[16,2048]{1,0:T(8,128)S(1)}, bf16[16,16,128]{2,1,0:T(8,128)(2,1)S(1)}, f32[16,16,128]{2,1,0:T(8,128)S(1)}) custom-call(bf16[16,16,128]{2,1,0:T(8,128)(2,1)S(1)} %collective-permute-done.8.ins__counts__, bf16[16,16,128]{2,1,0:T(8,128)(2,1)S(1)} %collective-permute-done.22.ins__got___0_, ...), custom_call_target="tpu_custom_call" | custom-call | flops 2147483648 | tf_op jit(solution)/shard_map/pallas_call | solution.py:194
  67.0 0.6 collective-permute-start.25
  67.6 2.1 %collective-permute-start.24 = (bf16[16,16,128]{2,1,0:T(8,128)(2,1)S(1)}, bf16[16,16,128]{2,1,0:T(8,128)(2,1)S(1)}, u32[]{:S(2)}, u32[]{:S(2)}) collective-permute-start(bf16[16,16,128]{2,1,0:T(8,128)(2,1)S(1)} %get-tuple-element.51), channel_id=1, source_target_pairs={{0,4},{1,5},{2,6},{3,7},{4,0},{5,1},{6,2},{7,3},{8,12},{9,13},{10,... | collective-permute-start | bytes 196616 | tf_op jit(solution)/shard_map/ppermute | solution.py:238
  69.7 0.8 %collective-permute-start.23 = (bf16[16,16,128]{2,1,0:T(8,128)(2,1)S(1)}, bf16[16,16,128]{2,1,0:T(8,128)(2,1)S(1)}, u32[]{:S(2)}, u32[]{:S(2)}) collective-permute-start(bf16[16,16,128]{2,1,0:T(8,128)(2,1)S(1)} %get-tuple-element.51), channel_id=1, source_target_pairs={{0,2},{1,3},{2,0},{3,1},{4,6},{5,7},{6,4},{7,5},{8,10},{9,11},{10,... | collective-permute-start | bytes 196616 | tf_op jit(solution)/shard_map/ppermute | solution.py:238
  70.5 1.7 %collective-permute-done.25 = bf16[16,16,128]{2,1,0:T(8,128)(2,1)S(1)} collective-permute-done((bf16[16,16,128]{2,1,0:T(8,128)(2,1)S(1)}, bf16[16,16,128]{2,1,0:T(8,128)(2,1)S(1)}, u32[]{:S(2)}, u32[]{:S(2)}) %collective-permute-start.25) | collective-permute-done | bytes 65568 | tf_op jit(solution)/shard_map/ppermute | solution.py:238
  72.6 1.3 %collective-permute-done.23 = bf16[16,16,128]{2,1,0:T(8,128)(2,1)S(1)} collective-permute-done((bf16[16,16,128]{2,1,0:T(8,128)(2,1)S(1)}, bf16[16,16,128]{2,1,0:T(8,128)(2,1)S(1)}, u32[]{:S(2)}, u32[]{:S(2)}) %collective-permute-start.23) | collective-permute-done | bytes 65568 | tf_op jit(solution)/shard_map/ppermute | solution.py:238
  74.0 1.9 %collective-permute-start.26 = (bf16[16,16,128]{2,1,0:T(8,128)(2,1)S(1)}, bf16[16,16,128]{2,1,0:T(8,128)(2,1)S(1)}, u32[]{:S(2)}, u32[]{:S(2)}) collective-permute-start(bf16[16,16,128]{2,1,0:T(8,128)(2,1)S(1)} %get-tuple-element.55), channel_id=1, source_target_pairs={{0,8},{1,9},{2,10},{3,11},{4,12},{5,13},{6,14},{7,15},{8,0},{9,1},... | collective-permute-start | bytes 196616 | tf_op jit(solution)/shard_map/ppermute | solution.py:238
  75.9 3.7 %collective-permute-done.26.ins__got___0_ = bf16[16,16,128]{2,1,0:T(8,128)(2,1)S(1)} collective-permute-done((bf16[16,16,128]{2,1,0:T(8,128)(2,1)S(1)}, bf16[16,16,128]{2,1,0:T(8,128)(2,1)S(1)}, u32[]{:S(2)}, u32[]{:S(2)}) %collective-permute-start.26) | collective-permute-done | bytes 65568 | tf_op jit(solution)/shard_map/ppermute | solution.py:238
  79.6 1.0 %shard_map.74 = (f32[16,2048]{1,0:T(8,128)S(1)}, bf16[16,16,128]{2,1,0:T(8,128)(2,1)S(1)}) custom-call(bf16[16,16,128]{2,1,0:T(8,128)(2,1)S(1)} %get-tuple-element.49.ins__counts__, bf16[16,16,128]{2,1,0:T(8,128)(2,1)S(1)} %collective-permute-done.26.ins__got___0_, f32[16,2048]{1,0:T(8,128)S(1)} %get-tuple-element.52.ins__held___1_, ...), custom_call_target="tpu_custom_call" | custom-call | flops 536870912 | tf_op jit(solution)/shard_map/pallas_call | solution.py:194
  80.7 0.9 %shard_map.75 = f32[16,2048]{1,0:T(8,128)S(1)} custom-call(f32[16,2048]{1,0:T(8,128)S(1)} %get-tuple-element.48.ins__held___0_, s32[8,128]{1,0:T(8,128)S(1)} %add_add_fusion.4.ins__index__.ins__next_index__, f32[32,8,128]{2,1,0:T(8,128)S(1)} %shard_map.65.ins__inverse__, bf16[16,16,128]{2,1,0:T(8,128)(2,1)S(1)} %get-tuple-element.53.ins__ratios__, ...), custom_call_target="tpu_custom_call" | custom-call | flops 536870912 | tf_op jit(solution)/shard_map/pallas_call | solution.py:194
  82.0 0.7 maximum_select_fusion
  (70 shorter events, 4.6 us)
Async XLA Ops:
  0.0 4.8 %collective-permute-start.3 = (bf16[32,128,128]{2,1,0:T(8,128)(2,1)}, bf16[32,128,128]{2,1,0:T(8,128)(2,1)S(1)}, u32[]{:S(2)}, u32[]{:S(2)}) collective-permute-start(bf16[32,128,128]{2,1,0:T(8,128)(2,1)} %bitcast.52), channel_id=1, source_target_pairs={{0,1},{1,0},{2,3},{3,2},{4,5},{5,4},{6,7},{7,6},{8,9},{9,8},{10,11... | collective-permute-start | bytes 3145736 | tf_op jit(solution)/shard_map/ppermute | solution.py:234
  1.1 0.7 copy-start.4
  1.1 0.7 copy-start.5
  1.9 2.8 %collective-permute-start.2 = (s32[8,128]{1,0:T(8,128)S(1)}, s32[8,128]{1,0:T(8,128)S(1)}, u32[]{:S(2)}, u32[]{:S(2)}) collective-permute-start(s32[8,128]{1,0:T(8,128)S(1)} %pad.8.ins__index___0_), channel_id=1, source_target_pairs={{0,1},{1,0},{2,3},{3,2},{4,5},{5,4},{6,7},{7,6},{8,9},{9,8},{10,11... | collective-permute-start | bytes 12296 | tf_op jit(solution)/shard_map/ppermute | solution.py:234
  1.9 2.9 %copy-start = (bf16[1,32,128,128]{3,2,1,0:T(8,128)(2,1)S(1)}, bf16[1,32,128,128]{3,2,1,0:T(8,128)(2,1)}, u32[]{:S(2)}) copy-start(bf16[1,32,128,128]{3,2,1,0:T(8,128)(2,1)} %param.7) | copy-start | bytes 3145732
  1.9 2.9 %collective-permute-start = (s32[64,128]{1,0:T(8,128)}, s32[64,128]{1,0:T(8,128)S(1)}, u32[]{:S(2)}, u32[]{:S(2)}) collective-permute-start(s32[64,128]{1,0:T(8,128)} %bitcast.60), channel_id=1, source_target_pairs={{0,1},{1,0},{2,3},{3,2},{4,5},{5,4},{6,7},{7,6},{8,9},{9,8},{10,11... | collective-permute-start | bytes 98312 | tf_op jit(solution)/shard_map/ppermute | solution.py:234
  2.4 2.4 %collective-permute-start.1 = (f32[32,2048]{1,0:T(8,128)}, f32[32,2048]{1,0:T(8,128)S(1)}, u32[]{:S(2)}, u32[]{:S(2)}) collective-permute-start(f32[32,2048]{1,0:T(8,128)} %ins__held___0_.3), channel_id=1, source_target_pairs={{0,1},{1,0},{2,3},{3,2},{4,5},{5,4},{6,7},{7,6},{8,9},{9,8},{10,11... | collective-permute-start | bytes 786440 | tf_op jit(solution)/shard_map/ppermute | solution.py:234
  2.5 2.3 %copy-start.1 = (f32[32,2048]{1,0:T(8,128)S(1)}, f32[32,2048]{1,0:T(8,128)}, u32[]{:S(2)}) copy-start(f32[32,2048]{1,0:T(8,128)} %ins__held___0_.3) | copy-start | bytes 786436
  4.6 0.8 copy-start.2
  7.1 6.7 %collective-permute-start.6 = (bf16[18,16,128]{2,1,0:T(8,128)(2,1)S(1)}, bf16[18,16,128]{2,1,0:T(8,128)(2,1)S(1)}, u32[]{:S(2)}, u32[]{:S(2)}) collective-permute-start(bf16[18,16,128]{2,1,0:T(8,128)(2,1)S(1)} %get-tuple-element.31), channel_id=1, source_target_pairs={{0,6},{1,7},{2,4},{3,5},{4,2},{5,3},{6,0},{7,1},{8,14},{9,15},{10,... | collective-permute-start | bytes 221192 | tf_op jit(solution)/shard_map/ppermute | solution.py:238
  11.1 4.4 %collective-permute-start.5 = (bf16[18,16,128]{2,1,0:T(8,128)(2,1)S(1)}, bf16[18,16,128]{2,1,0:T(8,128)(2,1)S(1)}, u32[]{:S(2)}, u32[]{:S(2)}) collective-permute-start(bf16[18,16,128]{2,1,0:T(8,128)(2,1)S(1)} %get-tuple-element.31), channel_id=1, source_target_pairs={{0,4},{1,5},{2,6},{3,7},{4,0},{5,1},{6,2},{7,3},{8,12},{9,13},{10,... | collective-permute-start | bytes 221192 | tf_op jit(solution)/shard_map/ppermute | solution.py:238
  11.6 4.4 %collective-permute-start.4 = (bf16[18,16,128]{2,1,0:T(8,128)(2,1)S(1)}, bf16[18,16,128]{2,1,0:T(8,128)(2,1)S(1)}, u32[]{:S(2)}, u32[]{:S(2)}) collective-permute-start(bf16[18,16,128]{2,1,0:T(8,128)(2,1)S(1)} %get-tuple-element.31), channel_id=1, source_target_pairs={{0,2},{1,3},{2,0},{3,1},{4,6},{5,7},{6,4},{7,5},{8,10},{9,11},{10,... | collective-permute-start | bytes 221192 | tf_op jit(solution)/shard_map/ppermute | solution.py:238
  11.8 21.4 %collective-permute-start.11 = (bf16[17,128,128]{2,1,0:T(8,128)(2,1)S(1)}, bf16[17,128,128]{2,1,0:T(8,128)(2,1)S(1)}, u32[]{:S(2)}, u32[]{:S(2)}) collective-permute-start(bf16[17,128,128]{2,1,0:T(8,128)(2,1)S(1)} %pad_maximum_fusion), channel_id=1, source_target_pairs={{0,16},{16,0},{1,17},{17,1},{2,18},{18,2},{3,19},{19,3},{4,20},{20... | collective-permute-start | bytes 1671176 | tf_op jit(solution)/shard_map/ppermute | solution.py:244
  16.1 6.9 %collective-permute-start.7 = (bf16[24,16,128]{2,1,0:T(8,128)(2,1)S(1)}, bf16[24,16,128]{2,1,0:T(8,128)(2,1)S(1)}, u32[]{:S(2)}, u32[]{:S(2)}) collective-permute-start(bf16[24,16,128]{2,1,0:T(8,128)(2,1)S(1)} %constant_dynamic-update-slice_fusion.ins__sent__), channel_id=1, source_target_pairs={{0,8},{1,9},{2,10},{3,11},{4,12},{5,13},{6,14},{7,15},{8,0},{9,1},... | collective-permute-start | bytes 294920 | tf_op jit(solution)/shard_map/ppermute | solution.py:238
  23.9 6.5 %collective-permute-start.9 = (f32[16,2048]{1,0:T(8,128)S(1)}, f32[16,2048]{1,0:T(8,128)S(1)}, u32[]{:S(2)}, u32[]{:S(2)}) collective-permute-start(f32[16,2048]{1,0:T(8,128)S(1)} %get-tuple-element.33), channel_id=1, source_target_pairs={{0,16},{16,0},{1,17},{17,1},{2,18},{18,2},{3,19},{19,3},{4,20},{20... | collective-permute-start | bytes 393224 | tf_op jit(solution)/shard_map/ppermute | solution.py:244
  25.5 1.5 %copy-start.3 = (bf16[16,128,128]{2,1,0:T(8,128)(2,1)S(1)}, bf16[16,128,128]{2,1,0:T(8,128)(2,1)}, u32[]{:S(2)}) copy-start(bf16[16,128,128]{2,1,0:T(8,128)(2,1)} %get-tuple-element.44) | copy-start | bytes 1572868
  26.4 6.8 %collective-permute-start.10 = (f32[16,2048]{1,0:T(8,128)S(1)}, f32[16,2048]{1,0:T(8,128)S(1)}, u32[]{:S(2)}, u32[]{:S(2)}) collective-permute-start(f32[16,2048]{1,0:T(8,128)S(1)} %shard_map.68), channel_id=1, source_target_pairs={{0,16},{16,0},{1,17},{17,1},{2,18},{18,2},{3,19},{19,3},{4,20},{20... | collective-permute-start | bytes 393224 | tf_op jit(solution)/shard_map/ppermute | solution.py:244
  27.0 17.7 %collective-permute-start.17 = (bf16[16,128,128]{2,1,0:T(8,128)(2,1)S(1)}, bf16[16,128,128]{2,1,0:T(8,128)(2,1)S(1)}, u32[]{:S(2)}, u32[]{:S(2)}) collective-permute-start(bf16[16,128,128]{2,1,0:T(8,128)(2,1)S(1)} %copy-done.3), channel_id=1, source_target_pairs={{0,16},{16,0},{1,17},{17,1},{2,18},{18,2},{3,19},{19,3},{4,20},{20... | collective-permute-start | bytes 1572872 | tf_op jit(solution)/shard_map/ppermute | solution.py:244
  34.3 5.3 %collective-permute-start.14 = (bf16[18,16,128]{2,1,0:T(8,128)(2,1)S(1)}, bf16[18,16,128]{2,1,0:T(8,128)(2,1)S(1)}, u32[]{:S(2)}, u32[]{:S(2)}) collective-permute-start(bf16[18,16,128]{2,1,0:T(8,128)(2,1)S(1)} %get-tuple-element.39), channel_id=1, source_target_pairs={{0,6},{1,7},{2,4},{3,5},{4,2},{5,3},{6,0},{7,1},{8,14},{9,15},{10,... | collective-permute-start | bytes 221192 | tf_op jit(solution)/shard_map/ppermute | solution.py:238
  36.0 4.6 %collective-permute-start.13 = (bf16[18,16,128]{2,1,0:T(8,128)(2,1)S(1)}, bf16[18,16,128]{2,1,0:T(8,128)(2,1)S(1)}, u32[]{:S(2)}, u32[]{:S(2)}) collective-permute-start(bf16[18,16,128]{2,1,0:T(8,128)(2,1)S(1)} %get-tuple-element.39), channel_id=1, source_target_pairs={{0,4},{1,5},{2,6},{3,7},{4,0},{5,1},{6,2},{7,3},{8,12},{9,13},{10,... | collective-permute-start | bytes 221192 | tf_op jit(solution)/shard_map/ppermute | solution.py:238
  37.5 4.4 %collective-permute-start.12 = (bf16[18,16,128]{2,1,0:T(8,128)(2,1)S(1)}, bf16[18,16,128]{2,1,0:T(8,128)(2,1)S(1)}, u32[]{:S(2)}, u32[]{:S(2)}) collective-permute-start(bf16[18,16,128]{2,1,0:T(8,128)(2,1)S(1)} %get-tuple-element.39), channel_id=1, source_target_pairs={{0,2},{1,3},{2,0},{3,1},{4,6},{5,7},{6,4},{7,5},{8,10},{9,11},{10,... | collective-permute-start | bytes 221192 | tf_op jit(solution)/shard_map/ppermute | solution.py:238
  37.9 12.0 %collective-permute-start.16 = (bf16[17,128,128]{2,1,0:T(8,128)(2,1)S(1)}, bf16[17,128,128]{2,1,0:T(8,128)(2,1)S(1)}, u32[]{:S(2)}, u32[]{:S(2)}) collective-permute-start(bf16[17,128,128]{2,1,0:T(8,128)(2,1)S(1)} %collective-permute-done.11.ins__tiles___0__1_), channel_id=1, source_target_pairs={{0,1},{1,0},{2,3},{3,2},{4,5},{5,4},{6,7},{7,6},{8,9},{9,8},{10,11... | collective-permute-start | bytes 1671176 | tf_op jit(solution)/shard_map/ppermute | solution.py:234
  42.0 6.6 %collective-permute-start.15 = (bf16[24,16,128]{2,1,0:T(8,128)(2,1)S(1)}, bf16[24,16,128]{2,1,0:T(8,128)(2,1)S(1)}, u32[]{:S(2)}, u32[]{:S(2)}) collective-permute-start(bf16[24,16,128]{2,1,0:T(8,128)(2,1)S(1)} %constant_dynamic-update-slice_fusion.4.ins__sent__), channel_id=1, source_target_pairs={{0,8},{1,9},{2,10},{3,11},{4,12},{5,13},{6,14},{7,15},{8,0},{9,1},... | collective-permute-start | bytes 294920 | tf_op jit(solution)/shard_map/ppermute | solution.py:238
  48.6 1.9 %collective-permute-start.18 = (bf16[16,128,128]{2,1,0:T(8,128)(2,1)S(1)}, bf16[16,128,128]{2,1,0:T(8,128)(2,1)S(1)}, u32[]{:S(2)}, u32[]{:S(2)}) collective-permute-start(bf16[16,128,128]{2,1,0:T(8,128)(2,1)S(1)} %collective-permute-done.17.ins__tiles___0__0_), channel_id=1, source_target_pairs={{0,1},{1,0},{2,3},{3,2},{4,5},{5,4},{6,7},{7,6},{8,9},{9,8},{10,11... | collective-permute-start | bytes 1572872 | tf_op jit(solution)/shard_map/ppermute | solution.py:234
  52.1 5.8 %collective-permute-start.21 = (bf16[16,16,128]{2,1,0:T(8,128)(2,1)S(1)}, bf16[16,16,128]{2,1,0:T(8,128)(2,1)S(1)}, u32[]{:S(2)}, u32[]{:S(2)}) collective-permute-start(bf16[16,16,128]{2,1,0:T(8,128)(2,1)S(1)} %get-tuple-element.47), channel_id=1, source_target_pairs={{0,6},{1,7},{2,4},{3,5},{4,2},{5,3},{6,0},{7,1},{8,14},{9,15},{10,... | collective-permute-start | bytes 196616 | tf_op jit(solution)/shard_map/ppermute | solution.py:238
  52.7 5.2 %collective-permute-start.20 = (bf16[16,16,128]{2,1,0:T(8,128)(2,1)S(1)}, bf16[16,16,128]{2,1,0:T(8,128)(2,1)S(1)}, u32[]{:S(2)}, u32[]{:S(2)}) collective-permute-start(bf16[16,16,128]{2,1,0:T(8,128)(2,1)S(1)} %get-tuple-element.47), channel_id=1, source_target_pairs={{0,4},{1,5},{2,6},{3,7},{4,0},{5,1},{6,2},{7,3},{8,12},{9,13},{10,... | collective-permute-start | bytes 196616 | tf_op jit(solution)/shard_map/ppermute | solution.py:238
  52.9 5.6 %collective-permute-start.19 = (bf16[16,16,128]{2,1,0:T(8,128)(2,1)S(1)}, bf16[16,16,128]{2,1,0:T(8,128)(2,1)S(1)}, u32[]{:S(2)}, u32[]{:S(2)}) collective-permute-start(bf16[16,16,128]{2,1,0:T(8,128)(2,1)S(1)} %get-tuple-element.47), channel_id=1, source_target_pairs={{0,2},{1,3},{2,0},{3,1},{4,6},{5,7},{6,4},{7,5},{8,10},{9,11},{10,... | collective-permute-start | bytes 196616 | tf_op jit(solution)/shard_map/ppermute | solution.py:238
  55.6 6.1 %collective-permute-start.8 = (bf16[16,16,128]{2,1,0:T(8,128)(2,1)S(1)}, bf16[16,16,128]{2,1,0:T(8,128)(2,1)S(1)}, u32[]{:S(2)}, u32[]{:S(2)}) collective-permute-start(bf16[16,16,128]{2,1,0:T(8,128)(2,1)S(1)} %get-tuple-element.32), channel_id=1, source_target_pairs={{0,16},{16,0},{1,17},{17,1},{2,18},{18,2},{3,19},{19,3},{4,20},{20... | collective-permute-start | bytes 196616 | tf_op jit(solution)/shard_map/ppermute | solution.py:244
  58.6 6.1 %collective-permute-start.22 = (bf16[16,16,128]{2,1,0:T(8,128)(2,1)S(1)}, bf16[16,16,128]{2,1,0:T(8,128)(2,1)S(1)}, u32[]{:S(2)}, u32[]{:S(2)}) collective-permute-start(bf16[16,16,128]{2,1,0:T(8,128)(2,1)S(1)} %get-tuple-element.57), channel_id=1, source_target_pairs={{0,8},{1,9},{2,10},{3,11},{4,12},{5,13},{6,14},{7,15},{8,0},{9,1},... | collective-permute-start | bytes 196616 | tf_op jit(solution)/shard_map/ppermute | solution.py:238
  67.0 5.2 %collective-permute-start.25 = (bf16[16,16,128]{2,1,0:T(8,128)(2,1)S(1)}, bf16[16,16,128]{2,1,0:T(8,128)(2,1)S(1)}, u32[]{:S(2)}, u32[]{:S(2)}) collective-permute-start(bf16[16,16,128]{2,1,0:T(8,128)(2,1)S(1)} %get-tuple-element.51), channel_id=1, source_target_pairs={{0,6},{1,7},{2,4},{3,5},{4,2},{5,3},{6,0},{7,1},{8,14},{9,15},{10,... | collective-permute-start | bytes 196616 | tf_op jit(solution)/shard_map/ppermute | solution.py:238
  67.6 5.0 %collective-permute-start.24 = (bf16[16,16,128]{2,1,0:T(8,128)(2,1)S(1)}, bf16[16,16,128]{2,1,0:T(8,128)(2,1)S(1)}, u32[]{:S(2)}, u32[]{:S(2)}) collective-permute-start(bf16[16,16,128]{2,1,0:T(8,128)(2,1)S(1)} %get-tuple-element.51), channel_id=1, source_target_pairs={{0,4},{1,5},{2,6},{3,7},{4,0},{5,1},{6,2},{7,3},{8,12},{9,13},{10,... | collective-permute-start | bytes 196616 | tf_op jit(solution)/shard_map/ppermute | solution.py:238
  69.7 4.3 %collective-permute-start.23 = (bf16[16,16,128]{2,1,0:T(8,128)(2,1)S(1)}, bf16[16,16,128]{2,1,0:T(8,128)(2,1)S(1)}, u32[]{:S(2)}, u32[]{:S(2)}) collective-permute-start(bf16[16,16,128]{2,1,0:T(8,128)(2,1)S(1)} %get-tuple-element.51), channel_id=1, source_target_pairs={{0,2},{1,3},{2,0},{3,1},{4,6},{5,7},{6,4},{7,5},{8,10},{9,11},{10,... | collective-permute-start | bytes 196616 | tf_op jit(solution)/shard_map/ppermute | solution.py:238
  74.0 5.6 %collective-permute-start.26 = (bf16[16,16,128]{2,1,0:T(8,128)(2,1)S(1)}, bf16[16,16,128]{2,1,0:T(8,128)(2,1)S(1)}, u32[]{:S(2)}, u32[]{:S(2)}) collective-permute-start(bf16[16,16,128]{2,1,0:T(8,128)(2,1)S(1)} %get-tuple-element.55), channel_id=1, source_target_pairs={{0,8},{1,9},{2,10},{3,11},{4,12},{5,13},{6,14},{7,15},{8,0},{9,1},... | collective-permute-start | bytes 196616 | tf_op jit(solution)/shard_map/ppermute | solution.py:238
  80.6 1.4 %collective-permute-start.27 = (f32[16,2048]{1,0:T(8,128)S(1)}, f32[16,2048]{1,0:T(8,128)S(1)}, u32[]{:S(2)}, u32[]{:S(2)}) collective-permute-start(f32[16,2048]{1,0:T(8,128)S(1)} %get-tuple-element.54), channel_id=1, source_target_pairs={{0,1},{1,0},{2,3},{3,2},{4,5},{5,4},{6,7},{7,6},{8,9},{9,8},{10,11... | collective-permute-start | bytes 393224 | tf_op jit(solution)/shard_map/ppermute | solution.py:234

commit v10 on v9

--- a/solution.py
+++ b/solution.py
@@ -18,7 +18,7 @@
 
 
 def entry(index, k, row, t):
-    return index[k][row, t] if isinstance(index, tuple) else index[3 * k + row, t]
+    return index[k][row][0, t] if isinstance(index, tuple) else index[3 * k + row, t]
 
 
 def core_here():
@@ -119,22 +119,10 @@
                 outs["sent"][rays + side * held + b] = block.astype(jnp.bfloat16)
 
 
-def first_kernel(ins, outs, low, acc, own, arrived):
-    copy = pltpu.make_async_copy(ins["own_hbm"], own, arrived)
-    copy.start()
-    for k, cols, at in columns(ins["held"], low.shape[-1]):
-        low[at] = frames_of(ins["held"][k], low.shape[1], cols).astype(jnp.bfloat16)
-    acc[...] = jnp.zeros_like(acc)
-    project_into(acc, low, ins["index"], (None, ins["tiles"]))
-    copy.wait()
-    project_into(acc, low, ins["index"], ((own,), None))
-    write_sums(0, ins, outs, acc)
-
-
 def project_kernel(r, ins, outs, low, acc):
     acc[...] = ins["begun"][...] if "begun" in ins else jnp.zeros_like(acc)
     for k, cols, at in columns(ins["held"], low.shape[-1]):
-        low[at] = ins["held"][k][:, cols].astype(jnp.bfloat16)
+        low[at] = frames_of(ins["held"][k], low.shape[1], cols).astype(jnp.bfloat16)
     project_into(acc, low, ins["index"], ins["tiles"])
     write_sums(r, ins, outs, acc)
 
@@ -188,7 +176,7 @@
 
     def spec(path, _):
         name = path[0].key
-        space = pltpu.SMEM if name.endswith("index") else pltpu.HBM if name.endswith("hbm") else pltpu.VMEM
+        space = pltpu.SMEM if name.endswith("index") else pltpu.VMEM
         return pl.BlockSpec(memory_space=space)
 
     return pl.pallas_call(
@@ -246,16 +234,15 @@
     def after(array, value):
         return lax.optimization_barrier((array, value))[0]
 
-    rows = jnp.concatenate([tile_vox, tile_ray, jnp.broadcast_to(live_blocks, tile_vox.shape)], axis=0)
-    own_index = jnp.pad(rows, ((0, 5), (0, -slots % LANES)))
+    rows = (tile_vox, tile_ray, live_blocks)
     tiles = ((own_tiles,), (swap_cores(own_tiles),))
     held = (images, swap_cores(images))
-    first_index = (own_index, swap_cores(own_index))
-
-    def merged(own, other):
-        return jnp.concatenate([own[:3], other[:3], jnp.zeros_like(own[:2])])
-
-    index = merged(*first_index)
+    first_index = (rows, tuple(swap_cores(row) for row in rows))
+
+    def packed(own, other):
+        spread = [jnp.broadcast_to(row, (1, slots)) for row in own + other]
+        return jnp.pad(jnp.concatenate(spread), ((0, 2), (0, -slots % LANES)))
+
     dealt = (counts[0], swap_cores(counts[0]))
 
     def sensitivity(index, tiles):
@@ -263,11 +250,10 @@
                     {"inverse": shaped((both, 8, size), f32)},
                     [pltpu.VMEM((both, 8, size), f32)])["inverse"]
 
-    sets = [(index, tiles, sensitivity(index, tiles))] * ROUNDS
     moves = [True] * (ROUNDS - 1)
     known = [None] * ROUNDS
     two = subset_count == 2 and ray_blocks <= 256 and slots <= size and size == LANES
-    late = slots // 2
+    late = slots * 19 // 32
     if two:
         moves = [r == 0 for r in range(ROUNDS - 1)]
 
@@ -286,13 +272,19 @@
                 {"wide": summed, "sent": shaped((sent, half, size), bf16)})
 
     extra, outs = sums(0)
-    out = call(first_kernel, {"held": held, "index": first_index, "own_hbm": own_tiles, "tiles": tiles[1], **extra},
-               outs, [low_scratch, sum_scratch, pltpu.VMEM(own_tiles.shape, bf16), pltpu.SemaphoreType.DMA])
+    begun = call(functools.partial(project_kernel, 0),
+                 {"held": only(0, held), "index": only(0, first_index), "tiles": only(0, tiles)},
+                 {"wide": summed}, [low_scratch, sum_scratch])["wide"]
+    out = call(functools.partial(project_kernel, 0),
+               {"held": only(1, held), "index": only(1, first_index), "tiles": only(1, tiles), "begun": begun, **extra},
+               outs, [low_scratch, sum_scratch])
+    index = packed(*after(first_index, out["sent"]))
+    sets = [(index, tiles, sensitivity(index, tiles))] * ROUNDS
     for r in range(ROUNDS):
         wide, sent = out["wide"], out["sent"]
         if two and r == 0:
-            tiles_then, rows_then = after((own_tiles[late:], own_index), sent)
-            slot = jnp.pad(rows_then.astype(bf16), ((0, size - 8), (0, 0)))[None]
+            tiles_then = after(own_tiles[late:], sent)
+            slot = jnp.pad(index.astype(bf16), ((0, size - 8), (0, 0)))[None]
             far_second = shift(jnp.concatenate([tiles_then, slot]))
         if two and r == 1:
             other_second = swap_cores(after(far_second, sent))
@@ -314,7 +306,7 @@
         if two and r == 1:
             other_first = swap_cores(after(far_first, tuple(got)))
             far_tiles = ((far_first, far_second), (other_first, other_second))
-            far_index = merged(*(piece[-1, :8].astype(jnp.int32) for piece in (far_second, other_second)))
+            far_index = far_second[-1, :8].astype(jnp.int32)
             far = (far_index, far_tiles, sensitivity(far_index, far_tiles))
             sets = [far if later >= 2 and later % 2 == 0 else sets[later] for later in range(ROUNDS)]
         now_index, now_tiles, now_inverse = sets[r]

time: 83 us -> 87.7 us (1.057)
  local copies, waits for them, and re-layouts: 3.61 us -> 6.18 us
  waiting for transfers between devices: 29.4 us -> 31.8 us
  starting transfers between devices: 32.4 us -> 30 us
  other arithmetic: 1.18 us -> 2.32 us
  Pallas kernels: 15.2 us -> 16.2 us
    ppermute x5, starting transfers between devices: 6.8 us -> 4.66 us  [shift(): lax.ppermute(array, 'subset', [(i, (i + 1) % subset_count) for i in range...]
    slice x1, local copies, waits for them, and re-layouts: 2.14 us -> 0.04 us  [shards(): far_first = shift(after(own_tiles[:late], moved[k]))]
    ppermute x16, starting transfers between devices: 24.5 us -> 22.8 us  [swap_chips(): return lax.ppermute(array, 'tile', pairs)]
    broadcast_in_dim x1 -> x3, local copies, waits for them, and re-layouts: 0.01 us -> 1.65 us  [the longest x2 1.65 us: packed(): spread = [jnp.broadcast_to(row, (1, slots)) for row in own + other]]
    ppermute x7 -> x9, starting transfers between devices: 1.14 us -> 2.58 us  [swap_cores(): return lax.ppermute(array, 'tile', [(i, i ^ 1) for i in range(tile_devs)])]
    ppermute x7 -> x9, waiting for transfers between devices: 0.94 us -> 2.13 us  [swap_cores(): return lax.ppermute(array, 'tile', [(i, i ^ 1) for i in range(tile_devs)])]
    slice x2 -> x1, local copies, waits for them, and re-layouts: 0.01 us -> 1.08 us  [shards(): tiles_then = after(own_tiles[late:], sent)]
    concatenate x2 -> x1, local copies, waits for them, and re-layouts: 0.15 us -> 1.22 us  [packed(): return jnp.pad(jnp.concatenate(spread), ((0, 2), (0, -slots % LANES)))]
  transfers between devices with their start and end apart: 28 -> 30, of which waited for: 19 -> 16; matrix products, arithmetic and copies ran while one was open for 3% -> 7% of each run, Pallas kernels for 10% -> 11%
where the time goes in v10:
time: 87.7 us; the launch traced here: 87.5 us
  waiting for transfers between devices  31.8 us (36%)
  starting transfers between devices  30 us (34%)
  Pallas kernels  16.2 us (18%)
  local copies, waits for them, and re-layouts  6.18 us (7%)
  other arithmetic  2.32 us (3%)
  between operations  0.97 us (1%)
    ppermute x16, waiting for transfers between devices, swap_chips(): return lax.ppermute(array, 'tile', pairs)  25.1 us
    ppermute x16, starting transfers between devices, swap_chips(): return lax.ppermute(array, 'tile', pairs)  22.8 us
    pallas_call x13, Pallas kernels, call(): pl.pallas_call(kernel, out_shape=outs, in_specs=[jax.tree_util.tree_map_w...  16.2 us
    ppermute x5, starting transfers between devices, shift(): lax.ppermute(array, 'subset', [(i, (i + 1) % subset_count) for i in range...  4.66 us
    ppermute x5, waiting for transfers between devices, shift(): lax.ppermute(array, 'subset', [(i, (i + 1) % subset_count) for i in range...  4.54 us
    ppermute x9, starting transfers between devices, swap_cores(): return lax.ppermute(array, 'tile', [(i, i ^ 1) for i in range(tile_devs)])  2.58 us
    ppermute x9, waiting for transfers between devices, swap_cores(): return lax.ppermute(array, 'tile', [(i, i ^ 1) for i in range(tile_devs)])  2.13 us
  transfers between devices with their start and end apart: 30, of which 16 were waited for; matrix products, arithmetic and copies ran while one was open for 7% of the time, Pallas kernels for 11%

profile of v10, /device:TPU:0, one launch (start us, length us, event | category | flops | bytes accessed | tf_op | source)
XLA Modules:
  0.0 87.5 jit_solution(17915899472533046127)
XLA Ops:
  2.4 1.1 %slice_bitcast_fusion.1 = bf16[13,128,128]{2,1,0:T(8,128)(2,1)S(1)} fusion(bf16[1,32,128,128]{3,2,1,0:T(8,128)(2,1)} %param.7), kind=kLoop, calls=%fused_computation.2 | loop fusion | bytes 851968 | tf_op jit(solution)/shard_map/slice | solution.py:286
  3.5 1.2 %copy-done = bf16[1,32,128,128]{3,2,1,0:T(8,128)(2,1)S(1)} copy-done((bf16[1,32,128,128]{3,2,1,0:T(8,128)(2,1)S(1)}, bf16[1,32,128,128]{3,2,1,0:T(8,128)(2,1)}, u32[]{:S(2)}) %copy-start) | copy-done | bytes 1048600
  4.7 1.0 %shard_map.64.ins__begun__ = f32[16,16,128]{2,1,0:T(8,128)S(1)} custom-call(f32[32,2048]{1,0:T(8,128)S(1)} %copy-done.4, s32[1,32]{1,0:T(1,128)S(1)} %copy-done.2, s32[1,32]{1,0:T(1,128)S(1)} %copy-done.3, s32[1,1]{1,0:T(1,128)} %copy.15.ins__index___0__2_, bf16[32,128,128]{2,1,0:T(8,128)(2,1)S(1)} %bitcast.47), custom_call_target="tpu_custom_call" | custom-call | flops 536870912 | tf_op jit(solution)/shard_map/pallas_call | solution.py:182
  6.2 0.8 collective-permute-done.3.ins__index___1__1_
  7.1 1.7 %shard_map.65 = (bf16[18,16,128]{2,1,0:T(8,128)(2,1)S(1)}, f32[16,16,128]{2,1,0:T(8,128)S(1)}) custom-call(f32[16,16,128]{2,1,0:T(8,128)S(1)} %shard_map.64.ins__begun__, s32[64,128]{1,0:T(8,128)S(1)} %bitcast.55, s32[64,128]{1,0:T(8,128)S(1)} %collective-permute-done.ins__dealt___1_, f32[32,2048]{1,0:T(8,128)S(1)} %collective-permute-done.1.ins__held___1_, ...), custom_call_target="tpu_custom_call" | custom-call | flops 536870912 | tf_op jit(solution)/shard_map/pallas_call | solution.py:182
  9.4 3.8 %collective-permute-start.8 = (bf16[18,16,128]{2,1,0:T(8,128)(2,1)S(1)}, bf16[18,16,128]{2,1,0:T(8,128)(2,1)S(1)}, u32[]{:S(2)}, u32[]{:S(2)}) collective-permute-start(bf16[18,16,128]{2,1,0:T(8,128)(2,1)S(1)} %get-tuple-element.36), channel_id=1, source_target_pairs={{0,6},{1,7},{2,4},{3,5},{4,2},{5,3},{6,0},{7,1},{8,14},{9,15},{10,... | collective-permute-start | bytes 221192 | tf_op jit(solution)/shard_map/ppermute | solution.py:226
  14.3 1.2 %broadcast_in_dim.20 = s32[1,32]{1,0:T(1,128)} broadcast(s32[]{:T(128)} %bitcast.11), dimensions={} | broadcast | bytes 132 | tf_op jit(solution)/shard_map/broadcast_in_dim | solution.py:243
  15.4 1.2 %concatenate.19 = s32[6,32]{1,0:T(8,128)} concatenate(s32[1,32]{1,0:T(1,128)S(1)} %copy-done.2, s32[1,32]{1,0:T(1,128)S(1)} %copy-done.3, s32[1,32]{1,0:T(1,128)} %broadcast_in_dim.18, s32[1,32]{1,0:T(1,128)S(1)} %collective-permute-done.2.ins__index___1__0_, s32[1,32]{1,0:T(1,128)S(1)} %collective-permute-done.3.ins__index___1__1_, s32[1,32]{1,0:T(1,128)} %broadcast_in_dim.20), dimensions={0} | concatenate | bytes 1536 | tf_op jit(solution)/shard_map/concatenate | solution.py:244
  16.6 0.7 pad_convert_fusion
  17.4 1.9 %collective-permute-start.13 = (bf16[14,128,128]{2,1,0:T(8,128)(2,1)S(1)}, bf16[14,128,128]{2,1,0:T(8,128)(2,1)S(1)}, u32[]{:S(2)}, u32[]{:S(2)}) collective-permute-start(bf16[14,128,128]{2,1,0:T(8,128)(2,1)S(1)} %pad_maximum_fusion), channel_id=1, source_target_pairs={{0,16},{16,0},{1,17},{17,1},{2,18},{18,2},{3,19},{19,3},{4,20},{20... | collective-permute-start | bytes 1376264 | tf_op jit(solution)/shard_map/ppermute | solution.py:232
  19.4 0.7 pad_maximum_fusion.1
  20.2 2.7 %collective-permute-start.9 = (bf16[24,16,128]{2,1,0:T(8,128)(2,1)S(1)}, bf16[24,16,128]{2,1,0:T(8,128)(2,1)S(1)}, u32[]{:S(2)}, u32[]{:S(2)}) collective-permute-start(bf16[24,16,128]{2,1,0:T(8,128)(2,1)S(1)} %constant_dynamic-update-slice_fusion.ins__sent__), channel_id=1, source_target_pairs={{0,8},{1,9},{2,10},{3,11},{4,12},{5,13},{6,14},{7,15},{8,0},{9,1},... | collective-permute-start | bytes 294920 | tf_op jit(solution)/shard_map/ppermute | solution.py:226
  22.8 1.2 %shard_map.66.ins__inverse__ = f32[32,8,128]{2,1,0:T(8,128)S(1)} custom-call(s32[8,128]{1,0:T(8,128)S(1)} %get-tuple-element.74.ins__index__.ins__next_index__, bf16[32,128,128]{2,1,0:T(8,128)(2,1)S(1)} %bitcast.48, bf16[32,128,128]{2,1,0:T(8,128)(2,1)S(1)} %collective-permute-done.5.ins__tiles___1__0_.ins__next_tiles___1__0_), custom_call_target="tpu_custom_call" | custom-call | flops 1073741824 | tf_op jit(solution)/shard_map/pallas_call | solution.py:182
  24.0 3.0 %collective-permute-done.9.ins__got___0_ = bf16[24,16,128]{2,1,0:T(8,128)(2,1)S(1)} collective-permute-done((bf16[24,16,128]{2,1,0:T(8,128)(2,1)S(1)}, bf16[24,16,128]{2,1,0:T(8,128)(2,1)S(1)}, u32[]{:S(2)}, u32[]{:S(2)}) %collective-permute-start.9) | collective-permute-done | bytes 98336 | tf_op jit(solution)/shard_map/ppermute | solution.py:226
  27.0 1.0 %shard_map.67 = (bf16[16,16,128]{2,1,0:T(8,128)(2,1)S(1)}, f32[16,2048]{1,0:T(8,128)S(1)}, bf16[16,16,128]{2,1,0:T(8,128)(2,1)S(1)}) custom-call(bf16[24,16,128]{2,1,0:T(8,128)(2,1)S(1)} %collective-permute-done.9.ins__got___0_, f32[32,2048]{1,0:T(8,128)S(1)} %copy-done.4, s32[8,128]{1,0:T(8,128)S(1)} %get-tuple-element.74.ins__index__.ins__next_index__, ...), custom_call_target="tpu_custom_call" | custom-call | flops 536870912 | tf_op jit(solution)/shard_map/pallas_call | solution.py:182
  28.6 0.9 %shard_map.69 = f32[16,2048]{1,0:T(8,128)S(1)} custom-call(f32[32,2048]{1,0:T(8,128)S(1)} %collective-permute-done.1.ins__held___1_, s32[8,128]{1,0:T(8,128)S(1)} %get-tuple-element.74.ins__index__.ins__next_index__, f32[32,8,128]{2,1,0:T(8,128)S(1)} %shard_map.66.ins__inverse__, bf16[16,16,128]{2,1,0:T(8,128)(2,1)S(1)} %get-tuple-element.45.ins__ratios__, ...), custom_call_target="tpu_custom_call" | custom-call | flops 536870912 | tf_op jit(solution)/shard_map/pallas_call | solution.py:182
  29.5 1.6 %collective-permute-start.12 = (f32[16,2048]{1,0:T(8,128)S(1)}, f32[16,2048]{1,0:T(8,128)S(1)}, u32[]{:S(2)}, u32[]{:S(2)}) collective-permute-start(f32[16,2048]{1,0:T(8,128)S(1)} %shard_map.69), channel_id=1, source_target_pairs={{0,16},{16,0},{1,17},{17,1},{2,18},{18,2},{3,19},{19,3},{4,20},{20... | collective-permute-start | bytes 393224 | tf_op jit(solution)/shard_map/ppermute | solution.py:232
  31.7 2.8 %collective-permute-done.11.ins__held___0_ = f32[16,2048]{1,0:T(8,128)S(1)} collective-permute-done((f32[16,2048]{1,0:T(8,128)S(1)}, f32[16,2048]{1,0:T(8,128)S(1)}, u32[]{:S(2)}, u32[]{:S(2)}) %collective-permute-start.11) | collective-permute-done | bytes 131104 | tf_op jit(solution)/shard_map/ppermute | solution.py:232
  34.5 1.1 %shard_map.68.ins__begun__ = f32[16,16,128]{2,1,0:T(8,128)S(1)} custom-call(f32[16,2048]{1,0:T(8,128)S(1)} %collective-permute-done.11.ins__held___0_, s32[8,128]{1,0:T(8,128)S(1)} %get-tuple-element.74.ins__index__.ins__next_index__, bf16[32,128,128]{2,1,0:T(8,128)(2,1)S(1)} %bitcast.50), custom_call_target="tpu_custom_call" | custom-call | flops 536870912 | tf_op jit(solution)/shard_map/pallas_call | solution.py:182
  35.6 1.7 %collective-permute-done.12.ins__held___1_ = f32[16,2048]{1,0:T(8,128)S(1)} collective-permute-done((f32[16,2048]{1,0:T(8,128)S(1)}, f32[16,2048]{1,0:T(8,128)S(1)}, u32[]{:S(2)}, u32[]{:S(2)}) %collective-permute-start.12) | collective-permute-done | bytes 131104 | tf_op jit(solution)/shard_map/ppermute | solution.py:232
  37.3 1.1 %shard_map.70 = (bf16[18,16,128]{2,1,0:T(8,128)(2,1)S(1)}, f32[16,16,128]{2,1,0:T(8,128)S(1)}) custom-call(f32[16,16,128]{2,1,0:T(8,128)S(1)} %shard_map.68.ins__begun__, s32[64,128]{1,0:T(8,128)S(1)} %bitcast.56, s32[64,128]{1,0:T(8,128)S(1)} %collective-permute-done.ins__dealt___1_, f32[16,2048]{1,0:T(8,128)S(1)} %collective-permute-done.12.ins__held___1_, ...), custom_call_target="tpu_custom_call" | custom-call | flops 536870912 | tf_op jit(solution)/shard_map/pallas_call | solution.py:182
  38.4 2.2 %collective-permute-start.16 = (bf16[18,16,128]{2,1,0:T(8,128)(2,1)S(1)}, bf16[18,16,128]{2,1,0:T(8,128)(2,1)S(1)}, u32[]{:S(2)}, u32[]{:S(2)}) collective-permute-start(bf16[18,16,128]{2,1,0:T(8,128)(2,1)S(1)} %get-tuple-element.49), channel_id=1, source_target_pairs={{0,6},{1,7},{2,4},{3,5},{4,2},{5,3},{6,0},{7,1},{8,14},{9,15},{10,... | collective-permute-start | bytes 221192 | tf_op jit(solution)/shard_map/ppermute | solution.py:226
  40.6 0.9 collective-permute-start.15
  42.0 1.8 %collective-permute-done.16 = bf16[18,16,128]{2,1,0:T(8,128)(2,1)S(1)} collective-permute-done((bf16[18,16,128]{2,1,0:T(8,128)(2,1)S(1)}, bf16[18,16,128]{2,1,0:T(8,128)(2,1)S(1)}, u32[]{:S(2)}, u32[]{:S(2)}) %collective-permute-start.16) | collective-permute-done | bytes 73760 | tf_op jit(solution)/shard_map/ppermute | solution.py:226
  43.7 2.3 %collective-permute-done.15 = bf16[18,16,128]{2,1,0:T(8,128)(2,1)S(1)} collective-permute-done((bf16[18,16,128]{2,1,0:T(8,128)(2,1)S(1)}, bf16[18,16,128]{2,1,0:T(8,128)(2,1)S(1)}, u32[]{:S(2)}, u32[]{:S(2)}) %collective-permute-start.15) | collective-permute-done | bytes 73760 | tf_op jit(solution)/shard_map/ppermute | solution.py:226
  46.2 2.0 %collective-permute-start.17 = (bf16[24,16,128]{2,1,0:T(8,128)(2,1)S(1)}, bf16[24,16,128]{2,1,0:T(8,128)(2,1)S(1)}, u32[]{:S(2)}, u32[]{:S(2)}) collective-permute-start(bf16[24,16,128]{2,1,0:T(8,128)(2,1)S(1)} %constant_dynamic-update-slice_fusion.4.ins__sent__), channel_id=1, source_target_pairs={{0,8},{1,9},{2,10},{3,11},{4,12},{5,13},{6,14},{7,15},{8,0},{9,1},... | collective-permute-start | bytes 294920 | tf_op jit(solution)/shard_map/ppermute | solution.py:226
  48.2 4.6 %collective-permute-done.17.ins__got___0_ = bf16[24,16,128]{2,1,0:T(8,128)(2,1)S(1)} collective-permute-done((bf16[24,16,128]{2,1,0:T(8,128)(2,1)S(1)}, bf16[24,16,128]{2,1,0:T(8,128)(2,1)S(1)}, u32[]{:S(2)}, u32[]{:S(2)}) %collective-permute-start.17) | collective-permute-done | bytes 98336 | tf_op jit(solution)/shard_map/ppermute | solution.py:226
  53.3 1.3 %shard_map.71 = (bf16[16,16,128]{2,1,0:T(8,128)(2,1)S(1)}, f32[16,2048]{1,0:T(8,128)S(1)}, f32[16,2048]{1,0:T(8,128)S(1)}) custom-call(bf16[24,16,128]{2,1,0:T(8,128)(2,1)S(1)} %collective-permute-done.17.ins__got___0_, f32[16,2048]{1,0:T(8,128)S(1)} %collective-permute-done.11.ins__held___0_, f32[16,2048]{1,0:T(8,128)S(1)} %collective-permute-done.12.ins__held___1_, ...), custom_call_target="tpu_custom_call" | custom-call | flops 1073741824 | tf_op jit(solution)/shard_map/pallas_call | solution.py:182
  54.6 0.9 %collective-permute-done.20.ins__tiles___1__1_ = bf16[14,128,128]{2,1,0:T(8,128)(2,1)S(1)} collective-permute-done((bf16[14,128,128]{2,1,0:T(8,128)(2,1)S(1)}, bf16[14,128,128]{2,1,0:T(8,128)(2,1)S(1)}, u32[]{:S(2)}, u32[]{:S(2)}) %collective-permute-start.20) | collective-permute-done | bytes 458784 | tf_op jit(solution)/shard_map/ppermute | solution.py:222
  55.5 1.6 %shard_map.72 = (bf16[16,16,128]{2,1,0:T(8,128)(2,1)S(1)}, f32[16,16,128]{2,1,0:T(8,128)S(1)}) custom-call(f32[16,2048]{1,0:T(8,128)S(1)} %get-tuple-element.50.ins__held___0_, f32[16,2048]{1,0:T(8,128)S(1)} %get-tuple-element.51.ins__held___1_, s32[8,128]{1,0:T(8,128)S(1)} %bitcast_convert_fusion.ins__index__, ...), custom_call_target="tpu_custom_call" | custom-call | flops 2147483648 | tf_op jit(solution)/shard_map/pallas_call | solution.py:182
  57.3 1.8 %collective-permute-start.22 = (bf16[16,16,128]{2,1,0:T(8,128)(2,1)S(1)}, bf16[16,16,128]{2,1,0:T(8,128)(2,1)S(1)}, u32[]{:S(2)}, u32[]{:S(2)}) collective-permute-start(bf16[16,16,128]{2,1,0:T(8,128)(2,1)S(1)} %get-tuple-element.57), channel_id=1, source_target_pairs={{0,4},{1,5},{2,6},{3,7},{4,0},{5,1},{6,2},{7,3},{8,12},{9,13},{10,... | collective-permute-start | bytes 196616 | tf_op jit(solution)/shard_map/ppermute | solution.py:226
  59.1 1.5 %collective-permute-start.21 = (bf16[16,16,128]{2,1,0:T(8,128)(2,1)S(1)}, bf16[16,16,128]{2,1,0:T(8,128)(2,1)S(1)}, u32[]{:S(2)}, u32[]{:S(2)}) collective-permute-start(bf16[16,16,128]{2,1,0:T(8,128)(2,1)S(1)} %get-tuple-element.57), channel_id=1, source_target_pairs={{0,2},{1,3},{2,0},{3,1},{4,6},{5,7},{6,4},{7,5},{8,10},{9,11},{10,... | collective-permute-start | bytes 196616 | tf_op jit(solution)/shard_map/ppermute | solution.py:226
  60.6 2.3 %collective-permute-done.23 = bf16[16,16,128]{2,1,0:T(8,128)(2,1)S(1)} collective-permute-done((bf16[16,16,128]{2,1,0:T(8,128)(2,1)S(1)}, bf16[16,16,128]{2,1,0:T(8,128)(2,1)S(1)}, u32[]{:S(2)}, u32[]{:S(2)}) %collective-permute-start.23) | collective-permute-done | bytes 65568 | tf_op jit(solution)/shard_map/ppermute | solution.py:226
  62.9 0.7 collective-permute-done.21
  63.6 1.4 %collective-permute-start.24 = (bf16[16,16,128]{2,1,0:T(8,128)(2,1)S(1)}, bf16[16,16,128]{2,1,0:T(8,128)(2,1)S(1)}, u32[]{:S(2)}, u32[]{:S(2)}) collective-permute-start(bf16[16,16,128]{2,1,0:T(8,128)(2,1)S(1)} %get-tuple-element.67), channel_id=1, source_target_pairs={{0,8},{1,9},{2,10},{3,11},{4,12},{5,13},{6,14},{7,15},{8,0},{9,1},... | collective-permute-start | bytes 196616 | tf_op jit(solution)/shard_map/ppermute | solution.py:226
  65.1 1.2 %shard_map.73.ins__inverse__ = f32[32,8,128]{2,1,0:T(8,128)S(1)} custom-call(s32[8,128]{1,0:T(8,128)S(1)} %bitcast_convert_fusion.ins__index__, bf16[19,128,128]{2,1,0:T(8,128)(2,1)S(1)} %collective-permute-done.18.ins__tiles___0__0_, bf16[14,128,128]{2,1,0:T(8,128)(2,1)S(1)} %collective-permute-done.13.ins__tiles___0__1_, ...), custom_call_target="tpu_custom_call" | custom-call | flops 2147483648 | tf_op jit(solution)/shard_map/pallas_call | solution.py:182
  66.3 3.2 %collective-permute-done.24.ins__got___0_ = bf16[16,16,128]{2,1,0:T(8,128)(2,1)S(1)} collective-permute-done((bf16[16,16,128]{2,1,0:T(8,128)(2,1)S(1)}, bf16[16,16,128]{2,1,0:T(8,128)(2,1)S(1)}, u32[]{:S(2)}, u32[]{:S(2)}) %collective-permute-start.24) | collective-permute-done | bytes 65568 | tf_op jit(solution)/shard_map/ppermute | solution.py:226
  69.5 2.3 %shard_map.74 = (f32[16,2048]{1,0:T(8,128)S(1)}, f32[16,2048]{1,0:T(8,128)S(1)}, bf16[16,16,128]{2,1,0:T(8,128)(2,1)S(1)}, f32[16,16,128]{2,1,0:T(8,128)S(1)}) custom-call(bf16[16,16,128]{2,1,0:T(8,128)(2,1)S(1)} %collective-permute-done.10.ins__counts__, bf16[16,16,128]{2,1,0:T(8,128)(2,1)S(1)} %collective-permute-done.24.ins__got___0_, ...), custom_call_target="tpu_custom_call" | custom-call | flops 2147483648 | tf_op jit(solution)/shard_map/pallas_call | solution.py:182
  71.8 0.7 collective-permute-start.27
  72.6 2.1 %collective-permute-start.26 = (bf16[16,16,128]{2,1,0:T(8,128)(2,1)S(1)}, bf16[16,16,128]{2,1,0:T(8,128)(2,1)S(1)}, u32[]{:S(2)}, u32[]{:S(2)}) collective-permute-start(bf16[16,16,128]{2,1,0:T(8,128)(2,1)S(1)} %get-tuple-element.61), channel_id=1, source_target_pairs={{0,4},{1,5},{2,6},{3,7},{4,0},{5,1},{6,2},{7,3},{8,12},{9,13},{10,... | collective-permute-start | bytes 196616 | tf_op jit(solution)/shard_map/ppermute | solution.py:226
  74.6 0.7 collective-permute-start.25
  75.4 1.7 %collective-permute-done.27 = bf16[16,16,128]{2,1,0:T(8,128)(2,1)S(1)} collective-permute-done((bf16[16,16,128]{2,1,0:T(8,128)(2,1)S(1)}, bf16[16,16,128]{2,1,0:T(8,128)(2,1)S(1)}, u32[]{:S(2)}, u32[]{:S(2)}) %collective-permute-start.27) | collective-permute-done | bytes 65568 | tf_op jit(solution)/shard_map/ppermute | solution.py:226
  77.6 1.3 %collective-permute-done.25 = bf16[16,16,128]{2,1,0:T(8,128)(2,1)S(1)} collective-permute-done((bf16[16,16,128]{2,1,0:T(8,128)(2,1)S(1)}, bf16[16,16,128]{2,1,0:T(8,128)(2,1)S(1)}, u32[]{:S(2)}, u32[]{:S(2)}) %collective-permute-start.25) | collective-permute-done | bytes 65568 | tf_op jit(solution)/shard_map/ppermute | solution.py:226
  79.0 1.6 %collective-permute-start.28 = (bf16[16,16,128]{2,1,0:T(8,128)(2,1)S(1)}, bf16[16,16,128]{2,1,0:T(8,128)(2,1)S(1)}, u32[]{:S(2)}, u32[]{:S(2)}) collective-permute-start(bf16[16,16,128]{2,1,0:T(8,128)(2,1)S(1)} %get-tuple-element.65), channel_id=1, source_target_pairs={{0,8},{1,9},{2,10},{3,11},{4,12},{5,13},{6,14},{7,15},{8,0},{9,1},... | collective-permute-start | bytes 196616 | tf_op jit(solution)/shard_map/ppermute | solution.py:226
  80.6 3.8 %collective-permute-done.28.ins__got___0_ = bf16[16,16,128]{2,1,0:T(8,128)(2,1)S(1)} collective-permute-done((bf16[16,16,128]{2,1,0:T(8,128)(2,1)S(1)}, bf16[16,16,128]{2,1,0:T(8,128)(2,1)S(1)}, u32[]{:S(2)}, u32[]{:S(2)}) %collective-permute-start.28) | collective-permute-done | bytes 65568 | tf_op jit(solution)/shard_map/ppermute | solution.py:226
  84.3 1.0 %shard_map.75 = (f32[16,2048]{1,0:T(8,128)S(1)}, bf16[16,16,128]{2,1,0:T(8,128)(2,1)S(1)}) custom-call(bf16[16,16,128]{2,1,0:T(8,128)(2,1)S(1)} %get-tuple-element.59.ins__counts__, bf16[16,16,128]{2,1,0:T(8,128)(2,1)S(1)} %collective-permute-done.28.ins__got___0_, f32[16,2048]{1,0:T(8,128)S(1)} %get-tuple-element.62.ins__held___1_, ...), custom_call_target="tpu_custom_call" | custom-call | flops 536870912 | tf_op jit(solution)/shard_map/pallas_call | solution.py:182
  85.4 0.9 %shard_map.76 = f32[16,2048]{1,0:T(8,128)S(1)} custom-call(f32[16,2048]{1,0:T(8,128)S(1)} %get-tuple-element.58.ins__held___0_, s32[8,128]{1,0:T(8,128)S(1)} %get-tuple-element.74.ins__index__.ins__next_index__, f32[32,8,128]{2,1,0:T(8,128)S(1)} %shard_map.66.ins__inverse__, bf16[16,16,128]{2,1,0:T(8,128)(2,1)S(1)} %get-tuple-element.63.ins__ratios__, ...), custom_call_target="tpu_custom_call" | custom-call | flops 536870912 | tf_op jit(solution)/shard_map/pallas_call | solution.py:182
  86.7 0.7 maximum_select_fusion
  (69 shorter events, 7.7 us)
Async XLA Ops:
  0.0 0.7 copy-start.2
  0.0 7.1 %collective-permute-start.5 = (bf16[32,128,128]{2,1,0:T(8,128)(2,1)}, bf16[32,128,128]{2,1,0:T(8,128)(2,1)S(1)}, u32[]{:S(2)}, u32[]{:S(2)}) collective-permute-start(bf16[32,128,128]{2,1,0:T(8,128)(2,1)} %bitcast.46), channel_id=1, source_target_pairs={{0,1},{1,0},{2,3},{3,2},{4,5},{5,4},{6,7},{7,6},{8,9},{9,8},{10,11... | collective-permute-start | bytes 3145736 | tf_op jit(solution)/shard_map/ppermute | solution.py:222
  0.7 5.6 %collective-permute-start.2 = (s32[1,32]{1,0:T(1,128)S(1)}, s32[1,32]{1,0:T(1,128)S(1)}, u32[]{:S(2)}, u32[]{:S(2)}) collective-permute-start(s32[1,32]{1,0:T(1,128)S(1)} %copy-done.2), channel_id=1, source_target_pairs={{0,1},{1,0},{2,3},{3,2},{4,5},{5,4},{6,7},{7,6},{8,9},{9,8},{10,11... | collective-permute-start | bytes 392 | tf_op jit(solution)/shard_map/ppermute | solution.py:222
  1.1 4.6 %collective-permute-start.4 = (s32[1,1]{1,0:T(1,128)}, s32[1,1]{1,0:T(1,128)}, u32[]{:S(2)}, u32[]{:S(2)}) collective-permute-start(s32[1,1]{1,0:T(1,128)} %param.10), channel_id=1, source_target_pairs={{0,1},{1,0},{2,3},{3,2},{4,5},{5,4},{6,7},{7,6},{8,9},{9,8},{10,11... | collective-permute-start | bytes 20 | tf_op jit(solution)/shard_map/ppermute | solution.py:222
  1.2 5.9 %collective-permute-start = (s32[64,128]{1,0:T(8,128)}, s32[64,128]{1,0:T(8,128)S(1)}, u32[]{:S(2)}, u32[]{:S(2)}) collective-permute-start(s32[64,128]{1,0:T(8,128)} %bitcast.54), channel_id=1, source_target_pairs={{0,1},{1,0},{2,3},{3,2},{4,5},{5,4},{6,7},{7,6},{8,9},{9,8},{10,11... | collective-permute-start | bytes 98312 | tf_op jit(solution)/shard_map/ppermute | solution.py:222
  1.6 5.5 %collective-permute-start.1 = (f32[32,2048]{1,0:T(8,128)}, f32[32,2048]{1,0:T(8,128)S(1)}, u32[]{:S(2)}, u32[]{:S(2)}) collective-permute-start(f32[32,2048]{1,0:T(8,128)} %ins__held___0_.3), channel_id=1, source_target_pairs={{0,1},{1,0},{2,3},{3,2},{4,5},{5,4},{6,7},{7,6},{8,9},{9,8},{10,11... | collective-permute-start | bytes 786440 | tf_op jit(solution)/shard_map/ppermute | solution.py:222
  2.3 1.1 %copy-start.3 = (s32[1,32]{1,0:T(1,128)S(1)}, s32[1,32]{1,0:T(1,128)}, u32[]{:S(2)}) copy-start(s32[1,32]{1,0:T(1,128)} %ins__index___0__1_.1) | copy-start | bytes 388
  2.3 1.1 %copy-start.4 = (f32[32,2048]{1,0:T(8,128)S(1)}, f32[32,2048]{1,0:T(8,128)}, u32[]{:S(2)}) copy-start(f32[32,2048]{1,0:T(8,128)} %ins__held___0_.3) | copy-start | bytes 786436
  3.5 1.2 %copy-start = (bf16[1,32,128,128]{3,2,1,0:T(8,128)(2,1)S(1)}, bf16[1,32,128,128]{3,2,1,0:T(8,128)(2,1)}, u32[]{:S(2)}) copy-start(bf16[1,32,128,128]{3,2,1,0:T(8,128)(2,1)} %param.7) | copy-start | bytes 3145732
  4.7 2.4 %copy-start.5 = (s32[1,64,128]{2,1,0:T(8,128)S(1)}, s32[1,64,128]{2,1,0:T(8,128)}, u32[]{:S(2)}) copy-start(s32[1,64,128]{2,1,0:T(8,128)} %param.11) | copy-start | bytes 98308
  5.7 1.3 %collective-permute-start.3 = (s32[1,32]{1,0:T(1,128)S(1)}, s32[1,32]{1,0:T(1,128)S(1)}, u32[]{:S(2)}, u32[]{:S(2)}) collective-permute-start(s32[1,32]{1,0:T(1,128)S(1)} %copy-done.3), channel_id=1, source_target_pairs={{0,1},{1,0},{2,3},{3,2},{4,5},{5,4},{6,7},{7,6},{8,9},{9,8},{10,11... | collective-permute-start | bytes 392 | tf_op jit(solution)/shard_map/ppermute | solution.py:222
  8.8 14.1 %copy-start.1 = (bf16[1,32,128,128]{3,2,1,0:T(8,128)(2,1)S(1)}, bf16[1,32,128,128]{3,2,1,0:T(8,128)(2,1)}, u32[]{:S(2)}) copy-start(bf16[1,32,128,128]{3,2,1,0:T(8,128)(2,1)} %param.7) | copy-start | bytes 3145732
  9.4 9.9 %collective-permute-start.8 = (bf16[18,16,128]{2,1,0:T(8,128)(2,1)S(1)}, bf16[18,16,128]{2,1,0:T(8,128)(2,1)S(1)}, u32[]{:S(2)}, u32[]{:S(2)}) collective-permute-start(bf16[18,16,128]{2,1,0:T(8,128)(2,1)S(1)} %get-tuple-element.36), channel_id=1, source_target_pairs={{0,6},{1,7},{2,4},{3,5},{4,2},{5,3},{6,0},{7,1},{8,14},{9,15},{10,... | collective-permute-start | bytes 221192 | tf_op jit(solution)/shard_map/ppermute | solution.py:226
  13.2 6.1 %collective-permute-start.7 = (bf16[18,16,128]{2,1,0:T(8,128)(2,1)S(1)}, bf16[18,16,128]{2,1,0:T(8,128)(2,1)S(1)}, u32[]{:S(2)}, u32[]{:S(2)}) collective-permute-start(bf16[18,16,128]{2,1,0:T(8,128)(2,1)S(1)} %get-tuple-element.36), channel_id=1, source_target_pairs={{0,4},{1,5},{2,6},{3,7},{4,0},{5,1},{6,2},{7,3},{8,12},{9,13},{10,... | collective-permute-start | bytes 221192 | tf_op jit(solution)/shard_map/ppermute | solution.py:226
  13.6 5.7 %collective-permute-start.6 = (bf16[18,16,128]{2,1,0:T(8,128)(2,1)S(1)}, bf16[18,16,128]{2,1,0:T(8,128)(2,1)S(1)}, u32[]{:S(2)}, u32[]{:S(2)}) collective-permute-start(bf16[18,16,128]{2,1,0:T(8,128)(2,1)S(1)} %get-tuple-element.36), channel_id=1, source_target_pairs={{0,2},{1,3},{2,0},{3,1},{4,6},{5,7},{6,4},{7,5},{8,10},{9,11},{10,... | collective-permute-start | bytes 221192 | tf_op jit(solution)/shard_map/ppermute | solution.py:226
  17.4 20.0 %collective-permute-start.13 = (bf16[14,128,128]{2,1,0:T(8,128)(2,1)S(1)}, bf16[14,128,128]{2,1,0:T(8,128)(2,1)S(1)}, u32[]{:S(2)}, u32[]{:S(2)}) collective-permute-start(bf16[14,128,128]{2,1,0:T(8,128)(2,1)S(1)} %pad_maximum_fusion), channel_id=1, source_target_pairs={{0,16},{16,0},{1,17},{17,1},{2,18},{18,2},{3,19},{19,3},{4,20},{20... | collective-permute-start | bytes 1376264 | tf_op jit(solution)/shard_map/ppermute | solution.py:232
  20.2 6.9 %collective-permute-start.9 = (bf16[24,16,128]{2,1,0:T(8,128)(2,1)S(1)}, bf16[24,16,128]{2,1,0:T(8,128)(2,1)S(1)}, u32[]{:S(2)}, u32[]{:S(2)}) collective-permute-start(bf16[24,16,128]{2,1,0:T(8,128)(2,1)S(1)} %constant_dynamic-update-slice_fusion.ins__sent__), channel_id=1, source_target_pairs={{0,8},{1,9},{2,10},{3,11},{4,12},{5,13},{6,14},{7,15},{8,0},{9,1},... | collective-permute-start | bytes 294920 | tf_op jit(solution)/shard_map/ppermute | solution.py:226
  28.0 6.5 %collective-permute-start.11 = (f32[16,2048]{1,0:T(8,128)S(1)}, f32[16,2048]{1,0:T(8,128)S(1)}, u32[]{:S(2)}, u32[]{:S(2)}) collective-permute-start(f32[16,2048]{1,0:T(8,128)S(1)} %get-tuple-element.44), channel_id=1, source_target_pairs={{0,16},{16,0},{1,17},{17,1},{2,18},{18,2},{3,19},{19,3},{4,20},{20... | collective-permute-start | bytes 393224 | tf_op jit(solution)/shard_map/ppermute | solution.py:232
  29.5 7.8 %collective-permute-start.12 = (f32[16,2048]{1,0:T(8,128)S(1)}, f32[16,2048]{1,0:T(8,128)S(1)}, u32[]{:S(2)}, u32[]{:S(2)}) collective-permute-start(f32[16,2048]{1,0:T(8,128)S(1)} %shard_map.69), channel_id=1, source_target_pairs={{0,16},{16,0},{1,17},{17,1},{2,18},{18,2},{3,19},{19,3},{4,20},{20... | collective-permute-start | bytes 393224 | tf_op jit(solution)/shard_map/ppermute | solution.py:232
  31.1 21.7 %collective-permute-start.18 = (bf16[19,128,128]{2,1,0:T(8,128)(2,1)S(1)}, bf16[19,128,128]{2,1,0:T(8,128)(2,1)S(1)}, u32[]{:S(2)}, u32[]{:S(2)}) collective-permute-start(bf16[19,128,128]{2,1,0:T(8,128)(2,1)S(1)} %slice_bitcast_fusion), channel_id=1, source_target_pairs={{0,16},{16,0},{1,17},{17,1},{2,18},{18,2},{3,19},{19,3},{4,20},{20... | collective-permute-start | bytes 1867784 | tf_op jit(solution)/shard_map/ppermute | solution.py:232
  38.4 5.3 %collective-permute-start.16 = (bf16[18,16,128]{2,1,0:T(8,128)(2,1)S(1)}, bf16[18,16,128]{2,1,0:T(8,128)(2,1)S(1)}, u32[]{:S(2)}, u32[]{:S(2)}) collective-permute-start(bf16[18,16,128]{2,1,0:T(8,128)(2,1)S(1)} %get-tuple-element.49), channel_id=1, source_target_pairs={{0,6},{1,7},{2,4},{3,5},{4,2},{5,3},{6,0},{7,1},{8,14},{9,15},{10,... | collective-permute-start | bytes 221192 | tf_op jit(solution)/shard_map/ppermute | solution.py:226
  40.6 5.4 %collective-permute-start.15 = (bf16[18,16,128]{2,1,0:T(8,128)(2,1)S(1)}, bf16[18,16,128]{2,1,0:T(8,128)(2,1)S(1)}, u32[]{:S(2)}, u32[]{:S(2)}) collective-permute-start(bf16[18,16,128]{2,1,0:T(8,128)(2,1)S(1)} %get-tuple-element.49), channel_id=1, source_target_pairs={{0,4},{1,5},{2,6},{3,7},{4,0},{5,1},{6,2},{7,3},{8,12},{9,13},{10,... | collective-permute-start | bytes 221192 | tf_op jit(solution)/shard_map/ppermute | solution.py:226
  41.5 4.5 %collective-permute-start.14 = (bf16[18,16,128]{2,1,0:T(8,128)(2,1)S(1)}, bf16[18,16,128]{2,1,0:T(8,128)(2,1)S(1)}, u32[]{:S(2)}, u32[]{:S(2)}) collective-permute-start(bf16[18,16,128]{2,1,0:T(8,128)(2,1)S(1)} %get-tuple-element.49), channel_id=1, source_target_pairs={{0,2},{1,3},{2,0},{3,1},{4,6},{5,7},{6,4},{7,5},{8,10},{9,11},{10,... | collective-permute-start | bytes 221192 | tf_op jit(solution)/shard_map/ppermute | solution.py:226
  46.2 6.6 %collective-permute-start.17 = (bf16[24,16,128]{2,1,0:T(8,128)(2,1)S(1)}, bf16[24,16,128]{2,1,0:T(8,128)(2,1)S(1)}, u32[]{:S(2)}, u32[]{:S(2)}) collective-permute-start(bf16[24,16,128]{2,1,0:T(8,128)(2,1)S(1)} %constant_dynamic-update-slice_fusion.4.ins__sent__), channel_id=1, source_target_pairs={{0,8},{1,9},{2,10},{3,11},{4,12},{5,13},{6,14},{7,15},{8,0},{9,1},... | collective-permute-start | bytes 294920 | tf_op jit(solution)/shard_map/ppermute | solution.py:226
  52.8 2.7 %collective-permute-start.19 = (bf16[19,128,128]{2,1,0:T(8,128)(2,1)S(1)}, bf16[19,128,128]{2,1,0:T(8,128)(2,1)S(1)}, u32[]{:S(2)}, u32[]{:S(2)}) collective-permute-start(bf16[19,128,128]{2,1,0:T(8,128)(2,1)S(1)} %collective-permute-done.18.ins__tiles___0__0_), channel_id=1, source_target_pairs={{0,1},{1,0},{2,3},{3,2},{4,5},{5,4},{6,7},{7,6},{8,9},{9,8},{10,11... | collective-permute-start | bytes 1867784 | tf_op jit(solution)/shard_map/ppermute | solution.py:222
  52.8 2.7 %collective-permute-start.20 = (bf16[14,128,128]{2,1,0:T(8,128)(2,1)S(1)}, bf16[14,128,128]{2,1,0:T(8,128)(2,1)S(1)}, u32[]{:S(2)}, u32[]{:S(2)}) collective-permute-start(bf16[14,128,128]{2,1,0:T(8,128)(2,1)S(1)} %collective-permute-done.13.ins__tiles___0__1_), channel_id=1, source_target_pairs={{0,1},{1,0},{2,3},{3,2},{4,5},{5,4},{6,7},{7,6},{8,9},{9,8},{10,11... | collective-permute-start | bytes 1376264 | tf_op jit(solution)/shard_map/ppermute | solution.py:222
  57.1 5.8 %collective-permute-start.23 = (bf16[16,16,128]{2,1,0:T(8,128)(2,1)S(1)}, bf16[16,16,128]{2,1,0:T(8,128)(2,1)S(1)}, u32[]{:S(2)}, u32[]{:S(2)}) collective-permute-start(bf16[16,16,128]{2,1,0:T(8,128)(2,1)S(1)} %get-tuple-element.57), channel_id=1, source_target_pairs={{0,6},{1,7},{2,4},{3,5},{4,2},{5,3},{6,0},{7,1},{8,14},{9,15},{10,... | collective-permute-start | bytes 196616 | tf_op jit(solution)/shard_map/ppermute | solution.py:226
  57.3 5.6 %collective-permute-start.22 = (bf16[16,16,128]{2,1,0:T(8,128)(2,1)S(1)}, bf16[16,16,128]{2,1,0:T(8,128)(2,1)S(1)}, u32[]{:S(2)}, u32[]{:S(2)}) collective-permute-start(bf16[16,16,128]{2,1,0:T(8,128)(2,1)S(1)} %get-tuple-element.57), channel_id=1, source_target_pairs={{0,4},{1,5},{2,6},{3,7},{4,0},{5,1},{6,2},{7,3},{8,12},{9,13},{10,... | collective-permute-start | bytes 196616 | tf_op jit(solution)/shard_map/ppermute | solution.py:226
  59.1 4.5 %collective-permute-start.21 = (bf16[16,16,128]{2,1,0:T(8,128)(2,1)S(1)}, bf16[16,16,128]{2,1,0:T(8,128)(2,1)S(1)}, u32[]{:S(2)}, u32[]{:S(2)}) collective-permute-start(bf16[16,16,128]{2,1,0:T(8,128)(2,1)S(1)} %get-tuple-element.57), channel_id=1, source_target_pairs={{0,2},{1,3},{2,0},{3,1},{4,6},{5,7},{6,4},{7,5},{8,10},{9,11},{10,... | collective-permute-start | bytes 196616 | tf_op jit(solution)/shard_map/ppermute | solution.py:226
  60.6 5.6 %collective-permute-start.10 = (bf16[16,16,128]{2,1,0:T(8,128)(2,1)S(1)}, bf16[16,16,128]{2,1,0:T(8,128)(2,1)S(1)}, u32[]{:S(2)}, u32[]{:S(2)}) collective-permute-start(bf16[16,16,128]{2,1,0:T(8,128)(2,1)S(1)} %get-tuple-element.43), channel_id=1, source_target_pairs={{0,16},{16,0},{1,17},{17,1},{2,18},{18,2},{3,19},{19,3},{4,20},{20... | collective-permute-start | bytes 196616 | tf_op jit(solution)/shard_map/ppermute | solution.py:232
  63.6 5.9 %collective-permute-start.24 = (bf16[16,16,128]{2,1,0:T(8,128)(2,1)S(1)}, bf16[16,16,128]{2,1,0:T(8,128)(2,1)S(1)}, u32[]{:S(2)}, u32[]{:S(2)}) collective-permute-start(bf16[16,16,128]{2,1,0:T(8,128)(2,1)S(1)} %get-tuple-element.67), channel_id=1, source_target_pairs={{0,8},{1,9},{2,10},{3,11},{4,12},{5,13},{6,14},{7,15},{8,0},{9,1},... | collective-permute-start | bytes 196616 | tf_op jit(solution)/shard_map/ppermute | solution.py:226
  71.8 5.2 %collective-permute-start.27 = (bf16[16,16,128]{2,1,0:T(8,128)(2,1)S(1)}, bf16[16,16,128]{2,1,0:T(8,128)(2,1)S(1)}, u32[]{:S(2)}, u32[]{:S(2)}) collective-permute-start(bf16[16,16,128]{2,1,0:T(8,128)(2,1)S(1)} %get-tuple-element.61), channel_id=1, source_target_pairs={{0,6},{1,7},{2,4},{3,5},{4,2},{5,3},{6,0},{7,1},{8,14},{9,15},{10,... | collective-permute-start | bytes 196616 | tf_op jit(solution)/shard_map/ppermute | solution.py:226
  72.6 5.0 %collective-permute-start.26 = (bf16[16,16,128]{2,1,0:T(8,128)(2,1)S(1)}, bf16[16,16,128]{2,1,0:T(8,128)(2,1)S(1)}, u32[]{:S(2)}, u32[]{:S(2)}) collective-permute-start(bf16[16,16,128]{2,1,0:T(8,128)(2,1)S(1)} %get-tuple-element.61), channel_id=1, source_target_pairs={{0,4},{1,5},{2,6},{3,7},{4,0},{5,1},{6,2},{7,3},{8,12},{9,13},{10,... | collective-permute-start | bytes 196616 | tf_op jit(solution)/shard_map/ppermute | solution.py:226
  74.6 4.3 %collective-permute-start.25 = (bf16[16,16,128]{2,1,0:T(8,128)(2,1)S(1)}, bf16[16,16,128]{2,1,0:T(8,128)(2,1)S(1)}, u32[]{:S(2)}, u32[]{:S(2)}) collective-permute-start(bf16[16,16,128]{2,1,0:T(8,128)(2,1)S(1)} %get-tuple-element.61), channel_id=1, source_target_pairs={{0,2},{1,3},{2,0},{3,1},{4,6},{5,7},{6,4},{7,5},{8,10},{9,11},{10,... | collective-permute-start | bytes 196616 | tf_op jit(solution)/shard_map/ppermute | solution.py:226
  79.0 5.4 %collective-permute-start.28 = (bf16[16,16,128]{2,1,0:T(8,128)(2,1)S(1)}, bf16[16,16,128]{2,1,0:T(8,128)(2,1)S(1)}, u32[]{:S(2)}, u32[]{:S(2)}) collective-permute-start(bf16[16,16,128]{2,1,0:T(8,128)(2,1)S(1)} %get-tuple-element.65), channel_id=1, source_target_pairs={{0,8},{1,9},{2,10},{3,11},{4,12},{5,13},{6,14},{7,15},{8,0},{9,1},... | collective-permute-start | bytes 196616 | tf_op jit(solution)/shard_map/ppermute | solution.py:226
  85.3 1.4 %collective-permute-start.29 = (f32[16,2048]{1,0:T(8,128)S(1)}, f32[16,2048]{1,0:T(8,128)S(1)}, u32[]{:S(2)}, u32[]{:S(2)}) collective-permute-start(f32[16,2048]{1,0:T(8,128)S(1)} %get-tuple-element.64), channel_id=1, source_target_pairs={{0,1},{1,0},{2,3},{3,2},{4,5},{5,4},{6,7},{7,6},{8,9},{9,8},{10,11... | collective-permute-start | bytes 393224 | tf_op jit(solution)/shard_map/ppermute | solution.py:222

commit v11 on v9

--- a/solution.py
+++ b/solution.py
@@ -267,7 +267,7 @@
     moves = [True] * (ROUNDS - 1)
     known = [None] * ROUNDS
     two = subset_count == 2 and ray_blocks <= 256 and slots <= size and size == LANES
-    late = slots // 2
+    late = slots * 19 // 32
     if two:
         moves = [r == 0 for r in range(ROUNDS - 1)]
 

time: 83 us -> 82.5 us (level)
  starting transfers between devices: 32.4 us -> 29.8 us
  waiting for transfers between devices: 29.4 us -> 31.6 us
    ppermute x16, starting transfers between devices: 24.5 us -> 21.9 us  [swap_chips(): return lax.ppermute(array, 'tile', pairs)]
    slice x1, local copies, waits for them, and re-layouts: 2.14 us -> 0.04 us  [shards(): far_first = shift(after(own_tiles[:late], moved[k]))]
    ppermute x16, waiting for transfers between devices: 24.8 us -> 26.7 us  [swap_chips(): return lax.ppermute(array, 'tile', pairs)]
    slice x0 -> x1, local copies, waits for them, and re-layouts: none -> 1.08 us  [shards(): tiles_then, rows_then = after((own_tiles[late:], own_index), sent)]
    unnamed x18, local copies, waits for them, and re-layouts: 1.25 us -> 2.11 us
  transfers between devices with their start and end apart: 28 -> 28, of which waited for: 19 -> 20; matrix products, arithmetic and copies ran while one was open for 3% -> 2% of each run, Pallas kernels for 10% -> 11%
where the time goes in v11:
time: 82.5 us; the launch traced here: 82.2 us
  waiting for transfers between devices  31.6 us (38%)
  starting transfers between devices  29.8 us (36%)
  Pallas kernels  15.2 us (18%)
  local copies, waits for them, and re-layouts  3.45 us (4%)
  other arithmetic  1.17 us (1%)
  between operations  0.99 us (1%)
    ppermute x16, waiting for transfers between devices, swap_chips(): return lax.ppermute(array, 'tile', pairs)  26.7 us
    ppermute x16, starting transfers between devices, swap_chips(): return lax.ppermute(array, 'tile', pairs)  21.9 us
    pallas_call x12, Pallas kernels, call(): pl.pallas_call(kernel, out_shape=outs, in_specs=[jax.tree_util.tree_map_w...  15.2 us
    ppermute x5, starting transfers between devices, shift(): lax.ppermute(array, 'subset', [(i, (i + 1) % subset_count) for i in range...  6.82 us
    ppermute x5, waiting for transfers between devices, shift(): lax.ppermute(array, 'subset', [(i, (i + 1) % subset_count) for i in range...  3.54 us
    unnamed x18, local copies, waits for them, and re-layouts  2.11 us
  transfers between devices with their start and end apart: 28, of which 20 were waited for; matrix products, arithmetic and copies ran while one was open for 2% of the time, Pallas kernels for 11%

profile of v11, /device:TPU:0, one launch (start us, length us, event | category | flops | bytes accessed | tf_op | source)
XLA Modules:
  0.0 82.2 jit_solution(4341689997371692916)
XLA Ops:
  1.2 0.6 copy-done.4
  2.5 1.1 %slice_bitcast_fusion.1 = bf16[13,128,128]{2,1,0:T(8,128)(2,1)S(1)} fusion(bf16[1,32,128,128]{3,2,1,0:T(8,128)(2,1)} %param.7), kind=kLoop, calls=%fused_computation.2 | loop fusion | bytes 851968 | tf_op jit(solution)/shard_map/slice | solution.py:294
  4.3 1.2 %copy-done = bf16[1,32,128,128]{3,2,1,0:T(8,128)(2,1)S(1)} copy-done((bf16[1,32,128,128]{3,2,1,0:T(8,128)(2,1)S(1)}, bf16[1,32,128,128]{3,2,1,0:T(8,128)(2,1)}, u32[]{:S(2)}) %copy-start) | copy-done | bytes 1048600
  5.6 1.7 %shard_map.64 = (bf16[18,16,128]{2,1,0:T(8,128)(2,1)S(1)}, f32[16,16,128]{2,1,0:T(8,128)S(1)}) custom-call(s32[64,128]{1,0:T(8,128)S(1)} %bitcast.61, s32[64,128]{1,0:T(8,128)S(1)} %collective-permute-done.ins__dealt___1_, f32[32,2048]{1,0:T(8,128)S(1)} %copy-done.2, f32[32,2048]{1,0:T(8,128)S(1)} %collective-permute-done.1.ins__held___1_, ...), custom_call_target="tpu_custom_call" | custom-call | flops 536870912 | tf_op jit(solution)/shard_map/pallas_call | solution.py:194
  7.3 4.0 %collective-permute-start.6 = (bf16[18,16,128]{2,1,0:T(8,128)(2,1)S(1)}, bf16[18,16,128]{2,1,0:T(8,128)(2,1)S(1)}, u32[]{:S(2)}, u32[]{:S(2)}) collective-permute-start(bf16[18,16,128]{2,1,0:T(8,128)(2,1)S(1)} %get-tuple-element.31), channel_id=1, source_target_pairs={{0,6},{1,7},{2,4},{3,5},{4,2},{5,3},{6,0},{7,1},{8,14},{9,15},{10,... | collective-permute-start | bytes 221192 | tf_op jit(solution)/shard_map/ppermute | solution.py:238
  12.0 1.9 %collective-permute-start.11 = (bf16[14,128,128]{2,1,0:T(8,128)(2,1)S(1)}, bf16[14,128,128]{2,1,0:T(8,128)(2,1)S(1)}, u32[]{:S(2)}, u32[]{:S(2)}) collective-permute-start(bf16[14,128,128]{2,1,0:T(8,128)(2,1)S(1)} %pad_maximum_fusion), channel_id=1, source_target_pairs={{0,16},{16,0},{1,17},{17,1},{2,18},{18,2},{3,19},{19,3},{4,20},{20... | collective-permute-start | bytes 1376264 | tf_op jit(solution)/shard_map/ppermute | solution.py:244
  14.0 1.6 %collective-permute-done.5 = bf16[18,16,128]{2,1,0:T(8,128)(2,1)S(1)} collective-permute-done((bf16[18,16,128]{2,1,0:T(8,128)(2,1)S(1)}, bf16[18,16,128]{2,1,0:T(8,128)(2,1)S(1)}, u32[]{:S(2)}, u32[]{:S(2)}) %collective-permute-start.5) | collective-permute-done | bytes 73760 | tf_op jit(solution)/shard_map/ppermute | solution.py:238
  16.3 2.6 %collective-permute-start.7 = (bf16[24,16,128]{2,1,0:T(8,128)(2,1)S(1)}, bf16[24,16,128]{2,1,0:T(8,128)(2,1)S(1)}, u32[]{:S(2)}, u32[]{:S(2)}) collective-permute-start(bf16[24,16,128]{2,1,0:T(8,128)(2,1)S(1)} %constant_dynamic-update-slice_fusion.ins__sent__), channel_id=1, source_target_pairs={{0,8},{1,9},{2,10},{3,11},{4,12},{5,13},{6,14},{7,15},{8,0},{9,1},... | collective-permute-start | bytes 294920 | tf_op jit(solution)/shard_map/ppermute | solution.py:238
  18.9 1.2 %shard_map.65.ins__inverse__ = f32[32,8,128]{2,1,0:T(8,128)S(1)} custom-call(s32[8,128]{1,0:T(8,128)S(1)} %add_add_fusion.4.ins__index__.ins__next_index__, bf16[32,128,128]{2,1,0:T(8,128)(2,1)S(1)} %bitcast.54, bf16[32,128,128]{2,1,0:T(8,128)(2,1)S(1)} %collective-permute-done.3.ins__tiles___0_.ins__tiles___1__0_.ins__next_tiles___1__0_), custom_call_target="tpu_custom_call" | custom-call | flops 1073741824 | tf_op jit(solution)/shard_map/pallas_call | solution.py:194
  20.1 3.0 %collective-permute-done.7.ins__got___0_ = bf16[24,16,128]{2,1,0:T(8,128)(2,1)S(1)} collective-permute-done((bf16[24,16,128]{2,1,0:T(8,128)(2,1)S(1)}, bf16[24,16,128]{2,1,0:T(8,128)(2,1)S(1)}, u32[]{:S(2)}, u32[]{:S(2)}) %collective-permute-start.7) | collective-permute-done | bytes 98336 | tf_op jit(solution)/shard_map/ppermute | solution.py:238
  23.1 1.0 %shard_map.66 = (bf16[16,16,128]{2,1,0:T(8,128)(2,1)S(1)}, f32[16,2048]{1,0:T(8,128)S(1)}, bf16[16,16,128]{2,1,0:T(8,128)(2,1)S(1)}) custom-call(bf16[24,16,128]{2,1,0:T(8,128)(2,1)S(1)} %collective-permute-done.7.ins__got___0_, f32[32,2048]{1,0:T(8,128)S(1)} %copy-done.2, s32[8,128]{1,0:T(8,128)S(1)} %add_add_fusion.4.ins__index__.ins__next_index__, ...), custom_call_target="tpu_custom_call" | custom-call | flops 536870912 | tf_op jit(solution)/shard_map/pallas_call | solution.py:194
  24.1 1.6 %collective-permute-start.9 = (f32[16,2048]{1,0:T(8,128)S(1)}, f32[16,2048]{1,0:T(8,128)S(1)}, u32[]{:S(2)}, u32[]{:S(2)}) collective-permute-start(f32[16,2048]{1,0:T(8,128)S(1)} %get-tuple-element.33), channel_id=1, source_target_pairs={{0,16},{16,0},{1,17},{17,1},{2,18},{18,2},{3,19},{19,3},{4,20},{20... | collective-permute-start | bytes 393224 | tf_op jit(solution)/shard_map/ppermute | solution.py:244
  25.7 0.9 %shard_map.68 = f32[16,2048]{1,0:T(8,128)S(1)} custom-call(f32[32,2048]{1,0:T(8,128)S(1)} %collective-permute-done.1.ins__held___1_, s32[8,128]{1,0:T(8,128)S(1)} %add_add_fusion.4.ins__index__.ins__next_index__, f32[32,8,128]{2,1,0:T(8,128)S(1)} %shard_map.65.ins__inverse__, bf16[16,16,128]{2,1,0:T(8,128)(2,1)S(1)} %get-tuple-element.34.ins__ratios__, ...), custom_call_target="tpu_custom_call" | custom-call | flops 536870912 | tf_op jit(solution)/shard_map/pallas_call | solution.py:194
  26.6 0.6 collective-permute-start.10
  27.2 1.6 %collective-permute-start.17 = (bf16[19,128,128]{2,1,0:T(8,128)(2,1)S(1)}, bf16[19,128,128]{2,1,0:T(8,128)(2,1)S(1)}, u32[]{:S(2)}, u32[]{:S(2)}) collective-permute-start(bf16[19,128,128]{2,1,0:T(8,128)(2,1)S(1)} %slice_bitcast_fusion), channel_id=1, source_target_pairs={{0,16},{16,0},{1,17},{17,1},{2,18},{18,2},{3,19},{19,3},{4,20},{20... | collective-permute-start | bytes 1867784 | tf_op jit(solution)/shard_map/ppermute | solution.py:244
  28.8 1.8 %collective-permute-done.9.ins__held___0_ = f32[16,2048]{1,0:T(8,128)S(1)} collective-permute-done((f32[16,2048]{1,0:T(8,128)S(1)}, f32[16,2048]{1,0:T(8,128)S(1)}, u32[]{:S(2)}, u32[]{:S(2)}) %collective-permute-start.9) | collective-permute-done | bytes 131104 | tf_op jit(solution)/shard_map/ppermute | solution.py:244
  30.6 1.1 %shard_map.67.ins__begun__ = f32[16,16,128]{2,1,0:T(8,128)S(1)} custom-call(f32[16,2048]{1,0:T(8,128)S(1)} %collective-permute-done.9.ins__held___0_, s32[8,128]{1,0:T(8,128)S(1)} %add_add_fusion.4.ins__index__.ins__next_index__, bf16[32,128,128]{2,1,0:T(8,128)(2,1)S(1)} %bitcast.56), custom_call_target="tpu_custom_call" | custom-call | flops 536870912 | tf_op jit(solution)/shard_map/pallas_call | solution.py:194
  31.7 1.7 %collective-permute-done.10.ins__held___1_ = f32[16,2048]{1,0:T(8,128)S(1)} collective-permute-done((f32[16,2048]{1,0:T(8,128)S(1)}, f32[16,2048]{1,0:T(8,128)S(1)}, u32[]{:S(2)}, u32[]{:S(2)}) %collective-permute-start.10) | collective-permute-done | bytes 131104 | tf_op jit(solution)/shard_map/ppermute | solution.py:244
  33.4 1.1 %shard_map.69 = (bf16[18,16,128]{2,1,0:T(8,128)(2,1)S(1)}, f32[16,16,128]{2,1,0:T(8,128)S(1)}) custom-call(f32[16,16,128]{2,1,0:T(8,128)S(1)} %shard_map.67.ins__begun__, s32[64,128]{1,0:T(8,128)S(1)} %bitcast.62, s32[64,128]{1,0:T(8,128)S(1)} %collective-permute-done.ins__dealt___1_, f32[16,2048]{1,0:T(8,128)S(1)} %collective-permute-done.10.ins__held___1_, ...), custom_call_target="tpu_custom_call" | custom-call | flops 536870912 | tf_op jit(solution)/shard_map/pallas_call | solution.py:194
  34.5 1.2 %collective-permute-start.14 = (bf16[18,16,128]{2,1,0:T(8,128)(2,1)S(1)}, bf16[18,16,128]{2,1,0:T(8,128)(2,1)S(1)}, u32[]{:S(2)}, u32[]{:S(2)}) collective-permute-start(bf16[18,16,128]{2,1,0:T(8,128)(2,1)S(1)} %get-tuple-element.39), channel_id=1, source_target_pairs={{0,6},{1,7},{2,4},{3,5},{4,2},{5,3},{6,0},{7,1},{8,14},{9,15},{10,... | collective-permute-start | bytes 221192 | tf_op jit(solution)/shard_map/ppermute | solution.py:238
  35.7 1.9 %collective-permute-start.13 = (bf16[18,16,128]{2,1,0:T(8,128)(2,1)S(1)}, bf16[18,16,128]{2,1,0:T(8,128)(2,1)S(1)}, u32[]{:S(2)}, u32[]{:S(2)}) collective-permute-start(bf16[18,16,128]{2,1,0:T(8,128)(2,1)S(1)} %get-tuple-element.39), channel_id=1, source_target_pairs={{0,4},{1,5},{2,6},{3,7},{4,0},{5,1},{6,2},{7,3},{8,12},{9,13},{10,... | collective-permute-start | bytes 221192 | tf_op jit(solution)/shard_map/ppermute | solution.py:238
  38.1 1.8 %collective-permute-done.14 = bf16[18,16,128]{2,1,0:T(8,128)(2,1)S(1)} collective-permute-done((bf16[18,16,128]{2,1,0:T(8,128)(2,1)S(1)}, bf16[18,16,128]{2,1,0:T(8,128)(2,1)S(1)}, u32[]{:S(2)}, u32[]{:S(2)}) %collective-permute-start.14) | collective-permute-done | bytes 73760 | tf_op jit(solution)/shard_map/ppermute | solution.py:238
  39.8 1.0 %collective-permute-done.13 = bf16[18,16,128]{2,1,0:T(8,128)(2,1)S(1)} collective-permute-done((bf16[18,16,128]{2,1,0:T(8,128)(2,1)S(1)}, bf16[18,16,128]{2,1,0:T(8,128)(2,1)S(1)}, u32[]{:S(2)}, u32[]{:S(2)}) %collective-permute-start.13) | collective-permute-done | bytes 73760 | tf_op jit(solution)/shard_map/ppermute | solution.py:238
  40.8 1.2 %collective-permute-done.12 = bf16[18,16,128]{2,1,0:T(8,128)(2,1)S(1)} collective-permute-done((bf16[18,16,128]{2,1,0:T(8,128)(2,1)S(1)}, bf16[18,16,128]{2,1,0:T(8,128)(2,1)S(1)}, u32[]{:S(2)}, u32[]{:S(2)}) %collective-permute-start.12) | collective-permute-done | bytes 73760 | tf_op jit(solution)/shard_map/ppermute | solution.py:238
  42.2 1.5 %collective-permute-start.15 = (bf16[24,16,128]{2,1,0:T(8,128)(2,1)S(1)}, bf16[24,16,128]{2,1,0:T(8,128)(2,1)S(1)}, u32[]{:S(2)}, u32[]{:S(2)}) collective-permute-start(bf16[24,16,128]{2,1,0:T(8,128)(2,1)S(1)} %constant_dynamic-update-slice_fusion.4.ins__sent__), channel_id=1, source_target_pairs={{0,8},{1,9},{2,10},{3,11},{4,12},{5,13},{6,14},{7,15},{8,0},{9,1},... | collective-permute-start | bytes 294920 | tf_op jit(solution)/shard_map/ppermute | solution.py:238
  43.7 5.1 %collective-permute-done.15.ins__got___0_ = bf16[24,16,128]{2,1,0:T(8,128)(2,1)S(1)} collective-permute-done((bf16[24,16,128]{2,1,0:T(8,128)(2,1)S(1)}, bf16[24,16,128]{2,1,0:T(8,128)(2,1)S(1)}, u32[]{:S(2)}, u32[]{:S(2)}) %collective-permute-start.15) | collective-permute-done | bytes 98336 | tf_op jit(solution)/shard_map/ppermute | solution.py:238
  48.8 1.3 %shard_map.70 = (bf16[16,16,128]{2,1,0:T(8,128)(2,1)S(1)}, f32[16,2048]{1,0:T(8,128)S(1)}, f32[16,2048]{1,0:T(8,128)S(1)}) custom-call(bf16[24,16,128]{2,1,0:T(8,128)(2,1)S(1)} %collective-permute-done.15.ins__got___0_, f32[16,2048]{1,0:T(8,128)S(1)} %collective-permute-done.9.ins__held___0_, f32[16,2048]{1,0:T(8,128)S(1)} %collective-permute-done.10.ins__held___1_, ...), custom_call_target="tpu_custom_call" | custom-call | flops 1073741824 | tf_op jit(solution)/shard_map/pallas_call | solution.py:194
  50.2 0.7 collective-permute-done.18.ins__tiles___1__0_
  50.8 1.6 %shard_map.71 = (bf16[16,16,128]{2,1,0:T(8,128)(2,1)S(1)}, f32[16,16,128]{2,1,0:T(8,128)S(1)}) custom-call(f32[16,2048]{1,0:T(8,128)S(1)} %get-tuple-element.40.ins__held___0_, f32[16,2048]{1,0:T(8,128)S(1)} %get-tuple-element.41.ins__held___1_, s32[8,128]{1,0:T(8,128)S(1)} %add_add_fusion.5.ins__index__, ...), custom_call_target="tpu_custom_call" | custom-call | flops 2147483648 | tf_op jit(solution)/shard_map/pallas_call | solution.py:194
  52.5 1.9 %collective-permute-start.20 = (bf16[16,16,128]{2,1,0:T(8,128)(2,1)S(1)}, bf16[16,16,128]{2,1,0:T(8,128)(2,1)S(1)}, u32[]{:S(2)}, u32[]{:S(2)}) collective-permute-start(bf16[16,16,128]{2,1,0:T(8,128)(2,1)S(1)} %get-tuple-element.47), channel_id=1, source_target_pairs={{0,4},{1,5},{2,6},{3,7},{4,0},{5,1},{6,2},{7,3},{8,12},{9,13},{10,... | collective-permute-start | bytes 196616 | tf_op jit(solution)/shard_map/ppermute | solution.py:238
  54.3 1.6 %collective-permute-start.19 = (bf16[16,16,128]{2,1,0:T(8,128)(2,1)S(1)}, bf16[16,16,128]{2,1,0:T(8,128)(2,1)S(1)}, u32[]{:S(2)}, u32[]{:S(2)}) collective-permute-start(bf16[16,16,128]{2,1,0:T(8,128)(2,1)S(1)} %get-tuple-element.47), channel_id=1, source_target_pairs={{0,2},{1,3},{2,0},{3,1},{4,6},{5,7},{6,4},{7,5},{8,10},{9,11},{10,... | collective-permute-start | bytes 196616 | tf_op jit(solution)/shard_map/ppermute | solution.py:238
  55.9 1.2 %collective-permute-start.8 = (bf16[16,16,128]{2,1,0:T(8,128)(2,1)S(1)}, bf16[16,16,128]{2,1,0:T(8,128)(2,1)S(1)}, u32[]{:S(2)}, u32[]{:S(2)}) collective-permute-start(bf16[16,16,128]{2,1,0:T(8,128)(2,1)S(1)} %get-tuple-element.32), channel_id=1, source_target_pairs={{0,16},{16,0},{1,17},{17,1},{2,18},{18,2},{3,19},{19,3},{4,20},{20... | collective-permute-start | bytes 196616 | tf_op jit(solution)/shard_map/ppermute | solution.py:244
  57.2 1.0 %collective-permute-done.21 = bf16[16,16,128]{2,1,0:T(8,128)(2,1)S(1)} collective-permute-done((bf16[16,16,128]{2,1,0:T(8,128)(2,1)S(1)}, bf16[16,16,128]{2,1,0:T(8,128)(2,1)S(1)}, u32[]{:S(2)}, u32[]{:S(2)}) %collective-permute-start.21) | collective-permute-done | bytes 65568 | tf_op jit(solution)/shard_map/ppermute | solution.py:238
  58.2 0.7 collective-permute-done.19
  58.9 1.1 %collective-permute-start.22 = (bf16[16,16,128]{2,1,0:T(8,128)(2,1)S(1)}, bf16[16,16,128]{2,1,0:T(8,128)(2,1)S(1)}, u32[]{:S(2)}, u32[]{:S(2)}) collective-permute-start(bf16[16,16,128]{2,1,0:T(8,128)(2,1)S(1)} %get-tuple-element.57), channel_id=1, source_target_pairs={{0,8},{1,9},{2,10},{3,11},{4,12},{5,13},{6,14},{7,15},{8,0},{9,1},... | collective-permute-start | bytes 196616 | tf_op jit(solution)/shard_map/ppermute | solution.py:238
  60.0 1.2 %shard_map.72.ins__inverse__ = f32[32,8,128]{2,1,0:T(8,128)S(1)} custom-call(s32[8,128]{1,0:T(8,128)S(1)} %add_add_fusion.5.ins__index__, bf16[19,128,128]{2,1,0:T(8,128)(2,1)S(1)} %collective-permute-done.17.ins__tiles___0__0_, bf16[14,128,128]{2,1,0:T(8,128)(2,1)S(1)} %collective-permute-done.11.ins__tiles___0__1_, ...), custom_call_target="tpu_custom_call" | custom-call | flops 2147483648 | tf_op jit(solution)/shard_map/pallas_call | solution.py:194
  61.2 3.3 %collective-permute-done.22.ins__got___0_ = bf16[16,16,128]{2,1,0:T(8,128)(2,1)S(1)} collective-permute-done((bf16[16,16,128]{2,1,0:T(8,128)(2,1)S(1)}, bf16[16,16,128]{2,1,0:T(8,128)(2,1)S(1)}, u32[]{:S(2)}, u32[]{:S(2)}) %collective-permute-start.22) | collective-permute-done | bytes 65568 | tf_op jit(solution)/shard_map/ppermute | solution.py:238
  64.5 2.3 %shard_map.73 = (f32[16,2048]{1,0:T(8,128)S(1)}, f32[16,2048]{1,0:T(8,128)S(1)}, bf16[16,16,128]{2,1,0:T(8,128)(2,1)S(1)}, f32[16,16,128]{2,1,0:T(8,128)S(1)}) custom-call(bf16[16,16,128]{2,1,0:T(8,128)(2,1)S(1)} %collective-permute-done.8.ins__counts__, bf16[16,16,128]{2,1,0:T(8,128)(2,1)S(1)} %collective-permute-done.22.ins__got___0_, ...), custom_call_target="tpu_custom_call" | custom-call | flops 2147483648 | tf_op jit(solution)/shard_map/pallas_call | solution.py:194
  66.8 0.5 collective-permute-start.25
  67.3 2.2 %collective-permute-start.24 = (bf16[16,16,128]{2,1,0:T(8,128)(2,1)S(1)}, bf16[16,16,128]{2,1,0:T(8,128)(2,1)S(1)}, u32[]{:S(2)}, u32[]{:S(2)}) collective-permute-start(bf16[16,16,128]{2,1,0:T(8,128)(2,1)S(1)} %get-tuple-element.51), channel_id=1, source_target_pairs={{0,4},{1,5},{2,6},{3,7},{4,0},{5,1},{6,2},{7,3},{8,12},{9,13},{10,... | collective-permute-start | bytes 196616 | tf_op jit(solution)/shard_map/ppermute | solution.py:238
  69.5 0.9 %collective-permute-start.23 = (bf16[16,16,128]{2,1,0:T(8,128)(2,1)S(1)}, bf16[16,16,128]{2,1,0:T(8,128)(2,1)S(1)}, u32[]{:S(2)}, u32[]{:S(2)}) collective-permute-start(bf16[16,16,128]{2,1,0:T(8,128)(2,1)S(1)} %get-tuple-element.51), channel_id=1, source_target_pairs={{0,2},{1,3},{2,0},{3,1},{4,6},{5,7},{6,4},{7,5},{8,10},{9,11},{10,... | collective-permute-start | bytes 196616 | tf_op jit(solution)/shard_map/ppermute | solution.py:238
  70.4 1.7 %collective-permute-done.25 = bf16[16,16,128]{2,1,0:T(8,128)(2,1)S(1)} collective-permute-done((bf16[16,16,128]{2,1,0:T(8,128)(2,1)S(1)}, bf16[16,16,128]{2,1,0:T(8,128)(2,1)S(1)}, u32[]{:S(2)}, u32[]{:S(2)}) %collective-permute-start.25) | collective-permute-done | bytes 65568 | tf_op jit(solution)/shard_map/ppermute | solution.py:238
  72.4 1.3 %collective-permute-done.23 = bf16[16,16,128]{2,1,0:T(8,128)(2,1)S(1)} collective-permute-done((bf16[16,16,128]{2,1,0:T(8,128)(2,1)S(1)}, bf16[16,16,128]{2,1,0:T(8,128)(2,1)S(1)}, u32[]{:S(2)}, u32[]{:S(2)}) %collective-permute-start.23) | collective-permute-done | bytes 65568 | tf_op jit(solution)/shard_map/ppermute | solution.py:238
  73.8 1.3 %collective-permute-start.26 = (bf16[16,16,128]{2,1,0:T(8,128)(2,1)S(1)}, bf16[16,16,128]{2,1,0:T(8,128)(2,1)S(1)}, u32[]{:S(2)}, u32[]{:S(2)}) collective-permute-start(bf16[16,16,128]{2,1,0:T(8,128)(2,1)S(1)} %get-tuple-element.55), channel_id=1, source_target_pairs={{0,8},{1,9},{2,10},{3,11},{4,12},{5,13},{6,14},{7,15},{8,0},{9,1},... | collective-permute-start | bytes 196616 | tf_op jit(solution)/shard_map/ppermute | solution.py:238
  75.1 4.1 %collective-permute-done.26.ins__got___0_ = bf16[16,16,128]{2,1,0:T(8,128)(2,1)S(1)} collective-permute-done((bf16[16,16,128]{2,1,0:T(8,128)(2,1)S(1)}, bf16[16,16,128]{2,1,0:T(8,128)(2,1)S(1)}, u32[]{:S(2)}, u32[]{:S(2)}) %collective-permute-start.26) | collective-permute-done | bytes 65568 | tf_op jit(solution)/shard_map/ppermute | solution.py:238
  79.1 1.0 %shard_map.74 = (f32[16,2048]{1,0:T(8,128)S(1)}, bf16[16,16,128]{2,1,0:T(8,128)(2,1)S(1)}) custom-call(bf16[16,16,128]{2,1,0:T(8,128)(2,1)S(1)} %get-tuple-element.49.ins__counts__, bf16[16,16,128]{2,1,0:T(8,128)(2,1)S(1)} %collective-permute-done.26.ins__got___0_, f32[16,2048]{1,0:T(8,128)S(1)} %get-tuple-element.52.ins__held___1_, ...), custom_call_target="tpu_custom_call" | custom-call | flops 536870912 | tf_op jit(solution)/shard_map/pallas_call | solution.py:194
  80.2 0.9 %shard_map.75 = f32[16,2048]{1,0:T(8,128)S(1)} custom-call(f32[16,2048]{1,0:T(8,128)S(1)} %get-tuple-element.48.ins__held___0_, s32[8,128]{1,0:T(8,128)S(1)} %add_add_fusion.4.ins__index__.ins__next_index__, f32[32,8,128]{2,1,0:T(8,128)S(1)} %shard_map.65.ins__inverse__, bf16[16,16,128]{2,1,0:T(8,128)(2,1)S(1)} %get-tuple-element.53.ins__ratios__, ...), custom_call_target="tpu_custom_call" | custom-call | flops 536870912 | tf_op jit(solution)/shard_map/pallas_call | solution.py:194
  81.5 0.7 maximum_select_fusion
  (71 shorter events, 5.0 us)
Async XLA Ops:
  0.0 4.1 %collective-permute-start.3 = (bf16[32,128,128]{2,1,0:T(8,128)(2,1)}, bf16[32,128,128]{2,1,0:T(8,128)(2,1)S(1)}, u32[]{:S(2)}, u32[]{:S(2)}) collective-permute-start(bf16[32,128,128]{2,1,0:T(8,128)(2,1)} %bitcast.52), channel_id=1, source_target_pairs={{0,1},{1,0},{2,3},{3,2},{4,5},{5,4},{6,7},{7,6},{8,9},{9,8},{10,11... | collective-permute-start | bytes 3145736 | tf_op jit(solution)/shard_map/ppermute | solution.py:234
  1.1 0.7 copy-start.4
  1.1 0.7 copy-start.5
  1.9 1.8 %collective-permute-start.2 = (s32[8,128]{1,0:T(8,128)S(1)}, s32[8,128]{1,0:T(8,128)S(1)}, u32[]{:S(2)}, u32[]{:S(2)}) collective-permute-start(s32[8,128]{1,0:T(8,128)S(1)} %pad.8.ins__index___0_), channel_id=1, source_target_pairs={{0,1},{1,0},{2,3},{3,2},{4,5},{5,4},{6,7},{7,6},{8,9},{9,8},{10,11... | collective-permute-start | bytes 12296 | tf_op jit(solution)/shard_map/ppermute | solution.py:234
  1.9 1.9 %collective-permute-start = (s32[64,128]{1,0:T(8,128)}, s32[64,128]{1,0:T(8,128)S(1)}, u32[]{:S(2)}, u32[]{:S(2)}) collective-permute-start(s32[64,128]{1,0:T(8,128)} %bitcast.60), channel_id=1, source_target_pairs={{0,1},{1,0},{2,3},{3,2},{4,5},{5,4},{6,7},{7,6},{8,9},{9,8},{10,11... | collective-permute-start | bytes 98312 | tf_op jit(solution)/shard_map/ppermute | solution.py:234
  2.4 1.7 %collective-permute-start.1 = (f32[32,2048]{1,0:T(8,128)}, f32[32,2048]{1,0:T(8,128)S(1)}, u32[]{:S(2)}, u32[]{:S(2)}) collective-permute-start(f32[32,2048]{1,0:T(8,128)} %ins__held___0_.3), channel_id=1, source_target_pairs={{0,1},{1,0},{2,3},{3,2},{4,5},{5,4},{6,7},{7,6},{8,9},{9,8},{10,11... | collective-permute-start | bytes 786440 | tf_op jit(solution)/shard_map/ppermute | solution.py:234
  2.5 1.7 %copy-start.2 = (f32[32,2048]{1,0:T(8,128)S(1)}, f32[32,2048]{1,0:T(8,128)}, u32[]{:S(2)}) copy-start(f32[32,2048]{1,0:T(8,128)} %ins__held___0_.3) | copy-start | bytes 786436
  3.6 0.8 copy-start.3
  4.3 1.2 %copy-start = (bf16[1,32,128,128]{3,2,1,0:T(8,128)(2,1)S(1)}, bf16[1,32,128,128]{3,2,1,0:T(8,128)(2,1)}, u32[]{:S(2)}) copy-start(bf16[1,32,128,128]{3,2,1,0:T(8,128)(2,1)} %param.7) | copy-start | bytes 3145732
  7.3 11.6 %copy-start.1 = (bf16[1,32,128,128]{3,2,1,0:T(8,128)(2,1)S(1)}, bf16[1,32,128,128]{3,2,1,0:T(8,128)(2,1)}, u32[]{:S(2)}) copy-start(bf16[1,32,128,128]{3,2,1,0:T(8,128)(2,1)} %param.7) | copy-start | bytes 3145732
  7.3 6.7 %collective-permute-start.6 = (bf16[18,16,128]{2,1,0:T(8,128)(2,1)S(1)}, bf16[18,16,128]{2,1,0:T(8,128)(2,1)S(1)}, u32[]{:S(2)}, u32[]{:S(2)}) collective-permute-start(bf16[18,16,128]{2,1,0:T(8,128)(2,1)S(1)} %get-tuple-element.31), channel_id=1, source_target_pairs={{0,6},{1,7},{2,4},{3,5},{4,2},{5,3},{6,0},{7,1},{8,14},{9,15},{10,... | collective-permute-start | bytes 221192 | tf_op jit(solution)/shard_map/ppermute | solution.py:238
  11.3 4.4 %collective-permute-start.5 = (bf16[18,16,128]{2,1,0:T(8,128)(2,1)S(1)}, bf16[18,16,128]{2,1,0:T(8,128)(2,1)S(1)}, u32[]{:S(2)}, u32[]{:S(2)}) collective-permute-start(bf16[18,16,128]{2,1,0:T(8,128)(2,1)S(1)} %get-tuple-element.31), channel_id=1, source_target_pairs={{0,4},{1,5},{2,6},{3,7},{4,0},{5,1},{6,2},{7,3},{8,12},{9,13},{10,... | collective-permute-start | bytes 221192 | tf_op jit(solution)/shard_map/ppermute | solution.py:238
  11.8 4.4 %collective-permute-start.4 = (bf16[18,16,128]{2,1,0:T(8,128)(2,1)S(1)}, bf16[18,16,128]{2,1,0:T(8,128)(2,1)S(1)}, u32[]{:S(2)}, u32[]{:S(2)}) collective-permute-start(bf16[18,16,128]{2,1,0:T(8,128)(2,1)S(1)} %get-tuple-element.31), channel_id=1, source_target_pairs={{0,2},{1,3},{2,0},{3,1},{4,6},{5,7},{6,4},{7,5},{8,10},{9,11},{10,... | collective-permute-start | bytes 221192 | tf_op jit(solution)/shard_map/ppermute | solution.py:238
  12.0 21.4 %collective-permute-start.11 = (bf16[14,128,128]{2,1,0:T(8,128)(2,1)S(1)}, bf16[14,128,128]{2,1,0:T(8,128)(2,1)S(1)}, u32[]{:S(2)}, u32[]{:S(2)}) collective-permute-start(bf16[14,128,128]{2,1,0:T(8,128)(2,1)S(1)} %pad_maximum_fusion), channel_id=1, source_target_pairs={{0,16},{16,0},{1,17},{17,1},{2,18},{18,2},{3,19},{19,3},{4,20},{20... | collective-permute-start | bytes 1376264 | tf_op jit(solution)/shard_map/ppermute | solution.py:244
  16.3 6.9 %collective-permute-start.7 = (bf16[24,16,128]{2,1,0:T(8,128)(2,1)S(1)}, bf16[24,16,128]{2,1,0:T(8,128)(2,1)S(1)}, u32[]{:S(2)}, u32[]{:S(2)}) collective-permute-start(bf16[24,16,128]{2,1,0:T(8,128)(2,1)S(1)} %constant_dynamic-update-slice_fusion.ins__sent__), channel_id=1, source_target_pairs={{0,8},{1,9},{2,10},{3,11},{4,12},{5,13},{6,14},{7,15},{8,0},{9,1},... | collective-permute-start | bytes 294920 | tf_op jit(solution)/shard_map/ppermute | solution.py:238
  24.1 6.5 %collective-permute-start.9 = (f32[16,2048]{1,0:T(8,128)S(1)}, f32[16,2048]{1,0:T(8,128)S(1)}, u32[]{:S(2)}, u32[]{:S(2)}) collective-permute-start(f32[16,2048]{1,0:T(8,128)S(1)} %get-tuple-element.33), channel_id=1, source_target_pairs={{0,16},{16,0},{1,17},{17,1},{2,18},{18,2},{3,19},{19,3},{4,20},{20... | collective-permute-start | bytes 393224 | tf_op jit(solution)/shard_map/ppermute | solution.py:244
  26.6 6.8 %collective-permute-start.10 = (f32[16,2048]{1,0:T(8,128)S(1)}, f32[16,2048]{1,0:T(8,128)S(1)}, u32[]{:S(2)}, u32[]{:S(2)}) collective-permute-start(f32[16,2048]{1,0:T(8,128)S(1)} %shard_map.68), channel_id=1, source_target_pairs={{0,16},{16,0},{1,17},{17,1},{2,18},{18,2},{3,19},{19,3},{4,20},{20... | collective-permute-start | bytes 393224 | tf_op jit(solution)/shard_map/ppermute | solution.py:244
  27.2 21.5 %collective-permute-start.17 = (bf16[19,128,128]{2,1,0:T(8,128)(2,1)S(1)}, bf16[19,128,128]{2,1,0:T(8,128)(2,1)S(1)}, u32[]{:S(2)}, u32[]{:S(2)}) collective-permute-start(bf16[19,128,128]{2,1,0:T(8,128)(2,1)S(1)} %slice_bitcast_fusion), channel_id=1, source_target_pairs={{0,16},{16,0},{1,17},{17,1},{2,18},{18,2},{3,19},{19,3},{4,20},{20... | collective-permute-start | bytes 1867784 | tf_op jit(solution)/shard_map/ppermute | solution.py:244
  34.5 5.3 %collective-permute-start.14 = (bf16[18,16,128]{2,1,0:T(8,128)(2,1)S(1)}, bf16[18,16,128]{2,1,0:T(8,128)(2,1)S(1)}, u32[]{:S(2)}, u32[]{:S(2)}) collective-permute-start(bf16[18,16,128]{2,1,0:T(8,128)(2,1)S(1)} %get-tuple-element.39), channel_id=1, source_target_pairs={{0,6},{1,7},{2,4},{3,5},{4,2},{5,3},{6,0},{7,1},{8,14},{9,15},{10,... | collective-permute-start | bytes 221192 | tf_op jit(solution)/shard_map/ppermute | solution.py:238
  35.7 5.1 %collective-permute-start.13 = (bf16[18,16,128]{2,1,0:T(8,128)(2,1)S(1)}, bf16[18,16,128]{2,1,0:T(8,128)(2,1)S(1)}, u32[]{:S(2)}, u32[]{:S(2)}) collective-permute-start(bf16[18,16,128]{2,1,0:T(8,128)(2,1)S(1)} %get-tuple-element.39), channel_id=1, source_target_pairs={{0,4},{1,5},{2,6},{3,7},{4,0},{5,1},{6,2},{7,3},{8,12},{9,13},{10,... | collective-permute-start | bytes 221192 | tf_op jit(solution)/shard_map/ppermute | solution.py:238
  37.7 4.4 %collective-permute-start.12 = (bf16[18,16,128]{2,1,0:T(8,128)(2,1)S(1)}, bf16[18,16,128]{2,1,0:T(8,128)(2,1)S(1)}, u32[]{:S(2)}, u32[]{:S(2)}) collective-permute-start(bf16[18,16,128]{2,1,0:T(8,128)(2,1)S(1)} %get-tuple-element.39), channel_id=1, source_target_pairs={{0,2},{1,3},{2,0},{3,1},{4,6},{5,7},{6,4},{7,5},{8,10},{9,11},{10,... | collective-permute-start | bytes 221192 | tf_op jit(solution)/shard_map/ppermute | solution.py:238
  38.1 12.0 %collective-permute-start.16 = (bf16[14,128,128]{2,1,0:T(8,128)(2,1)S(1)}, bf16[14,128,128]{2,1,0:T(8,128)(2,1)S(1)}, u32[]{:S(2)}, u32[]{:S(2)}) collective-permute-start(bf16[14,128,128]{2,1,0:T(8,128)(2,1)S(1)} %collective-permute-done.11.ins__tiles___0__1_), channel_id=1, source_target_pairs={{0,1},{1,0},{2,3},{3,2},{4,5},{5,4},{6,7},{7,6},{8,9},{9,8},{10,11... | collective-permute-start | bytes 1376264 | tf_op jit(solution)/shard_map/ppermute | solution.py:234
  42.2 6.6 %collective-permute-start.15 = (bf16[24,16,128]{2,1,0:T(8,128)(2,1)S(1)}, bf16[24,16,128]{2,1,0:T(8,128)(2,1)S(1)}, u32[]{:S(2)}, u32[]{:S(2)}) collective-permute-start(bf16[24,16,128]{2,1,0:T(8,128)(2,1)S(1)} %constant_dynamic-update-slice_fusion.4.ins__sent__), channel_id=1, source_target_pairs={{0,8},{1,9},{2,10},{3,11},{4,12},{5,13},{6,14},{7,15},{8,0},{9,1},... | collective-permute-start | bytes 294920 | tf_op jit(solution)/shard_map/ppermute | solution.py:238
  48.8 2.1 %collective-permute-start.18 = (bf16[19,128,128]{2,1,0:T(8,128)(2,1)S(1)}, bf16[19,128,128]{2,1,0:T(8,128)(2,1)S(1)}, u32[]{:S(2)}, u32[]{:S(2)}) collective-permute-start(bf16[19,128,128]{2,1,0:T(8,128)(2,1)S(1)} %collective-permute-done.17.ins__tiles___0__0_), channel_id=1, source_target_pairs={{0,1},{1,0},{2,3},{3,2},{4,5},{5,4},{6,7},{7,6},{8,9},{9,8},{10,11... | collective-permute-start | bytes 1867784 | tf_op jit(solution)/shard_map/ppermute | solution.py:234
  52.4 5.8 %collective-permute-start.21 = (bf16[16,16,128]{2,1,0:T(8,128)(2,1)S(1)}, bf16[16,16,128]{2,1,0:T(8,128)(2,1)S(1)}, u32[]{:S(2)}, u32[]{:S(2)}) collective-permute-start(bf16[16,16,128]{2,1,0:T(8,128)(2,1)S(1)} %get-tuple-element.47), channel_id=1, source_target_pairs={{0,6},{1,7},{2,4},{3,5},{4,2},{5,3},{6,0},{7,1},{8,14},{9,15},{10,... | collective-permute-start | bytes 196616 | tf_op jit(solution)/shard_map/ppermute | solution.py:238
  52.5 5.7 %collective-permute-start.20 = (bf16[16,16,128]{2,1,0:T(8,128)(2,1)S(1)}, bf16[16,16,128]{2,1,0:T(8,128)(2,1)S(1)}, u32[]{:S(2)}, u32[]{:S(2)}) collective-permute-start(bf16[16,16,128]{2,1,0:T(8,128)(2,1)S(1)} %get-tuple-element.47), channel_id=1, source_target_pairs={{0,4},{1,5},{2,6},{3,7},{4,0},{5,1},{6,2},{7,3},{8,12},{9,13},{10,... | collective-permute-start | bytes 196616 | tf_op jit(solution)/shard_map/ppermute | solution.py:238
  54.3 4.6 %collective-permute-start.19 = (bf16[16,16,128]{2,1,0:T(8,128)(2,1)S(1)}, bf16[16,16,128]{2,1,0:T(8,128)(2,1)S(1)}, u32[]{:S(2)}, u32[]{:S(2)}) collective-permute-start(bf16[16,16,128]{2,1,0:T(8,128)(2,1)S(1)} %get-tuple-element.47), channel_id=1, source_target_pairs={{0,2},{1,3},{2,0},{3,1},{4,6},{5,7},{6,4},{7,5},{8,10},{9,11},{10,... | collective-permute-start | bytes 196616 | tf_op jit(solution)/shard_map/ppermute | solution.py:238
  55.9 5.3 %collective-permute-start.8 = (bf16[16,16,128]{2,1,0:T(8,128)(2,1)S(1)}, bf16[16,16,128]{2,1,0:T(8,128)(2,1)S(1)}, u32[]{:S(2)}, u32[]{:S(2)}) collective-permute-start(bf16[16,16,128]{2,1,0:T(8,128)(2,1)S(1)} %get-tuple-element.32), channel_id=1, source_target_pairs={{0,16},{16,0},{1,17},{17,1},{2,18},{18,2},{3,19},{19,3},{4,20},{20... | collective-permute-start | bytes 196616 | tf_op jit(solution)/shard_map/ppermute | solution.py:244
  58.9 5.6 %collective-permute-start.22 = (bf16[16,16,128]{2,1,0:T(8,128)(2,1)S(1)}, bf16[16,16,128]{2,1,0:T(8,128)(2,1)S(1)}, u32[]{:S(2)}, u32[]{:S(2)}) collective-permute-start(bf16[16,16,128]{2,1,0:T(8,128)(2,1)S(1)} %get-tuple-element.57), channel_id=1, source_target_pairs={{0,8},{1,9},{2,10},{3,11},{4,12},{5,13},{6,14},{7,15},{8,0},{9,1},... | collective-permute-start | bytes 196616 | tf_op jit(solution)/shard_map/ppermute | solution.py:238
  66.8 5.2 %collective-permute-start.25 = (bf16[16,16,128]{2,1,0:T(8,128)(2,1)S(1)}, bf16[16,16,128]{2,1,0:T(8,128)(2,1)S(1)}, u32[]{:S(2)}, u32[]{:S(2)}) collective-permute-start(bf16[16,16,128]{2,1,0:T(8,128)(2,1)S(1)} %get-tuple-element.51), channel_id=1, source_target_pairs={{0,6},{1,7},{2,4},{3,5},{4,2},{5,3},{6,0},{7,1},{8,14},{9,15},{10,... | collective-permute-start | bytes 196616 | tf_op jit(solution)/shard_map/ppermute | solution.py:238
  67.3 5.1 %collective-permute-start.24 = (bf16[16,16,128]{2,1,0:T(8,128)(2,1)S(1)}, bf16[16,16,128]{2,1,0:T(8,128)(2,1)S(1)}, u32[]{:S(2)}, u32[]{:S(2)}) collective-permute-start(bf16[16,16,128]{2,1,0:T(8,128)(2,1)S(1)} %get-tuple-element.51), channel_id=1, source_target_pairs={{0,4},{1,5},{2,6},{3,7},{4,0},{5,1},{6,2},{7,3},{8,12},{9,13},{10,... | collective-permute-start | bytes 196616 | tf_op jit(solution)/shard_map/ppermute | solution.py:238
  69.5 4.3 %collective-permute-start.23 = (bf16[16,16,128]{2,1,0:T(8,128)(2,1)S(1)}, bf16[16,16,128]{2,1,0:T(8,128)(2,1)S(1)}, u32[]{:S(2)}, u32[]{:S(2)}) collective-permute-start(bf16[16,16,128]{2,1,0:T(8,128)(2,1)S(1)} %get-tuple-element.51), channel_id=1, source_target_pairs={{0,2},{1,3},{2,0},{3,1},{4,6},{5,7},{6,4},{7,5},{8,10},{9,11},{10,... | collective-permute-start | bytes 196616 | tf_op jit(solution)/shard_map/ppermute | solution.py:238
  73.8 5.4 %collective-permute-start.26 = (bf16[16,16,128]{2,1,0:T(8,128)(2,1)S(1)}, bf16[16,16,128]{2,1,0:T(8,128)(2,1)S(1)}, u32[]{:S(2)}, u32[]{:S(2)}) collective-permute-start(bf16[16,16,128]{2,1,0:T(8,128)(2,1)S(1)} %get-tuple-element.55), channel_id=1, source_target_pairs={{0,8},{1,9},{2,10},{3,11},{4,12},{5,13},{6,14},{7,15},{8,0},{9,1},... | collective-permute-start | bytes 196616 | tf_op jit(solution)/shard_map/ppermute | solution.py:238
  80.1 1.4 %collective-permute-start.27 = (f32[16,2048]{1,0:T(8,128)S(1)}, f32[16,2048]{1,0:T(8,128)S(1)}, u32[]{:S(2)}, u32[]{:S(2)}) collective-permute-start(f32[16,2048]{1,0:T(8,128)S(1)} %get-tuple-element.54), channel_id=1, source_target_pairs={{0,1},{1,0},{2,3},{3,2},{4,5},{5,4},{6,7},{7,6},{8,9},{9,8},{10,11... | collective-permute-start | bytes 393224 | tf_op jit(solution)/shard_map/ppermute | solution.py:234
